TPU v7x, 128 devices: a whole 4x4x4 slice. The times are simulated.
128 devices in a mesh: gx: 8 (over x, core), yz: 16 (over y, z).
Axes of the slice: x: 4, y: 4, z: 4, core: 2. Of those that a mesh axis runs over, the one named last changes fastest.
Arguments:
- tokens: bfloat16 [512, 2, 18432], P('yz', None, 'gx'), may hold values from -15 to 15
- gain: float32 [18432], P('gx'), may hold values from 0.25 to 1.75
- w_query: bfloat16 [18432, 12288], P('gx', 'yz'), may hold values from -0.046875 to 0.046875
- w_keyval: bfloat16 [18432, 512], P('gx'), may hold values from -0.046875 to 0.046875
- w_out: bfloat16 [12288, 18432], P('yz', 'gx'), may hold values from -0.21875 to 0.21875
- key_cache: bfloat16 [512, 2048, 256], P(('gx', 'yz')), may hold values from -256 to 256
- value_cache: bfloat16 [512, 2048, 256], P(('gx', 'yz')), may hold values from -5 to 5
- lengths: int32 [512], P(('gx', 'yz')), may hold values from 1 to 2048, as said below
Outputs:
- mixed: bfloat16 [512, 2, 18432], P('yz', None, 'gx')
- new_keyval: bfloat16 [512, 2, 512], P(('gx', 'yz'))
Inputs may be any that keep to these rules, and one draw needn't show every extreme that they name: `lengths`: each sequence has this many filled cache positions from the start; its two new tokens stand at this position and the next; in every draw some sequence fills all 2048.
All inputs are finite; a program needn't handle non-finite values.
Results may differ from a plain program's by a relative error of at most 0.009.
The roundings to bfloat16 on the way count: a program that leaves them out, or rounds other values in their place, can miss the bound.
Values may be sent and summed in bfloat16 or wider, within the bound.
No kernel may reach another device: no remote copies, remote signals or barrier semaphores. Data moves between devices by JAX's collectives and lax.ppermute only.
A program may use at most 128 MiB of HBM per device.

v0:
```python
import functools

import jax
import jax.numpy as jnp
from jax import lax
from jax.experimental import pallas as pl
from jax.experimental.pallas import tpu as pltpu
from jax.sharding import PartitionSpec as P

D = 18432
HEADS = 48
HEAD = 256
RING = 4
F32 = jnp.float32
BF16 = jnp.bfloat16


def shift(value, move):
    pairs = []
    for x in range(RING):
        for core in range(2):
            for y in range(RING):
                for z in range(RING):
                    dx, dy, dz = move(core)
                    target = (2 * ((x + dx) % RING) + core) * 16
                    target += RING * ((y + dy) % RING) + (z + dz) % RING
                    pairs.append(((2 * x + core) * 16 + RING * y + z, target))
    return lax.ppermute(value, ("gx", "yz"), pairs)


def send_core(value):
    pairs = [(2 * x + c, 2 * x + 1 - c) for x in range(RING) for c in range(2)]
    return lax.ppermute(value, "gx", pairs)


def send_x(value, step):
    return shift(value, lambda core: ((1 - 2 * core) * step, 0, 0))


def send_ahead(value, step):
    return shift(value, lambda core: (step, 0, 0))


def send_inner(value, step):
    return shift(value, lambda core: (0, core * step, (1 - core) * step))


def send_outer(value, step):
    return shift(value, lambda core: (0, (1 - core) * step, core * step))


def rotation_tables(positions):
    half = HEAD // 2
    freq = 10000.0 ** (-jnp.arange(half, dtype=F32) * 2.0 / HEAD)
    angle = positions.astype(F32)[..., None] * freq
    return jnp.cos(angle), jnp.sin(angle)


def stage_kernel(count, *refs):
    sources, targets, sems = refs[:count], refs[count : 2 * count], refs[2 * count]
    copies = []
    for index, (source, target) in enumerate(zip(sources, targets)):
        size = source.shape[0] // 4
        for part in range(4):
            at = pl.ds(part * size, size)
            copies.append(
                pltpu.make_async_copy(source.at[at], target.at[at], sems.at[index, part])
            )
    for copy in copies:
        copy.start()
    for copy in copies:
        copy.wait()


def stage(*arrays):
    count = len(arrays)
    size = sum(a.size * a.dtype.itemsize for a in arrays)
    return pl.pallas_call(
        functools.partial(stage_kernel, count),
        out_shape=[jax.ShapeDtypeStruct(a.shape, a.dtype) for a in arrays],
        in_specs=[pl.BlockSpec(memory_space=pl.ANY)] * count,
        out_specs=[pl.BlockSpec(memory_space=pltpu.VMEM)] * count,
        scratch_shapes=[pltpu.SemaphoreType.DMA((count, 4))],
        compiler_params=pltpu.CompilerParams(vmem_limit_bytes=20 * 2**20),
        cost_estimate=pl.CostEstimate(flops=0, bytes_accessed=2 * size, transcendentals=0),
        name="stage",
    )(*arrays)


def query_kernel(other, place, *refs):
    pieces, (w_ref, out_ref, rows_ref, sems) = refs[:8], refs[8:]
    x, y, z, core = place[0], place[1], place[2], place[3]
    for index, piece in enumerate(pieces):
        for part in range(2):
            outer = (0, 3, 1, 2)[index % 4]
            inner = ((0, 3), (1, 2))[index // 4][part]
            at_y = lax.rem(y + jnp.where(core == 0, outer, inner), RING)
            at_z = lax.rem(z + jnp.where(core == 0, inner, outer), RING)
            to_core = at_z // 2
            ahead = lax.rem(at_y - x + RING, RING)
            slot = jnp.where(to_core == 0, ahead, lax.rem(RING - ahead, RING))
            position = slot * 2 + lax.rem(at_z, 2)
            copy = pltpu.make_async_copy(
                piece.at[part * 64 : (part + 1) * 64], rows_ref.at[position], sems.at[position]
            )
            pl.when((to_core != core) == other)(copy.start)
    for m in range(2):
        for position in range(4 * m, 4 * m + 4):
            pltpu.make_async_copy(
                pieces[0].at[0:64], rows_ref.at[position], sems.at[position]
            ).wait()
        rows = rows_ref[4 * m : 4 * m + 4].reshape(256, w_ref.shape[0])
        out_ref[m * 256 : (m + 1) * 256, :] = jnp.dot(
            rows, w_ref[...], preferred_element_type=F32
        )


def project_query(place, pieces, w_query, other):
    depth, columns = w_query.shape
    vmem_spec = pl.BlockSpec(memory_space=pltpu.VMEM)
    return pl.pallas_call(
        functools.partial(query_kernel, other),
        out_shape=jax.ShapeDtypeStruct((512, columns), F32),
        in_specs=[pl.BlockSpec(memory_space=pltpu.SMEM)]
        + [pl.BlockSpec(memory_space=pl.ANY)] * 8
        + [vmem_spec],
        out_specs=vmem_spec,
        scratch_shapes=[pltpu.VMEM((8, 64, depth), BF16), pltpu.SemaphoreType.DMA((8,))],
        compiler_params=pltpu.CompilerParams(vmem_limit_bytes=20 * 2**20),
        cost_estimate=pl.CostEstimate(
            flops=2 * 512 * depth * columns, bytes_accessed=8 * 2**20, transcendentals=0
        ),
        name="query_projection",
    )(place, *pieces, w_query)


def attend_kernel(
    lengths, q_ref, cos_ref, sin_ref, new_ref, k_hbm, v_hbm, out_ref, acc_ref, k_ref, v_ref, sems
):
    loads = []
    for r in range(k_ref.shape[0]):
        loads.append(pltpu.make_async_copy(k_hbm.at[r], k_ref.at[r], sems.at[0, r]))
        loads.append(pltpu.make_async_copy(v_hbm.at[r], v_ref.at[r], sems.at[1, r]))
    for load in loads[:4]:
        load.start()
    half = HEAD // 2
    rows = q_ref.shape[0]
    scale = HEAD ** (-0.5)
    contract_last = (((1,), (1,)), ((), ()))
    pick_row = lax.broadcasted_iota(jnp.int32, (32, rows), 0)
    pick_col = lax.broadcasted_iota(jnp.int32, (32, rows), 1)
    odd = lax.rem(lax.broadcasted_iota(jnp.int32, (32, half), 0), 2) == 1
    second_step = lax.rem(lax.broadcasted_iota(jnp.int32, (96, 1), 0), 2) == 1
    for r in range(k_ref.shape[0]):
        pick = (pick_col == (pick_row // 2) * 8 + 2 * r + lax.rem(pick_row, 2)).astype(BF16)
        cosine = jnp.where(odd, cos_ref[r, 1:2, :], cos_ref[r, 0:1, :])
        sine = jnp.where(odd, sin_ref[r, 1:2, :], sin_ref[r, 0:1, :])
        parts = []
        for h in range(3):
            chosen = jnp.dot(pick, q_ref[:, h * HEAD : (h + 1) * HEAD], preferred_element_type=F32)
            first, second = chosen[:, :half], chosen[:, half:]
            parts.append(
                jnp.concatenate([first * cosine - second * sine, second * cosine + first * sine], 1)
            )
        query = jnp.concatenate(parts, 0).astype(BF16)
        loads[2 * r].wait()
        for load in loads[2 * r + 4 : 2 * r + 6]:
            load.start()
        cached = lax.dot_general(query, k_ref[r], contract_last, preferred_element_type=F32) * scale
        valid = lax.broadcasted_iota(jnp.int32, cached.shape, 1) < lengths[r]
        cached = jnp.where(valid, cached, -jnp.inf)
        new = new_ref[r].astype(F32)
        wide = query.astype(F32)
        fresh0 = jnp.sum(wide * new[0:1, :HEAD], -1, keepdims=True) * scale
        fresh1 = jnp.sum(wide * new[1:2, :HEAD], -1, keepdims=True) * scale
        fresh1 = jnp.where(second_step, fresh1, -jnp.inf)
        top = jnp.maximum(jnp.max(cached, -1, keepdims=True), jnp.maximum(fresh0, fresh1))
        exp_cached = jnp.exp(cached - top)
        exp0 = jnp.exp(fresh0 - top)
        exp1 = jnp.exp(fresh1 - top)
        inverse = 1.0 / (jnp.sum(exp_cached, -1, keepdims=True) + exp0 + exp1)
        weights = (exp_cached * inverse).astype(BF16)
        weight0 = (exp0 * inverse).astype(BF16).astype(F32)
        weight1 = (exp1 * inverse).astype(BF16).astype(F32)
        loads[2 * r + 1].wait()
        result = jnp.dot(weights, v_ref[r], preferred_element_type=F32)
        result = result + weight0 * new[0:1, HEAD:] + weight1 * new[1:2, HEAD:]
        result = result.astype(BF16)
        for h in range(3):
            spread = lax.dot_general(
                pick,
                result[h * 32 : (h + 1) * 32],
                (((0,), (0,)), ((), ())),
                preferred_element_type=F32,
            )
            columns = slice(h * HEAD, (h + 1) * HEAD)
            if r == 0:
                acc_ref[:, columns] = spread
            else:
                acc_ref[:, columns] += spread
    out_ref[...] = acc_ref[...].astype(BF16)


def attend(lengths, query, cosine, sine, new_keyval, keys, values):
    seqs, context, _ = keys.shape
    rows, columns = query.shape
    vmem_spec = pl.BlockSpec(memory_space=pltpu.VMEM)
    return pl.pallas_call(
        attend_kernel,
        out_shape=jax.ShapeDtypeStruct((rows, columns), BF16),
        in_specs=[pl.BlockSpec(memory_space=pltpu.SMEM)]
        + [vmem_spec] * 4
        + [pl.BlockSpec(memory_space=pltpu.HBM)] * 2,
        out_specs=vmem_spec,
        scratch_shapes=[
            pltpu.VMEM((rows, columns), F32),
            pltpu.VMEM(keys.shape, BF16),
            pltpu.VMEM(values.shape, BF16),
            pltpu.SemaphoreType.DMA((2, seqs)),
        ],
        compiler_params=pltpu.CompilerParams(vmem_limit_bytes=54 * 2**20),
        cost_estimate=pl.CostEstimate(
            flops=4 * seqs * 96 * context * HEAD,
            bytes_accessed=4 * seqs * context * HEAD,
            transcendentals=seqs * 96 * context,
        ),
        name="attention",
    )(lengths, query, cosine, sine, new_keyval, keys, values)


def output_kernel(groups, place, *refs):
    pieces, (w_ref, *outs), rows_ref = refs[:8], refs[8:-1], refs[-1]
    x, y, z, core = place[0], place[1], place[2], place[3]
    for index, piece in enumerate(pieces):
        at_core = core if index < 4 else 1 - core
        slot = (0, 3, 1, 2)[index % 4]
        ahead = jnp.where(at_core == 0, slot, (RING - slot) % RING)
        dy = lax.rem(x + ahead - y + RING, RING)
        for part in range(2):
            dz = lax.rem(2 * at_core + part - z + RING, RING)
            outer, inner = jnp.where(core == 0, dy, dz), jnp.where(core == 0, dz, dy)
            for position, group in enumerate(groups):

                @pl.when(outer == group)
                def _():
                    rows_ref[position * RING + inner] = piece[part * 64 : (part + 1) * 64, :]

    outs = list(outs)
    for position, group in enumerate(groups):
        rows = rows_ref[RING * position : RING * position + RING].reshape(256, w_ref.shape[0])
        targets = [outs.pop(0)] if group == 0 else [outs.pop(0), outs.pop(0)]
        for start in range(0, w_ref.shape[1], 768):
            columns = slice(start, start + 768)
            result = jnp.dot(rows, w_ref[:, columns], preferred_element_type=F32)
            if group == 0:
                targets[0][:, columns] = result
            else:
                targets[0][:, columns] = result[:128].astype(BF16)
                targets[1][:, columns] = result[128:].astype(BF16)


def project_output(place, pieces, w_out, groups):
    depth, columns = w_out.shape
    vmem_spec = pl.BlockSpec(memory_space=pltpu.VMEM)
    shapes = []
    for group in groups:
        if group == 0:
            shapes.append(jax.ShapeDtypeStruct((256, columns), F32))
        else:
            shapes += [jax.ShapeDtypeStruct((128, columns), BF16)] * 2
    return pl.pallas_call(
        functools.partial(output_kernel, groups),
        out_shape=shapes,
        in_specs=[pl.BlockSpec(memory_space=pltpu.SMEM)] + [vmem_spec] * 9,
        out_specs=[vmem_spec] * len(shapes),
        scratch_shapes=[pltpu.VMEM((RING * len(groups), 64, depth), BF16)],
        compiler_params=pltpu.CompilerParams(vmem_limit_bytes=20 * 2**20),
        cost_estimate=pl.CostEstimate(
            flops=2 * 256 * len(groups) * depth * columns,
            bytes_accessed=8 * 2**20,
            transcendentals=0,
        ),
        name="output_projection",
    )(place, *pieces, w_out)


def body(tokens, gain, w_query, w_keyval, w_out, key_cache, value_cache, lengths):
    seqs = lengths.shape[0]
    gx, yz = lax.axis_index("gx"), lax.axis_index("yz")
    place = jnp.stack([gx // 2, yz // RING, lax.rem(yz, RING), lax.rem(gx, 2)]).astype(jnp.int32)
    positions = lengths[:, None] + jnp.arange(2, dtype=jnp.int32)[None, :]
    cosine, sine = rotation_tables(positions)

    count = tokens.shape[0] * 2
    features = tokens.shape[2]
    xfull = tokens.reshape(count, features).astype(F32)
    stats = jnp.stack([jnp.sum(xfull, -1), jnp.sum(xfull * xfull, -1)])
    stats = stats + send_core(stats)
    stats = stats + send_x(stats, 1) + send_x(stats, 2) + send_x(stats, 3)
    mean = stats[0] / D
    var = stats[1] / D - mean * mean
    normed = ((xfull - mean[:, None]) * lax.rsqrt(var + 1e-05)[:, None] * gain).astype(BF16)

    normed = lax.optimization_barrier(normed)
    keyval = lax.optimization_barrier(jnp.dot(normed, w_keyval, preferred_element_type=F32))

    before = send_inner(normed, 1)
    after = send_inner(normed, -1)
    far = send_inner(before, 1)
    near = jnp.concatenate([normed, before], 0)
    near, keyval = lax.optimization_barrier((near, keyval))
    wide = jnp.concatenate([after, far], 0)
    near_before, near_after = send_outer(near, 1), send_outer(near, -1)
    near_before, near_after = lax.optimization_barrier((near_before, near_after))
    wide_before, wide_after = send_outer(wide, 1), send_outer(wide, -1)
    near_far = send_outer(near_before, 1)
    near_far, wide_after = lax.optimization_barrier((near_far, wide_after))
    wide_far = send_outer(wide_after, -1)

    blocks = keyval.reshape(RING, 2, count // 8, 2 * HEAD)
    blocks = lax.dynamic_slice_in_dim(jnp.concatenate([blocks, blocks], 0), place[0], RING, 0)
    kept = lax.dynamic_index_in_dim(blocks, place[3], 1, keepdims=False)
    kept = kept + send_core(lax.dynamic_index_in_dim(blocks, 1 - place[3], 1, keepdims=False))
    keyval = kept[0] + send_ahead(kept[1], 1) + send_ahead(kept[2], 2) + send_ahead(kept[3], 3)
    keyval = keyval.astype(BF16)
    moves = [
        (g * 16 + j, (j // 2) * 16 + (j % 2) * 8 + g) for g in range(8) for j in range(16)
    ]
    keyval = lax.ppermute(keyval, ("gx", "yz"), moves).reshape(seqs, 2, 2 * HEAD)
    first = keyval[..., : HEAD // 2].astype(F32)
    second = keyval[..., HEAD // 2 : HEAD].astype(F32)
    new_keyval = jnp.concatenate(
        [
            (first * cosine - second * sine).astype(BF16),
            (second * cosine + first * sine).astype(BF16),
            keyval[..., HEAD:],
        ],
        -1,
    )

    pieces = [near, near_before, near_after, near_far, wide, wide_before, wide_after, wide_far]
    columns = w_query.shape[1]
    staged_query = stage(w_query)[0]
    pieces, new_keyval, staged_query = lax.optimization_barrier((pieces, new_keyval, staged_query))
    away = project_query(place, pieces, staged_query, True)
    keep = project_query(place, pieces, staged_query, False)
    summed = (keep + send_core(away)).reshape(RING, 128, columns)
    far = send_x(summed[2], 1)
    behind = send_x(summed[3], -1)
    ahead = send_x(summed[1] + far, 1)
    query = (summed[0] + ahead + behind).astype(BF16).reshape(16, 8, columns)
    query = lax.all_to_all(query, "yz", split_axis=0, concat_axis=0)

    heads_out = attend(
        lengths, query.reshape(128, columns), cosine, sine, new_keyval, key_cache, value_cache
    )
    heads_out = lax.all_to_all(
        heads_out.reshape(16, 8, columns), "yz", split_axis=0, concat_axis=0
    ).reshape(128, columns)
    before = send_x(heads_out, 1)
    after = send_x(heads_out, -1)
    pieces = [heads_out, before, after, send_x(before, 1)]
    pieces = pieces + [send_core(p) for p in pieces]
    two_low, two_high = project_output(place, pieces, w_out, (2,))
    one_low, one_high, three_low, three_high, own = project_output(
        place, pieces, w_out, (1, 3, 0)
    )

    far_low, far_high = send_outer(two_low, 1), send_outer(two_high, -1)
    far_low, far_high = lax.optimization_barrier((far_low, far_high))
    early_high, early_low = send_outer(one_high, 1), send_outer(three_low, -1)
    late_low = send_outer((one_low.astype(F32) + far_low.astype(F32)).astype(BF16), 1)
    late_high = send_outer((three_high.astype(F32) + far_high.astype(F32)).astype(BF16), -1)
    low = own[:128] + early_low.astype(F32) + late_low.astype(F32)
    high = own[128:] + early_high.astype(F32) + late_high.astype(F32)
    here, one, two, three = low[:64], low[64:], high[:64], high[64:]
    far_low, far_high = send_inner(two[:32], 1), send_inner(two[32:], -1)
    early_high, early_low = send_inner(one[32:], 1), send_inner(three[:32], -1)
    late_low = send_inner(one[:32] + far_low, 1)
    late_high = send_inner(three[32:] + far_high, -1)
    branch = here + jnp.concatenate([early_low + late_low, early_high + late_high], 0)
    mixed = (xfull + branch).astype(BF16).reshape(tokens.shape)
    return (mixed, new_keyval)


def solution(mesh):
    return jax.shard_map(
        body,
        mesh=mesh,
        in_specs=(
            P("yz", None, "gx"),
            P("gx"),
            P("gx", "yz"),
            P("gx", None),
            P("yz", "gx"),
            P(("gx", "yz"), None, None),
            P(("gx", "yz"), None, None),
            P(("gx", "yz")),
        ),
        out_specs=(P("yz", None, "gx"), P(("gx", "yz"), None, None)),
        check_vma=False,
    )
```

profile of v0, /device:TPU:0, one launch (start us, length us, event | category | flops | bytes accessed | tf_op | source)
XLA Modules:
  0.0 197.0 jit_solution(12090311764883702246)
XLA Ops:
  3.8 3.2 %collective-permute-start.2 = (f32[2,64]{1,0:T(2,128)S(1)}, f32[2,64]{1,0:T(2,128)S(1)}, u32[]{:S(2)}, u32[]{:S(2)}) collective-permute-start(f32[2,64]{1,0:T(2,128)S(1)} %fusion.20), channel_id=1, source_target_pairs={{0,64},{1,65},{2,66},{3,67},{4,68},{5,69},{6,70},{7,71},{8,72},{9,... | collective-permute-start | bytes 1544 | tf_op jit(solution)/shard_map/ppermute | solution.py:28
  17.8 4.2 %collective-permute-done.4 = bf16[64,2304]{1,0:T(8,128)(2,1)} collective-permute-done((bf16[64,2304]{1,0:T(8,128)(2,1)S(1)}, bf16[64,2304]{1,0:T(8,128)(2,1)}, u32[]{:S(2)}, u32[]{:S(2)}) %collective-permute-start.4) | collective-permute-done | bytes 294944 | tf_op jit(solution)/shard_map/ppermute | solution.py:28
  23.0 3.1 %collective-permute-start.6 = (bf16[128,2304]{1,0:T(8,128)(2,1)S(1)}, bf16[128,2304]{1,0:T(8,128)(2,1)S(1)}, u32[]{:S(2)}, u32[]{:S(2)}) collective-permute-start(bf16[128,2304]{1,0:T(8,128)(2,1)S(1)} %pad_maximum_fusion.refs_0_), channel_id=1, source_target_pairs={{0,12},{1,13},{2,14},{3,15},{4,0},{5,1},{6,2},{7,3},{8,4},{9,5},{1... | collective-permute-start | bytes 1769480 | tf_op jit(solution)/shard_map/ppermute | solution.py:28
  26.8 9.5 %collective-permute-done.9 = bf16[64,2304]{1,0:T(8,128)(2,1)S(1)} collective-permute-done((bf16[64,2304]{1,0:T(8,128)(2,1)}, bf16[64,2304]{1,0:T(8,128)(2,1)S(1)}, u32[]{:S(2)}, u32[]{:S(2)}) %collective-permute-start.9) | collective-permute-done | bytes 294944 | tf_op jit(solution)/shard_map/ppermute | solution.py:28
  43.3 3.2 %collective-permute-start.16 = (f32[8,512]{1,0:T(8,128)}, f32[8,512]{1,0:T(8,128)}, u32[]{:S(2)}, u32[]{:S(2)}) collective-permute-start(f32[8,512]{1,0:T(8,128)} %get-tuple-element.64), channel_id=1, source_target_pairs={{0,96},{1,97},{2,98},{3,99},{4,100},{5,101},{6,102},{7,103},{8,104... | collective-permute-start | bytes 49160 | tf_op jit(solution)/shard_map/ppermute | solution.py:28
  47.0 4.8 %collective-permute-done.7.refs_3_ = bf16[128,2304]{1,0:T(8,128)(2,1)} collective-permute-done((bf16[128,2304]{1,0:T(8,128)(2,1)}, bf16[128,2304]{1,0:T(8,128)(2,1)}, u32[]{:S(2)}, u32[]{:S(2)}) %collective-permute-start.7) | collective-permute-done | bytes 589856 | tf_op jit(solution)/shard_map/ppermute | solution.py:28
  65.1 4.8 %query_projection.3 = f32[512,768]{1,0:T(8,128)S(1)} custom-call(s32[4]{0:T(128)S(1)} %pad_add_fusion.place, bf16[128,2304]{1,0:T(8,128)(2,1)S(1)} %pad_maximum_fusion.refs_0_, bf16[128,2304]{1,0:T(8,128)(2,1)} %collective-permute-done.5.refs_1_, bf16[128,2304]{1,0:T(8,128)(2,1)S(1)} %copy-done.6, bf16[128,2304]{1,0:T(8,128)(2,1)} %collective-permute-done.7.refs_3_, ...), custom_call_target="tpu_custom_call" | custom-call | flops 1811939328 | bytes 8388608 | tf_op jit(solution)/shard_map/query_projection/pallas_call | solution.py:121
  70.1 5.0 %query_projection.2 = f32[512,768]{1,0:T(8,128)S(1)} custom-call(s32[4]{0:T(128)S(1)} %pad_add_fusion.place, bf16[128,2304]{1,0:T(8,128)(2,1)S(1)} %pad_maximum_fusion.refs_0_, bf16[128,2304]{1,0:T(8,128)(2,1)} %collective-permute-done.5.refs_1_, bf16[128,2304]{1,0:T(8,128)(2,1)S(1)} %copy-done.6, bf16[128,2304]{1,0:T(8,128)(2,1)} %collective-permute-done.7.refs_3_, ...), custom_call_target="tpu_custom_call" | custom-call | flops 1811939328 | bytes 8388608 | tf_op jit(solution)/shard_map/query_projection/pallas_call | solution.py:121
  75.4 3.8 %collective-permute-start.19 = (f32[128,768]{1,0:T(8,128)S(1)}, f32[128,768]{1,0:T(8,128)S(1)}, u32[]{:S(2)}, u32[]{:S(2)}) collective-permute-start(f32[128,768]{1,0:T(8,128)S(1)} %slice.110), channel_id=1, source_target_pairs={{0,32},{1,33},{2,34},{3,35},{4,36},{5,37},{6,38},{7,39},{8,40},{9,... | collective-permute-start | bytes 1179656 | tf_op jit(solution)/shard_map/ppermute | solution.py:28
  79.2 7.7 %collective-permute-done.19 = f32[128,768]{1,0:T(8,128)S(1)} collective-permute-done((f32[128,768]{1,0:T(8,128)S(1)}, f32[128,768]{1,0:T(8,128)S(1)}, u32[]{:S(2)}, u32[]{:S(2)}) %collective-permute-start.19) | collective-permute-done | bytes 393248 | tf_op jit(solution)/shard_map/ppermute | solution.py:28
  87.1 3.2 %collective-permute-start.21 = (f32[128,768]{1,0:T(8,128)S(1)}, f32[128,768]{1,0:T(8,128)S(1)}, u32[]{:S(2)}, u32[]{:S(2)}) collective-permute-start(f32[128,768]{1,0:T(8,128)S(1)} %get-tuple-element.57), channel_id=1, source_target_pairs={{0,96},{1,97},{2,98},{3,99},{4,100},{5,101},{6,102},{7,103},{8,104... | collective-permute-start | bytes 1179656 | tf_op jit(solution)/shard_map/ppermute | solution.py:28
  90.3 8.4 %collective-permute-done.20 = f32[128,768]{1,0:T(8,128)S(1)} collective-permute-done((f32[128,768]{1,0:T(8,128)S(1)}, f32[128,768]{1,0:T(8,128)S(1)}, u32[]{:S(2)}, u32[]{:S(2)}) %collective-permute-start.20) | collective-permute-done | bytes 393248 | tf_op jit(solution)/shard_map/ppermute | solution.py:28
  98.8 14.7 %all_to_all.10 = bf16[16,8,768]{2,1,0:T(8,128)(2,1)} all-to-all(bf16[16,8,768]{2,1,0:T(8,128)(2,1)S(1)} %fusion.4), channel_id=1, replica_groups=mesh['gx'=8,'yz'=16] {'yz'}, dimensions={0} | all-to-all | bytes 393216 | tf_op jit(solution)/shard_map/all_to_all | solution.py:352
  113.5 8.8 %attention.1 = bf16[128,768]{1,0:T(8,128)(2,1)} custom-call(s32[4]{0:T(128)} %lengths.1, bf16[128,768]{1,0:T(8,128)(2,1)} %bitcast.51, f32[4,2,128]{2,1,0:T(2,128)} %get-tuple-element.69.cos_ref, f32[4,2,128]{2,1,0:T(2,128)} %get-tuple-element.68.sin_ref, bf16[4,2,512]{2,1,0:T(2,128)(2,1)} %pad_maximum_fusion.1.new_ref, bf16[4,2048,256]{2,1,0:T(8,128)(2,1)} %k_hbm.1, ...), custom_call_target="tpu_custom_call" | custom-call | flops 805306368 | bytes 8388608 | tf_op jit(solution)/shard_map/attention/pallas_call | solution.py:208
  122.3 11.8 %all_to_all.11 = bf16[16,8,768]{2,1,0:T(8,128)(2,1)S(1)} all-to-all(bf16[16,8,768]{2,1,0:T(8,128)(2,1)} %bitcast.52), channel_id=1, replica_groups=mesh['gx'=8,'yz'=16] {'yz'}, dimensions={0} | all-to-all | bytes 393216 | tf_op jit(solution)/shard_map/all_to_all | solution.py:357
  134.1 3.2 %collective-permute-start.23 = (bf16[128,768]{1,0:T(8,128)(2,1)S(1)}, bf16[128,768]{1,0:T(8,128)(2,1)S(1)}, u32[]{:S(2)}, u32[]{:S(2)}) collective-permute-start(bf16[128,768]{1,0:T(8,128)(2,1)S(1)} %bitcast.45), channel_id=1, source_target_pairs={{0,96},{1,97},{2,98},{3,99},{4,100},{5,101},{6,102},{7,103},{8,104... | collective-permute-start | bytes 589832 | tf_op jit(solution)/shard_map/ppermute | solution.py:28
  137.4 3.6 %collective-permute-done.22.refs_1_ = bf16[128,768]{1,0:T(8,128)(2,1)S(1)} collective-permute-done((bf16[128,768]{1,0:T(8,128)(2,1)S(1)}, bf16[128,768]{1,0:T(8,128)(2,1)S(1)}, u32[]{:S(2)}, u32[]{:S(2)}) %collective-permute-start.22) | collective-permute-done | bytes 196640 | tf_op jit(solution)/shard_map/ppermute | solution.py:28
  141.5 6.4 %collective-permute-done.24.refs_3_ = bf16[128,768]{1,0:T(8,128)(2,1)S(1)} collective-permute-done((bf16[128,768]{1,0:T(8,128)(2,1)S(1)}, bf16[128,768]{1,0:T(8,128)(2,1)S(1)}, u32[]{:S(2)}, u32[]{:S(2)}) %collective-permute-start.24) | collective-permute-done | bytes 196640 | tf_op jit(solution)/shard_map/ppermute | solution.py:28
  151.6 2.8 %collective-permute-start.31 = (bf16[128,2304]{1,0:T(8,128)(2,1)S(1)}, bf16[128,2304]{1,0:T(8,128)(2,1)S(1)}, u32[]{:S(2)}, u32[]{:S(2)}) collective-permute-start(bf16[128,2304]{1,0:T(8,128)(2,1)S(1)} %get-tuple-element.47), channel_id=1, source_target_pairs={{0,12},{1,13},{2,14},{3,15},{4,0},{5,1},{6,2},{7,3},{8,4},{9,5},{1... | collective-permute-start | bytes 1769480 | tf_op jit(solution)/shard_map/ppermute | solution.py:28
  154.5 4.0 %output_projection.2 = (bf16[128,2304]{1,0:T(8,128)(2,1)S(1)}, bf16[128,2304]{1,0:T(8,128)(2,1)S(1)}, bf16[128,2304]{1,0:T(8,128)(2,1)S(1)}, bf16[128,2304]{1,0:T(8,128)(2,1)S(1)}, f32[256,2304]{1,0:T(8,128)S(1)}) custom-call(s32[4]{0:T(128)S(1)} %pad_add_fusion.place, bf16[128,768]{1,0:T(8,128)(2,1)S(1)} %bitcast.48, ...), custom_call_target="tpu_custom_call" | custom-call | flops 2717908992 | bytes 8388608 | tf_op jit(solution)/shard_map/output_projection/pallas_call | solution.py:271
  162.8 3.2 %collective-permute-start.34 = (bf16[128,2304]{1,0:T(8,128)(2,1)S(1)}, bf16[128,2304]{1,0:T(8,128)(2,1)S(1)}, u32[]{:S(2)}, u32[]{:S(2)}) collective-permute-start(bf16[128,2304]{1,0:T(8,128)(2,1)S(1)} %add_convert_fusion), channel_id=1, source_target_pairs={{0,12},{1,13},{2,14},{3,15},{4,0},{5,1},{6,2},{7,3},{8,4},{9,5},{1... | collective-permute-start | bytes 1769480 | tf_op jit(solution)/shard_map/ppermute | solution.py:28
  169.7 6.3 %collective-permute-done.32 = bf16[128,2304]{1,0:T(8,128)(2,1)S(1)} collective-permute-done((bf16[128,2304]{1,0:T(8,128)(2,1)S(1)}, bf16[128,2304]{1,0:T(8,128)(2,1)S(1)}, u32[]{:S(2)}, u32[]{:S(2)}) %collective-permute-start.32) | collective-permute-done | bytes 589856 | tf_op jit(solution)/shard_map/ppermute | solution.py:28
  179.8 4.7 %collective-permute-done.36 = f32[32,2304]{1,0:T(8,128)S(1)} collective-permute-done((f32[32,2304]{1,0:T(8,128)S(1)}, f32[32,2304]{1,0:T(8,128)S(1)}, u32[]{:S(2)}, u32[]{:S(2)}) %collective-permute-start.36) | collective-permute-done | bytes 294944 | tf_op jit(solution)/shard_map/ppermute | solution.py:28
  184.7 3.3 %collective-permute-start.40 = (f32[32,2304]{1,0:T(8,128)S(1)}, f32[32,2304]{1,0:T(8,128)S(1)}, u32[]{:S(2)}, u32[]{:S(2)}) collective-permute-start(f32[32,2304]{1,0:T(8,128)S(1)} %slice_add_fusion.3), channel_id=1, source_target_pairs={{0,3},{1,0},{2,1},{3,2},{4,7},{5,4},{6,5},{7,6},{8,11},{9,8},{10,9... | collective-permute-start | bytes 884744 | tf_op jit(solution)/shard_map/ppermute | solution.py:28
  (133 shorter events, 62.2 us)
Async XLA Ops:
  13.1 8.9 %collective-permute-start.4 = (bf16[64,2304]{1,0:T(8,128)(2,1)S(1)}, bf16[64,2304]{1,0:T(8,128)(2,1)}, u32[]{:S(2)}, u32[]{:S(2)}) collective-permute-start(bf16[64,2304]{1,0:T(8,128)(2,1)S(1)} %multiply_convert_fusion), channel_id=1, source_target_pairs={{0,1},{1,2},{2,3},{3,0},{4,5},{5,6},{6,7},{7,4},{8,9},{9,10},{10,1... | collective-permute-start | bytes 884744 | tf_op jit(solution)/shard_map/ppermute | solution.py:28
  15.1 11.7 %collective-permute-start.8 = (bf16[64,2304]{1,0:T(8,128)(2,1)S(1)}, bf16[64,2304]{1,0:T(8,128)(2,1)S(1)}, u32[]{:S(2)}, u32[]{:S(2)}) collective-permute-start(bf16[64,2304]{1,0:T(8,128)(2,1)S(1)} %multiply_convert_fusion), channel_id=1, source_target_pairs={{0,3},{1,0},{2,1},{3,2},{4,7},{5,4},{6,5},{7,6},{8,11},{9,8},{10,9... | collective-permute-start | bytes 884744 | tf_op jit(solution)/shard_map/ppermute | solution.py:28
  23.0 15.2 %collective-permute-start.6 = (bf16[128,2304]{1,0:T(8,128)(2,1)S(1)}, bf16[128,2304]{1,0:T(8,128)(2,1)S(1)}, u32[]{:S(2)}, u32[]{:S(2)}) collective-permute-start(bf16[128,2304]{1,0:T(8,128)(2,1)S(1)} %pad_maximum_fusion.refs_0_), channel_id=1, source_target_pairs={{0,12},{1,13},{2,14},{3,15},{4,0},{5,1},{6,2},{7,3},{8,4},{9,5},{1... | collective-permute-start | bytes 1769480 | tf_op jit(solution)/shard_map/ppermute | solution.py:28
  26.1 14.4 %collective-permute-start.5 = (bf16[128,2304]{1,0:T(8,128)(2,1)S(1)}, bf16[128,2304]{1,0:T(8,128)(2,1)}, u32[]{:S(2)}, u32[]{:S(2)}) collective-permute-start(bf16[128,2304]{1,0:T(8,128)(2,1)S(1)} %pad_maximum_fusion.refs_0_), channel_id=1, source_target_pairs={{0,4},{1,5},{2,6},{3,7},{4,8},{5,9},{6,10},{7,11},{8,12},{9,13},{1... | collective-permute-start | bytes 1769480 | tf_op jit(solution)/shard_map/ppermute | solution.py:28
  26.7 14.4 %collective-permute-start.13 = (f32[4,8,512]{2,1,0:T(8,128)}, f32[4,8,512]{2,1,0:T(8,128)}, u32[]{:S(2)}, u32[]{:S(2)}) collective-permute-start(f32[4,8,512]{2,1,0:T(8,128)} %fusion.6), channel_id=1, source_target_pairs={{0,16},{16,0},{32,48},{48,32},{64,80},{80,64},{96,112},{112,96},{1... | collective-permute-start | bytes 196616 | tf_op jit(solution)/shard_map/ppermute | solution.py:33
  26.7 9.6 %collective-permute-start.9 = (bf16[64,2304]{1,0:T(8,128)(2,1)}, bf16[64,2304]{1,0:T(8,128)(2,1)S(1)}, u32[]{:S(2)}, u32[]{:S(2)}) collective-permute-start(bf16[64,2304]{1,0:T(8,128)(2,1)} %collective-permute-done.4), channel_id=1, source_target_pairs={{0,1},{1,2},{2,3},{3,0},{4,5},{5,6},{6,7},{7,4},{8,9},{9,10},{10,1... | collective-permute-start | bytes 884744 | tf_op jit(solution)/shard_map/ppermute | solution.py:28
  36.3 10.7 %collective-permute-start.10 = (bf16[128,2304]{1,0:T(8,128)(2,1)S(1)}, bf16[128,2304]{1,0:T(8,128)(2,1)}, u32[]{:S(2)}, u32[]{:S(2)}) collective-permute-start(bf16[128,2304]{1,0:T(8,128)(2,1)S(1)} %constant_dynamic-update-slice_fusion.refs_4_), channel_id=1, source_target_pairs={{0,12},{1,13},{2,14},{3,15},{4,0},{5,1},{6,2},{7,3},{8,4},{9,5},{1... | collective-permute-start | bytes 1769480 | tf_op jit(solution)/shard_map/ppermute | solution.py:28
  40.4 11.4 %collective-permute-start.7 = (bf16[128,2304]{1,0:T(8,128)(2,1)}, bf16[128,2304]{1,0:T(8,128)(2,1)}, u32[]{:S(2)}, u32[]{:S(2)}) collective-permute-start(bf16[128,2304]{1,0:T(8,128)(2,1)} %collective-permute-done.5.refs_1_), channel_id=1, source_target_pairs={{0,4},{1,5},{2,6},{3,7},{4,8},{5,9},{6,10},{7,11},{8,12},{9,13},{1... | collective-permute-start | bytes 1769480 | tf_op jit(solution)/shard_map/ppermute | solution.py:28
  43.3 8.6 %collective-permute-start.14 = (f32[8,512]{1,0:T(8,128)}, f32[8,512]{1,0:T(8,128)S(1)}, u32[]{:S(2)}, u32[]{:S(2)}) collective-permute-start(f32[8,512]{1,0:T(8,128)} %get-tuple-element.63), channel_id=1, source_target_pairs={{0,32},{1,33},{2,34},{3,35},{4,36},{5,37},{6,38},{7,39},{8,40},{9,... | collective-permute-start | bytes 49160 | tf_op jit(solution)/shard_map/ppermute | solution.py:28
  43.3 8.6 %collective-permute-start.16 = (f32[8,512]{1,0:T(8,128)}, f32[8,512]{1,0:T(8,128)}, u32[]{:S(2)}, u32[]{:S(2)}) collective-permute-start(f32[8,512]{1,0:T(8,128)} %get-tuple-element.64), channel_id=1, source_target_pairs={{0,96},{1,97},{2,98},{3,99},{4,100},{5,101},{6,102},{7,103},{8,104... | collective-permute-start | bytes 49160 | tf_op jit(solution)/shard_map/ppermute | solution.py:28
  47.0 14.3 %collective-permute-start.11 = (bf16[128,2304]{1,0:T(8,128)(2,1)S(1)}, bf16[128,2304]{1,0:T(8,128)(2,1)}, u32[]{:S(2)}, u32[]{:S(2)}) collective-permute-start(bf16[128,2304]{1,0:T(8,128)(2,1)S(1)} %constant_dynamic-update-slice_fusion.refs_4_), channel_id=1, source_target_pairs={{0,4},{1,5},{2,6},{3,7},{4,8},{5,9},{6,10},{7,11},{8,12},{9,13},{1... | collective-permute-start | bytes 1769480 | tf_op jit(solution)/shard_map/ppermute | solution.py:28
  51.8 10.2 %collective-permute-start.12 = (bf16[128,2304]{1,0:T(8,128)(2,1)}, bf16[128,2304]{1,0:T(8,128)(2,1)}, u32[]{:S(2)}, u32[]{:S(2)}) collective-permute-start(bf16[128,2304]{1,0:T(8,128)(2,1)} %collective-permute-done.10.refs_6_), channel_id=1, source_target_pairs={{0,12},{1,13},{2,14},{3,15},{4,0},{5,1},{6,2},{7,3},{8,4},{9,5},{1... | collective-permute-start | bytes 1769480 | tf_op jit(solution)/shard_map/ppermute | solution.py:28
  75.4 11.6 %collective-permute-start.19 = (f32[128,768]{1,0:T(8,128)S(1)}, f32[128,768]{1,0:T(8,128)S(1)}, u32[]{:S(2)}, u32[]{:S(2)}) collective-permute-start(f32[128,768]{1,0:T(8,128)S(1)} %slice.110), channel_id=1, source_target_pairs={{0,32},{1,33},{2,34},{3,35},{4,36},{5,37},{6,38},{7,39},{8,40},{9,... | collective-permute-start | bytes 1179656 | tf_op jit(solution)/shard_map/ppermute | solution.py:28
  87.0 11.7 %collective-permute-start.20 = (f32[128,768]{1,0:T(8,128)S(1)}, f32[128,768]{1,0:T(8,128)S(1)}, u32[]{:S(2)}, u32[]{:S(2)}) collective-permute-start(f32[128,768]{1,0:T(8,128)S(1)} %get-tuple-element.56), channel_id=1, source_target_pairs={{0,32},{1,33},{2,34},{3,35},{4,36},{5,37},{6,38},{7,39},{8,40},{9,... | collective-permute-start | bytes 1179656 | tf_op jit(solution)/shard_map/ppermute | solution.py:28
  87.1 11.6 %collective-permute-start.21 = (f32[128,768]{1,0:T(8,128)S(1)}, f32[128,768]{1,0:T(8,128)S(1)}, u32[]{:S(2)}, u32[]{:S(2)}) collective-permute-start(f32[128,768]{1,0:T(8,128)S(1)} %get-tuple-element.57), channel_id=1, source_target_pairs={{0,96},{1,97},{2,98},{3,99},{4,100},{5,101},{6,102},{7,103},{8,104... | collective-permute-start | bytes 1179656 | tf_op jit(solution)/shard_map/ppermute | solution.py:28
  151.1 11.2 %collective-permute-start.30 = (bf16[128,2304]{1,0:T(8,128)(2,1)S(1)}, bf16[128,2304]{1,0:T(8,128)(2,1)S(1)}, u32[]{:S(2)}, u32[]{:S(2)}) collective-permute-start(bf16[128,2304]{1,0:T(8,128)(2,1)S(1)} %get-tuple-element.46), channel_id=1, source_target_pairs={{0,4},{1,5},{2,6},{3,7},{4,8},{5,9},{6,10},{7,11},{8,12},{9,13},{1... | collective-permute-start | bytes 1769480 | tf_op jit(solution)/shard_map/ppermute | solution.py:28
  151.6 10.7 %collective-permute-start.31 = (bf16[128,2304]{1,0:T(8,128)(2,1)S(1)}, bf16[128,2304]{1,0:T(8,128)(2,1)S(1)}, u32[]{:S(2)}, u32[]{:S(2)}) collective-permute-start(bf16[128,2304]{1,0:T(8,128)(2,1)S(1)} %get-tuple-element.47), channel_id=1, source_target_pairs={{0,12},{1,13},{2,14},{3,15},{4,0},{5,1},{6,2},{7,3},{8,4},{9,5},{1... | collective-permute-start | bytes 1769480 | tf_op jit(solution)/shard_map/ppermute | solution.py:28
  158.5 10.0 %collective-permute-start.29 = (bf16[128,2304]{1,0:T(8,128)(2,1)S(1)}, bf16[128,2304]{1,0:T(8,128)(2,1)S(1)}, u32[]{:S(2)}, u32[]{:S(2)}) collective-permute-start(bf16[128,2304]{1,0:T(8,128)(2,1)S(1)} %get-tuple-element.44), channel_id=1, source_target_pairs={{0,12},{1,13},{2,14},{3,15},{4,0},{5,1},{6,2},{7,3},{8,4},{9,5},{1... | collective-permute-start | bytes 1769480 | tf_op jit(solution)/shard_map/ppermute | solution.py:28
  158.6 11.2 %collective-permute-start.33 = (bf16[128,2304]{1,0:T(8,128)(2,1)S(1)}, bf16[128,2304]{1,0:T(8,128)(2,1)S(1)}, u32[]{:S(2)}, u32[]{:S(2)}) collective-permute-start(bf16[128,2304]{1,0:T(8,128)(2,1)S(1)} %get-tuple-element.49), channel_id=1, source_target_pairs={{0,4},{1,5},{2,6},{3,7},{4,8},{5,9},{6,10},{7,11},{8,12},{9,13},{1... | collective-permute-start | bytes 1769480 | tf_op jit(solution)/shard_map/ppermute | solution.py:28
  162.5 13.6 %collective-permute-start.32 = (bf16[128,2304]{1,0:T(8,128)(2,1)S(1)}, bf16[128,2304]{1,0:T(8,128)(2,1)S(1)}, u32[]{:S(2)}, u32[]{:S(2)}) collective-permute-start(bf16[128,2304]{1,0:T(8,128)(2,1)S(1)} %add_convert_fusion.1), channel_id=1, source_target_pairs={{0,4},{1,5},{2,6},{3,7},{4,8},{5,9},{6,10},{7,11},{8,12},{9,13},{1... | collective-permute-start | bytes 1769480 | tf_op jit(solution)/shard_map/ppermute | solution.py:28
  162.8 13.3 %collective-permute-start.34 = (bf16[128,2304]{1,0:T(8,128)(2,1)S(1)}, bf16[128,2304]{1,0:T(8,128)(2,1)S(1)}, u32[]{:S(2)}, u32[]{:S(2)}) collective-permute-start(bf16[128,2304]{1,0:T(8,128)(2,1)S(1)} %add_convert_fusion), channel_id=1, source_target_pairs={{0,12},{1,13},{2,14},{3,15},{4,0},{5,1},{6,2},{7,3},{8,4},{9,5},{1... | collective-permute-start | bytes 1769480 | tf_op jit(solution)/shard_map/ppermute | solution.py:28
  176.5 8.0 %collective-permute-start.36 = (f32[32,2304]{1,0:T(8,128)S(1)}, f32[32,2304]{1,0:T(8,128)S(1)}, u32[]{:S(2)}, u32[]{:S(2)}) collective-permute-start(f32[32,2304]{1,0:T(8,128)S(1)} %get-tuple-element.60), channel_id=1, source_target_pairs={{0,1},{1,2},{2,3},{3,0},{4,5},{5,6},{6,7},{7,4},{8,9},{9,10},{10,1... | collective-permute-start | bytes 884744 | tf_op jit(solution)/shard_map/ppermute | solution.py:28
  184.6 8.0 %collective-permute-start.38 = (f32[32,2304]{1,0:T(8,128)S(1)}, f32[32,2304]{1,0:T(8,128)S(1)}, u32[]{:S(2)}, u32[]{:S(2)}) collective-permute-start(f32[32,2304]{1,0:T(8,128)S(1)} %get-tuple-element.59), channel_id=1, source_target_pairs={{0,1},{1,2},{2,3},{3,0},{4,5},{5,6},{6,7},{7,4},{8,9},{9,10},{10,1... | collective-permute-start | bytes 884744 | tf_op jit(solution)/shard_map/ppermute | solution.py:28
  188.1 7.9 %collective-permute-start.37 = (f32[32,2304]{1,0:T(8,128)S(1)}, f32[32,2304]{1,0:T(8,128)S(1)}, u32[]{:S(2)}, u32[]{:S(2)}) collective-permute-start(f32[32,2304]{1,0:T(8,128)S(1)} %get-tuple-element.58), channel_id=1, source_target_pairs={{0,1},{1,2},{2,3},{3,0},{4,5},{5,6},{6,7},{7,4},{8,9},{9,10},{10,1... | collective-permute-start | bytes 884744 | tf_op jit(solution)/shard_map/ppermute | solution.py:28
  (31 other events, 240.1 us)
where the time goes:
time: 198 us; the launch traced here: 197 us
  waiting for transfers between devices  74.7 us (38%)
  starting transfers between devices  47.6 us (24%)
  blocking collectives  26.5 us (13%)
  Pallas kernels  25.2 us (13%)
  local copies, waits for them, and re-layouts  11.9 us (6%)
  other arithmetic  9.63 us (5%)
    ppermute x33, waiting for transfers between devices, shift(): return lax.ppermute(value, ('gx', 'yz'), pairs)  73.3 us
    ppermute x33, starting transfers between devices, shift(): return lax.ppermute(value, ('gx', 'yz'), pairs)  45.5 us
    all_to_all x1, blocking collectives, body(): query = lax.all_to_all(query, 'yz', split_axis=0, concat_axis=0)  14.7 us
    all_to_all x1, blocking collectives, body(): lax.all_to_all(heads_out.reshape(16, 8, columns), 'yz', split_axis=0, con...  11.8 us
    pallas_call x2, Pallas kernels, project_query(): pl.pallas_call(functools.partial(query_kernel, other), out_shape=jax.Shap...  9.78 us
    pallas_call x1, Pallas kernels, attend(): pl.pallas_call(attend_kernel, out_shape=jax.ShapeDtypeStruct((rows, colum...  8.8 us
    unnamed x29, local copies, waits for them, and re-layouts  8.34 us
    pallas_call x2, Pallas kernels, project_output(): pl.pallas_call(functools.partial(output_kernel, groups), out_shape=shapes...  5.83 us
  transfers between devices with their start and end apart: 41, of which 21 were waited for; matrix products, arithmetic and copies ran while one was open for 5% of the time, Pallas kernels for 5%

commit v1 on v0

v1 whole, which is shorter than its diff:
```python
import functools

import jax
import jax.numpy as jnp
from jax import lax
from jax.experimental import pallas as pl
from jax.experimental.pallas import tpu as pltpu
from jax.sharding import PartitionSpec as P

D = 18432
HEADS = 48
HEAD = 256
RING = 4
F32 = jnp.float32
BF16 = jnp.bfloat16


def shift(value, move):
    pairs = []
    for x in range(RING):
        for core in range(2):
            for y in range(RING):
                for z in range(RING):
                    dx, dy, dz = move(core)
                    target = (2 * ((x + dx) % RING) + core) * 16
                    target += RING * ((y + dy) % RING) + (z + dz) % RING
                    pairs.append(((2 * x + core) * 16 + RING * y + z, target))
    return lax.ppermute(value, ("gx", "yz"), pairs)


def send_core(value):
    pairs = [(2 * x + c, 2 * x + 1 - c) for x in range(RING) for c in range(2)]
    return lax.ppermute(value, "gx", pairs)


def send_x(value, step):
    return shift(value, lambda core: ((1 - 2 * core) * step, 0, 0))


def send_ahead(value, step):
    return shift(value, lambda core: (step, 0, 0))


def send_inner(value, step):
    return shift(value, lambda core: (0, core * step, (1 - core) * step))


def send_outer(value, step):
    return shift(value, lambda core: (0, (1 - core) * step, core * step))


def exchange(value, along_y):
    groups = [
        [RING * i + k if along_y else RING * k + i for i in range(RING)] for k in range(RING)
    ]
    return lax.all_to_all(
        value, "yz", split_axis=0, concat_axis=0, axis_index_groups=groups, tiled=True
    )


def rotation_tables(positions):
    half = HEAD // 2
    freq = 10000.0 ** (-jnp.arange(half, dtype=F32) * 2.0 / HEAD)
    angle = positions.astype(F32)[..., None] * freq
    return jnp.cos(angle), jnp.sin(angle)


def keyval_kernel(place, rows_ref, w_ref, away_ref, keep_ref, sums_ref):
    x, core = place[0], place[3]
    sums_ref[...] = jnp.dot(rows_ref[...], w_ref[...], preferred_element_type=F32)
    for slot in range(RING):
        block = 2 * lax.rem(x + slot, RING)
        target = pl.ds(8 * slot, 8)
        keep_ref[target, :] = sums_ref[pl.ds(pl.multiple_of(8 * (block + core), 8), 8), :]
        away_ref[target, :] = sums_ref[pl.ds(pl.multiple_of(8 * (block + 1 - core), 8), 8), :]


def project_keyval(place, rows, w_keyval):
    count, depth = rows.shape
    columns = w_keyval.shape[1]
    vmem_spec = pl.BlockSpec(memory_space=pltpu.VMEM)
    half = jax.ShapeDtypeStruct((count // 2, columns), F32)
    return pl.pallas_call(
        keyval_kernel,
        out_shape=[half, half],
        in_specs=[pl.BlockSpec(memory_space=pltpu.SMEM)] + [vmem_spec] * 2,
        out_specs=[vmem_spec] * 2,
        scratch_shapes=[pltpu.VMEM((count, columns), F32)],
        compiler_params=pltpu.CompilerParams(vmem_limit_bytes=12 * 2**20),
        cost_estimate=pl.CostEstimate(
            flops=2 * count * depth * columns, bytes_accessed=3 * 2**20, transcendentals=0
        ),
        name="keyval_projection",
    )(place, rows, w_keyval)


def query_kernel(other, place, *refs):
    pieces, (w_ref, out_ref, rows_ref) = refs[:8], refs[8:]
    x, y, z, core = place[0], place[1], place[2], place[3]
    for index, piece in enumerate(pieces):
        for part in range(2):
            outer = (0, 3, 1, 2)[index % 4]
            inner = ((0, 3), (1, 2))[index // 4][part]
            at_y = lax.rem(y + jnp.where(core == 0, outer, inner), RING)
            at_z = lax.rem(z + jnp.where(core == 0, inner, outer), RING)
            to_core = at_z // 2
            ahead = lax.rem(at_y - x + RING, RING)
            slot = jnp.where(to_core == 0, ahead, lax.rem(RING - ahead, RING))
            position = slot * 2 + lax.rem(at_z, 2)

            @pl.when((to_core != core) == other)
            def _():
                rows_ref[position] = piece[part * 64 : (part + 1) * 64, :]

    rows = rows_ref[...].reshape(512, w_ref.shape[0])
    out_ref[...] = jnp.dot(rows, w_ref[...], preferred_element_type=F32)


def project_query(place, pieces, w_query, other):
    depth, columns = w_query.shape
    vmem_spec = pl.BlockSpec(memory_space=pltpu.VMEM)
    return pl.pallas_call(
        functools.partial(query_kernel, other),
        out_shape=jax.ShapeDtypeStruct((512, columns), F32),
        in_specs=[pl.BlockSpec(memory_space=pltpu.SMEM)] + [vmem_spec] * 9,
        out_specs=vmem_spec,
        scratch_shapes=[pltpu.VMEM((8, 64, depth), BF16)],
        compiler_params=pltpu.CompilerParams(vmem_limit_bytes=20 * 2**20),
        cost_estimate=pl.CostEstimate(
            flops=2 * 512 * depth * columns, bytes_accessed=8 * 2**20, transcendentals=0
        ),
        name="query_projection",
    )(place, *pieces, w_query)


def attend_kernel(lengths, q_ref, cos_ref, sin_ref, kv_ref, k_ref, v_ref, out_ref, new_ref, acc_ref):
    seqs = k_ref.shape[0]
    half = HEAD // 2
    rows = q_ref.shape[0]
    scale = HEAD ** (-0.5)
    contract_last = (((1,), (1,)), ((), ()))
    pick_row = lax.broadcasted_iota(jnp.int32, (32, rows), 0)
    pick_col = lax.broadcasted_iota(jnp.int32, (32, rows), 1)
    odd = lax.rem(lax.broadcasted_iota(jnp.int32, (32, half), 0), 2) == 1
    second_step = lax.rem(lax.broadcasted_iota(jnp.int32, (96, 1), 0), 2) == 1
    first = kv_ref[:, :half].astype(F32)
    second = kv_ref[:, half:HEAD].astype(F32)
    cosine, sine = cos_ref[...], sin_ref[...]
    new_ref[:, :half] = (first * cosine - second * sine).astype(BF16)
    new_ref[:, half:HEAD] = (second * cosine + first * sine).astype(BF16)
    new_ref[:, HEAD:] = kv_ref[:, HEAD:]
    new_rows = new_ref[...].astype(F32)

    def pick_of(r):
        return (pick_col == (pick_row // 2) * 8 + 2 * r + lax.rem(pick_row, 2)).astype(BF16)

    def query_of(r):
        pick = pick_of(r)
        cosine = jnp.where(odd, cos_ref[2 * r + 1 : 2 * r + 2, :], cos_ref[2 * r : 2 * r + 1, :])
        sine = jnp.where(odd, sin_ref[2 * r + 1 : 2 * r + 2, :], sin_ref[2 * r : 2 * r + 1, :])
        parts = []
        for h in range(3):
            chosen = jnp.dot(pick, q_ref[:, h * HEAD : (h + 1) * HEAD], preferred_element_type=F32)
            first, second = chosen[:, :half], chosen[:, half:]
            parts.append(
                jnp.concatenate([first * cosine - second * sine, second * cosine + first * sine], 1)
            )
        return jnp.concatenate(parts, 0).astype(BF16)

    def scores_of(r, query):
        return lax.dot_general(query, k_ref[r], contract_last, preferred_element_type=F32) * scale

    query = query_of(0)
    scores = scores_of(0, query)
    for r in range(seqs):
        if r + 1 < seqs:
            next_query = query_of(r + 1)
            next_scores = scores_of(r + 1, next_query)
        valid = lax.broadcasted_iota(jnp.int32, scores.shape, 1) < lengths[r]
        cached = jnp.where(valid, scores, -jnp.inf)
        new = new_rows[2 * r : 2 * r + 2, :]
        wide = query.astype(F32)
        fresh0 = jnp.sum(wide * new[0:1, :HEAD], -1, keepdims=True) * scale
        fresh1 = jnp.sum(wide * new[1:2, :HEAD], -1, keepdims=True) * scale
        fresh1 = jnp.where(second_step, fresh1, -jnp.inf)
        top = jnp.maximum(jnp.max(cached, -1, keepdims=True), jnp.maximum(fresh0, fresh1))
        exp_cached = jnp.exp(cached - top)
        exp0 = jnp.exp(fresh0 - top)
        exp1 = jnp.exp(fresh1 - top)
        inverse = 1.0 / (jnp.sum(exp_cached, -1, keepdims=True) + exp0 + exp1)
        weights = (exp_cached * inverse).astype(BF16)
        weight0 = (exp0 * inverse).astype(BF16).astype(F32)
        weight1 = (exp1 * inverse).astype(BF16).astype(F32)
        result = jnp.dot(weights, v_ref[r], preferred_element_type=F32)
        result = result + weight0 * new[0:1, HEAD:] + weight1 * new[1:2, HEAD:]
        result = result.astype(BF16)
        pick = pick_of(r)
        for h in range(3):
            spread = lax.dot_general(
                pick,
                result[h * 32 : (h + 1) * 32],
                (((0,), (0,)), ((), ())),
                preferred_element_type=F32,
            )
            columns = slice(h * HEAD, (h + 1) * HEAD)
            if r == 0:
                acc_ref[:, columns] = spread
            else:
                acc_ref[:, columns] += spread
        if r + 1 < seqs:
            query, scores = next_query, next_scores
    out_ref[...] = acc_ref[...].astype(BF16)


def attend(lengths, query, cosine, sine, keyval, keys, values):
    seqs, context, _ = keys.shape
    rows, columns = query.shape
    vmem_spec = pl.BlockSpec(memory_space=pltpu.VMEM)
    return pl.pallas_call(
        attend_kernel,
        out_shape=[
            jax.ShapeDtypeStruct((rows, columns), BF16),
            jax.ShapeDtypeStruct(keyval.shape, BF16),
        ],
        in_specs=[pl.BlockSpec(memory_space=pltpu.SMEM)] + [vmem_spec] * 6,
        out_specs=[vmem_spec] * 2,
        scratch_shapes=[pltpu.VMEM((rows, columns), F32)],
        compiler_params=pltpu.CompilerParams(vmem_limit_bytes=20 * 2**20),
        cost_estimate=pl.CostEstimate(
            flops=4 * seqs * 96 * context * HEAD,
            bytes_accessed=4 * seqs * context * HEAD,
            transcendentals=seqs * 96 * context,
        ),
        name="attention",
    )(lengths, query, cosine, sine, keyval, keys, values)


def output_kernel(groups, place, *refs):
    pieces, (w_ref, *outs), rows_ref = refs[:8], refs[8:-1], refs[-1]
    x, y, z, core = place[0], place[1], place[2], place[3]
    for index, piece in enumerate(pieces):
        at_core = core if index < 4 else 1 - core
        slot = (0, 3, 1, 2)[index % 4]
        ahead = jnp.where(at_core == 0, slot, (RING - slot) % RING)
        dy = lax.rem(x + ahead - y + RING, RING)
        for part in range(2):
            dz = lax.rem(2 * at_core + part - z + RING, RING)
            outer, inner = jnp.where(core == 0, dy, dz), jnp.where(core == 0, dz, dy)
            for position, group in enumerate(groups):

                @pl.when(outer == group)
                def _():
                    rows_ref[position * RING + inner] = piece[part * 64 : (part + 1) * 64, :]

    outs = list(outs)
    for position, group in enumerate(groups):
        rows = rows_ref[RING * position : RING * position + RING].reshape(256, w_ref.shape[0])
        targets = [outs.pop(0)] if group == 0 else [outs.pop(0), outs.pop(0)]
        for start in range(0, w_ref.shape[1], 768):
            columns = slice(start, start + 768)
            result = jnp.dot(rows, w_ref[:, columns], preferred_element_type=F32)
            if group == 0:
                targets[0][:, columns] = result
            else:
                targets[0][:, columns] = result[:128].astype(BF16)
                targets[1][:, columns] = result[128:].astype(BF16)


def project_output(place, pieces, w_out, groups):
    depth, columns = w_out.shape
    vmem_spec = pl.BlockSpec(memory_space=pltpu.VMEM)
    shapes = []
    for group in groups:
        if group == 0:
            shapes.append(jax.ShapeDtypeStruct((256, columns), F32))
        else:
            shapes += [jax.ShapeDtypeStruct((128, columns), BF16)] * 2
    return pl.pallas_call(
        functools.partial(output_kernel, groups),
        out_shape=shapes,
        in_specs=[pl.BlockSpec(memory_space=pltpu.SMEM)] + [vmem_spec] * 9,
        out_specs=[vmem_spec] * len(shapes),
        scratch_shapes=[pltpu.VMEM((RING * len(groups), 64, depth), BF16)],
        compiler_params=pltpu.CompilerParams(vmem_limit_bytes=20 * 2**20),
        cost_estimate=pl.CostEstimate(
            flops=2 * 256 * len(groups) * depth * columns,
            bytes_accessed=8 * 2**20,
            transcendentals=0,
        ),
        name="output_projection",
    )(place, *pieces, w_out)


def body(tokens, gain, w_query, w_keyval, w_out, key_cache, value_cache, lengths):
    seqs = lengths.shape[0]
    gx, yz = lax.axis_index("gx"), lax.axis_index("yz")
    place = jnp.stack([gx // 2, yz // RING, lax.rem(yz, RING), lax.rem(gx, 2)]).astype(jnp.int32)
    positions = jnp.repeat(lengths, 2) + lax.rem(jnp.arange(2 * seqs, dtype=jnp.int32), 2)
    cosine, sine = rotation_tables(positions)

    count = tokens.shape[0] * 2
    features = tokens.shape[2]
    xfull = tokens.reshape(count, features).astype(F32)
    stats = jnp.stack([jnp.sum(xfull, -1), jnp.sum(xfull * xfull, -1)])
    stats = stats + send_core(stats)
    stats, cosine, sine, place = lax.optimization_barrier((stats, cosine, sine, place))
    stats = stats + send_x(stats, 1) + send_x(stats, 2) + send_x(stats, 3)
    mean = stats[0] / D
    var = stats[1] / D - mean * mean
    normed = ((xfull - mean[:, None]) * lax.rsqrt(var + 1e-05)[:, None] * gain).astype(BF16)

    normed = lax.optimization_barrier(normed)
    keyval_away, keyval_keep = project_keyval(place, normed, w_keyval)

    before = send_inner(normed, 1)
    after = send_inner(normed, -1)
    far = send_inner(before, 1)
    near = jnp.concatenate([normed, before], 0)
    near, keyval_away = lax.optimization_barrier((near, keyval_away))
    wide = jnp.concatenate([after, far], 0)
    near_before, near_after = send_outer(near, 1), send_outer(near, -1)
    near_before, near_after = lax.optimization_barrier((near_before, near_after))
    wide_after = send_outer(wide, -1)
    near_far = send_outer(near_before, 1)
    near_far, wide_again = lax.optimization_barrier((near_far, wide))
    wide_before = send_outer(wide_again, 1)
    wide_far = send_outer(wide_after, -1)

    kept = (keyval_keep + send_core(keyval_away)).reshape(RING, count // 8, 2 * HEAD)
    keyval = kept[0] + send_ahead(kept[1], 1) + send_ahead(kept[2], 2) + send_ahead(kept[3], 3)
    keyval = keyval.astype(BF16)

    pieces = [near, near_before, near_after, near_far, wide, wide_before, wide_after, wide_far]
    columns = w_query.shape[1]
    pieces, keyval = lax.optimization_barrier((pieces, keyval))
    away = project_query(place, pieces, w_query, True)
    keep = project_query(place, pieces, w_query, False)
    summed = (keep + send_core(away)).reshape(RING, 128, columns)
    far = send_x(summed[2], 1)
    behind = send_x(summed[3], -1)
    ahead = send_x(summed[1] + far, 1)
    query = (summed[0] + ahead + behind).astype(BF16).reshape(16, 8, columns)
    moves = [
        (g * 16 + j, (j // 2) * 16 + (j % 2) * 8 + g) for g in range(8) for j in range(16)
    ]
    keyval = lax.ppermute(keyval, ("gx", "yz"), moves)
    query, keyval = lax.optimization_barrier((query, keyval))
    query = exchange(query.reshape(RING, RING, 8, columns), True)
    query = exchange(jnp.swapaxes(query, 0, 1), False)

    heads_out, new_keyval = attend(
        lengths, query.reshape(128, columns), cosine, sine, keyval, key_cache, value_cache
    )
    heads_out = exchange(heads_out.reshape(RING, RING, 8, columns), False)
    heads_out = exchange(jnp.swapaxes(heads_out, 0, 1), True).reshape(128, columns)
    before = send_x(heads_out, 1)
    after = send_x(heads_out, -1)
    pieces = [heads_out, before, after, send_x(before, 1)]
    pieces = pieces + [send_core(p) for p in pieces]
    two_low, two_high = project_output(place, pieces, w_out, (2,))
    one_low, one_high, three_low, three_high, own = project_output(
        place, pieces, w_out, (1, 3, 0)
    )

    far_low, far_high = send_outer(two_low, 1), send_outer(two_high, -1)
    far_low, far_high = lax.optimization_barrier((far_low, far_high))
    early_high, early_low = send_outer(one_high, 1), send_outer(three_low, -1)
    late_low = send_outer((one_low.astype(F32) + far_low.astype(F32)).astype(BF16), 1)
    late_high = send_outer((three_high.astype(F32) + far_high.astype(F32)).astype(BF16), -1)
    low = own[:128] + early_low.astype(F32) + late_low.astype(F32)
    high = own[128:] + early_high.astype(F32) + late_high.astype(F32)
    here, one, two, three = low[:64], low[64:], high[:64], high[64:]
    far_low, far_high = send_inner(two[:32], 1), send_inner(two[32:], -1)
    one = jnp.concatenate([one[:32] + far_low, one[32:]], 0)
    three = jnp.concatenate([three[:32], three[32:] + far_high], 0)
    branch = here + send_inner(one, 1) + send_inner(three, -1)
    mixed = (xfull + branch).astype(BF16).reshape(tokens.shape)
    return (mixed, new_keyval.reshape(seqs, 2, 2 * HEAD))


def solution(mesh):
    return jax.shard_map(
        body,
        mesh=mesh,
        in_specs=(
            P("yz", None, "gx"),
            P("gx"),
            P("gx", "yz"),
            P("gx", None),
            P("yz", "gx"),
            P(("gx", "yz"), None, None),
            P(("gx", "yz"), None, None),
            P(("gx", "yz")),
        ),
        out_specs=(P("yz", None, "gx"), P(("gx", "yz"), None, None)),
        check_vma=False,
    )
```

time: 198 us -> 195 us (0.985)
  waiting for transfers between devices: 74.7 us -> 86.6 us
  blocking collectives: 26.5 us -> 36.7 us
  Pallas kernels: 25.2 us -> 17 us
  local copies, waits for them, and re-layouts: 11.9 us -> 5.35 us
  other arithmetic: 9.63 us -> 4.45 us
  starting transfers between devices: 47.6 us -> 43.3 us
    all_to_all x2 -> x4, blocking collectives: 26.5 us -> 36.7 us  [exchange(): lax.all_to_all(value, 'yz', split_axis=0, concat_axis=0, axis_index_group...]
    ppermute x33 -> x31, waiting for transfers between devices: 73.3 us -> 83.4 us  [shift(): return lax.ppermute(value, ('gx', 'yz'), pairs)]
    unnamed x29 -> x15, local copies, waits for them, and re-layouts: 8.34 us -> 1.71 us
    pallas_call x2, Pallas kernels: 9.56 us -> 5.42 us  [the longest x1 4.35 us: attend(): pl.pallas_call(attend_kernel, out_shape=[jax.ShapeDtypeStruct((rows, colu...]
    pallas_call x2, Pallas kernels: 9.78 us -> 5.9 us  [project_query(): pl.pallas_call(functools.partial(query_kernel, other), out_shape=jax.Shap...]
    ppermute x33 -> x31, starting transfers between devices: 45.5 us -> 42 us  [shift(): return lax.ppermute(value, ('gx', 'yz'), pairs)]
  transfers between devices with their start and end apart: 41 -> 39, of which waited for: 21 -> 23; matrix products, arithmetic and copies ran while one was open for 5% -> 2% of each run, Pallas kernels for 5% -> 4%
where the time goes in v1:
time: 195 us; the launch traced here: 194 us
  waiting for transfers between devices  86.6 us (44%)
  starting transfers between devices  43.3 us (22%)
  blocking collectives  36.7 us (19%)
  Pallas kernels  17 us (9%)
  local copies, waits for them, and re-layouts  5.35 us (3%)
  other arithmetic  4.45 us (2%)
    ppermute x31, waiting for transfers between devices, shift(): return lax.ppermute(value, ('gx', 'yz'), pairs)  83.4 us
    ppermute x31, starting transfers between devices, shift(): return lax.ppermute(value, ('gx', 'yz'), pairs)  42 us
    all_to_all x4, blocking collectives, exchange(): lax.all_to_all(value, 'yz', split_axis=0, concat_axis=0, axis_index_group...  36.7 us
    pallas_call x2, Pallas kernels, project_query(): pl.pallas_call(functools.partial(query_kernel, other), out_shape=jax.Shap...  5.9 us
    pallas_call x2, Pallas kernels, project_output(): pl.pallas_call(functools.partial(output_kernel, groups), out_shape=shapes...  5.64 us
    pallas_call x1, Pallas kernels, attend(): pl.pallas_call(attend_kernel, out_shape=[jax.ShapeDtypeStruct((rows, colu...  4.35 us
  transfers between devices with their start and end apart: 39, of which 23 were waited for; matrix products, arithmetic and copies ran while one was open for 2% of the time, Pallas kernels for 4%

profile of v1, /device:TPU:0, one launch (start us, length us, event | category | flops | bytes accessed | tf_op | source)
XLA Modules:
  0.0 194.3 jit_solution(16400057724679282197)
XLA Ops:
  21.1 3.1 %collective-permute-start.6 = (bf16[128,2304]{1,0:T(8,128)(2,1)S(1)}, bf16[128,2304]{1,0:T(8,128)(2,1)S(1)}, u32[]{:S(2)}, u32[]{:S(2)}) collective-permute-start(bf16[128,2304]{1,0:T(8,128)(2,1)S(1)} %pad_maximum_fusion.refs_0_), channel_id=1, source_target_pairs={{0,12},{1,13},{2,14},{3,15},{4,0},{5,1},{6,2},{7,3},{8,4},{9,5},{1... | collective-permute-start | bytes 1769480 | tf_op jit(solution)/shard_map/ppermute | solution.py:28
  24.3 10.5 %collective-permute-done.9 = bf16[64,2304]{1,0:T(8,128)(2,1)S(1)} collective-permute-done((bf16[64,2304]{1,0:T(8,128)(2,1)S(1)}, bf16[64,2304]{1,0:T(8,128)(2,1)S(1)}, u32[]{:S(2)}, u32[]{:S(2)}) %collective-permute-start.9) | collective-permute-done | bytes 294944 | tf_op jit(solution)/shard_map/ppermute | solution.py:28
  36.9 7.8 %collective-permute-done.11.refs_6_ = bf16[128,2304]{1,0:T(8,128)(2,1)S(1)} collective-permute-done((bf16[128,2304]{1,0:T(8,128)(2,1)S(1)}, bf16[128,2304]{1,0:T(8,128)(2,1)S(1)}, u32[]{:S(2)}, u32[]{:S(2)}) %collective-permute-start.11) | collective-permute-done | bytes 589856 | tf_op jit(solution)/shard_map/ppermute | solution.py:28
  44.8 3.0 %collective-permute-start.12 = (bf16[128,2304]{1,0:T(8,128)(2,1)S(1)}, bf16[128,2304]{1,0:T(8,128)(2,1)S(1)}, u32[]{:S(2)}, u32[]{:S(2)}) collective-permute-start(bf16[128,2304]{1,0:T(8,128)(2,1)S(1)} %collective-permute-done.11.refs_6_), channel_id=1, source_target_pairs={{0,12},{1,13},{2,14},{3,15},{4,0},{5,1},{6,2},{7,3},{8,4},{9,5},{1... | collective-permute-start | bytes 1769480 | tf_op jit(solution)/shard_map/ppermute | solution.py:28
  54.0 3.5 %collective-permute-done.15 = f32[8,512]{1,0:T(8,128)S(1)} collective-permute-done((f32[8,512]{1,0:T(8,128)S(1)}, f32[8,512]{1,0:T(8,128)S(1)}, u32[]{:S(2)}, u32[]{:S(2)}) %collective-permute-start.15) | collective-permute-done | bytes 16416 | tf_op jit(solution)/shard_map/ppermute | solution.py:28
  58.8 2.9 %query_projection.3 = f32[512,768]{1,0:T(8,128)S(1)} custom-call(s32[4]{0:T(128)S(1)} %pad_add_fusion.place, bf16[128,2304]{1,0:T(8,128)(2,1)S(1)} %pad_maximum_fusion.refs_0_, bf16[128,2304]{1,0:T(8,128)(2,1)S(1)} %collective-permute-done.5.refs_1_, bf16[128,2304]{1,0:T(8,128)(2,1)S(1)} %collective-permute-done.6.refs_2_, ...), custom_call_target="tpu_custom_call" | custom-call | flops 1811939328 | bytes 8388608 | tf_op jit(solution)/shard_map/query_projection/pallas_call | solution.py:122
  61.9 3.0 %query_projection.2 = f32[512,768]{1,0:T(8,128)S(1)} custom-call(s32[4]{0:T(128)S(1)} %pad_add_fusion.place, bf16[128,2304]{1,0:T(8,128)(2,1)S(1)} %pad_maximum_fusion.refs_0_, bf16[128,2304]{1,0:T(8,128)(2,1)S(1)} %collective-permute-done.5.refs_1_, bf16[128,2304]{1,0:T(8,128)(2,1)S(1)} %collective-permute-done.6.refs_2_, ...), custom_call_target="tpu_custom_call" | custom-call | flops 1811939328 | bytes 8388608 | tf_op jit(solution)/shard_map/query_projection/pallas_call | solution.py:122
  66.5 8.2 %collective-permute-done.18 = f32[128,768]{1,0:T(8,128)S(1)} collective-permute-done((f32[128,768]{1,0:T(8,128)S(1)}, f32[128,768]{1,0:T(8,128)S(1)}, u32[]{:S(2)}, u32[]{:S(2)}) %collective-permute-start.18) | collective-permute-done | bytes 393248 | tf_op jit(solution)/shard_map/ppermute | solution.py:28
  74.9 3.2 %collective-permute-start.20 = (f32[128,768]{1,0:T(8,128)S(1)}, f32[128,768]{1,0:T(8,128)S(1)}, u32[]{:S(2)}, u32[]{:S(2)}) collective-permute-start(f32[128,768]{1,0:T(8,128)S(1)} %get-tuple-element.75), channel_id=1, source_target_pairs={{0,96},{1,97},{2,98},{3,99},{4,100},{5,101},{6,102},{7,103},{8,104... | collective-permute-start | bytes 1179656 | tf_op jit(solution)/shard_map/ppermute | solution.py:28
  78.8 9.3 %collective-permute-done.19 = f32[128,768]{1,0:T(8,128)S(1)} collective-permute-done((f32[128,768]{1,0:T(8,128)S(1)}, f32[128,768]{1,0:T(8,128)S(1)}, u32[]{:S(2)}, u32[]{:S(2)}) %collective-permute-start.19) | collective-permute-done | bytes 393248 | tf_op jit(solution)/shard_map/ppermute | solution.py:28
  88.2 9.4 %all_to_all.20 = bf16[4,4,8,768]{3,2,1,0:T(8,128)(2,1)S(1)} all-to-all(bf16[4,4,8,768]{3,2,1,0:T(8,128)(2,1)S(1)} %bitcast.31), channel_id=1, replica_groups={{0,4,8,12},{1,5,9,13},{2,6,10,14},{3,7,11,15},{16,20,24,28},{17,21,25,2..., dimensions={0} | all-to-all | bytes 393216 | tf_op jit(solution)/shard_map/all_to_all | solution.py:56
  97.6 9.9 %all_to_all.21 = bf16[4,4,8,768]{3,2,1,0:T(8,128)(2,1)S(1)} all-to-all(bf16[4,4,8,768]{3,2,1,0:T(8,128)(2,1)S(1)} %copy.15), channel_id=1, replica_groups={{0,1,2,3},{4,5,6,7},{8,9,10,11},{12,13,14,15},{16,17,18,19},{20,21,22,2..., dimensions={0} | all-to-all | bytes 393216 | tf_op jit(solution)/shard_map/all_to_all | solution.py:56
  107.5 4.3 %attention.1 = (bf16[128,768]{1,0:T(8,128)(2,1)S(1)}, bf16[8,512]{1,0:T(8,128)(2,1)S(1)}) custom-call(s32[4]{0:T(128)S(1)} %copy-done.5, bf16[128,768]{1,0:T(8,128)(2,1)S(1)} %bitcast.27, f32[8,128]{1,0:T(8,128)S(1)} %get-tuple-element.56.cos_ref, f32[8,128]{1,0:T(8,128)S(1)} %get-tuple-element.57.sin_ref, ...), custom_call_target="tpu_custom_call" | custom-call | flops 805306368 | bytes 8388608 | tf_op jit(solution)/shard_map/attention/pallas_call | solution.py:219
  111.9 8.7 %all_to_all.22 = bf16[4,4,8,768]{3,2,1,0:T(8,128)(2,1)S(1)} all-to-all(bf16[4,4,8,768]{3,2,1,0:T(8,128)(2,1)S(1)} %bitcast.28), channel_id=1, replica_groups={{0,1,2,3},{4,5,6,7},{8,9,10,11},{12,13,14,15},{16,17,18,19},{20,21,22,2..., dimensions={0} | all-to-all | bytes 393216 | tf_op jit(solution)/shard_map/all_to_all | solution.py:56
  120.6 8.7 %all_to_all.23 = bf16[4,4,8,768]{3,2,1,0:T(8,128)(2,1)S(1)} all-to-all(bf16[4,4,8,768]{3,2,1,0:T(8,128)(2,1)S(1)} %copy.16), channel_id=1, replica_groups={{0,4,8,12},{1,5,9,13},{2,6,10,14},{3,7,11,15},{16,20,24,28},{17,21,25,2..., dimensions={0} | all-to-all | bytes 393216 | tf_op jit(solution)/shard_map/all_to_all | solution.py:56
  129.3 3.2 %collective-permute-start.23 = (bf16[128,768]{1,0:T(8,128)(2,1)S(1)}, bf16[128,768]{1,0:T(8,128)(2,1)S(1)}, u32[]{:S(2)}, u32[]{:S(2)}) collective-permute-start(bf16[128,768]{1,0:T(8,128)(2,1)S(1)} %bitcast.23), channel_id=1, source_target_pairs={{0,96},{1,97},{2,98},{3,99},{4,100},{5,101},{6,102},{7,103},{8,104... | collective-permute-start | bytes 589832 | tf_op jit(solution)/shard_map/ppermute | solution.py:28
  132.5 3.6 %collective-permute-done.22.refs_1_ = bf16[128,768]{1,0:T(8,128)(2,1)S(1)} collective-permute-done((bf16[128,768]{1,0:T(8,128)(2,1)S(1)}, bf16[128,768]{1,0:T(8,128)(2,1)S(1)}, u32[]{:S(2)}, u32[]{:S(2)}) %collective-permute-start.22) | collective-permute-done | bytes 196640 | tf_op jit(solution)/shard_map/ppermute | solution.py:28
  136.7 6.4 %collective-permute-done.24.refs_3_ = bf16[128,768]{1,0:T(8,128)(2,1)S(1)} collective-permute-done((bf16[128,768]{1,0:T(8,128)(2,1)S(1)}, bf16[128,768]{1,0:T(8,128)(2,1)S(1)}, u32[]{:S(2)}, u32[]{:S(2)}) %collective-permute-start.24) | collective-permute-done | bytes 196640 | tf_op jit(solution)/shard_map/ppermute | solution.py:28
  149.6 3.8 %output_projection.2 = (bf16[128,2304]{1,0:T(8,128)(2,1)S(1)}, bf16[128,2304]{1,0:T(8,128)(2,1)S(1)}, bf16[128,2304]{1,0:T(8,128)(2,1)S(1)}, bf16[128,2304]{1,0:T(8,128)(2,1)S(1)}, f32[256,2304]{1,0:T(8,128)S(1)}) custom-call(s32[4]{0:T(128)S(1)} %pad_add_fusion.place, bf16[128,768]{1,0:T(8,128)(2,1)S(1)} %bitcast.26, ...), custom_call_target="tpu_custom_call" | custom-call | flops 2717908992 | bytes 8388608 | tf_op jit(solution)/shard_map/output_projection/pallas_call | solution.py:278
  158.1 3.3 %collective-permute-start.34 = (bf16[128,2304]{1,0:T(8,128)(2,1)S(1)}, bf16[128,2304]{1,0:T(8,128)(2,1)S(1)}, u32[]{:S(2)}, u32[]{:S(2)}) collective-permute-start(bf16[128,2304]{1,0:T(8,128)(2,1)S(1)} %add_convert_fusion), channel_id=1, source_target_pairs={{0,12},{1,13},{2,14},{3,15},{4,0},{5,1},{6,2},{7,3},{8,4},{9,5},{1... | collective-permute-start | bytes 1769480 | tf_op jit(solution)/shard_map/ppermute | solution.py:28
  164.7 6.3 %collective-permute-done.32 = bf16[128,2304]{1,0:T(8,128)(2,1)S(1)} collective-permute-done((bf16[128,2304]{1,0:T(8,128)(2,1)S(1)}, bf16[128,2304]{1,0:T(8,128)(2,1)S(1)}, u32[]{:S(2)}, u32[]{:S(2)}) %collective-permute-start.32) | collective-permute-done | bytes 589856 | tf_op jit(solution)/shard_map/ppermute | solution.py:28
  173.5 4.7 %collective-permute-done.37 = f32[32,2304]{1,0:T(8,128)S(1)} collective-permute-done((f32[32,2304]{1,0:T(8,128)S(1)}, f32[32,2304]{1,0:T(8,128)S(1)}, u32[]{:S(2)}, u32[]{:S(2)}) %collective-permute-start.37) | collective-permute-done | bytes 294944 | tf_op jit(solution)/shard_map/ppermute | solution.py:28
  181.5 6.8 %collective-permute-done.38 = f32[64,2304]{1,0:T(8,128)} collective-permute-done((f32[64,2304]{1,0:T(8,128)S(1)}, f32[64,2304]{1,0:T(8,128)}, u32[]{:S(2)}, u32[]{:S(2)}) %collective-permute-start.38) | collective-permute-done | bytes 589856 | tf_op jit(solution)/shard_map/ppermute | solution.py:28
  188.4 3.8 %collective-permute-done.36 = f32[64,2304]{1,0:T(8,128)} collective-permute-done((f32[64,2304]{1,0:T(8,128)S(1)}, f32[64,2304]{1,0:T(8,128)}, u32[]{:S(2)}, u32[]{:S(2)}) %collective-permute-start.36) | collective-permute-done | bytes 589856 | tf_op jit(solution)/shard_map/ppermute | solution.py:28
  (117 shorter events, 55.7 us)
Async XLA Ops:
  12.3 8.8 %collective-permute-start.4 = (bf16[64,2304]{1,0:T(8,128)(2,1)S(1)}, bf16[64,2304]{1,0:T(8,128)(2,1)S(1)}, u32[]{:S(2)}, u32[]{:S(2)}) collective-permute-start(bf16[64,2304]{1,0:T(8,128)(2,1)S(1)} %multiply_convert_fusion.rows_ref), channel_id=1, source_target_pairs={{0,1},{1,2},{2,3},{3,0},{4,5},{5,6},{6,7},{7,4},{8,9},{9,10},{10,1... | collective-permute-start | bytes 884744 | tf_op jit(solution)/shard_map/ppermute | solution.py:28
  14.3 10.0 %collective-permute-start.8 = (bf16[64,2304]{1,0:T(8,128)(2,1)S(1)}, bf16[64,2304]{1,0:T(8,128)(2,1)S(1)}, u32[]{:S(2)}, u32[]{:S(2)}) collective-permute-start(bf16[64,2304]{1,0:T(8,128)(2,1)S(1)} %multiply_convert_fusion.rows_ref), channel_id=1, source_target_pairs={{0,3},{1,0},{2,1},{3,2},{4,7},{5,4},{6,5},{7,6},{8,11},{9,8},{10,9... | collective-permute-start | bytes 884744 | tf_op jit(solution)/shard_map/ppermute | solution.py:28
  21.1 15.5 %collective-permute-start.6 = (bf16[128,2304]{1,0:T(8,128)(2,1)S(1)}, bf16[128,2304]{1,0:T(8,128)(2,1)S(1)}, u32[]{:S(2)}, u32[]{:S(2)}) collective-permute-start(bf16[128,2304]{1,0:T(8,128)(2,1)S(1)} %pad_maximum_fusion.refs_0_), channel_id=1, source_target_pairs={{0,12},{1,13},{2,14},{3,15},{4,0},{5,1},{6,2},{7,3},{8,4},{9,5},{1... | collective-permute-start | bytes 1769480 | tf_op jit(solution)/shard_map/ppermute | solution.py:28
  24.2 12.4 %collective-permute-start.5 = (bf16[128,2304]{1,0:T(8,128)(2,1)S(1)}, bf16[128,2304]{1,0:T(8,128)(2,1)S(1)}, u32[]{:S(2)}, u32[]{:S(2)}) collective-permute-start(bf16[128,2304]{1,0:T(8,128)(2,1)S(1)} %pad_maximum_fusion.refs_0_), channel_id=1, source_target_pairs={{0,4},{1,5},{2,6},{3,7},{4,8},{5,9},{6,10},{7,11},{8,12},{9,13},{1... | collective-permute-start | bytes 1769480 | tf_op jit(solution)/shard_map/ppermute | solution.py:28
  24.2 10.6 %collective-permute-start.9 = (bf16[64,2304]{1,0:T(8,128)(2,1)S(1)}, bf16[64,2304]{1,0:T(8,128)(2,1)S(1)}, u32[]{:S(2)}, u32[]{:S(2)}) collective-permute-start(bf16[64,2304]{1,0:T(8,128)(2,1)S(1)} %collective-permute-done.4), channel_id=1, source_target_pairs={{0,1},{1,2},{2,3},{3,0},{4,5},{5,6},{6,7},{7,4},{8,9},{9,10},{10,1... | collective-permute-start | bytes 884744 | tf_op jit(solution)/shard_map/ppermute | solution.py:28
  34.8 10.0 %collective-permute-start.11 = (bf16[128,2304]{1,0:T(8,128)(2,1)S(1)}, bf16[128,2304]{1,0:T(8,128)(2,1)S(1)}, u32[]{:S(2)}, u32[]{:S(2)}) collective-permute-start(bf16[128,2304]{1,0:T(8,128)(2,1)S(1)} %constant_dynamic-update-slice_fusion.refs_4_), channel_id=1, source_target_pairs={{0,12},{1,13},{2,14},{3,15},{4,0},{5,1},{6,2},{7,3},{8,4},{9,5},{1... | collective-permute-start | bytes 1769480 | tf_op jit(solution)/shard_map/ppermute | solution.py:28
  36.6 11.1 %collective-permute-start.7 = (bf16[128,2304]{1,0:T(8,128)(2,1)S(1)}, bf16[128,2304]{1,0:T(8,128)(2,1)S(1)}, u32[]{:S(2)}, u32[]{:S(2)}) collective-permute-start(bf16[128,2304]{1,0:T(8,128)(2,1)S(1)} %collective-permute-done.5.refs_1_), channel_id=1, source_target_pairs={{0,4},{1,5},{2,6},{3,7},{4,8},{5,9},{6,10},{7,11},{8,12},{9,13},{1... | collective-permute-start | bytes 1769480 | tf_op jit(solution)/shard_map/ppermute | solution.py:28
  44.8 12.8 %collective-permute-start.12 = (bf16[128,2304]{1,0:T(8,128)(2,1)S(1)}, bf16[128,2304]{1,0:T(8,128)(2,1)S(1)}, u32[]{:S(2)}, u32[]{:S(2)}) collective-permute-start(bf16[128,2304]{1,0:T(8,128)(2,1)S(1)} %collective-permute-done.11.refs_6_), channel_id=1, source_target_pairs={{0,12},{1,13},{2,14},{3,15},{4,0},{5,1},{6,2},{7,3},{8,4},{9,5},{1... | collective-permute-start | bytes 1769480 | tf_op jit(solution)/shard_map/ppermute | solution.py:28
  47.7 11.1 %collective-permute-start.10 = (bf16[128,2304]{1,0:T(8,128)(2,1)S(1)}, bf16[128,2304]{1,0:T(8,128)(2,1)S(1)}, u32[]{:S(2)}, u32[]{:S(2)}) collective-permute-start(bf16[128,2304]{1,0:T(8,128)(2,1)S(1)} %constant_dynamic-update-slice_fusion.refs_4_), channel_id=1, source_target_pairs={{0,4},{1,5},{2,6},{3,7},{4,8},{5,9},{6,10},{7,11},{8,12},{9,13},{1... | collective-permute-start | bytes 1769480 | tf_op jit(solution)/shard_map/ppermute | solution.py:28
  65.5 9.2 %collective-permute-start.18 = (f32[128,768]{1,0:T(8,128)S(1)}, f32[128,768]{1,0:T(8,128)S(1)}, u32[]{:S(2)}, u32[]{:S(2)}) collective-permute-start(f32[128,768]{1,0:T(8,128)S(1)} %slice.99), channel_id=1, source_target_pairs={{0,32},{1,33},{2,34},{3,35},{4,36},{5,37},{6,38},{7,39},{8,40},{9,... | collective-permute-start | bytes 1179656 | tf_op jit(solution)/shard_map/ppermute | solution.py:28
  74.8 13.3 %collective-permute-start.19 = (f32[128,768]{1,0:T(8,128)S(1)}, f32[128,768]{1,0:T(8,128)S(1)}, u32[]{:S(2)}, u32[]{:S(2)}) collective-permute-start(f32[128,768]{1,0:T(8,128)S(1)} %get-tuple-element.74), channel_id=1, source_target_pairs={{0,32},{1,33},{2,34},{3,35},{4,36},{5,37},{6,38},{7,39},{8,40},{9,... | collective-permute-start | bytes 1179656 | tf_op jit(solution)/shard_map/ppermute | solution.py:28
  74.9 13.2 %collective-permute-start.20 = (f32[128,768]{1,0:T(8,128)S(1)}, f32[128,768]{1,0:T(8,128)S(1)}, u32[]{:S(2)}, u32[]{:S(2)}) collective-permute-start(f32[128,768]{1,0:T(8,128)S(1)} %get-tuple-element.75), channel_id=1, source_target_pairs={{0,96},{1,97},{2,98},{3,99},{4,100},{5,101},{6,102},{7,103},{8,104... | collective-permute-start | bytes 1179656 | tf_op jit(solution)/shard_map/ppermute | solution.py:28
  78.1 10.1 %collective-permute-start.21 = (bf16[8,512]{1,0:T(8,128)(2,1)S(1)}, bf16[8,512]{1,0:T(8,128)(2,1)S(1)}, u32[]{:S(2)}, u32[]{:S(2)}) collective-permute-start(bf16[8,512]{1,0:T(8,128)(2,1)S(1)} %fusion.8), channel_id=1, source_target_pairs={{0,0},{1,8},{2,16},{3,24},{4,32},{5,40},{6,48},{7,56},{8,64},{9,72... | collective-permute-start | bytes 24584 | tf_op jit(solution)/shard_map/ppermute | solution.py:346
  129.3 7.4 %collective-permute-start.23 = (bf16[128,768]{1,0:T(8,128)(2,1)S(1)}, bf16[128,768]{1,0:T(8,128)(2,1)S(1)}, u32[]{:S(2)}, u32[]{:S(2)}) collective-permute-start(bf16[128,768]{1,0:T(8,128)(2,1)S(1)} %bitcast.23), channel_id=1, source_target_pairs={{0,96},{1,97},{2,98},{3,99},{4,100},{5,101},{6,102},{7,103},{8,104... | collective-permute-start | bytes 589832 | tf_op jit(solution)/shard_map/ppermute | solution.py:28
  136.2 6.9 %collective-permute-start.26 = (bf16[128,768]{1,0:T(8,128)(2,1)S(1)}, bf16[128,768]{1,0:T(8,128)(2,1)S(1)}, u32[]{:S(2)}, u32[]{:S(2)}) collective-permute-start(bf16[128,768]{1,0:T(8,128)(2,1)S(1)} %collective-permute-done.22.refs_1_), channel_id=1, source_target_pairs={{0,16},{16,0},{32,48},{48,32},{64,80},{80,64},{96,112},{112,96},{1... | collective-permute-start | bytes 589832 | tf_op jit(solution)/shard_map/ppermute | solution.py:33
  146.3 11.2 %collective-permute-start.30 = (bf16[128,2304]{1,0:T(8,128)(2,1)S(1)}, bf16[128,2304]{1,0:T(8,128)(2,1)S(1)}, u32[]{:S(2)}, u32[]{:S(2)}) collective-permute-start(bf16[128,2304]{1,0:T(8,128)(2,1)S(1)} %get-tuple-element.63), channel_id=1, source_target_pairs={{0,4},{1,5},{2,6},{3,7},{4,8},{5,9},{6,10},{7,11},{8,12},{9,13},{1... | collective-permute-start | bytes 1769480 | tf_op jit(solution)/shard_map/ppermute | solution.py:28
  146.9 10.5 %collective-permute-start.31 = (bf16[128,2304]{1,0:T(8,128)(2,1)S(1)}, bf16[128,2304]{1,0:T(8,128)(2,1)S(1)}, u32[]{:S(2)}, u32[]{:S(2)}) collective-permute-start(bf16[128,2304]{1,0:T(8,128)(2,1)S(1)} %get-tuple-element.64), channel_id=1, source_target_pairs={{0,12},{1,13},{2,14},{3,15},{4,0},{5,1},{6,2},{7,3},{8,4},{9,5},{1... | collective-permute-start | bytes 1769480 | tf_op jit(solution)/shard_map/ppermute | solution.py:28
  153.5 10.0 %collective-permute-start.29 = (bf16[128,2304]{1,0:T(8,128)(2,1)S(1)}, bf16[128,2304]{1,0:T(8,128)(2,1)S(1)}, u32[]{:S(2)}, u32[]{:S(2)}) collective-permute-start(bf16[128,2304]{1,0:T(8,128)(2,1)S(1)} %get-tuple-element.61), channel_id=1, source_target_pairs={{0,12},{1,13},{2,14},{3,15},{4,0},{5,1},{6,2},{7,3},{8,4},{9,5},{1... | collective-permute-start | bytes 1769480 | tf_op jit(solution)/shard_map/ppermute | solution.py:28
  153.5 11.2 %collective-permute-start.33 = (bf16[128,2304]{1,0:T(8,128)(2,1)S(1)}, bf16[128,2304]{1,0:T(8,128)(2,1)S(1)}, u32[]{:S(2)}, u32[]{:S(2)}) collective-permute-start(bf16[128,2304]{1,0:T(8,128)(2,1)S(1)} %get-tuple-element.66), channel_id=1, source_target_pairs={{0,4},{1,5},{2,6},{3,7},{4,8},{5,9},{6,10},{7,11},{8,12},{9,13},{1... | collective-permute-start | bytes 1769480 | tf_op jit(solution)/shard_map/ppermute | solution.py:28
  157.6 13.4 %collective-permute-start.32 = (bf16[128,2304]{1,0:T(8,128)(2,1)S(1)}, bf16[128,2304]{1,0:T(8,128)(2,1)S(1)}, u32[]{:S(2)}, u32[]{:S(2)}) collective-permute-start(bf16[128,2304]{1,0:T(8,128)(2,1)S(1)} %add_convert_fusion.1), channel_id=1, source_target_pairs={{0,4},{1,5},{2,6},{3,7},{4,8},{5,9},{6,10},{7,11},{8,12},{9,13},{1... | collective-permute-start | bytes 1769480 | tf_op jit(solution)/shard_map/ppermute | solution.py:28
  158.1 13.0 %collective-permute-start.34 = (bf16[128,2304]{1,0:T(8,128)(2,1)S(1)}, bf16[128,2304]{1,0:T(8,128)(2,1)S(1)}, u32[]{:S(2)}, u32[]{:S(2)}) collective-permute-start(bf16[128,2304]{1,0:T(8,128)(2,1)S(1)} %add_convert_fusion), channel_id=1, source_target_pairs={{0,12},{1,13},{2,14},{3,15},{4,0},{5,1},{6,2},{7,3},{8,4},{9,5},{1... | collective-permute-start | bytes 1769480 | tf_op jit(solution)/shard_map/ppermute | solution.py:28
  172.7 8.1 %collective-permute-start.35 = (f32[32,2304]{1,0:T(8,128)S(1)}, f32[32,2304]{1,0:T(8,128)S(1)}, u32[]{:S(2)}, u32[]{:S(2)}) collective-permute-start(f32[32,2304]{1,0:T(8,128)S(1)} %get-tuple-element.78), channel_id=1, source_target_pairs={{0,1},{1,2},{2,3},{3,0},{4,5},{5,6},{6,7},{7,4},{8,9},{9,10},{10,1... | collective-permute-start | bytes 884744 | tf_op jit(solution)/shard_map/ppermute | solution.py:28
  178.3 10.1 %collective-permute-start.38 = (f32[64,2304]{1,0:T(8,128)S(1)}, f32[64,2304]{1,0:T(8,128)}, u32[]{:S(2)}, u32[]{:S(2)}) collective-permute-start(f32[64,2304]{1,0:T(8,128)S(1)} %pad_maximum_fusion.2), channel_id=1, source_target_pairs={{0,3},{1,0},{2,1},{3,2},{4,7},{5,4},{6,5},{7,6},{8,11},{9,8},{10,9... | collective-permute-start | bytes 1769480 | tf_op jit(solution)/shard_map/ppermute | solution.py:28
  180.8 11.3 %collective-permute-start.36 = (f32[64,2304]{1,0:T(8,128)S(1)}, f32[64,2304]{1,0:T(8,128)}, u32[]{:S(2)}, u32[]{:S(2)}) collective-permute-start(f32[64,2304]{1,0:T(8,128)S(1)} %pad_maximum_fusion.1), channel_id=1, source_target_pairs={{0,1},{1,2},{2,3},{3,0},{4,5},{5,6},{6,7},{7,4},{8,9},{9,10},{10,1... | collective-permute-start | bytes 1769480 | tf_op jit(solution)/shard_map/ppermute | solution.py:28
  (22 other events, 269.7 us)

commit v2 on v1

--- a/solution.py
+++ b/solution.py
@@ -49,15 +49,6 @@
     return shift(value, lambda core: (0, (1 - core) * step, core * step))
 
 
-def exchange(value, along_y):
-    groups = [
-        [RING * i + k if along_y else RING * k + i for i in range(RING)] for k in range(RING)
-    ]
-    return lax.all_to_all(
-        value, "yz", split_axis=0, concat_axis=0, axis_index_groups=groups, tiled=True
-    )
-
-
 def rotation_tables(positions):
     half = HEAD // 2
     freq = 10000.0 ** (-jnp.arange(half, dtype=F32) * 2.0 / HEAD)
@@ -65,9 +56,51 @@
     return jnp.cos(angle), jnp.sin(angle)
 
 
+def sums_kernel(rows_ref, out_ref):
+    rows = rows_ref[...].astype(F32)
+    total = jnp.sum(rows, -1, keepdims=True)
+    squares = jnp.sum(rows * rows, -1, keepdims=True)
+    out_ref[...] = jnp.concatenate([total, squares], 1)
+
+
+def row_sums(rows):
+    vmem_spec = pl.BlockSpec(memory_space=pltpu.VMEM)
+    return pl.pallas_call(
+        sums_kernel,
+        out_shape=jax.ShapeDtypeStruct((rows.shape[0], 2), F32),
+        in_specs=[vmem_spec],
+        out_specs=vmem_spec,
+        compiler_params=pltpu.CompilerParams(vmem_limit_bytes=12 * 2**20),
+        name="row_sums",
+    )(rows)
+
+
+def normalize_kernel(one_ref, two_ref, one_sums, two_sums, gain_ref, out_ref):
+    count = one_ref.shape[0]
+    for index, (rows_ref, sums_ref) in enumerate(((one_ref, one_sums), (two_ref, two_sums))):
+        mean = sums_ref[:, 0:1] / D
+        var = sums_ref[:, 1:2] / D - mean * mean
+        rows = rows_ref[...].astype(F32)
+        normed = (rows - mean) * lax.rsqrt(var + 1e-05) * gain_ref[...]
+        out_ref[index * count : (index + 1) * count, :] = normed.astype(BF16)
+
+
+def normalize(one, two, one_sums, two_sums, gain):
+    vmem_spec = pl.BlockSpec(memory_space=pltpu.VMEM)
+    return pl.pallas_call(
+        normalize_kernel,
+        out_shape=jax.ShapeDtypeStruct((2 * one.shape[0], one.shape[1]), BF16),
+        in_specs=[vmem_spec] * 5,
+        out_specs=vmem_spec,
+        compiler_params=pltpu.CompilerParams(vmem_limit_bytes=12 * 2**20),
+        name="normalize",
+    )(one, two, one_sums, two_sums, gain)
+
+
 def keyval_kernel(place, rows_ref, w_ref, away_ref, keep_ref, sums_ref):
     x, core = place[0], place[3]
-    sums_ref[...] = jnp.dot(rows_ref[...], w_ref[...], preferred_element_type=F32)
+    rows = rows_ref[: sums_ref.shape[0], :]
+    sums_ref[...] = jnp.dot(rows, w_ref[...], preferred_element_type=F32)
     for slot in range(RING):
         block = 2 * lax.rem(x + slot, RING)
         target = pl.ds(8 * slot, 8)
@@ -76,7 +109,7 @@
 
 
 def project_keyval(place, rows, w_keyval):
-    count, depth = rows.shape
+    count, depth = rows.shape[0] // 2, rows.shape[1]
     columns = w_keyval.shape[1]
     vmem_spec = pl.BlockSpec(memory_space=pltpu.VMEM)
     half = jax.ShapeDtypeStruct((count // 2, columns), F32)
@@ -94,8 +127,8 @@
     )(place, rows, w_keyval)
 
 
-def query_kernel(other, place, *refs):
-    pieces, (w_ref, out_ref, rows_ref) = refs[:8], refs[8:]
+def query_kernel(pair, place, *refs):
+    pieces, (w_ref, away_ref, keep_ref, rows_ref) = refs[:8], refs[8:]
     x, y, z, core = place[0], place[1], place[2], place[3]
     for index, piece in enumerate(pieces):
         for part in range(2):
@@ -106,24 +139,28 @@
             to_core = at_z // 2
             ahead = lax.rem(at_y - x + RING, RING)
             slot = jnp.where(to_core == 0, ahead, lax.rem(RING - ahead, RING))
-            position = slot * 2 + lax.rem(at_z, 2)
-
-            @pl.when((to_core != core) == other)
+            mine = jnp.where(to_core == core, 4, 0)
+            position = mine + lax.rem(slot, 2) * 2 + lax.rem(at_z, 2)
+
+            @pl.when(slot // 2 == pair)
             def _():
                 rows_ref[position] = piece[part * 64 : (part + 1) * 64, :]
 
     rows = rows_ref[...].reshape(512, w_ref.shape[0])
-    out_ref[...] = jnp.dot(rows, w_ref[...], preferred_element_type=F32)
-
-
-def project_query(place, pieces, w_query, other):
+    result = jnp.dot(rows, w_ref[...], preferred_element_type=F32)
+    away_ref[...] = result[:256]
+    keep_ref[...] = result[256:]
+
+
+def project_query(place, pieces, w_query, pair):
     depth, columns = w_query.shape
     vmem_spec = pl.BlockSpec(memory_space=pltpu.VMEM)
-    return pl.pallas_call(
-        functools.partial(query_kernel, other),
-        out_shape=jax.ShapeDtypeStruct((512, columns), F32),
+    half = jax.ShapeDtypeStruct((256, columns), F32)
+    return pl.pallas_call(
+        functools.partial(query_kernel, pair),
+        out_shape=[half, half],
         in_specs=[pl.BlockSpec(memory_space=pltpu.SMEM)] + [vmem_spec] * 9,
-        out_specs=vmem_spec,
+        out_specs=[vmem_spec] * 2,
         scratch_shapes=[pltpu.VMEM((8, 64, depth), BF16)],
         compiler_params=pltpu.CompilerParams(vmem_limit_bytes=20 * 2**20),
         cost_estimate=pl.CostEstimate(
@@ -300,24 +337,21 @@
 
     count = tokens.shape[0] * 2
     features = tokens.shape[2]
-    xfull = tokens.reshape(count, features).astype(F32)
-    stats = jnp.stack([jnp.sum(xfull, -1), jnp.sum(xfull * xfull, -1)])
-    stats = stats + send_core(stats)
-    stats, cosine, sine, place = lax.optimization_barrier((stats, cosine, sine, place))
-    stats = stats + send_x(stats, 1) + send_x(stats, 2) + send_x(stats, 3)
-    mean = stats[0] / D
-    var = stats[1] / D - mean * mean
-    normed = ((xfull - mean[:, None]) * lax.rsqrt(var + 1e-05)[:, None] * gain).astype(BF16)
-
-    normed = lax.optimization_barrier(normed)
-    keyval_away, keyval_keep = project_keyval(place, normed, w_keyval)
-
-    before = send_inner(normed, 1)
-    after = send_inner(normed, -1)
+    raw = lax.optimization_barrier(tokens.reshape(count, features))
+    sums = row_sums(raw)
+    before, after = send_inner(raw, 1), send_inner(raw, -1)
+    sums = sums + send_core(sums)
+    sums, cosine, sine, place = lax.optimization_barrier((sums, cosine, sine, place))
+    sums = sums + send_x(sums, 1) + send_x(sums, 2) + send_x(sums, 3)
+    sums, before, after = lax.optimization_barrier((sums, before, after))
     far = send_inner(before, 1)
-    near = jnp.concatenate([normed, before], 0)
-    near, keyval_away = lax.optimization_barrier((near, keyval_away))
-    wide = jnp.concatenate([after, far], 0)
+    scale = gain.reshape(1, features)
+    near = normalize(raw, before, sums, send_inner(sums, 1), scale)
+    near, far = lax.optimization_barrier((near, far))
+    wide = normalize(after, far, send_inner(sums, -1), send_inner(sums, 2), scale)
+
+    keyval_away, keyval_keep = project_keyval(place, near, w_keyval)
+
     near_before, near_after = send_outer(near, 1), send_outer(near, -1)
     near_before, near_after = lax.optimization_barrier((near_before, near_after))
     wide_after = send_outer(wide, -1)
@@ -333,11 +367,11 @@
     pieces = [near, near_before, near_after, near_far, wide, wide_before, wide_after, wide_far]
     columns = w_query.shape[1]
     pieces, keyval = lax.optimization_barrier((pieces, keyval))
-    away = project_query(place, pieces, w_query, True)
-    keep = project_query(place, pieces, w_query, False)
-    summed = (keep + send_core(away)).reshape(RING, 128, columns)
-    far = send_x(summed[2], 1)
-    behind = send_x(summed[3], -1)
+    away, keep = project_query(place, pieces, w_query, 1)
+    summed = (keep + send_core(away)).reshape(2, 128, columns)
+    far, behind = send_x(summed[0], 1), send_x(summed[1], -1)
+    away, keep = project_query(place, pieces, w_query, 0)
+    summed = (keep + send_core(away)).reshape(2, 128, columns)
     ahead = send_x(summed[1] + far, 1)
     query = (summed[0] + ahead + behind).astype(BF16).reshape(16, 8, columns)
     moves = [
@@ -345,14 +379,14 @@
     ]
     keyval = lax.ppermute(keyval, ("gx", "yz"), moves)
     query, keyval = lax.optimization_barrier((query, keyval))
-    query = exchange(query.reshape(RING, RING, 8, columns), True)
-    query = exchange(jnp.swapaxes(query, 0, 1), False)
+    query = lax.all_to_all(query, "yz", split_axis=0, concat_axis=0)
 
     heads_out, new_keyval = attend(
         lengths, query.reshape(128, columns), cosine, sine, keyval, key_cache, value_cache
     )
-    heads_out = exchange(heads_out.reshape(RING, RING, 8, columns), False)
-    heads_out = exchange(jnp.swapaxes(heads_out, 0, 1), True).reshape(128, columns)
+    heads_out = lax.all_to_all(
+        heads_out.reshape(16, 8, columns), "yz", split_axis=0, concat_axis=0
+    ).reshape(128, columns)
     before = send_x(heads_out, 1)
     after = send_x(heads_out, -1)
     pieces = [heads_out, before, after, send_x(before, 1)]
@@ -374,7 +408,7 @@
     one = jnp.concatenate([one[:32] + far_low, one[32:]], 0)
     three = jnp.concatenate([three[:32], three[32:] + far_high], 0)
     branch = here + send_inner(one, 1) + send_inner(three, -1)
-    mixed = (xfull + branch).astype(BF16).reshape(tokens.shape)
+    mixed = (raw.astype(F32) + branch).astype(BF16).reshape(tokens.shape)
     return (mixed, new_keyval.reshape(seqs, 2, 2 * HEAD))
 
 

time: 195 us -> 183 us (0.938)
  blocking collectives: 36.7 us -> 28 us
  waiting for transfers between devices: 86.6 us -> 78.3 us
  starting transfers between devices: 43.3 us -> 51.5 us
    all_to_all x4 -> x2, blocking collectives: 36.7 us -> 28 us  [the longest x1 16.4 us: body(): query = lax.all_to_all(query, 'yz', split_axis=0, concat_axis=0)]
    ppermute x31 -> x34, waiting for transfers between devices: 83.4 us -> 75.5 us  [shift(): return lax.ppermute(value, ('gx', 'yz'), pairs)]
    ppermute x31 -> x34, starting transfers between devices: 42 us -> 49.5 us  [shift(): return lax.ppermute(value, ('gx', 'yz'), pairs)]
    pallas_call x2 -> x5, Pallas kernels: 5.9 us -> 7.08 us  [the longest x2 6.35 us: project_query(): pl.pallas_call(functools.partial(query_kernel, pair), out_shape=[half, ha...]
  transfers between devices with their start and end apart: 39 -> 43, of which waited for: 23 -> 23; matrix products, arithmetic and copies ran while one was open for 2% -> 1% of each run, Pallas kernels for 4% -> 5%
where the time goes in v2:
time: 183 us
  waiting for transfers between devices  78.3 us (43%)
  starting transfers between devices  51.5 us (28%)
  blocking collectives  28 us (15%)
  Pallas kernels  18.4 us (10%)
  local copies, waits for them, and re-layouts  3.48 us (2%)
  other arithmetic  2.51 us (1%)
    ppermute x34, waiting for transfers between devices, shift(): return lax.ppermute(value, ('gx', 'yz'), pairs)  75.5 us
    ppermute x34, starting transfers between devices, shift(): return lax.ppermute(value, ('gx', 'yz'), pairs)  49.5 us
    all_to_all x1, blocking collectives, body(): query = lax.all_to_all(query, 'yz', split_axis=0, concat_axis=0)  16.4 us
    all_to_all x1, blocking collectives, body(): lax.all_to_all(heads_out.reshape(16, 8, columns), 'yz', split_axis=0, con...  11.6 us
    pallas_call x2, Pallas kernels, project_query(): pl.pallas_call(functools.partial(query_kernel, pair), out_shape=[half, ha...  6.35 us
    pallas_call x2, Pallas kernels, project_output(): pl.pallas_call(functools.partial(output_kernel, groups), out_shape=shapes...  5.86 us
    pallas_call x1, Pallas kernels, attend(): pl.pallas_call(attend_kernel, out_shape=[jax.ShapeDtypeStruct((rows, colu...  4.36 us
  transfers between devices with their start and end apart: 43, of which 23 were waited for; matrix products, arithmetic and copies ran while one was open for 1% of the time, Pallas kernels for 5%

profile of v2, /device:TPU:0, one launch (start us, length us, event | category | flops | bytes accessed | tf_op | source)
XLA Modules:
  0.0 183.2 jit_solution(8044427275242938543)
XLA Ops:
  8.9 2.7 %collective-permute-start.2 = (f32[64,2]{1,0:T(8,128)S(1)}, f32[64,2]{1,0:T(8,128)S(1)}, u32[]{:S(2)}, u32[]{:S(2)}) collective-permute-start(f32[64,2]{1,0:T(8,128)S(1)} %add.81), channel_id=1, source_target_pairs={{0,64},{1,65},{2,66},{3,67},{4,68},{5,69},{6,70},{7,71},{8,72},{9,... | collective-permute-start | bytes 1544 | tf_op jit(solution)/shard_map/ppermute | solution.py:28
  18.0 6.0 %collective-permute-done.6.two_sums = f32[64,2]{1,0:T(8,128)S(1)} collective-permute-done((f32[64,2]{1,0:T(8,128)S(1)}, f32[64,2]{1,0:T(8,128)S(1)}, u32[]{:S(2)}, u32[]{:S(2)}) %collective-permute-start.6) | collective-permute-done | bytes 544 | tf_op jit(solution)/shard_map/ppermute | solution.py:28
  28.8 3.1 %collective-permute-done.11.one_sums = f32[64,2]{1,0:T(8,128)S(1)} collective-permute-done((f32[64,2]{1,0:T(8,128)S(1)}, f32[64,2]{1,0:T(8,128)S(1)}, u32[]{:S(2)}, u32[]{:S(2)}) %collective-permute-start.11) | collective-permute-done | bytes 544 | tf_op jit(solution)/shard_map/ppermute | solution.py:28
  37.7 6.8 %collective-permute-done.14.refs_6_ = bf16[128,2304]{1,0:T(8,128)(2,1)S(1)} collective-permute-done((bf16[128,2304]{1,0:T(8,128)(2,1)S(1)}, bf16[128,2304]{1,0:T(8,128)(2,1)S(1)}, u32[]{:S(2)}, u32[]{:S(2)}) %collective-permute-start.14) | collective-permute-done | bytes 589856 | tf_op jit(solution)/shard_map/ppermute | solution.py:28
  50.1 4.3 %collective-permute-start.18 = (f32[8,512]{1,0:T(8,128)S(1)}, f32[8,512]{1,0:T(8,128)S(1)}, u32[]{:S(2)}, u32[]{:S(2)}) collective-permute-start(f32[8,512]{1,0:T(8,128)S(1)} %get-tuple-element.95), channel_id=1, source_target_pairs={{0,64},{1,65},{2,66},{3,67},{4,68},{5,69},{6,70},{7,71},{8,72},{9,... | collective-permute-start | bytes 49160 | tf_op jit(solution)/shard_map/ppermute | solution.py:28
  58.2 3.1 %query_projection.3 = (f32[256,768]{1,0:T(8,128)S(1)}, f32[256,768]{1,0:T(8,128)S(1)}) custom-call(s32[4]{0:T(128)S(1)} %pad_add_fusion.place, bf16[128,2304]{1,0:T(8,128)(2,1)S(1)} %normalize.2.rows_ref.refs_0_, bf16[128,2304]{1,0:T(8,128)(2,1)S(1)} %collective-permute-done.8.refs_1_, bf16[128,2304]{1,0:T(8,128)(2,1)S(1)} %collective-permute-done.9.refs_2_, ...), custom_call_target="tpu_custom_call" | custom-call | flops 1811939328 | bytes 8388608 | tf_op jit(solution)/shard_map/query_projection/pallas_call | solution.py:159
  61.4 3.3 %query_projection.2 = (f32[256,768]{1,0:T(8,128)S(1)}, f32[256,768]{1,0:T(8,128)S(1)}) custom-call(s32[4]{0:T(128)S(1)} %pad_add_fusion.place, bf16[128,2304]{1,0:T(8,128)(2,1)S(1)} %normalize.2.rows_ref.refs_0_, bf16[128,2304]{1,0:T(8,128)(2,1)S(1)} %collective-permute-done.8.refs_1_, bf16[128,2304]{1,0:T(8,128)(2,1)S(1)} %collective-permute-done.9.refs_2_, ...), custom_call_target="tpu_custom_call" | custom-call | flops 1811939328 | bytes 8388608 | tf_op jit(solution)/shard_map/query_projection/pallas_call | solution.py:159
  65.6 3.0 %collective-permute-start.24 = (f32[128,768]{1,0:T(8,128)S(1)}, f32[128,768]{1,0:T(8,128)S(1)}, u32[]{:S(2)}, u32[]{:S(2)}) collective-permute-start(f32[128,768]{1,0:T(8,128)S(1)} %get-tuple-element.92), channel_id=1, source_target_pairs={{0,96},{1,97},{2,98},{3,99},{4,100},{5,101},{6,102},{7,103},{8,104... | collective-permute-start | bytes 1179656 | tf_op jit(solution)/shard_map/ppermute | solution.py:28
  68.8 8.1 %collective-permute-done.22 = f32[128,768]{1,0:T(8,128)S(1)} collective-permute-done((f32[128,768]{1,0:T(8,128)S(1)}, f32[128,768]{1,0:T(8,128)S(1)}, u32[]{:S(2)}, u32[]{:S(2)}) %collective-permute-start.22) | collective-permute-done | bytes 393248 | tf_op jit(solution)/shard_map/ppermute | solution.py:28
  77.7 8.5 %collective-permute-done.23 = f32[128,768]{1,0:T(8,128)S(1)} collective-permute-done((f32[128,768]{1,0:T(8,128)S(1)}, f32[128,768]{1,0:T(8,128)S(1)}, u32[]{:S(2)}, u32[]{:S(2)}) %collective-permute-start.23) | collective-permute-done | bytes 393248 | tf_op jit(solution)/shard_map/ppermute | solution.py:28
  86.2 16.4 %all_to_all.10 = bf16[16,8,768]{2,1,0:T(8,128)(2,1)S(1)} all-to-all(bf16[16,8,768]{2,1,0:T(8,128)(2,1)S(1)} %fusion.5), channel_id=1, replica_groups=mesh['gx'=8,'yz'=16] {'yz'}, dimensions={0} | all-to-all | bytes 393216 | tf_op jit(solution)/shard_map/all_to_all | solution.py:382
  102.6 4.4 %attention.1 = (bf16[128,768]{1,0:T(8,128)(2,1)S(1)}, bf16[8,512]{1,0:T(8,128)(2,1)S(1)}) custom-call(s32[4]{0:T(128)S(1)} %copy-done.5, bf16[128,768]{1,0:T(8,128)(2,1)S(1)} %bitcast.14, f32[8,128]{1,0:T(8,128)S(1)} %get-tuple-element.70.cos_ref, f32[8,128]{1,0:T(8,128)S(1)} %get-tuple-element.71.sin_ref, ...), custom_call_target="tpu_custom_call" | custom-call | flops 805306368 | bytes 8388608 | tf_op jit(solution)/shard_map/attention/pallas_call | solution.py:256
  107.0 11.6 %all_to_all.11 = bf16[16,8,768]{2,1,0:T(8,128)(2,1)S(1)} all-to-all(bf16[16,8,768]{2,1,0:T(8,128)(2,1)S(1)} %bitcast.15), channel_id=1, replica_groups=mesh['gx'=8,'yz'=16] {'yz'}, dimensions={0} | all-to-all | bytes 393216 | tf_op jit(solution)/shard_map/all_to_all | solution.py:387
  119.0 2.8 %collective-permute-start.27 = (bf16[128,768]{1,0:T(8,128)(2,1)S(1)}, bf16[128,768]{1,0:T(8,128)(2,1)S(1)}, u32[]{:S(2)}, u32[]{:S(2)}) collective-permute-start(bf16[128,768]{1,0:T(8,128)(2,1)S(1)} %bitcast.10), channel_id=1, source_target_pairs={{0,96},{1,97},{2,98},{3,99},{4,100},{5,101},{6,102},{7,103},{8,104... | collective-permute-start | bytes 589832 | tf_op jit(solution)/shard_map/ppermute | solution.py:28
  121.8 3.6 %collective-permute-done.26.refs_1_ = bf16[128,768]{1,0:T(8,128)(2,1)S(1)} collective-permute-done((bf16[128,768]{1,0:T(8,128)(2,1)S(1)}, bf16[128,768]{1,0:T(8,128)(2,1)S(1)}, u32[]{:S(2)}, u32[]{:S(2)}) %collective-permute-start.26) | collective-permute-done | bytes 196640 | tf_op jit(solution)/shard_map/ppermute | solution.py:28
  126.0 6.4 %collective-permute-done.28.refs_3_ = bf16[128,768]{1,0:T(8,128)(2,1)S(1)} collective-permute-done((bf16[128,768]{1,0:T(8,128)(2,1)S(1)}, bf16[128,768]{1,0:T(8,128)(2,1)S(1)}, u32[]{:S(2)}, u32[]{:S(2)}) %collective-permute-start.28) | collective-permute-done | bytes 196640 | tf_op jit(solution)/shard_map/ppermute | solution.py:28
  136.1 2.8 %collective-permute-start.35 = (bf16[128,2304]{1,0:T(8,128)(2,1)S(1)}, bf16[128,2304]{1,0:T(8,128)(2,1)S(1)}, u32[]{:S(2)}, u32[]{:S(2)}) collective-permute-start(bf16[128,2304]{1,0:T(8,128)(2,1)S(1)} %get-tuple-element.78), channel_id=1, source_target_pairs={{0,12},{1,13},{2,14},{3,15},{4,0},{5,1},{6,2},{7,3},{8,4},{9,5},{1... | collective-permute-start | bytes 1769480 | tf_op jit(solution)/shard_map/ppermute | solution.py:28
  138.9 4.1 %output_projection.2 = (bf16[128,2304]{1,0:T(8,128)(2,1)S(1)}, bf16[128,2304]{1,0:T(8,128)(2,1)S(1)}, bf16[128,2304]{1,0:T(8,128)(2,1)S(1)}, bf16[128,2304]{1,0:T(8,128)(2,1)S(1)}, f32[256,2304]{1,0:T(8,128)S(1)}) custom-call(s32[4]{0:T(128)S(1)} %pad_add_fusion.place, bf16[128,768]{1,0:T(8,128)(2,1)S(1)} %bitcast.13, ...), custom_call_target="tpu_custom_call" | custom-call | flops 2717908992 | bytes 8388608 | tf_op jit(solution)/shard_map/output_projection/pallas_call | solution.py:315
  146.9 3.3 %collective-permute-start.38 = (bf16[128,2304]{1,0:T(8,128)(2,1)S(1)}, bf16[128,2304]{1,0:T(8,128)(2,1)S(1)}, u32[]{:S(2)}, u32[]{:S(2)}) collective-permute-start(bf16[128,2304]{1,0:T(8,128)(2,1)S(1)} %add_convert_fusion), channel_id=1, source_target_pairs={{0,12},{1,13},{2,14},{3,15},{4,0},{5,1},{6,2},{7,3},{8,4},{9,5},{1... | collective-permute-start | bytes 1769480 | tf_op jit(solution)/shard_map/ppermute | solution.py:28
  154.2 5.0 %collective-permute-done.38 = bf16[128,2304]{1,0:T(8,128)(2,1)S(1)} collective-permute-done((bf16[128,2304]{1,0:T(8,128)(2,1)S(1)}, bf16[128,2304]{1,0:T(8,128)(2,1)S(1)}, u32[]{:S(2)}, u32[]{:S(2)}) %collective-permute-start.38) | collective-permute-done | bytes 589856 | tf_op jit(solution)/shard_map/ppermute | solution.py:28
  162.4 2.7 %collective-permute-start.41 = (f32[32,2304]{1,0:T(8,128)S(1)}, f32[32,2304]{1,0:T(8,128)S(1)}, u32[]{:S(2)}, u32[]{:S(2)}) collective-permute-start(f32[32,2304]{1,0:T(8,128)S(1)} %get-tuple-element.89), channel_id=1, source_target_pairs={{0,3},{1,0},{2,1},{3,2},{4,7},{5,4},{6,5},{7,6},{8,11},{9,8},{10,9... | collective-permute-start | bytes 884744 | tf_op jit(solution)/shard_map/ppermute | solution.py:28
  165.2 4.7 %collective-permute-done.39 = f32[32,2304]{1,0:T(8,128)S(1)} collective-permute-done((f32[32,2304]{1,0:T(8,128)S(1)}, f32[32,2304]{1,0:T(8,128)S(1)}, u32[]{:S(2)}, u32[]{:S(2)}) %collective-permute-start.39) | collective-permute-done | bytes 294944 | tf_op jit(solution)/shard_map/ppermute | solution.py:28
  170.2 3.3 %collective-permute-start.42 = (f32[64,2304]{1,0:T(8,128)S(1)}, f32[64,2304]{1,0:T(8,128)}, u32[]{:S(2)}, u32[]{:S(2)}) collective-permute-start(f32[64,2304]{1,0:T(8,128)S(1)} %pad_maximum_fusion.1), channel_id=1, source_target_pairs={{0,3},{1,0},{2,1},{3,2},{4,7},{5,4},{6,5},{7,6},{8,11},{9,8},{10,9... | collective-permute-start | bytes 1769480 | tf_op jit(solution)/shard_map/ppermute | solution.py:28
  174.1 7.1 %collective-permute-done.40 = f32[64,2304]{1,0:T(8,128)S(1)} collective-permute-done((f32[64,2304]{1,0:T(8,128)S(1)}, f32[64,2304]{1,0:T(8,128)S(1)}, u32[]{:S(2)}, u32[]{:S(2)}) %collective-permute-start.40) | collective-permute-done | bytes 589856 | tf_op jit(solution)/shard_map/ppermute | solution.py:28
  (116 shorter events, 55.3 us)
Async XLA Ops:
  1.7 13.9 %collective-permute-start.4 = (bf16[64,2304]{1,0:T(8,128)(2,1)S(1)}, bf16[64,2304]{1,0:T(8,128)(2,1)S(1)}, u32[]{:S(2)}, u32[]{:S(2)}) collective-permute-start(bf16[64,2304]{1,0:T(8,128)(2,1)S(1)} %reshape.66.rows_ref.one_ref), channel_id=1, source_target_pairs={{0,1},{1,2},{2,3},{3,0},{4,5},{5,6},{6,7},{7,4},{8,9},{9,10},{10,1... | collective-permute-start | bytes 884744 | tf_op jit(solution)/shard_map/ppermute | solution.py:28
  3.8 11.8 %collective-permute-start.5 = (bf16[64,2304]{1,0:T(8,128)(2,1)S(1)}, bf16[64,2304]{1,0:T(8,128)(2,1)S(1)}, u32[]{:S(2)}, u32[]{:S(2)}) collective-permute-start(bf16[64,2304]{1,0:T(8,128)(2,1)S(1)} %reshape.66.rows_ref.one_ref), channel_id=1, source_target_pairs={{0,3},{1,0},{2,1},{3,2},{4,7},{5,4},{6,5},{7,6},{8,11},{9,8},{10,9... | collective-permute-start | bytes 884744 | tf_op jit(solution)/shard_map/ppermute | solution.py:28
  15.6 8.7 %collective-permute-start.7 = (bf16[64,2304]{1,0:T(8,128)(2,1)S(1)}, bf16[64,2304]{1,0:T(8,128)(2,1)S(1)}, u32[]{:S(2)}, u32[]{:S(2)}) collective-permute-start(bf16[64,2304]{1,0:T(8,128)(2,1)S(1)} %collective-permute-done.4.two_ref), channel_id=1, source_target_pairs={{0,1},{1,2},{2,3},{3,0},{4,5},{5,6},{6,7},{7,4},{8,9},{9,10},{10,1... | collective-permute-start | bytes 884744 | tf_op jit(solution)/shard_map/ppermute | solution.py:28
  16.0 7.9 %collective-permute-start.6 = (f32[64,2]{1,0:T(8,128)S(1)}, f32[64,2]{1,0:T(8,128)S(1)}, u32[]{:S(2)}, u32[]{:S(2)}) collective-permute-start(f32[64,2]{1,0:T(8,128)S(1)} %add_add_fusion.one_sums), channel_id=1, source_target_pairs={{0,1},{1,2},{2,3},{3,0},{4,5},{5,6},{6,7},{7,4},{8,9},{9,10},{10,1... | collective-permute-start | bytes 1544 | tf_op jit(solution)/shard_map/ppermute | solution.py:28
  24.3 11.6 %collective-permute-start.8 = (bf16[128,2304]{1,0:T(8,128)(2,1)S(1)}, bf16[128,2304]{1,0:T(8,128)(2,1)S(1)}, u32[]{:S(2)}, u32[]{:S(2)}) collective-permute-start(bf16[128,2304]{1,0:T(8,128)(2,1)S(1)} %normalize.2.rows_ref.refs_0_), channel_id=1, source_target_pairs={{0,4},{1,5},{2,6},{3,7},{4,8},{5,9},{6,10},{7,11},{8,12},{9,13},{1... | collective-permute-start | bytes 1769480 | tf_op jit(solution)/shard_map/ppermute | solution.py:28
  25.9 10.0 %collective-permute-start.9 = (bf16[128,2304]{1,0:T(8,128)(2,1)S(1)}, bf16[128,2304]{1,0:T(8,128)(2,1)S(1)}, u32[]{:S(2)}, u32[]{:S(2)}) collective-permute-start(bf16[128,2304]{1,0:T(8,128)(2,1)S(1)} %normalize.2.rows_ref.refs_0_), channel_id=1, source_target_pairs={{0,12},{1,13},{2,14},{3,15},{4,0},{5,1},{6,2},{7,3},{8,4},{9,5},{1... | collective-permute-start | bytes 1769480 | tf_op jit(solution)/shard_map/ppermute | solution.py:28
  34.6 10.0 %collective-permute-start.14 = (bf16[128,2304]{1,0:T(8,128)(2,1)S(1)}, bf16[128,2304]{1,0:T(8,128)(2,1)S(1)}, u32[]{:S(2)}, u32[]{:S(2)}) collective-permute-start(bf16[128,2304]{1,0:T(8,128)(2,1)S(1)} %normalize.3.refs_4_), channel_id=1, source_target_pairs={{0,12},{1,13},{2,14},{3,15},{4,0},{5,1},{6,2},{7,3},{8,4},{9,5},{1... | collective-permute-start | bytes 1769480 | tf_op jit(solution)/shard_map/ppermute | solution.py:28
  35.9 11.1 %collective-permute-start.10 = (bf16[128,2304]{1,0:T(8,128)(2,1)S(1)}, bf16[128,2304]{1,0:T(8,128)(2,1)S(1)}, u32[]{:S(2)}, u32[]{:S(2)}) collective-permute-start(bf16[128,2304]{1,0:T(8,128)(2,1)S(1)} %collective-permute-done.8.refs_1_), channel_id=1, source_target_pairs={{0,4},{1,5},{2,6},{3,7},{4,8},{5,9},{6,10},{7,11},{8,12},{9,13},{1... | collective-permute-start | bytes 1769480 | tf_op jit(solution)/shard_map/ppermute | solution.py:28
  44.5 13.6 %collective-permute-start.15 = (bf16[128,2304]{1,0:T(8,128)(2,1)S(1)}, bf16[128,2304]{1,0:T(8,128)(2,1)S(1)}, u32[]{:S(2)}, u32[]{:S(2)}) collective-permute-start(bf16[128,2304]{1,0:T(8,128)(2,1)S(1)} %collective-permute-done.14.refs_6_), channel_id=1, source_target_pairs={{0,12},{1,13},{2,14},{3,15},{4,0},{5,1},{6,2},{7,3},{8,4},{9,5},{1... | collective-permute-start | bytes 1769480 | tf_op jit(solution)/shard_map/ppermute | solution.py:28
  47.0 11.2 %collective-permute-start.13 = (bf16[128,2304]{1,0:T(8,128)(2,1)S(1)}, bf16[128,2304]{1,0:T(8,128)(2,1)S(1)}, u32[]{:S(2)}, u32[]{:S(2)}) collective-permute-start(bf16[128,2304]{1,0:T(8,128)(2,1)S(1)} %normalize.3.refs_4_), channel_id=1, source_target_pairs={{0,4},{1,5},{2,6},{3,7},{4,8},{5,9},{6,10},{7,11},{8,12},{9,13},{1... | collective-permute-start | bytes 1769480 | tf_op jit(solution)/shard_map/ppermute | solution.py:28
  65.4 11.5 %collective-permute-start.22 = (f32[128,768]{1,0:T(8,128)S(1)}, f32[128,768]{1,0:T(8,128)S(1)}, u32[]{:S(2)}, u32[]{:S(2)}) collective-permute-start(f32[128,768]{1,0:T(8,128)S(1)} %get-tuple-element.91), channel_id=1, source_target_pairs={{0,32},{1,33},{2,34},{3,35},{4,36},{5,37},{6,38},{7,39},{8,40},{9,... | collective-permute-start | bytes 1179656 | tf_op jit(solution)/shard_map/ppermute | solution.py:28
  65.6 12.0 %collective-permute-start.24 = (f32[128,768]{1,0:T(8,128)S(1)}, f32[128,768]{1,0:T(8,128)S(1)}, u32[]{:S(2)}, u32[]{:S(2)}) collective-permute-start(f32[128,768]{1,0:T(8,128)S(1)} %get-tuple-element.92), channel_id=1, source_target_pairs={{0,96},{1,97},{2,98},{3,99},{4,100},{5,101},{6,102},{7,103},{8,104... | collective-permute-start | bytes 1179656 | tf_op jit(solution)/shard_map/ppermute | solution.py:28
  76.9 9.2 %collective-permute-start.23 = (f32[128,768]{1,0:T(8,128)S(1)}, f32[128,768]{1,0:T(8,128)S(1)}, u32[]{:S(2)}, u32[]{:S(2)}) collective-permute-start(f32[128,768]{1,0:T(8,128)S(1)} %slice_add_fusion.1), channel_id=1, source_target_pairs={{0,32},{1,33},{2,34},{3,35},{4,36},{5,37},{6,38},{7,39},{8,40},{9,... | collective-permute-start | bytes 1179656 | tf_op jit(solution)/shard_map/ppermute | solution.py:28
  77.0 9.2 %collective-permute-start.25 = (bf16[8,512]{1,0:T(8,128)(2,1)S(1)}, bf16[8,512]{1,0:T(8,128)(2,1)S(1)}, u32[]{:S(2)}, u32[]{:S(2)}) collective-permute-start(bf16[8,512]{1,0:T(8,128)(2,1)S(1)} %fusion.8), channel_id=1, source_target_pairs={{0,0},{1,8},{2,16},{3,24},{4,32},{5,40},{6,48},{7,56},{8,64},{9,72... | collective-permute-start | bytes 24584 | tf_op jit(solution)/shard_map/ppermute | solution.py:380
  135.6 11.2 %collective-permute-start.34 = (bf16[128,2304]{1,0:T(8,128)(2,1)S(1)}, bf16[128,2304]{1,0:T(8,128)(2,1)S(1)}, u32[]{:S(2)}, u32[]{:S(2)}) collective-permute-start(bf16[128,2304]{1,0:T(8,128)(2,1)S(1)} %get-tuple-element.77), channel_id=1, source_target_pairs={{0,4},{1,5},{2,6},{3,7},{4,8},{5,9},{6,10},{7,11},{8,12},{9,13},{1... | collective-permute-start | bytes 1769480 | tf_op jit(solution)/shard_map/ppermute | solution.py:28
  136.1 10.7 %collective-permute-start.35 = (bf16[128,2304]{1,0:T(8,128)(2,1)S(1)}, bf16[128,2304]{1,0:T(8,128)(2,1)S(1)}, u32[]{:S(2)}, u32[]{:S(2)}) collective-permute-start(bf16[128,2304]{1,0:T(8,128)(2,1)S(1)} %get-tuple-element.78), channel_id=1, source_target_pairs={{0,12},{1,13},{2,14},{3,15},{4,0},{5,1},{6,2},{7,3},{8,4},{9,5},{1... | collective-permute-start | bytes 1769480 | tf_op jit(solution)/shard_map/ppermute | solution.py:28
  142.9 10.0 %collective-permute-start.33 = (bf16[128,2304]{1,0:T(8,128)(2,1)S(1)}, bf16[128,2304]{1,0:T(8,128)(2,1)S(1)}, u32[]{:S(2)}, u32[]{:S(2)}) collective-permute-start(bf16[128,2304]{1,0:T(8,128)(2,1)S(1)} %get-tuple-element.75), channel_id=1, source_target_pairs={{0,12},{1,13},{2,14},{3,15},{4,0},{5,1},{6,2},{7,3},{8,4},{9,5},{1... | collective-permute-start | bytes 1769480 | tf_op jit(solution)/shard_map/ppermute | solution.py:28
  143.0 11.2 %collective-permute-start.37 = (bf16[128,2304]{1,0:T(8,128)(2,1)S(1)}, bf16[128,2304]{1,0:T(8,128)(2,1)S(1)}, u32[]{:S(2)}, u32[]{:S(2)}) collective-permute-start(bf16[128,2304]{1,0:T(8,128)(2,1)S(1)} %get-tuple-element.80), channel_id=1, source_target_pairs={{0,4},{1,5},{2,6},{3,7},{4,8},{5,9},{6,10},{7,11},{8,12},{9,13},{1... | collective-permute-start | bytes 1769480 | tf_op jit(solution)/shard_map/ppermute | solution.py:28
  146.9 12.3 %collective-permute-start.38 = (bf16[128,2304]{1,0:T(8,128)(2,1)S(1)}, bf16[128,2304]{1,0:T(8,128)(2,1)S(1)}, u32[]{:S(2)}, u32[]{:S(2)}) collective-permute-start(bf16[128,2304]{1,0:T(8,128)(2,1)S(1)} %add_convert_fusion), channel_id=1, source_target_pairs={{0,12},{1,13},{2,14},{3,15},{4,0},{5,1},{6,2},{7,3},{8,4},{9,5},{1... | collective-permute-start | bytes 1769480 | tf_op jit(solution)/shard_map/ppermute | solution.py:28
  150.3 11.2 %collective-permute-start.36 = (bf16[128,2304]{1,0:T(8,128)(2,1)S(1)}, bf16[128,2304]{1,0:T(8,128)(2,1)S(1)}, u32[]{:S(2)}, u32[]{:S(2)}) collective-permute-start(bf16[128,2304]{1,0:T(8,128)(2,1)S(1)} %add_convert_fusion.1), channel_id=1, source_target_pairs={{0,4},{1,5},{2,6},{3,7},{4,8},{5,9},{6,10},{7,11},{8,12},{9,13},{1... | collective-permute-start | bytes 1769480 | tf_op jit(solution)/shard_map/ppermute | solution.py:28
  161.9 8.0 %collective-permute-start.39 = (f32[32,2304]{1,0:T(8,128)S(1)}, f32[32,2304]{1,0:T(8,128)S(1)}, u32[]{:S(2)}, u32[]{:S(2)}) collective-permute-start(f32[32,2304]{1,0:T(8,128)S(1)} %get-tuple-element.88), channel_id=1, source_target_pairs={{0,1},{1,2},{2,3},{3,0},{4,5},{5,6},{6,7},{7,4},{8,9},{9,10},{10,1... | collective-permute-start | bytes 884744 | tf_op jit(solution)/shard_map/ppermute | solution.py:28
  162.4 7.6 %collective-permute-start.41 = (f32[32,2304]{1,0:T(8,128)S(1)}, f32[32,2304]{1,0:T(8,128)S(1)}, u32[]{:S(2)}, u32[]{:S(2)}) collective-permute-start(f32[32,2304]{1,0:T(8,128)S(1)} %get-tuple-element.89), channel_id=1, source_target_pairs={{0,3},{1,0},{2,1},{3,2},{4,7},{5,4},{6,5},{7,6},{8,11},{9,8},{10,9... | collective-permute-start | bytes 884744 | tf_op jit(solution)/shard_map/ppermute | solution.py:28
  170.0 11.2 %collective-permute-start.40 = (f32[64,2304]{1,0:T(8,128)S(1)}, f32[64,2304]{1,0:T(8,128)S(1)}, u32[]{:S(2)}, u32[]{:S(2)}) collective-permute-start(f32[64,2304]{1,0:T(8,128)S(1)} %pad_maximum_fusion), channel_id=1, source_target_pairs={{0,1},{1,2},{2,3},{3,0},{4,5},{5,6},{6,7},{7,4},{8,9},{9,10},{10,1... | collective-permute-start | bytes 1769480 | tf_op jit(solution)/shard_map/ppermute | solution.py:28
  170.2 11.0 %collective-permute-start.42 = (f32[64,2304]{1,0:T(8,128)S(1)}, f32[64,2304]{1,0:T(8,128)}, u32[]{:S(2)}, u32[]{:S(2)}) collective-permute-start(f32[64,2304]{1,0:T(8,128)S(1)} %pad_maximum_fusion.1), channel_id=1, source_target_pairs={{0,3},{1,0},{2,1},{3,2},{4,7},{5,4},{6,5},{7,6},{8,11},{9,8},{10,9... | collective-permute-start | bytes 1769480 | tf_op jit(solution)/shard_map/ppermute | solution.py:28
  (26 other events, 294.0 us)

commit v3 on v2

--- a/solution.py
+++ b/solution.py
@@ -339,28 +339,32 @@
     features = tokens.shape[2]
     raw = lax.optimization_barrier(tokens.reshape(count, features))
     sums = row_sums(raw)
+    sums = sums + send_core(sums)
+    sums, cosine, sine, place, raw = lax.optimization_barrier((sums, cosine, sine, place, raw))
     before, after = send_inner(raw, 1), send_inner(raw, -1)
-    sums = sums + send_core(sums)
-    sums, cosine, sine, place = lax.optimization_barrier((sums, cosine, sine, place))
     sums = sums + send_x(sums, 1) + send_x(sums, 2) + send_x(sums, 3)
     sums, before, after = lax.optimization_barrier((sums, before, after))
-    far = send_inner(before, 1)
+    before_sums, after_sums = send_inner(sums, 1), send_inner(sums, -1)
+    before, before_sums = lax.optimization_barrier((before, before_sums))
+    far, far_sums = send_inner(before, 1), send_inner(sums, 2)
     scale = gain.reshape(1, features)
-    near = normalize(raw, before, sums, send_inner(sums, 1), scale)
-    near, far = lax.optimization_barrier((near, far))
-    wide = normalize(after, far, send_inner(sums, -1), send_inner(sums, 2), scale)
+    near = normalize(raw, before, sums, before_sums, scale)
+    wide = normalize(after, far, after_sums, far_sums, scale)
 
     keyval_away, keyval_keep = project_keyval(place, near, w_keyval)
+    kept = keyval_keep + send_core(keyval_away)
 
     near_before, near_after = send_outer(near, 1), send_outer(near, -1)
-    near_before, near_after = lax.optimization_barrier((near_before, near_after))
+    near_before, near_after, wide, kept = lax.optimization_barrier(
+        (near_before, near_after, wide, kept)
+    )
     wide_after = send_outer(wide, -1)
     near_far = send_outer(near_before, 1)
     near_far, wide_again = lax.optimization_barrier((near_far, wide))
     wide_before = send_outer(wide_again, 1)
     wide_far = send_outer(wide_after, -1)
 
-    kept = (keyval_keep + send_core(keyval_away)).reshape(RING, count // 8, 2 * HEAD)
+    kept = kept.reshape(RING, count // 8, 2 * HEAD)
     keyval = kept[0] + send_ahead(kept[1], 1) + send_ahead(kept[2], 2) + send_ahead(kept[3], 3)
     keyval = keyval.astype(BF16)
 
@@ -372,13 +376,13 @@
     far, behind = send_x(summed[0], 1), send_x(summed[1], -1)
     away, keep = project_query(place, pieces, w_query, 0)
     summed = (keep + send_core(away)).reshape(2, 128, columns)
-    ahead = send_x(summed[1] + far, 1)
-    query = (summed[0] + ahead + behind).astype(BF16).reshape(16, 8, columns)
     moves = [
         (g * 16 + j, (j // 2) * 16 + (j % 2) * 8 + g) for g in range(8) for j in range(16)
     ]
     keyval = lax.ppermute(keyval, ("gx", "yz"), moves)
-    query, keyval = lax.optimization_barrier((query, keyval))
+    far, keyval = lax.optimization_barrier((far, keyval))
+    ahead = send_x(summed[1] + far, 1)
+    query = (summed[0] + ahead + behind).astype(BF16).reshape(16, 8, columns)
     query = lax.all_to_all(query, "yz", split_axis=0, concat_axis=0)
 
     heads_out, new_keyval = attend(

time: 183 us -> 179 us (0.978)
  blocking collectives: 28 us -> 24.9 us
  waiting for transfers between devices: 78.3 us -> 75.6 us
    all_to_all x1, blocking collectives: 16.4 us -> 13.3 us  [body(): query = lax.all_to_all(query, 'yz', split_axis=0, concat_axis=0)]
  transfers between devices with their start and end apart: 43 -> 43, of which waited for: 23 -> 26; matrix products, arithmetic and copies ran while one was open for 1% -> 1% of each run, Pallas kernels for 5% -> 5%
where the time goes in v3:
time: 179 us
  waiting for transfers between devices  75.6 us (42%)
  starting transfers between devices  52.8 us (29%)
  blocking collectives  24.9 us (14%)
  Pallas kernels  18.4 us (10%)
  local copies, waits for them, and re-layouts  3.63 us (2%)
  other arithmetic  2.51 us (1%)
    ppermute x34, waiting for transfers between devices, shift(): return lax.ppermute(value, ('gx', 'yz'), pairs)  74 us
    ppermute x34, starting transfers between devices, shift(): return lax.ppermute(value, ('gx', 'yz'), pairs)  50.7 us
    all_to_all x1, blocking collectives, body(): query = lax.all_to_all(query, 'yz', split_axis=0, concat_axis=0)  13.3 us
    all_to_all x1, blocking collectives, body(): lax.all_to_all(heads_out.reshape(16, 8, columns), 'yz', split_axis=0, con...  11.6 us
    pallas_call x2, Pallas kernels, project_query(): pl.pallas_call(functools.partial(query_kernel, pair), out_shape=[half, ha...  6.34 us
    pallas_call x2, Pallas kernels, project_output(): pl.pallas_call(functools.partial(output_kernel, groups), out_shape=shapes...  5.86 us
    pallas_call x1, Pallas kernels, attend(): pl.pallas_call(attend_kernel, out_shape=[jax.ShapeDtypeStruct((rows, colu...  4.36 us
  transfers between devices with their start and end apart: 43, of which 26 were waited for; matrix products, arithmetic and copies ran while one was open for 1% of the time, Pallas kernels for 5%

profile of v3, /device:TPU:0, one launch (start us, length us, event | category | flops | bytes accessed | tf_op | source)
XLA Modules:
  0.0 178.8 jit_solution(18420574476119564171)
XLA Ops:
  15.8 5.1 %collective-permute-done.6.two_sums = f32[64,2]{1,0:T(8,128)S(1)} collective-permute-done((f32[64,2]{1,0:T(8,128)S(1)}, f32[64,2]{1,0:T(8,128)S(1)}, u32[]{:S(2)}, u32[]{:S(2)}) %collective-permute-start.6) | collective-permute-done | bytes 544 | tf_op jit(solution)/shard_map/ppermute | solution.py:28
  25.7 3.3 %collective-permute-start.10 = (f32[64,2]{1,0:T(8,128)S(1)}, f32[64,2]{1,0:T(8,128)S(1)}, u32[]{:S(2)}, u32[]{:S(2)}) collective-permute-start(f32[64,2]{1,0:T(8,128)S(1)} %add_add_fusion.one_sums), channel_id=1, source_target_pairs={{0,3},{1,0},{2,1},{3,2},{4,7},{5,4},{6,5},{7,6},{8,11},{9,8},{10,9... | collective-permute-start | bytes 1544 | tf_op jit(solution)/shard_map/ppermute | solution.py:28
  30.6 3.8 %collective-permute-done.11.two_sums = f32[64,2]{1,0:T(8,128)S(1)} collective-permute-done((f32[64,2]{1,0:T(8,128)S(1)}, f32[64,2]{1,0:T(8,128)S(1)}, u32[]{:S(2)}, u32[]{:S(2)}) %collective-permute-start.11) | collective-permute-done | bytes 544 | tf_op jit(solution)/shard_map/ppermute | solution.py:28
  35.7 3.2 %collective-permute-start.15 = (bf16[128,2304]{1,0:T(8,128)(2,1)S(1)}, bf16[128,2304]{1,0:T(8,128)(2,1)S(1)}, u32[]{:S(2)}, u32[]{:S(2)}) collective-permute-start(bf16[128,2304]{1,0:T(8,128)(2,1)S(1)} %normalize.3.refs_4_), channel_id=1, source_target_pairs={{0,12},{1,13},{2,14},{3,15},{4,0},{5,1},{6,2},{7,3},{8,4},{9,5},{1... | collective-permute-start | bytes 1769480 | tf_op jit(solution)/shard_map/ppermute | solution.py:28
  38.9 7.9 %collective-permute-done.13.refs_3_ = bf16[128,2304]{1,0:T(8,128)(2,1)S(1)} collective-permute-done((bf16[128,2304]{1,0:T(8,128)(2,1)S(1)}, bf16[128,2304]{1,0:T(8,128)(2,1)S(1)}, u32[]{:S(2)}, u32[]{:S(2)}) %collective-permute-start.13) | collective-permute-done | bytes 589856 | tf_op jit(solution)/shard_map/ppermute | solution.py:28
  46.8 3.2 %collective-permute-start.16 = (bf16[128,2304]{1,0:T(8,128)(2,1)S(1)}, bf16[128,2304]{1,0:T(8,128)(2,1)S(1)}, u32[]{:S(2)}, u32[]{:S(2)}) collective-permute-start(bf16[128,2304]{1,0:T(8,128)(2,1)S(1)} %collective-permute-done.15.refs_6_), channel_id=1, source_target_pairs={{0,12},{1,13},{2,14},{3,15},{4,0},{5,1},{6,2},{7,3},{8,4},{9,5},{1... | collective-permute-start | bytes 1769480 | tf_op jit(solution)/shard_map/ppermute | solution.py:28
  50.1 3.4 %collective-permute-start.18 = (f32[8,512]{1,0:T(8,128)S(1)}, f32[8,512]{1,0:T(8,128)S(1)}, u32[]{:S(2)}, u32[]{:S(2)}) collective-permute-start(f32[8,512]{1,0:T(8,128)S(1)} %get-tuple-element.101), channel_id=1, source_target_pairs={{0,64},{1,65},{2,66},{3,67},{4,68},{5,69},{6,70},{7,71},{8,72},{9,... | collective-permute-start | bytes 49160 | tf_op jit(solution)/shard_map/ppermute | solution.py:28
  57.8 3.1 %query_projection.3 = (f32[256,768]{1,0:T(8,128)S(1)}, f32[256,768]{1,0:T(8,128)S(1)}) custom-call(s32[4]{0:T(128)S(1)} %pad_add_fusion.place, bf16[128,2304]{1,0:T(8,128)(2,1)S(1)} %normalize.2.rows_ref.refs_0_, bf16[128,2304]{1,0:T(8,128)(2,1)S(1)} %collective-permute-done.7.refs_1_, bf16[128,2304]{1,0:T(8,128)(2,1)S(1)} %collective-permute-done.8.refs_2_, ...), custom_call_target="tpu_custom_call" | custom-call | flops 1811939328 | bytes 8388608 | tf_op jit(solution)/shard_map/query_projection/pallas_call | solution.py:159
  61.0 3.3 %query_projection.2 = (f32[256,768]{1,0:T(8,128)S(1)}, f32[256,768]{1,0:T(8,128)S(1)}) custom-call(s32[4]{0:T(128)S(1)} %pad_add_fusion.place, bf16[128,2304]{1,0:T(8,128)(2,1)S(1)} %normalize.2.rows_ref.refs_0_, bf16[128,2304]{1,0:T(8,128)(2,1)S(1)} %collective-permute-done.7.refs_1_, bf16[128,2304]{1,0:T(8,128)(2,1)S(1)} %collective-permute-done.8.refs_2_, ...), custom_call_target="tpu_custom_call" | custom-call | flops 1811939328 | bytes 8388608 | tf_op jit(solution)/shard_map/query_projection/pallas_call | solution.py:159
  66.0 4.4 %collective-permute-start.25 = (f32[128,768]{1,0:T(8,128)S(1)}, f32[128,768]{1,0:T(8,128)S(1)}, u32[]{:S(2)}, u32[]{:S(2)}) collective-permute-start(f32[128,768]{1,0:T(8,128)S(1)} %get-tuple-element.98), channel_id=1, source_target_pairs={{0,96},{1,97},{2,98},{3,99},{4,100},{5,101},{6,102},{7,103},{8,104... | collective-permute-start | bytes 1179656 | tf_op jit(solution)/shard_map/ppermute | solution.py:28
  70.4 5.3 %collective-permute-done.22 = f32[128,768]{1,0:T(8,128)S(1)} collective-permute-done((f32[128,768]{1,0:T(8,128)S(1)}, f32[128,768]{1,0:T(8,128)S(1)}, u32[]{:S(2)}, u32[]{:S(2)}) %collective-permute-start.22) | collective-permute-done | bytes 393248 | tf_op jit(solution)/shard_map/ppermute | solution.py:28
  76.3 8.5 %collective-permute-done.24 = f32[128,768]{1,0:T(8,128)S(1)} collective-permute-done((f32[128,768]{1,0:T(8,128)S(1)}, f32[128,768]{1,0:T(8,128)S(1)}, u32[]{:S(2)}, u32[]{:S(2)}) %collective-permute-start.24) | collective-permute-done | bytes 393248 | tf_op jit(solution)/shard_map/ppermute | solution.py:28
  84.9 13.3 %all_to_all.10 = bf16[16,8,768]{2,1,0:T(8,128)(2,1)S(1)} all-to-all(bf16[16,8,768]{2,1,0:T(8,128)(2,1)S(1)} %fusion.5), channel_id=1, replica_groups=mesh['gx'=8,'yz'=16] {'yz'}, dimensions={0} | all-to-all | bytes 393216 | tf_op jit(solution)/shard_map/all_to_all | solution.py:386
  98.3 4.4 %attention.1 = (bf16[128,768]{1,0:T(8,128)(2,1)S(1)}, bf16[8,512]{1,0:T(8,128)(2,1)S(1)}) custom-call(s32[4]{0:T(128)S(1)} %copy-done.5, bf16[128,768]{1,0:T(8,128)(2,1)S(1)} %bitcast.14, f32[8,128]{1,0:T(8,128)S(1)} %get-tuple-element.76.cos_ref, f32[8,128]{1,0:T(8,128)S(1)} %get-tuple-element.77.sin_ref, ...), custom_call_target="tpu_custom_call" | custom-call | flops 805306368 | bytes 8388608 | tf_op jit(solution)/shard_map/attention/pallas_call | solution.py:256
  102.6 11.6 %all_to_all.11 = bf16[16,8,768]{2,1,0:T(8,128)(2,1)S(1)} all-to-all(bf16[16,8,768]{2,1,0:T(8,128)(2,1)S(1)} %bitcast.15), channel_id=1, replica_groups=mesh['gx'=8,'yz'=16] {'yz'}, dimensions={0} | all-to-all | bytes 393216 | tf_op jit(solution)/shard_map/all_to_all | solution.py:391
  117.5 3.6 %collective-permute-done.26.refs_1_ = bf16[128,768]{1,0:T(8,128)(2,1)S(1)} collective-permute-done((bf16[128,768]{1,0:T(8,128)(2,1)S(1)}, bf16[128,768]{1,0:T(8,128)(2,1)S(1)}, u32[]{:S(2)}, u32[]{:S(2)}) %collective-permute-start.26) | collective-permute-done | bytes 196640 | tf_op jit(solution)/shard_map/ppermute | solution.py:28
  122.7 5.3 %collective-permute-done.28.refs_3_ = bf16[128,768]{1,0:T(8,128)(2,1)S(1)} collective-permute-done((bf16[128,768]{1,0:T(8,128)(2,1)S(1)}, bf16[128,768]{1,0:T(8,128)(2,1)S(1)}, u32[]{:S(2)}, u32[]{:S(2)}) %collective-permute-start.28) | collective-permute-done | bytes 196640 | tf_op jit(solution)/shard_map/ppermute | solution.py:28
  131.7 2.8 %collective-permute-start.35 = (bf16[128,2304]{1,0:T(8,128)(2,1)S(1)}, bf16[128,2304]{1,0:T(8,128)(2,1)S(1)}, u32[]{:S(2)}, u32[]{:S(2)}) collective-permute-start(bf16[128,2304]{1,0:T(8,128)(2,1)S(1)} %get-tuple-element.84), channel_id=1, source_target_pairs={{0,12},{1,13},{2,14},{3,15},{4,0},{5,1},{6,2},{7,3},{8,4},{9,5},{1... | collective-permute-start | bytes 1769480 | tf_op jit(solution)/shard_map/ppermute | solution.py:28
  134.5 4.1 %output_projection.2 = (bf16[128,2304]{1,0:T(8,128)(2,1)S(1)}, bf16[128,2304]{1,0:T(8,128)(2,1)S(1)}, bf16[128,2304]{1,0:T(8,128)(2,1)S(1)}, bf16[128,2304]{1,0:T(8,128)(2,1)S(1)}, f32[256,2304]{1,0:T(8,128)S(1)}) custom-call(s32[4]{0:T(128)S(1)} %pad_add_fusion.place, bf16[128,768]{1,0:T(8,128)(2,1)S(1)} %bitcast.13, ...), custom_call_target="tpu_custom_call" | custom-call | flops 2717908992 | bytes 8388608 | tf_op jit(solution)/shard_map/output_projection/pallas_call | solution.py:315
  142.5 3.3 %collective-permute-start.38 = (bf16[128,2304]{1,0:T(8,128)(2,1)S(1)}, bf16[128,2304]{1,0:T(8,128)(2,1)S(1)}, u32[]{:S(2)}, u32[]{:S(2)}) collective-permute-start(bf16[128,2304]{1,0:T(8,128)(2,1)S(1)} %add_convert_fusion), channel_id=1, source_target_pairs={{0,12},{1,13},{2,14},{3,15},{4,0},{5,1},{6,2},{7,3},{8,4},{9,5},{1... | collective-permute-start | bytes 1769480 | tf_op jit(solution)/shard_map/ppermute | solution.py:28
  149.9 5.0 %collective-permute-done.38 = bf16[128,2304]{1,0:T(8,128)(2,1)S(1)} collective-permute-done((bf16[128,2304]{1,0:T(8,128)(2,1)S(1)}, bf16[128,2304]{1,0:T(8,128)(2,1)S(1)}, u32[]{:S(2)}, u32[]{:S(2)}) %collective-permute-start.38) | collective-permute-done | bytes 589856 | tf_op jit(solution)/shard_map/ppermute | solution.py:28
  160.8 4.7 %collective-permute-done.39 = f32[32,2304]{1,0:T(8,128)S(1)} collective-permute-done((f32[32,2304]{1,0:T(8,128)S(1)}, f32[32,2304]{1,0:T(8,128)S(1)}, u32[]{:S(2)}, u32[]{:S(2)}) %collective-permute-start.39) | collective-permute-done | bytes 294944 | tf_op jit(solution)/shard_map/ppermute | solution.py:28
  165.8 3.3 %collective-permute-start.42 = (f32[64,2304]{1,0:T(8,128)S(1)}, f32[64,2304]{1,0:T(8,128)}, u32[]{:S(2)}, u32[]{:S(2)}) collective-permute-start(f32[64,2304]{1,0:T(8,128)S(1)} %pad_maximum_fusion.1), channel_id=1, source_target_pairs={{0,3},{1,0},{2,1},{3,2},{4,7},{5,4},{6,5},{7,6},{8,11},{9,8},{10,9... | collective-permute-start | bytes 1769480 | tf_op jit(solution)/shard_map/ppermute | solution.py:28
  169.7 7.1 %collective-permute-done.40 = f32[64,2304]{1,0:T(8,128)S(1)} collective-permute-done((f32[64,2304]{1,0:T(8,128)S(1)}, f32[64,2304]{1,0:T(8,128)S(1)}, u32[]{:S(2)}, u32[]{:S(2)}) %collective-permute-start.40) | collective-permute-done | bytes 589856 | tf_op jit(solution)/shard_map/ppermute | solution.py:28
  (116 shorter events, 54.9 us)
Async XLA Ops:
  3.3 12.4 %collective-permute-start.4 = (bf16[64,2304]{1,0:T(8,128)(2,1)S(1)}, bf16[64,2304]{1,0:T(8,128)(2,1)S(1)}, u32[]{:S(2)}, u32[]{:S(2)}) collective-permute-start(bf16[64,2304]{1,0:T(8,128)(2,1)S(1)} %reshape.66.rows_ref.one_ref), channel_id=1, source_target_pairs={{0,1},{1,2},{2,3},{3,0},{4,5},{5,6},{6,7},{7,4},{8,9},{9,10},{10,1... | collective-permute-start | bytes 884744 | tf_op jit(solution)/shard_map/ppermute | solution.py:28
  5.3 10.4 %collective-permute-start.5 = (bf16[64,2304]{1,0:T(8,128)(2,1)S(1)}, bf16[64,2304]{1,0:T(8,128)(2,1)S(1)}, u32[]{:S(2)}, u32[]{:S(2)}) collective-permute-start(bf16[64,2304]{1,0:T(8,128)(2,1)S(1)} %reshape.66.rows_ref.one_ref), channel_id=1, source_target_pairs={{0,3},{1,0},{2,1},{3,2},{4,7},{5,4},{6,5},{7,6},{8,11},{9,8},{10,9... | collective-permute-start | bytes 884744 | tf_op jit(solution)/shard_map/ppermute | solution.py:28
  21.2 14.5 %collective-permute-start.7 = (bf16[128,2304]{1,0:T(8,128)(2,1)S(1)}, bf16[128,2304]{1,0:T(8,128)(2,1)S(1)}, u32[]{:S(2)}, u32[]{:S(2)}) collective-permute-start(bf16[128,2304]{1,0:T(8,128)(2,1)S(1)} %normalize.2.rows_ref.refs_0_), channel_id=1, source_target_pairs={{0,4},{1,5},{2,6},{3,7},{4,8},{5,9},{6,10},{7,11},{8,12},{9,13},{1... | collective-permute-start | bytes 1769480 | tf_op jit(solution)/shard_map/ppermute | solution.py:28
  22.8 12.8 %collective-permute-start.8 = (bf16[128,2304]{1,0:T(8,128)(2,1)S(1)}, bf16[128,2304]{1,0:T(8,128)(2,1)S(1)}, u32[]{:S(2)}, u32[]{:S(2)}) collective-permute-start(bf16[128,2304]{1,0:T(8,128)(2,1)S(1)} %normalize.2.rows_ref.refs_0_), channel_id=1, source_target_pairs={{0,12},{1,13},{2,14},{3,15},{4,0},{5,1},{6,2},{7,3},{8,4},{9,5},{1... | collective-permute-start | bytes 1769480 | tf_op jit(solution)/shard_map/ppermute | solution.py:28
  24.5 9.9 %collective-permute-start.9 = (bf16[64,2304]{1,0:T(8,128)(2,1)S(1)}, bf16[64,2304]{1,0:T(8,128)(2,1)S(1)}, u32[]{:S(2)}, u32[]{:S(2)}) collective-permute-start(bf16[64,2304]{1,0:T(8,128)(2,1)S(1)} %collective-permute-done.4.two_ref), channel_id=1, source_target_pairs={{0,1},{1,2},{2,3},{3,0},{4,5},{5,6},{6,7},{7,4},{8,9},{9,10},{10,1... | collective-permute-start | bytes 884744 | tf_op jit(solution)/shard_map/ppermute | solution.py:28
  35.7 11.1 %collective-permute-start.13 = (bf16[128,2304]{1,0:T(8,128)(2,1)S(1)}, bf16[128,2304]{1,0:T(8,128)(2,1)S(1)}, u32[]{:S(2)}, u32[]{:S(2)}) collective-permute-start(bf16[128,2304]{1,0:T(8,128)(2,1)S(1)} %collective-permute-done.7.refs_1_), channel_id=1, source_target_pairs={{0,4},{1,5},{2,6},{3,7},{4,8},{5,9},{6,10},{7,11},{8,12},{9,13},{1... | collective-permute-start | bytes 1769480 | tf_op jit(solution)/shard_map/ppermute | solution.py:28
  35.7 11.1 %collective-permute-start.15 = (bf16[128,2304]{1,0:T(8,128)(2,1)S(1)}, bf16[128,2304]{1,0:T(8,128)(2,1)S(1)}, u32[]{:S(2)}, u32[]{:S(2)}) collective-permute-start(bf16[128,2304]{1,0:T(8,128)(2,1)S(1)} %normalize.3.refs_4_), channel_id=1, source_target_pairs={{0,12},{1,13},{2,14},{3,15},{4,0},{5,1},{6,2},{7,3},{8,4},{9,5},{1... | collective-permute-start | bytes 1769480 | tf_op jit(solution)/shard_map/ppermute | solution.py:28
  46.7 11.1 %collective-permute-start.14 = (bf16[128,2304]{1,0:T(8,128)(2,1)S(1)}, bf16[128,2304]{1,0:T(8,128)(2,1)S(1)}, u32[]{:S(2)}, u32[]{:S(2)}) collective-permute-start(bf16[128,2304]{1,0:T(8,128)(2,1)S(1)} %normalize.3.refs_4_), channel_id=1, source_target_pairs={{0,4},{1,5},{2,6},{3,7},{4,8},{5,9},{6,10},{7,11},{8,12},{9,13},{1... | collective-permute-start | bytes 1769480 | tf_op jit(solution)/shard_map/ppermute | solution.py:28
  46.8 11.1 %collective-permute-start.16 = (bf16[128,2304]{1,0:T(8,128)(2,1)S(1)}, bf16[128,2304]{1,0:T(8,128)(2,1)S(1)}, u32[]{:S(2)}, u32[]{:S(2)}) collective-permute-start(bf16[128,2304]{1,0:T(8,128)(2,1)S(1)} %collective-permute-done.15.refs_6_), channel_id=1, source_target_pairs={{0,12},{1,13},{2,14},{3,15},{4,0},{5,1},{6,2},{7,3},{8,4},{9,5},{1... | collective-permute-start | bytes 1769480 | tf_op jit(solution)/shard_map/ppermute | solution.py:28
  65.0 10.7 %collective-permute-start.22 = (f32[128,768]{1,0:T(8,128)S(1)}, f32[128,768]{1,0:T(8,128)S(1)}, u32[]{:S(2)}, u32[]{:S(2)}) collective-permute-start(f32[128,768]{1,0:T(8,128)S(1)} %get-tuple-element.97), channel_id=1, source_target_pairs={{0,32},{1,33},{2,34},{3,35},{4,36},{5,37},{6,38},{7,39},{8,40},{9,... | collective-permute-start | bytes 1179656 | tf_op jit(solution)/shard_map/ppermute | solution.py:28
  66.0 10.4 %collective-permute-start.25 = (f32[128,768]{1,0:T(8,128)S(1)}, f32[128,768]{1,0:T(8,128)S(1)}, u32[]{:S(2)}, u32[]{:S(2)}) collective-permute-start(f32[128,768]{1,0:T(8,128)S(1)} %get-tuple-element.98), channel_id=1, source_target_pairs={{0,96},{1,97},{2,98},{3,99},{4,100},{5,101},{6,102},{7,103},{8,104... | collective-permute-start | bytes 1179656 | tf_op jit(solution)/shard_map/ppermute | solution.py:28
  75.8 9.1 %collective-permute-start.24 = (f32[128,768]{1,0:T(8,128)S(1)}, f32[128,768]{1,0:T(8,128)S(1)}, u32[]{:S(2)}, u32[]{:S(2)}) collective-permute-start(f32[128,768]{1,0:T(8,128)S(1)} %slice_add_fusion.1), channel_id=1, source_target_pairs={{0,32},{1,33},{2,34},{3,35},{4,36},{5,37},{6,38},{7,39},{8,40},{9,... | collective-permute-start | bytes 1179656 | tf_op jit(solution)/shard_map/ppermute | solution.py:28
  115.0 7.7 %collective-permute-start.27 = (bf16[128,768]{1,0:T(8,128)(2,1)S(1)}, bf16[128,768]{1,0:T(8,128)(2,1)S(1)}, u32[]{:S(2)}, u32[]{:S(2)}) collective-permute-start(bf16[128,768]{1,0:T(8,128)(2,1)S(1)} %bitcast.10), channel_id=1, source_target_pairs={{0,96},{1,97},{2,98},{3,99},{4,100},{5,101},{6,102},{7,103},{8,104... | collective-permute-start | bytes 589832 | tf_op jit(solution)/shard_map/ppermute | solution.py:28
  121.1 6.9 %collective-permute-start.29 = (bf16[128,768]{1,0:T(8,128)(2,1)S(1)}, bf16[128,768]{1,0:T(8,128)(2,1)S(1)}, u32[]{:S(2)}, u32[]{:S(2)}) collective-permute-start(bf16[128,768]{1,0:T(8,128)(2,1)S(1)} %bitcast.11), channel_id=1, source_target_pairs={{0,16},{16,0},{32,48},{48,32},{64,80},{80,64},{96,112},{112,96},{1... | collective-permute-start | bytes 589832 | tf_op jit(solution)/shard_map/ppermute | solution.py:33
  131.2 11.2 %collective-permute-start.34 = (bf16[128,2304]{1,0:T(8,128)(2,1)S(1)}, bf16[128,2304]{1,0:T(8,128)(2,1)S(1)}, u32[]{:S(2)}, u32[]{:S(2)}) collective-permute-start(bf16[128,2304]{1,0:T(8,128)(2,1)S(1)} %get-tuple-element.83), channel_id=1, source_target_pairs={{0,4},{1,5},{2,6},{3,7},{4,8},{5,9},{6,10},{7,11},{8,12},{9,13},{1... | collective-permute-start | bytes 1769480 | tf_op jit(solution)/shard_map/ppermute | solution.py:28
  131.7 10.7 %collective-permute-start.35 = (bf16[128,2304]{1,0:T(8,128)(2,1)S(1)}, bf16[128,2304]{1,0:T(8,128)(2,1)S(1)}, u32[]{:S(2)}, u32[]{:S(2)}) collective-permute-start(bf16[128,2304]{1,0:T(8,128)(2,1)S(1)} %get-tuple-element.84), channel_id=1, source_target_pairs={{0,12},{1,13},{2,14},{3,15},{4,0},{5,1},{6,2},{7,3},{8,4},{9,5},{1... | collective-permute-start | bytes 1769480 | tf_op jit(solution)/shard_map/ppermute | solution.py:28
  138.6 10.0 %collective-permute-start.33 = (bf16[128,2304]{1,0:T(8,128)(2,1)S(1)}, bf16[128,2304]{1,0:T(8,128)(2,1)S(1)}, u32[]{:S(2)}, u32[]{:S(2)}) collective-permute-start(bf16[128,2304]{1,0:T(8,128)(2,1)S(1)} %get-tuple-element.81), channel_id=1, source_target_pairs={{0,12},{1,13},{2,14},{3,15},{4,0},{5,1},{6,2},{7,3},{8,4},{9,5},{1... | collective-permute-start | bytes 1769480 | tf_op jit(solution)/shard_map/ppermute | solution.py:28
  138.7 11.2 %collective-permute-start.37 = (bf16[128,2304]{1,0:T(8,128)(2,1)S(1)}, bf16[128,2304]{1,0:T(8,128)(2,1)S(1)}, u32[]{:S(2)}, u32[]{:S(2)}) collective-permute-start(bf16[128,2304]{1,0:T(8,128)(2,1)S(1)} %get-tuple-element.86), channel_id=1, source_target_pairs={{0,4},{1,5},{2,6},{3,7},{4,8},{5,9},{6,10},{7,11},{8,12},{9,13},{1... | collective-permute-start | bytes 1769480 | tf_op jit(solution)/shard_map/ppermute | solution.py:28
  142.5 12.3 %collective-permute-start.38 = (bf16[128,2304]{1,0:T(8,128)(2,1)S(1)}, bf16[128,2304]{1,0:T(8,128)(2,1)S(1)}, u32[]{:S(2)}, u32[]{:S(2)}) collective-permute-start(bf16[128,2304]{1,0:T(8,128)(2,1)S(1)} %add_convert_fusion), channel_id=1, source_target_pairs={{0,12},{1,13},{2,14},{3,15},{4,0},{5,1},{6,2},{7,3},{8,4},{9,5},{1... | collective-permute-start | bytes 1769480 | tf_op jit(solution)/shard_map/ppermute | solution.py:28
  146.0 11.2 %collective-permute-start.36 = (bf16[128,2304]{1,0:T(8,128)(2,1)S(1)}, bf16[128,2304]{1,0:T(8,128)(2,1)S(1)}, u32[]{:S(2)}, u32[]{:S(2)}) collective-permute-start(bf16[128,2304]{1,0:T(8,128)(2,1)S(1)} %add_convert_fusion.1), channel_id=1, source_target_pairs={{0,4},{1,5},{2,6},{3,7},{4,8},{5,9},{6,10},{7,11},{8,12},{9,13},{1... | collective-permute-start | bytes 1769480 | tf_op jit(solution)/shard_map/ppermute | solution.py:28
  157.5 8.0 %collective-permute-start.39 = (f32[32,2304]{1,0:T(8,128)S(1)}, f32[32,2304]{1,0:T(8,128)S(1)}, u32[]{:S(2)}, u32[]{:S(2)}) collective-permute-start(f32[32,2304]{1,0:T(8,128)S(1)} %get-tuple-element.94), channel_id=1, source_target_pairs={{0,1},{1,2},{2,3},{3,0},{4,5},{5,6},{6,7},{7,4},{8,9},{9,10},{10,1... | collective-permute-start | bytes 884744 | tf_op jit(solution)/shard_map/ppermute | solution.py:28
  158.1 7.6 %collective-permute-start.41 = (f32[32,2304]{1,0:T(8,128)S(1)}, f32[32,2304]{1,0:T(8,128)S(1)}, u32[]{:S(2)}, u32[]{:S(2)}) collective-permute-start(f32[32,2304]{1,0:T(8,128)S(1)} %get-tuple-element.95), channel_id=1, source_target_pairs={{0,3},{1,0},{2,1},{3,2},{4,7},{5,4},{6,5},{7,6},{8,11},{9,8},{10,9... | collective-permute-start | bytes 884744 | tf_op jit(solution)/shard_map/ppermute | solution.py:28
  165.6 11.2 %collective-permute-start.40 = (f32[64,2304]{1,0:T(8,128)S(1)}, f32[64,2304]{1,0:T(8,128)S(1)}, u32[]{:S(2)}, u32[]{:S(2)}) collective-permute-start(f32[64,2304]{1,0:T(8,128)S(1)} %pad_maximum_fusion), channel_id=1, source_target_pairs={{0,1},{1,2},{2,3},{3,0},{4,5},{5,6},{6,7},{7,4},{8,9},{9,10},{10,1... | collective-permute-start | bytes 1769480 | tf_op jit(solution)/shard_map/ppermute | solution.py:28
  165.8 11.0 %collective-permute-start.42 = (f32[64,2304]{1,0:T(8,128)S(1)}, f32[64,2304]{1,0:T(8,128)}, u32[]{:S(2)}, u32[]{:S(2)}) collective-permute-start(f32[64,2304]{1,0:T(8,128)S(1)} %pad_maximum_fusion.1), channel_id=1, source_target_pairs={{0,3},{1,0},{2,1},{3,2},{4,7},{5,4},{6,5},{7,6},{8,11},{9,8},{10,9... | collective-permute-start | bytes 1769480 | tf_op jit(solution)/shard_map/ppermute | solution.py:28
  (26 other events, 279.2 us)

commit v4 on v3

--- a/solution.py
+++ b/solution.py
@@ -299,8 +299,8 @@
             if group == 0:
                 targets[0][:, columns] = result
             else:
-                targets[0][:, columns] = result[:128].astype(BF16)
-                targets[1][:, columns] = result[128:].astype(BF16)
+                targets[0][:, columns] = result[:128].astype(targets[0].dtype)
+                targets[1][:, columns] = result[128:].astype(targets[1].dtype)
 
 
 def project_output(place, pieces, w_out, groups):
@@ -311,7 +311,8 @@
         if group == 0:
             shapes.append(jax.ShapeDtypeStruct((256, columns), F32))
         else:
-            shapes += [jax.ShapeDtypeStruct((128, columns), BF16)] * 2
+            for added in (group == 1, group == 3):
+                shapes.append(jax.ShapeDtypeStruct((128, columns), F32 if added else BF16))
     return pl.pallas_call(
         functools.partial(output_kernel, groups),
         out_shape=shapes,
@@ -403,15 +404,19 @@
     far_low, far_high = send_outer(two_low, 1), send_outer(two_high, -1)
     far_low, far_high = lax.optimization_barrier((far_low, far_high))
     early_high, early_low = send_outer(one_high, 1), send_outer(three_low, -1)
-    late_low = send_outer((one_low.astype(F32) + far_low.astype(F32)).astype(BF16), 1)
-    late_high = send_outer((three_high.astype(F32) + far_high.astype(F32)).astype(BF16), -1)
+    late_low = send_outer((one_low + far_low.astype(F32)).astype(BF16), 1)
+    late_high = send_outer((three_high + far_high.astype(F32)).astype(BF16), -1)
     low = own[:128] + early_low.astype(F32) + late_low.astype(F32)
     high = own[128:] + early_high.astype(F32) + late_high.astype(F32)
-    here, one, two, three = low[:64], low[64:], high[:64], high[64:]
-    far_low, far_high = send_inner(two[:32], 1), send_inner(two[32:], -1)
-    one = jnp.concatenate([one[:32] + far_low, one[32:]], 0)
-    three = jnp.concatenate([three[:32], three[32:] + far_high], 0)
-    branch = here + send_inner(one, 1) + send_inner(three, -1)
+    halves = []
+    for columns in (slice(0, features // 2), slice(features // 2, features)):
+        here, one = low[:64, columns], low[64:, columns]
+        two, three = high[:64, columns], high[64:, columns]
+        far_low, far_high = send_inner(two[:32], 1), send_inner(two[32:], -1)
+        one = jnp.concatenate([one[:32] + far_low, one[32:]], 0)
+        three = jnp.concatenate([three[:32], three[32:] + far_high], 0)
+        halves.append(here + send_inner(one, 1) + send_inner(three, -1))
+    branch = jnp.concatenate(halves, 1)
     mixed = (raw.astype(F32) + branch).astype(BF16).reshape(tokens.shape)
     return (mixed, new_keyval.reshape(seqs, 2, 2 * HEAD))
 

time: 179 us -> 180 us (level)
  starting transfers between devices: 52.8 us -> 56.1 us
  waiting for transfers between devices: 75.6 us -> 72.9 us
    ppermute x34 -> x38, starting transfers between devices: 50.7 us -> 54 us  [shift(): return lax.ppermute(value, ('gx', 'yz'), pairs)]
    ppermute x34 -> x38, waiting for transfers between devices: 74 us -> 71.3 us  [shift(): return lax.ppermute(value, ('gx', 'yz'), pairs)]
  transfers between devices with their start and end apart: 43 -> 47, of which waited for: 26 -> 26; matrix products, arithmetic and copies ran while one was open for 1% -> 2% of each run, Pallas kernels for 5% -> 5%
where the time goes in v4:
time: 180 us
  waiting for transfers between devices  72.9 us (41%)
  starting transfers between devices  56.1 us (31%)
  blocking collectives  25.5 us (14%)
  Pallas kernels  18.4 us (10%)
  local copies, waits for them, and re-layouts  3.63 us (2%)
  other arithmetic  2.1 us (1%)
    ppermute x38, waiting for transfers between devices, shift(): return lax.ppermute(value, ('gx', 'yz'), pairs)  71.3 us
    ppermute x38, starting transfers between devices, shift(): return lax.ppermute(value, ('gx', 'yz'), pairs)  54 us
    all_to_all x1, blocking collectives, body(): query = lax.all_to_all(query, 'yz', split_axis=0, concat_axis=0)  13.9 us
    all_to_all x1, blocking collectives, body(): lax.all_to_all(heads_out.reshape(16, 8, columns), 'yz', split_axis=0, con...  11.6 us
    pallas_call x2, Pallas kernels, project_query(): pl.pallas_call(functools.partial(query_kernel, pair), out_shape=[half, ha...  6.35 us
    pallas_call x2, Pallas kernels, project_output(): pl.pallas_call(functools.partial(output_kernel, groups), out_shape=shapes...  5.86 us
    pallas_call x1, Pallas kernels, attend(): pl.pallas_call(attend_kernel, out_shape=[jax.ShapeDtypeStruct((rows, colu...  4.36 us
  transfers between devices with their start and end apart: 47, of which 26 were waited for; matrix products, arithmetic and copies ran while one was open for 2% of the time, Pallas kernels for 5%

profile of v4, /device:TPU:0, one launch (start us, length us, event | category | flops | bytes accessed | tf_op | source)
XLA Modules:
  0.0 179.6 jit_solution(14405138992150793045)
XLA Ops:
  3.3 4.1 %collective-permute-start.5 = (bf16[64,2304]{1,0:T(8,128)(2,1)S(1)}, bf16[64,2304]{1,0:T(8,128)(2,1)S(1)}, u32[]{:S(2)}, u32[]{:S(2)}) collective-permute-start(bf16[64,2304]{1,0:T(8,128)(2,1)S(1)} %reshape.66.rows_ref.one_ref), channel_id=1, source_target_pairs={{0,3},{1,0},{2,1},{3,2},{4,7},{5,4},{6,5},{7,6},{8,11},{9,8},{10,9... | collective-permute-start | bytes 884744 | tf_op jit(solution)/shard_map/ppermute | solution.py:28
  11.9 3.7 %collective-permute-done.2 = f32[64,2]{1,0:T(8,128)S(1)} collective-permute-done((f32[64,2]{1,0:T(8,128)S(1)}, f32[64,2]{1,0:T(8,128)S(1)}, u32[]{:S(2)}, u32[]{:S(2)}) %collective-permute-start.2) | collective-permute-done | bytes 544 | tf_op jit(solution)/shard_map/ppermute | solution.py:28
  16.3 5.1 %collective-permute-done.6.two_sums = f32[64,2]{1,0:T(8,128)S(1)} collective-permute-done((f32[64,2]{1,0:T(8,128)S(1)}, f32[64,2]{1,0:T(8,128)S(1)}, u32[]{:S(2)}, u32[]{:S(2)}) %collective-permute-start.6) | collective-permute-done | bytes 544 | tf_op jit(solution)/shard_map/ppermute | solution.py:28
  21.7 3.1 %collective-permute-start.8 = (bf16[128,2304]{1,0:T(8,128)(2,1)S(1)}, bf16[128,2304]{1,0:T(8,128)(2,1)S(1)}, u32[]{:S(2)}, u32[]{:S(2)}) collective-permute-start(bf16[128,2304]{1,0:T(8,128)(2,1)S(1)} %normalize.2.rows_ref.refs_0_), channel_id=1, source_target_pairs={{0,12},{1,13},{2,14},{3,15},{4,0},{5,1},{6,2},{7,3},{8,4},{9,5},{1... | collective-permute-start | bytes 1769480 | tf_op jit(solution)/shard_map/ppermute | solution.py:28
  25.9 3.7 %collective-permute-start.11 = (f32[64,2]{1,0:T(8,128)S(1)}, f32[64,2]{1,0:T(8,128)S(1)}, u32[]{:S(2)}, u32[]{:S(2)}) collective-permute-start(f32[64,2]{1,0:T(8,128)S(1)} %add_add_fusion.one_sums), channel_id=1, source_target_pairs={{0,2},{1,3},{2,0},{3,1},{4,6},{5,7},{6,4},{7,5},{8,10},{9,11},{10,... | collective-permute-start | bytes 1544 | tf_op jit(solution)/shard_map/ppermute | solution.py:28
  30.4 3.7 %collective-permute-done.11.two_sums = f32[64,2]{1,0:T(8,128)S(1)} collective-permute-done((f32[64,2]{1,0:T(8,128)S(1)}, f32[64,2]{1,0:T(8,128)S(1)}, u32[]{:S(2)}, u32[]{:S(2)}) %collective-permute-start.11) | collective-permute-done | bytes 544 | tf_op jit(solution)/shard_map/ppermute | solution.py:28
  36.2 3.2 %collective-permute-start.15 = (bf16[128,2304]{1,0:T(8,128)(2,1)S(1)}, bf16[128,2304]{1,0:T(8,128)(2,1)S(1)}, u32[]{:S(2)}, u32[]{:S(2)}) collective-permute-start(bf16[128,2304]{1,0:T(8,128)(2,1)S(1)} %normalize.3.refs_4_), channel_id=1, source_target_pairs={{0,12},{1,13},{2,14},{3,15},{4,0},{5,1},{6,2},{7,3},{8,4},{9,5},{1... | collective-permute-start | bytes 1769480 | tf_op jit(solution)/shard_map/ppermute | solution.py:28
  39.4 7.9 %collective-permute-done.13.refs_3_ = bf16[128,2304]{1,0:T(8,128)(2,1)S(1)} collective-permute-done((bf16[128,2304]{1,0:T(8,128)(2,1)S(1)}, bf16[128,2304]{1,0:T(8,128)(2,1)S(1)}, u32[]{:S(2)}, u32[]{:S(2)}) %collective-permute-start.13) | collective-permute-done | bytes 589856 | tf_op jit(solution)/shard_map/ppermute | solution.py:28
  47.3 3.2 %collective-permute-start.16 = (bf16[128,2304]{1,0:T(8,128)(2,1)S(1)}, bf16[128,2304]{1,0:T(8,128)(2,1)S(1)}, u32[]{:S(2)}, u32[]{:S(2)}) collective-permute-start(bf16[128,2304]{1,0:T(8,128)(2,1)S(1)} %collective-permute-done.15.refs_6_), channel_id=1, source_target_pairs={{0,12},{1,13},{2,14},{3,15},{4,0},{5,1},{6,2},{7,3},{8,4},{9,5},{1... | collective-permute-start | bytes 1769480 | tf_op jit(solution)/shard_map/ppermute | solution.py:28
  55.5 3.5 %collective-permute-done.18 = f32[8,512]{1,0:T(8,128)S(1)} collective-permute-done((f32[8,512]{1,0:T(8,128)S(1)}, f32[8,512]{1,0:T(8,128)S(1)}, u32[]{:S(2)}, u32[]{:S(2)}) %collective-permute-start.18) | collective-permute-done | bytes 16416 | tf_op jit(solution)/shard_map/ppermute | solution.py:28
  59.1 3.1 %query_projection.3 = (f32[256,768]{1,0:T(8,128)S(1)}, f32[256,768]{1,0:T(8,128)S(1)}) custom-call(s32[4]{0:T(128)S(1)} %pad_add_fusion.place, bf16[128,2304]{1,0:T(8,128)(2,1)S(1)} %normalize.2.rows_ref.refs_0_, bf16[128,2304]{1,0:T(8,128)(2,1)S(1)} %collective-permute-done.7.refs_1_, bf16[128,2304]{1,0:T(8,128)(2,1)S(1)} %collective-permute-done.8.refs_2_, ...), custom_call_target="tpu_custom_call" | custom-call | flops 1811939328 | bytes 8388608 | tf_op jit(solution)/shard_map/query_projection/pallas_call | solution.py:159
  62.2 3.3 %query_projection.2 = (f32[256,768]{1,0:T(8,128)S(1)}, f32[256,768]{1,0:T(8,128)S(1)}) custom-call(s32[4]{0:T(128)S(1)} %pad_add_fusion.place, bf16[128,2304]{1,0:T(8,128)(2,1)S(1)} %normalize.2.rows_ref.refs_0_, bf16[128,2304]{1,0:T(8,128)(2,1)S(1)} %collective-permute-done.7.refs_1_, bf16[128,2304]{1,0:T(8,128)(2,1)S(1)} %collective-permute-done.8.refs_2_, ...), custom_call_target="tpu_custom_call" | custom-call | flops 1811939328 | bytes 8388608 | tf_op jit(solution)/shard_map/query_projection/pallas_call | solution.py:159
  67.2 4.3 %collective-permute-start.25 = (f32[128,768]{1,0:T(8,128)S(1)}, f32[128,768]{1,0:T(8,128)S(1)}, u32[]{:S(2)}, u32[]{:S(2)}) collective-permute-start(f32[128,768]{1,0:T(8,128)S(1)} %get-tuple-element.107), channel_id=1, source_target_pairs={{0,96},{1,97},{2,98},{3,99},{4,100},{5,101},{6,102},{7,103},{8,104... | collective-permute-start | bytes 1179656 | tf_op jit(solution)/shard_map/ppermute | solution.py:28
  71.6 6.1 %collective-permute-done.22 = f32[128,768]{1,0:T(8,128)S(1)} collective-permute-done((f32[128,768]{1,0:T(8,128)S(1)}, f32[128,768]{1,0:T(8,128)S(1)}, u32[]{:S(2)}, u32[]{:S(2)}) %collective-permute-start.22) | collective-permute-done | bytes 393248 | tf_op jit(solution)/shard_map/ppermute | solution.py:28
  77.8 9.0 %collective-permute-done.24 = f32[128,768]{1,0:T(8,128)S(1)} collective-permute-done((f32[128,768]{1,0:T(8,128)S(1)}, f32[128,768]{1,0:T(8,128)S(1)}, u32[]{:S(2)}, u32[]{:S(2)}) %collective-permute-start.24) | collective-permute-done | bytes 393248 | tf_op jit(solution)/shard_map/ppermute | solution.py:28
  86.9 13.9 %all_to_all.10 = bf16[16,8,768]{2,1,0:T(8,128)(2,1)S(1)} all-to-all(bf16[16,8,768]{2,1,0:T(8,128)(2,1)S(1)} %fusion.5), channel_id=1, replica_groups=mesh['gx'=8,'yz'=16] {'yz'}, dimensions={0} | all-to-all | bytes 393216 | tf_op jit(solution)/shard_map/all_to_all | solution.py:387
  100.8 4.4 %attention.1 = (bf16[128,768]{1,0:T(8,128)(2,1)S(1)}, bf16[8,512]{1,0:T(8,128)(2,1)S(1)}) custom-call(s32[4]{0:T(128)S(1)} %copy-done.5, bf16[128,768]{1,0:T(8,128)(2,1)S(1)} %bitcast.14, f32[8,128]{1,0:T(8,128)S(1)} %get-tuple-element.76.cos_ref, f32[8,128]{1,0:T(8,128)S(1)} %get-tuple-element.77.sin_ref, ...), custom_call_target="tpu_custom_call" | custom-call | flops 805306368 | bytes 8388608 | tf_op jit(solution)/shard_map/attention/pallas_call | solution.py:256
  105.2 11.6 %all_to_all.11 = bf16[16,8,768]{2,1,0:T(8,128)(2,1)S(1)} all-to-all(bf16[16,8,768]{2,1,0:T(8,128)(2,1)S(1)} %bitcast.15), channel_id=1, replica_groups=mesh['gx'=8,'yz'=16] {'yz'}, dimensions={0} | all-to-all | bytes 393216 | tf_op jit(solution)/shard_map/all_to_all | solution.py:392
  120.0 3.6 %collective-permute-done.26.refs_1_ = bf16[128,768]{1,0:T(8,128)(2,1)S(1)} collective-permute-done((bf16[128,768]{1,0:T(8,128)(2,1)S(1)}, bf16[128,768]{1,0:T(8,128)(2,1)S(1)}, u32[]{:S(2)}, u32[]{:S(2)}) %collective-permute-start.26) | collective-permute-done | bytes 196640 | tf_op jit(solution)/shard_map/ppermute | solution.py:28
  125.2 5.3 %collective-permute-done.28.refs_3_ = bf16[128,768]{1,0:T(8,128)(2,1)S(1)} collective-permute-done((bf16[128,768]{1,0:T(8,128)(2,1)S(1)}, bf16[128,768]{1,0:T(8,128)(2,1)S(1)}, u32[]{:S(2)}, u32[]{:S(2)}) %collective-permute-start.28) | collective-permute-done | bytes 196640 | tf_op jit(solution)/shard_map/ppermute | solution.py:28
  137.1 4.1 %output_projection.2 = (f32[128,2304]{1,0:T(8,128)S(1)}, bf16[128,2304]{1,0:T(8,128)(2,1)S(1)}, bf16[128,2304]{1,0:T(8,128)(2,1)S(1)}, f32[128,2304]{1,0:T(8,128)S(1)}, f32[256,2304]{1,0:T(8,128)S(1)}) custom-call(s32[4]{0:T(128)S(1)} %pad_add_fusion.place, bf16[128,768]{1,0:T(8,128)(2,1)S(1)} %bitcast.13, ...), custom_call_target="tpu_custom_call" | custom-call | flops 2717908992 | bytes 8388608 | tf_op jit(solution)/shard_map/output_projection/pallas_call | solution.py:316
  145.3 3.2 %collective-permute-start.38 = (bf16[128,2304]{1,0:T(8,128)(2,1)S(1)}, bf16[128,2304]{1,0:T(8,128)(2,1)S(1)}, u32[]{:S(2)}, u32[]{:S(2)}) collective-permute-start(bf16[128,2304]{1,0:T(8,128)(2,1)S(1)} %add_convert_fusion), channel_id=1, source_target_pairs={{0,12},{1,13},{2,14},{3,15},{4,0},{5,1},{6,2},{7,3},{8,4},{9,5},{1... | collective-permute-start | bytes 1769480 | tf_op jit(solution)/shard_map/ppermute | solution.py:28
  152.4 6.3 %collective-permute-done.36 = bf16[128,2304]{1,0:T(8,128)(2,1)S(1)} collective-permute-done((bf16[128,2304]{1,0:T(8,128)(2,1)S(1)}, bf16[128,2304]{1,0:T(8,128)(2,1)S(1)}, u32[]{:S(2)}, u32[]{:S(2)}) %collective-permute-start.36) | collective-permute-done | bytes 589856 | tf_op jit(solution)/shard_map/ppermute | solution.py:28
  175.2 3.2 %collective-permute-done.40 = f32[64,1152]{1,0:T(8,128)S(1)} collective-permute-done((f32[64,1152]{1,0:T(8,128)S(1)}, f32[64,1152]{1,0:T(8,128)S(1)}, u32[]{:S(2)}, u32[]{:S(2)}) %collective-permute-start.40) | collective-permute-done | bytes 294944 | tf_op jit(solution)/shard_map/ppermute | solution.py:28
  (127 shorter events, 56.1 us)
Async XLA Ops:
  3.3 12.8 %collective-permute-start.5 = (bf16[64,2304]{1,0:T(8,128)(2,1)S(1)}, bf16[64,2304]{1,0:T(8,128)(2,1)S(1)}, u32[]{:S(2)}, u32[]{:S(2)}) collective-permute-start(bf16[64,2304]{1,0:T(8,128)(2,1)S(1)} %reshape.66.rows_ref.one_ref), channel_id=1, source_target_pairs={{0,3},{1,0},{2,1},{3,2},{4,7},{5,4},{6,5},{7,6},{8,11},{9,8},{10,9... | collective-permute-start | bytes 884744 | tf_op jit(solution)/shard_map/ppermute | solution.py:28
  7.4 8.7 %collective-permute-start.4 = (bf16[64,2304]{1,0:T(8,128)(2,1)S(1)}, bf16[64,2304]{1,0:T(8,128)(2,1)S(1)}, u32[]{:S(2)}, u32[]{:S(2)}) collective-permute-start(bf16[64,2304]{1,0:T(8,128)(2,1)S(1)} %reshape.66.rows_ref.one_ref), channel_id=1, source_target_pairs={{0,1},{1,2},{2,3},{3,0},{4,5},{5,6},{6,7},{7,4},{8,9},{9,10},{10,1... | collective-permute-start | bytes 884744 | tf_op jit(solution)/shard_map/ppermute | solution.py:28
  21.7 13.7 %collective-permute-start.8 = (bf16[128,2304]{1,0:T(8,128)(2,1)S(1)}, bf16[128,2304]{1,0:T(8,128)(2,1)S(1)}, u32[]{:S(2)}, u32[]{:S(2)}) collective-permute-start(bf16[128,2304]{1,0:T(8,128)(2,1)S(1)} %normalize.2.rows_ref.refs_0_), channel_id=1, source_target_pairs={{0,12},{1,13},{2,14},{3,15},{4,0},{5,1},{6,2},{7,3},{8,4},{9,5},{1... | collective-permute-start | bytes 1769480 | tf_op jit(solution)/shard_map/ppermute | solution.py:28
  24.7 11.4 %collective-permute-start.7 = (bf16[128,2304]{1,0:T(8,128)(2,1)S(1)}, bf16[128,2304]{1,0:T(8,128)(2,1)S(1)}, u32[]{:S(2)}, u32[]{:S(2)}) collective-permute-start(bf16[128,2304]{1,0:T(8,128)(2,1)S(1)} %normalize.2.rows_ref.refs_0_), channel_id=1, source_target_pairs={{0,4},{1,5},{2,6},{3,7},{4,8},{5,9},{6,10},{7,11},{8,12},{9,13},{1... | collective-permute-start | bytes 1769480 | tf_op jit(solution)/shard_map/ppermute | solution.py:28
  24.7 10.3 %collective-permute-start.9 = (bf16[64,2304]{1,0:T(8,128)(2,1)S(1)}, bf16[64,2304]{1,0:T(8,128)(2,1)S(1)}, u32[]{:S(2)}, u32[]{:S(2)}) collective-permute-start(bf16[64,2304]{1,0:T(8,128)(2,1)S(1)} %collective-permute-done.4.two_ref), channel_id=1, source_target_pairs={{0,1},{1,2},{2,3},{3,0},{4,5},{5,6},{6,7},{7,4},{8,9},{9,10},{10,1... | collective-permute-start | bytes 884744 | tf_op jit(solution)/shard_map/ppermute | solution.py:28
  25.9 8.2 %collective-permute-start.11 = (f32[64,2]{1,0:T(8,128)S(1)}, f32[64,2]{1,0:T(8,128)S(1)}, u32[]{:S(2)}, u32[]{:S(2)}) collective-permute-start(f32[64,2]{1,0:T(8,128)S(1)} %add_add_fusion.one_sums), channel_id=1, source_target_pairs={{0,2},{1,3},{2,0},{3,1},{4,6},{5,7},{6,4},{7,5},{8,10},{9,11},{10,... | collective-permute-start | bytes 1544 | tf_op jit(solution)/shard_map/ppermute | solution.py:28
  36.2 11.1 %collective-permute-start.13 = (bf16[128,2304]{1,0:T(8,128)(2,1)S(1)}, bf16[128,2304]{1,0:T(8,128)(2,1)S(1)}, u32[]{:S(2)}, u32[]{:S(2)}) collective-permute-start(bf16[128,2304]{1,0:T(8,128)(2,1)S(1)} %collective-permute-done.7.refs_1_), channel_id=1, source_target_pairs={{0,4},{1,5},{2,6},{3,7},{4,8},{5,9},{6,10},{7,11},{8,12},{9,13},{1... | collective-permute-start | bytes 1769480 | tf_op jit(solution)/shard_map/ppermute | solution.py:28
  36.2 11.1 %collective-permute-start.15 = (bf16[128,2304]{1,0:T(8,128)(2,1)S(1)}, bf16[128,2304]{1,0:T(8,128)(2,1)S(1)}, u32[]{:S(2)}, u32[]{:S(2)}) collective-permute-start(bf16[128,2304]{1,0:T(8,128)(2,1)S(1)} %normalize.3.refs_4_), channel_id=1, source_target_pairs={{0,12},{1,13},{2,14},{3,15},{4,0},{5,1},{6,2},{7,3},{8,4},{9,5},{1... | collective-permute-start | bytes 1769480 | tf_op jit(solution)/shard_map/ppermute | solution.py:28
  47.3 11.7 %collective-permute-start.14 = (bf16[128,2304]{1,0:T(8,128)(2,1)S(1)}, bf16[128,2304]{1,0:T(8,128)(2,1)S(1)}, u32[]{:S(2)}, u32[]{:S(2)}) collective-permute-start(bf16[128,2304]{1,0:T(8,128)(2,1)S(1)} %normalize.3.refs_4_), channel_id=1, source_target_pairs={{0,4},{1,5},{2,6},{3,7},{4,8},{5,9},{6,10},{7,11},{8,12},{9,13},{1... | collective-permute-start | bytes 1769480 | tf_op jit(solution)/shard_map/ppermute | solution.py:28
  47.3 11.7 %collective-permute-start.16 = (bf16[128,2304]{1,0:T(8,128)(2,1)S(1)}, bf16[128,2304]{1,0:T(8,128)(2,1)S(1)}, u32[]{:S(2)}, u32[]{:S(2)}) collective-permute-start(bf16[128,2304]{1,0:T(8,128)(2,1)S(1)} %collective-permute-done.15.refs_6_), channel_id=1, source_target_pairs={{0,12},{1,13},{2,14},{3,15},{4,0},{5,1},{6,2},{7,3},{8,4},{9,5},{1... | collective-permute-start | bytes 1769480 | tf_op jit(solution)/shard_map/ppermute | solution.py:28
  66.2 11.4 %collective-permute-start.22 = (f32[128,768]{1,0:T(8,128)S(1)}, f32[128,768]{1,0:T(8,128)S(1)}, u32[]{:S(2)}, u32[]{:S(2)}) collective-permute-start(f32[128,768]{1,0:T(8,128)S(1)} %get-tuple-element.106), channel_id=1, source_target_pairs={{0,32},{1,33},{2,34},{3,35},{4,36},{5,37},{6,38},{7,39},{8,40},{9,... | collective-permute-start | bytes 1179656 | tf_op jit(solution)/shard_map/ppermute | solution.py:28
  67.2 10.6 %collective-permute-start.25 = (f32[128,768]{1,0:T(8,128)S(1)}, f32[128,768]{1,0:T(8,128)S(1)}, u32[]{:S(2)}, u32[]{:S(2)}) collective-permute-start(f32[128,768]{1,0:T(8,128)S(1)} %get-tuple-element.107), channel_id=1, source_target_pairs={{0,96},{1,97},{2,98},{3,99},{4,100},{5,101},{6,102},{7,103},{8,104... | collective-permute-start | bytes 1179656 | tf_op jit(solution)/shard_map/ppermute | solution.py:28
  77.8 9.1 %collective-permute-start.24 = (f32[128,768]{1,0:T(8,128)S(1)}, f32[128,768]{1,0:T(8,128)S(1)}, u32[]{:S(2)}, u32[]{:S(2)}) collective-permute-start(f32[128,768]{1,0:T(8,128)S(1)} %slice_add_fusion), channel_id=1, source_target_pairs={{0,32},{1,33},{2,34},{3,35},{4,36},{5,37},{6,38},{7,39},{8,40},{9,... | collective-permute-start | bytes 1179656 | tf_op jit(solution)/shard_map/ppermute | solution.py:28
  117.7 7.5 %collective-permute-start.27 = (bf16[128,768]{1,0:T(8,128)(2,1)S(1)}, bf16[128,768]{1,0:T(8,128)(2,1)S(1)}, u32[]{:S(2)}, u32[]{:S(2)}) collective-permute-start(bf16[128,768]{1,0:T(8,128)(2,1)S(1)} %bitcast.10), channel_id=1, source_target_pairs={{0,96},{1,97},{2,98},{3,99},{4,100},{5,101},{6,102},{7,103},{8,104... | collective-permute-start | bytes 589832 | tf_op jit(solution)/shard_map/ppermute | solution.py:28
  133.7 11.2 %collective-permute-start.34 = (bf16[128,2304]{1,0:T(8,128)(2,1)S(1)}, bf16[128,2304]{1,0:T(8,128)(2,1)S(1)}, u32[]{:S(2)}, u32[]{:S(2)}) collective-permute-start(bf16[128,2304]{1,0:T(8,128)(2,1)S(1)} %get-tuple-element.83), channel_id=1, source_target_pairs={{0,4},{1,5},{2,6},{3,7},{4,8},{5,9},{6,10},{7,11},{8,12},{9,13},{1... | collective-permute-start | bytes 1769480 | tf_op jit(solution)/shard_map/ppermute | solution.py:28
  134.3 10.7 %collective-permute-start.35 = (bf16[128,2304]{1,0:T(8,128)(2,1)S(1)}, bf16[128,2304]{1,0:T(8,128)(2,1)S(1)}, u32[]{:S(2)}, u32[]{:S(2)}) collective-permute-start(bf16[128,2304]{1,0:T(8,128)(2,1)S(1)} %get-tuple-element.84), channel_id=1, source_target_pairs={{0,12},{1,13},{2,14},{3,15},{4,0},{5,1},{6,2},{7,3},{8,4},{9,5},{1... | collective-permute-start | bytes 1769480 | tf_op jit(solution)/shard_map/ppermute | solution.py:28
  141.1 10.0 %collective-permute-start.33 = (bf16[128,2304]{1,0:T(8,128)(2,1)S(1)}, bf16[128,2304]{1,0:T(8,128)(2,1)S(1)}, u32[]{:S(2)}, u32[]{:S(2)}) collective-permute-start(bf16[128,2304]{1,0:T(8,128)(2,1)S(1)} %get-tuple-element.81), channel_id=1, source_target_pairs={{0,12},{1,13},{2,14},{3,15},{4,0},{5,1},{6,2},{7,3},{8,4},{9,5},{1... | collective-permute-start | bytes 1769480 | tf_op jit(solution)/shard_map/ppermute | solution.py:28
  141.2 11.2 %collective-permute-start.37 = (bf16[128,2304]{1,0:T(8,128)(2,1)S(1)}, bf16[128,2304]{1,0:T(8,128)(2,1)S(1)}, u32[]{:S(2)}, u32[]{:S(2)}) collective-permute-start(bf16[128,2304]{1,0:T(8,128)(2,1)S(1)} %get-tuple-element.86), channel_id=1, source_target_pairs={{0,4},{1,5},{2,6},{3,7},{4,8},{5,9},{6,10},{7,11},{8,12},{9,13},{1... | collective-permute-start | bytes 1769480 | tf_op jit(solution)/shard_map/ppermute | solution.py:28
  145.0 13.7 %collective-permute-start.36 = (bf16[128,2304]{1,0:T(8,128)(2,1)S(1)}, bf16[128,2304]{1,0:T(8,128)(2,1)S(1)}, u32[]{:S(2)}, u32[]{:S(2)}) collective-permute-start(bf16[128,2304]{1,0:T(8,128)(2,1)S(1)} %add_convert_fusion.1), channel_id=1, source_target_pairs={{0,4},{1,5},{2,6},{3,7},{4,8},{5,9},{6,10},{7,11},{8,12},{9,13},{1... | collective-permute-start | bytes 1769480 | tf_op jit(solution)/shard_map/ppermute | solution.py:28
  145.3 13.4 %collective-permute-start.38 = (bf16[128,2304]{1,0:T(8,128)(2,1)S(1)}, bf16[128,2304]{1,0:T(8,128)(2,1)S(1)}, u32[]{:S(2)}, u32[]{:S(2)}) collective-permute-start(bf16[128,2304]{1,0:T(8,128)(2,1)S(1)} %add_convert_fusion), channel_id=1, source_target_pairs={{0,12},{1,13},{2,14},{3,15},{4,0},{5,1},{6,2},{7,3},{8,4},{9,5},{1... | collective-permute-start | bytes 1769480 | tf_op jit(solution)/shard_map/ppermute | solution.py:28
  159.7 7.4 %collective-permute-start.43 = (f32[32,1152]{1,0:T(8,128)S(1)}, f32[32,1152]{1,0:T(8,128)S(1)}, u32[]{:S(2)}, u32[]{:S(2)}) collective-permute-start(f32[32,1152]{1,0:T(8,128)S(1)} %get-tuple-element.101), channel_id=1, source_target_pairs={{0,1},{1,2},{2,3},{3,0},{4,5},{5,6},{6,7},{7,4},{8,9},{9,10},{10,1... | collective-permute-start | bytes 442376 | tf_op jit(solution)/shard_map/ppermute | solution.py:28
  167.2 8.0 %collective-permute-start.44 = (f32[64,1152]{1,0:T(8,128)S(1)}, f32[64,1152]{1,0:T(8,128)S(1)}, u32[]{:S(2)}, u32[]{:S(2)}) collective-permute-start(f32[64,1152]{1,0:T(8,128)S(1)} %pad_maximum_fusion.2), channel_id=1, source_target_pairs={{0,1},{1,2},{2,3},{3,0},{4,5},{5,6},{6,7},{7,4},{8,9},{9,10},{10,1... | collective-permute-start | bytes 884744 | tf_op jit(solution)/shard_map/ppermute | solution.py:28
  167.3 11.1 %collective-permute-start.40 = (f32[64,1152]{1,0:T(8,128)S(1)}, f32[64,1152]{1,0:T(8,128)S(1)}, u32[]{:S(2)}, u32[]{:S(2)}) collective-permute-start(f32[64,1152]{1,0:T(8,128)S(1)} %pad_maximum_fusion), channel_id=1, source_target_pairs={{0,1},{1,2},{2,3},{3,0},{4,5},{5,6},{6,7},{7,4},{8,9},{9,10},{10,1... | collective-permute-start | bytes 884744 | tf_op jit(solution)/shard_map/ppermute | solution.py:28
  168.1 10.2 %collective-permute-start.46 = (f32[64,1152]{1,0:T(8,128)S(1)}, f32[64,1152]{1,0:T(8,128)S(1)}, u32[]{:S(2)}, u32[]{:S(2)}) collective-permute-start(f32[64,1152]{1,0:T(8,128)S(1)} %pad_maximum_fusion.3), channel_id=1, source_target_pairs={{0,3},{1,0},{2,1},{3,2},{4,7},{5,4},{6,5},{7,6},{8,11},{9,8},{10,9... | collective-permute-start | bytes 884744 | tf_op jit(solution)/shard_map/ppermute | solution.py:28
  (30 other events, 311.2 us)

commit v5 on v4

--- a/solution.py
+++ b/solution.py
@@ -359,15 +359,20 @@
     near_before, near_after, wide, kept = lax.optimization_barrier(
         (near_before, near_after, wide, kept)
     )
-    wide_after = send_outer(wide, -1)
-    near_far = send_outer(near_before, 1)
-    near_far, wide_again = lax.optimization_barrier((near_far, wide))
-    wide_before = send_outer(wide_again, 1)
-    wide_far = send_outer(wide_after, -1)
-
     kept = kept.reshape(RING, count // 8, 2 * HEAD)
     keyval = kept[0] + send_ahead(kept[1], 1) + send_ahead(kept[2], 2) + send_ahead(kept[3], 3)
     keyval = keyval.astype(BF16)
+
+    wide_after = send_outer(wide, -1)
+    near_far = send_outer(near_before, 1)
+    near_far, wide_again, keyval = lax.optimization_barrier((near_far, wide, keyval))
+    wide_before = send_outer(wide_again, 1)
+    wide_far = send_outer(wide_after, -1)
+
+    moves = [
+        (g * 16 + j, (j // 2) * 16 + (j % 2) * 8 + g) for g in range(8) for j in range(16)
+    ]
+    keyval = lax.ppermute(keyval, ("gx", "yz"), moves)
 
     pieces = [near, near_before, near_after, near_far, wide, wide_before, wide_after, wide_far]
     columns = w_query.shape[1]
@@ -377,11 +382,6 @@
     far, behind = send_x(summed[0], 1), send_x(summed[1], -1)
     away, keep = project_query(place, pieces, w_query, 0)
     summed = (keep + send_core(away)).reshape(2, 128, columns)
-    moves = [
-        (g * 16 + j, (j // 2) * 16 + (j % 2) * 8 + g) for g in range(8) for j in range(16)
-    ]
-    keyval = lax.ppermute(keyval, ("gx", "yz"), moves)
-    far, keyval = lax.optimization_barrier((far, keyval))
     ahead = send_x(summed[1] + far, 1)
     query = (summed[0] + ahead + behind).astype(BF16).reshape(16, 8, columns)
     query = lax.all_to_all(query, "yz", split_axis=0, concat_axis=0)
@@ -408,15 +408,12 @@
     late_high = send_outer((three_high + far_high.astype(F32)).astype(BF16), -1)
     low = own[:128] + early_low.astype(F32) + late_low.astype(F32)
     high = own[128:] + early_high.astype(F32) + late_high.astype(F32)
-    halves = []
-    for columns in (slice(0, features // 2), slice(features // 2, features)):
-        here, one = low[:64, columns], low[64:, columns]
-        two, three = high[:64, columns], high[64:, columns]
-        far_low, far_high = send_inner(two[:32], 1), send_inner(two[32:], -1)
-        one = jnp.concatenate([one[:32] + far_low, one[32:]], 0)
-        three = jnp.concatenate([three[:32], three[32:] + far_high], 0)
-        halves.append(here + send_inner(one, 1) + send_inner(three, -1))
-    branch = jnp.concatenate(halves, 1)
+    here, one, two, three = low[:64], low[64:], high[:64], high[64:]
+    two = two.astype(BF16)
+    far_low, far_high = send_inner(two[:32], 1), send_inner(two[32:], -1)
+    one = jnp.concatenate([one[:32] + far_low.astype(F32), one[32:]], 0)
+    three = jnp.concatenate([three[:32], three[32:] + far_high.astype(F32)], 0)
+    branch = here + send_inner(one, 1) + send_inner(three, -1)
     mixed = (raw.astype(F32) + branch).astype(BF16).reshape(tokens.shape)
     return (mixed, new_keyval.reshape(seqs, 2, 2 * HEAD))
 

time: 180 us -> 181 us (level)
  starting transfers between devices: 56.1 us -> 51.1 us
  waiting for transfers between devices: 72.9 us -> 77.4 us
    ppermute x38 -> x34, starting transfers between devices: 54 us -> 49.1 us  [shift(): return lax.ppermute(value, ('gx', 'yz'), pairs)]
    ppermute x38 -> x34, waiting for transfers between devices: 71.3 us -> 75.9 us  [shift(): return lax.ppermute(value, ('gx', 'yz'), pairs)]
  transfers between devices with their start and end apart: 47 -> 43, of which waited for: 26 -> 21; matrix products, arithmetic and copies ran while one was open for 2% -> 1% of each run, Pallas kernels for 5% -> 5%
where the time goes in v5:
time: 181 us
  waiting for transfers between devices  77.4 us (43%)
  starting transfers between devices  51.1 us (28%)
  blocking collectives  26.8 us (15%)
  Pallas kernels  18.4 us (10%)
  local copies, waits for them, and re-layouts  3.59 us (2%)
  other arithmetic  2.44 us (1%)
    ppermute x34, waiting for transfers between devices, shift(): return lax.ppermute(value, ('gx', 'yz'), pairs)  75.9 us
    ppermute x34, starting transfers between devices, shift(): return lax.ppermute(value, ('gx', 'yz'), pairs)  49.1 us
    all_to_all x1, blocking collectives, body(): query = lax.all_to_all(query, 'yz', split_axis=0, concat_axis=0)  15.2 us
    all_to_all x1, blocking collectives, body(): lax.all_to_all(heads_out.reshape(16, 8, columns), 'yz', split_axis=0, con...  11.6 us
    pallas_call x2, Pallas kernels, project_query(): pl.pallas_call(functools.partial(query_kernel, pair), out_shape=[half, ha...  6.34 us
    pallas_call x2, Pallas kernels, project_output(): pl.pallas_call(functools.partial(output_kernel, groups), out_shape=shapes...  5.86 us
    pallas_call x1, Pallas kernels, attend(): pl.pallas_call(attend_kernel, out_shape=[jax.ShapeDtypeStruct((rows, colu...  4.36 us
  transfers between devices with their start and end apart: 43, of which 21 were waited for; matrix products, arithmetic and copies ran while one was open for 1% of the time, Pallas kernels for 5%

profile of v5, /device:TPU:0, one launch (start us, length us, event | category | flops | bytes accessed | tf_op | source)
XLA Modules:
  0.0 180.8 jit_solution(7220701992117278209)
XLA Ops:
  3.3 4.1 %collective-permute-start.5 = (bf16[64,2304]{1,0:T(8,128)(2,1)S(1)}, bf16[64,2304]{1,0:T(8,128)(2,1)S(1)}, u32[]{:S(2)}, u32[]{:S(2)}) collective-permute-start(bf16[64,2304]{1,0:T(8,128)(2,1)S(1)} %reshape.66.rows_ref.one_ref), channel_id=1, source_target_pairs={{0,3},{1,0},{2,1},{3,2},{4,7},{5,4},{6,5},{7,6},{8,11},{9,8},{10,9... | collective-permute-start | bytes 884744 | tf_op jit(solution)/shard_map/ppermute | solution.py:28
  11.9 3.7 %collective-permute-done.2 = f32[64,2]{1,0:T(8,128)S(1)} collective-permute-done((f32[64,2]{1,0:T(8,128)S(1)}, f32[64,2]{1,0:T(8,128)S(1)}, u32[]{:S(2)}, u32[]{:S(2)}) %collective-permute-start.2) | collective-permute-done | bytes 544 | tf_op jit(solution)/shard_map/ppermute | solution.py:28
  16.3 5.1 %collective-permute-done.6.two_sums = f32[64,2]{1,0:T(8,128)S(1)} collective-permute-done((f32[64,2]{1,0:T(8,128)S(1)}, f32[64,2]{1,0:T(8,128)S(1)}, u32[]{:S(2)}, u32[]{:S(2)}) %collective-permute-start.6) | collective-permute-done | bytes 544 | tf_op jit(solution)/shard_map/ppermute | solution.py:28
  25.9 3.7 %collective-permute-start.11 = (f32[64,2]{1,0:T(8,128)S(1)}, f32[64,2]{1,0:T(8,128)S(1)}, u32[]{:S(2)}, u32[]{:S(2)}) collective-permute-start(f32[64,2]{1,0:T(8,128)S(1)} %add_add_fusion.one_sums), channel_id=1, source_target_pairs={{0,2},{1,3},{2,0},{3,1},{4,6},{5,7},{6,4},{7,5},{8,10},{9,11},{10,... | collective-permute-start | bytes 1544 | tf_op jit(solution)/shard_map/ppermute | solution.py:28
  30.4 3.7 %collective-permute-done.11.two_sums = f32[64,2]{1,0:T(8,128)S(1)} collective-permute-done((f32[64,2]{1,0:T(8,128)S(1)}, f32[64,2]{1,0:T(8,128)S(1)}, u32[]{:S(2)}, u32[]{:S(2)}) %collective-permute-start.11) | collective-permute-done | bytes 544 | tf_op jit(solution)/shard_map/ppermute | solution.py:28
  36.2 3.2 %collective-permute-start.18 = (bf16[128,2304]{1,0:T(8,128)(2,1)S(1)}, bf16[128,2304]{1,0:T(8,128)(2,1)S(1)}, u32[]{:S(2)}, u32[]{:S(2)}) collective-permute-start(bf16[128,2304]{1,0:T(8,128)(2,1)S(1)} %normalize.3.refs_4_), channel_id=1, source_target_pairs={{0,12},{1,13},{2,14},{3,15},{4,0},{5,1},{6,2},{7,3},{8,4},{9,5},{1... | collective-permute-start | bytes 1769480 | tf_op jit(solution)/shard_map/ppermute | solution.py:28
  44.4 3.5 %collective-permute-done.15 = f32[8,512]{1,0:T(8,128)S(1)} collective-permute-done((f32[8,512]{1,0:T(8,128)S(1)}, f32[8,512]{1,0:T(8,128)S(1)}, u32[]{:S(2)}, u32[]{:S(2)}) %collective-permute-start.15) | collective-permute-done | bytes 16416 | tf_op jit(solution)/shard_map/ppermute | solution.py:28
  48.0 3.2 %collective-permute-start.19 = (bf16[128,2304]{1,0:T(8,128)(2,1)S(1)}, bf16[128,2304]{1,0:T(8,128)(2,1)S(1)}, u32[]{:S(2)}, u32[]{:S(2)}) collective-permute-start(bf16[128,2304]{1,0:T(8,128)(2,1)S(1)} %collective-permute-done.18.refs_6_), channel_id=1, source_target_pairs={{0,12},{1,13},{2,14},{3,15},{4,0},{5,1},{6,2},{7,3},{8,4},{9,5},{1... | collective-permute-start | bytes 1769480 | tf_op jit(solution)/shard_map/ppermute | solution.py:28
  51.9 7.2 %collective-permute-done.17.refs_5_ = bf16[128,2304]{1,0:T(8,128)(2,1)S(1)} collective-permute-done((bf16[128,2304]{1,0:T(8,128)(2,1)S(1)}, bf16[128,2304]{1,0:T(8,128)(2,1)S(1)}, u32[]{:S(2)}, u32[]{:S(2)}) %collective-permute-start.17) | collective-permute-done | bytes 589856 | tf_op jit(solution)/shard_map/ppermute | solution.py:28
  62.3 3.3 %query_projection.2 = (f32[256,768]{1,0:T(8,128)S(1)}, f32[256,768]{1,0:T(8,128)S(1)}) custom-call(s32[4]{0:T(128)S(1)} %pad_add_fusion.place, bf16[128,2304]{1,0:T(8,128)(2,1)S(1)} %normalize.2.rows_ref.refs_0_, bf16[128,2304]{1,0:T(8,128)(2,1)S(1)} %collective-permute-done.7.refs_1_, bf16[128,2304]{1,0:T(8,128)(2,1)S(1)} %collective-permute-done.8.refs_2_, ...), custom_call_target="tpu_custom_call" | custom-call | flops 1811939328 | bytes 8388608 | tf_op jit(solution)/shard_map/query_projection/pallas_call | solution.py:159
  66.4 3.2 %collective-permute-start.25 = (f32[128,768]{1,0:T(8,128)S(1)}, f32[128,768]{1,0:T(8,128)S(1)}, u32[]{:S(2)}, u32[]{:S(2)}) collective-permute-start(f32[128,768]{1,0:T(8,128)S(1)} %get-tuple-element.96), channel_id=1, source_target_pairs={{0,96},{1,97},{2,98},{3,99},{4,100},{5,101},{6,102},{7,103},{8,104... | collective-permute-start | bytes 1179656 | tf_op jit(solution)/shard_map/ppermute | solution.py:28
  69.7 8.7 %collective-permute-done.23 = f32[128,768]{1,0:T(8,128)S(1)} collective-permute-done((f32[128,768]{1,0:T(8,128)S(1)}, f32[128,768]{1,0:T(8,128)S(1)}, u32[]{:S(2)}, u32[]{:S(2)}) %collective-permute-start.23) | collective-permute-done | bytes 393248 | tf_op jit(solution)/shard_map/ppermute | solution.py:28
  78.5 9.0 %collective-permute-done.24 = f32[128,768]{1,0:T(8,128)S(1)} collective-permute-done((f32[128,768]{1,0:T(8,128)S(1)}, f32[128,768]{1,0:T(8,128)S(1)}, u32[]{:S(2)}, u32[]{:S(2)}) %collective-permute-start.24) | collective-permute-done | bytes 393248 | tf_op jit(solution)/shard_map/ppermute | solution.py:28
  87.5 15.2 %all_to_all.10 = bf16[16,8,768]{2,1,0:T(8,128)(2,1)S(1)} all-to-all(bf16[16,8,768]{2,1,0:T(8,128)(2,1)S(1)} %fusion.5), channel_id=1, replica_groups=mesh['gx'=8,'yz'=16] {'yz'}, dimensions={0} | all-to-all | bytes 393216 | tf_op jit(solution)/shard_map/all_to_all | solution.py:387
  102.8 4.4 %attention.1 = (bf16[128,768]{1,0:T(8,128)(2,1)S(1)}, bf16[8,512]{1,0:T(8,128)(2,1)S(1)}) custom-call(s32[4]{0:T(128)S(1)} %copy-done.5, bf16[128,768]{1,0:T(8,128)(2,1)S(1)} %bitcast.14, f32[8,128]{1,0:T(8,128)S(1)} %get-tuple-element.74.cos_ref, f32[8,128]{1,0:T(8,128)S(1)} %get-tuple-element.75.sin_ref, ...), custom_call_target="tpu_custom_call" | custom-call | flops 805306368 | bytes 8388608 | tf_op jit(solution)/shard_map/attention/pallas_call | solution.py:256
  107.2 11.6 %all_to_all.11 = bf16[16,8,768]{2,1,0:T(8,128)(2,1)S(1)} all-to-all(bf16[16,8,768]{2,1,0:T(8,128)(2,1)S(1)} %bitcast.15), channel_id=1, replica_groups=mesh['gx'=8,'yz'=16] {'yz'}, dimensions={0} | all-to-all | bytes 393216 | tf_op jit(solution)/shard_map/all_to_all | solution.py:392
  118.8 3.2 %collective-permute-start.27 = (bf16[128,768]{1,0:T(8,128)(2,1)S(1)}, bf16[128,768]{1,0:T(8,128)(2,1)S(1)}, u32[]{:S(2)}, u32[]{:S(2)}) collective-permute-start(bf16[128,768]{1,0:T(8,128)(2,1)S(1)} %bitcast.10), channel_id=1, source_target_pairs={{0,96},{1,97},{2,98},{3,99},{4,100},{5,101},{6,102},{7,103},{8,104... | collective-permute-start | bytes 589832 | tf_op jit(solution)/shard_map/ppermute | solution.py:28
  122.0 3.6 %collective-permute-done.26.refs_1_ = bf16[128,768]{1,0:T(8,128)(2,1)S(1)} collective-permute-done((bf16[128,768]{1,0:T(8,128)(2,1)S(1)}, bf16[128,768]{1,0:T(8,128)(2,1)S(1)}, u32[]{:S(2)}, u32[]{:S(2)}) %collective-permute-start.26) | collective-permute-done | bytes 196640 | tf_op jit(solution)/shard_map/ppermute | solution.py:28
  126.2 6.4 %collective-permute-done.28.refs_3_ = bf16[128,768]{1,0:T(8,128)(2,1)S(1)} collective-permute-done((bf16[128,768]{1,0:T(8,128)(2,1)S(1)}, bf16[128,768]{1,0:T(8,128)(2,1)S(1)}, u32[]{:S(2)}, u32[]{:S(2)}) %collective-permute-start.28) | collective-permute-done | bytes 196640 | tf_op jit(solution)/shard_map/ppermute | solution.py:28
  139.1 4.1 %output_projection.2 = (f32[128,2304]{1,0:T(8,128)S(1)}, bf16[128,2304]{1,0:T(8,128)(2,1)S(1)}, bf16[128,2304]{1,0:T(8,128)(2,1)S(1)}, f32[128,2304]{1,0:T(8,128)S(1)}, f32[256,2304]{1,0:T(8,128)S(1)}) custom-call(s32[4]{0:T(128)S(1)} %pad_add_fusion.place, bf16[128,768]{1,0:T(8,128)(2,1)S(1)} %bitcast.13, ...), custom_call_target="tpu_custom_call" | custom-call | flops 2717908992 | bytes 8388608 | tf_op jit(solution)/shard_map/output_projection/pallas_call | solution.py:316
  147.3 3.2 %collective-permute-start.38 = (bf16[128,2304]{1,0:T(8,128)(2,1)S(1)}, bf16[128,2304]{1,0:T(8,128)(2,1)S(1)}, u32[]{:S(2)}, u32[]{:S(2)}) collective-permute-start(bf16[128,2304]{1,0:T(8,128)(2,1)S(1)} %add_convert_fusion), channel_id=1, source_target_pairs={{0,12},{1,13},{2,14},{3,15},{4,0},{5,1},{6,2},{7,3},{8,4},{9,5},{1... | collective-permute-start | bytes 1769480 | tf_op jit(solution)/shard_map/ppermute | solution.py:28
  154.4 6.3 %collective-permute-done.36 = bf16[128,2304]{1,0:T(8,128)(2,1)S(1)} collective-permute-done((bf16[128,2304]{1,0:T(8,128)(2,1)S(1)}, bf16[128,2304]{1,0:T(8,128)(2,1)S(1)}, u32[]{:S(2)}, u32[]{:S(2)}) %collective-permute-start.36) | collective-permute-done | bytes 589856 | tf_op jit(solution)/shard_map/ppermute | solution.py:28
  167.8 3.3 %collective-permute-start.42 = (f32[64,2304]{1,0:T(8,128)S(1)}, f32[64,2304]{1,0:T(8,128)}, u32[]{:S(2)}, u32[]{:S(2)}) collective-permute-start(f32[64,2304]{1,0:T(8,128)S(1)} %pad_maximum_fusion.1), channel_id=1, source_target_pairs={{0,3},{1,0},{2,1},{3,2},{4,7},{5,4},{6,5},{7,6},{8,11},{9,8},{10,9... | collective-permute-start | bytes 1769480 | tf_op jit(solution)/shard_map/ppermute | solution.py:28
  171.7 7.1 %collective-permute-done.40 = f32[64,2304]{1,0:T(8,128)S(1)} collective-permute-done((f32[64,2304]{1,0:T(8,128)S(1)}, f32[64,2304]{1,0:T(8,128)S(1)}, u32[]{:S(2)}, u32[]{:S(2)}) %collective-permute-start.40) | collective-permute-done | bytes 589856 | tf_op jit(solution)/shard_map/ppermute | solution.py:28
  (116 shorter events, 49.8 us)
Async XLA Ops:
  3.3 12.8 %collective-permute-start.5 = (bf16[64,2304]{1,0:T(8,128)(2,1)S(1)}, bf16[64,2304]{1,0:T(8,128)(2,1)S(1)}, u32[]{:S(2)}, u32[]{:S(2)}) collective-permute-start(bf16[64,2304]{1,0:T(8,128)(2,1)S(1)} %reshape.66.rows_ref.one_ref), channel_id=1, source_target_pairs={{0,3},{1,0},{2,1},{3,2},{4,7},{5,4},{6,5},{7,6},{8,11},{9,8},{10,9... | collective-permute-start | bytes 884744 | tf_op jit(solution)/shard_map/ppermute | solution.py:28
  7.4 8.7 %collective-permute-start.4 = (bf16[64,2304]{1,0:T(8,128)(2,1)S(1)}, bf16[64,2304]{1,0:T(8,128)(2,1)S(1)}, u32[]{:S(2)}, u32[]{:S(2)}) collective-permute-start(bf16[64,2304]{1,0:T(8,128)(2,1)S(1)} %reshape.66.rows_ref.one_ref), channel_id=1, source_target_pairs={{0,1},{1,2},{2,3},{3,0},{4,5},{5,6},{6,7},{7,4},{8,9},{9,10},{10,1... | collective-permute-start | bytes 884744 | tf_op jit(solution)/shard_map/ppermute | solution.py:28
  21.7 13.7 %collective-permute-start.8 = (bf16[128,2304]{1,0:T(8,128)(2,1)S(1)}, bf16[128,2304]{1,0:T(8,128)(2,1)S(1)}, u32[]{:S(2)}, u32[]{:S(2)}) collective-permute-start(bf16[128,2304]{1,0:T(8,128)(2,1)S(1)} %normalize.2.rows_ref.refs_0_), channel_id=1, source_target_pairs={{0,12},{1,13},{2,14},{3,15},{4,0},{5,1},{6,2},{7,3},{8,4},{9,5},{1... | collective-permute-start | bytes 1769480 | tf_op jit(solution)/shard_map/ppermute | solution.py:28
  24.7 11.4 %collective-permute-start.7 = (bf16[128,2304]{1,0:T(8,128)(2,1)S(1)}, bf16[128,2304]{1,0:T(8,128)(2,1)S(1)}, u32[]{:S(2)}, u32[]{:S(2)}) collective-permute-start(bf16[128,2304]{1,0:T(8,128)(2,1)S(1)} %normalize.2.rows_ref.refs_0_), channel_id=1, source_target_pairs={{0,4},{1,5},{2,6},{3,7},{4,8},{5,9},{6,10},{7,11},{8,12},{9,13},{1... | collective-permute-start | bytes 1769480 | tf_op jit(solution)/shard_map/ppermute | solution.py:28
  24.7 10.3 %collective-permute-start.9 = (bf16[64,2304]{1,0:T(8,128)(2,1)S(1)}, bf16[64,2304]{1,0:T(8,128)(2,1)S(1)}, u32[]{:S(2)}, u32[]{:S(2)}) collective-permute-start(bf16[64,2304]{1,0:T(8,128)(2,1)S(1)} %collective-permute-done.4.two_ref), channel_id=1, source_target_pairs={{0,1},{1,2},{2,3},{3,0},{4,5},{5,6},{6,7},{7,4},{8,9},{9,10},{10,1... | collective-permute-start | bytes 884744 | tf_op jit(solution)/shard_map/ppermute | solution.py:28
  25.9 8.2 %collective-permute-start.11 = (f32[64,2]{1,0:T(8,128)S(1)}, f32[64,2]{1,0:T(8,128)S(1)}, u32[]{:S(2)}, u32[]{:S(2)}) collective-permute-start(f32[64,2]{1,0:T(8,128)S(1)} %add_add_fusion.one_sums), channel_id=1, source_target_pairs={{0,2},{1,3},{2,0},{3,1},{4,6},{5,7},{6,4},{7,5},{8,10},{9,11},{10,... | collective-permute-start | bytes 1544 | tf_op jit(solution)/shard_map/ppermute | solution.py:28
  36.2 11.7 %collective-permute-start.13 = (bf16[128,2304]{1,0:T(8,128)(2,1)S(1)}, bf16[128,2304]{1,0:T(8,128)(2,1)S(1)}, u32[]{:S(2)}, u32[]{:S(2)}) collective-permute-start(bf16[128,2304]{1,0:T(8,128)(2,1)S(1)} %collective-permute-done.7.refs_1_), channel_id=1, source_target_pairs={{0,4},{1,5},{2,6},{3,7},{4,8},{5,9},{6,10},{7,11},{8,12},{9,13},{1... | collective-permute-start | bytes 1769480 | tf_op jit(solution)/shard_map/ppermute | solution.py:28
  36.2 11.8 %collective-permute-start.18 = (bf16[128,2304]{1,0:T(8,128)(2,1)S(1)}, bf16[128,2304]{1,0:T(8,128)(2,1)S(1)}, u32[]{:S(2)}, u32[]{:S(2)}) collective-permute-start(bf16[128,2304]{1,0:T(8,128)(2,1)S(1)} %normalize.3.refs_4_), channel_id=1, source_target_pairs={{0,12},{1,13},{2,14},{3,15},{4,0},{5,1},{6,2},{7,3},{8,4},{9,5},{1... | collective-permute-start | bytes 1769480 | tf_op jit(solution)/shard_map/ppermute | solution.py:28
  47.9 11.2 %collective-permute-start.17 = (bf16[128,2304]{1,0:T(8,128)(2,1)S(1)}, bf16[128,2304]{1,0:T(8,128)(2,1)S(1)}, u32[]{:S(2)}, u32[]{:S(2)}) collective-permute-start(bf16[128,2304]{1,0:T(8,128)(2,1)S(1)} %normalize.3.refs_4_), channel_id=1, source_target_pairs={{0,4},{1,5},{2,6},{3,7},{4,8},{5,9},{6,10},{7,11},{8,12},{9,13},{1... | collective-permute-start | bytes 1769480 | tf_op jit(solution)/shard_map/ppermute | solution.py:28
  48.0 11.1 %collective-permute-start.19 = (bf16[128,2304]{1,0:T(8,128)(2,1)S(1)}, bf16[128,2304]{1,0:T(8,128)(2,1)S(1)}, u32[]{:S(2)}, u32[]{:S(2)}) collective-permute-start(bf16[128,2304]{1,0:T(8,128)(2,1)S(1)} %collective-permute-done.18.refs_6_), channel_id=1, source_target_pairs={{0,12},{1,13},{2,14},{3,15},{4,0},{5,1},{6,2},{7,3},{8,4},{9,5},{1... | collective-permute-start | bytes 1769480 | tf_op jit(solution)/shard_map/ppermute | solution.py:28
  66.3 12.1 %collective-permute-start.23 = (f32[128,768]{1,0:T(8,128)S(1)}, f32[128,768]{1,0:T(8,128)S(1)}, u32[]{:S(2)}, u32[]{:S(2)}) collective-permute-start(f32[128,768]{1,0:T(8,128)S(1)} %get-tuple-element.95), channel_id=1, source_target_pairs={{0,32},{1,33},{2,34},{3,35},{4,36},{5,37},{6,38},{7,39},{8,40},{9,... | collective-permute-start | bytes 1179656 | tf_op jit(solution)/shard_map/ppermute | solution.py:28
  66.4 12.1 %collective-permute-start.25 = (f32[128,768]{1,0:T(8,128)S(1)}, f32[128,768]{1,0:T(8,128)S(1)}, u32[]{:S(2)}, u32[]{:S(2)}) collective-permute-start(f32[128,768]{1,0:T(8,128)S(1)} %get-tuple-element.96), channel_id=1, source_target_pairs={{0,96},{1,97},{2,98},{3,99},{4,100},{5,101},{6,102},{7,103},{8,104... | collective-permute-start | bytes 1179656 | tf_op jit(solution)/shard_map/ppermute | solution.py:28
  78.4 9.1 %collective-permute-start.24 = (f32[128,768]{1,0:T(8,128)S(1)}, f32[128,768]{1,0:T(8,128)S(1)}, u32[]{:S(2)}, u32[]{:S(2)}) collective-permute-start(f32[128,768]{1,0:T(8,128)S(1)} %slice_add_fusion.1), channel_id=1, source_target_pairs={{0,32},{1,33},{2,34},{3,35},{4,36},{5,37},{6,38},{7,39},{8,40},{9,... | collective-permute-start | bytes 1179656 | tf_op jit(solution)/shard_map/ppermute | solution.py:28
  118.8 7.4 %collective-permute-start.27 = (bf16[128,768]{1,0:T(8,128)(2,1)S(1)}, bf16[128,768]{1,0:T(8,128)(2,1)S(1)}, u32[]{:S(2)}, u32[]{:S(2)}) collective-permute-start(bf16[128,768]{1,0:T(8,128)(2,1)S(1)} %bitcast.10), channel_id=1, source_target_pairs={{0,96},{1,97},{2,98},{3,99},{4,100},{5,101},{6,102},{7,103},{8,104... | collective-permute-start | bytes 589832 | tf_op jit(solution)/shard_map/ppermute | solution.py:28
  125.6 6.9 %collective-permute-start.29 = (bf16[128,768]{1,0:T(8,128)(2,1)S(1)}, bf16[128,768]{1,0:T(8,128)(2,1)S(1)}, u32[]{:S(2)}, u32[]{:S(2)}) collective-permute-start(bf16[128,768]{1,0:T(8,128)(2,1)S(1)} %bitcast.11), channel_id=1, source_target_pairs={{0,16},{16,0},{32,48},{48,32},{64,80},{80,64},{96,112},{112,96},{1... | collective-permute-start | bytes 589832 | tf_op jit(solution)/shard_map/ppermute | solution.py:33
  125.6 6.9 %collective-permute-start.30 = (bf16[128,768]{1,0:T(8,128)(2,1)S(1)}, bf16[128,768]{1,0:T(8,128)(2,1)S(1)}, u32[]{:S(2)}, u32[]{:S(2)}) collective-permute-start(bf16[128,768]{1,0:T(8,128)(2,1)S(1)} %collective-permute-done.26.refs_1_), channel_id=1, source_target_pairs={{0,16},{16,0},{32,48},{48,32},{64,80},{80,64},{96,112},{112,96},{1... | collective-permute-start | bytes 589832 | tf_op jit(solution)/shard_map/ppermute | solution.py:33
  135.8 11.2 %collective-permute-start.34 = (bf16[128,2304]{1,0:T(8,128)(2,1)S(1)}, bf16[128,2304]{1,0:T(8,128)(2,1)S(1)}, u32[]{:S(2)}, u32[]{:S(2)}) collective-permute-start(bf16[128,2304]{1,0:T(8,128)(2,1)S(1)} %get-tuple-element.81), channel_id=1, source_target_pairs={{0,4},{1,5},{2,6},{3,7},{4,8},{5,9},{6,10},{7,11},{8,12},{9,13},{1... | collective-permute-start | bytes 1769480 | tf_op jit(solution)/shard_map/ppermute | solution.py:28
  136.3 10.7 %collective-permute-start.35 = (bf16[128,2304]{1,0:T(8,128)(2,1)S(1)}, bf16[128,2304]{1,0:T(8,128)(2,1)S(1)}, u32[]{:S(2)}, u32[]{:S(2)}) collective-permute-start(bf16[128,2304]{1,0:T(8,128)(2,1)S(1)} %get-tuple-element.82), channel_id=1, source_target_pairs={{0,12},{1,13},{2,14},{3,15},{4,0},{5,1},{6,2},{7,3},{8,4},{9,5},{1... | collective-permute-start | bytes 1769480 | tf_op jit(solution)/shard_map/ppermute | solution.py:28
  143.1 10.0 %collective-permute-start.33 = (bf16[128,2304]{1,0:T(8,128)(2,1)S(1)}, bf16[128,2304]{1,0:T(8,128)(2,1)S(1)}, u32[]{:S(2)}, u32[]{:S(2)}) collective-permute-start(bf16[128,2304]{1,0:T(8,128)(2,1)S(1)} %get-tuple-element.79), channel_id=1, source_target_pairs={{0,12},{1,13},{2,14},{3,15},{4,0},{5,1},{6,2},{7,3},{8,4},{9,5},{1... | collective-permute-start | bytes 1769480 | tf_op jit(solution)/shard_map/ppermute | solution.py:28
  143.2 11.2 %collective-permute-start.37 = (bf16[128,2304]{1,0:T(8,128)(2,1)S(1)}, bf16[128,2304]{1,0:T(8,128)(2,1)S(1)}, u32[]{:S(2)}, u32[]{:S(2)}) collective-permute-start(bf16[128,2304]{1,0:T(8,128)(2,1)S(1)} %get-tuple-element.84), channel_id=1, source_target_pairs={{0,4},{1,5},{2,6},{3,7},{4,8},{5,9},{6,10},{7,11},{8,12},{9,13},{1... | collective-permute-start | bytes 1769480 | tf_op jit(solution)/shard_map/ppermute | solution.py:28
  147.0 13.7 %collective-permute-start.36 = (bf16[128,2304]{1,0:T(8,128)(2,1)S(1)}, bf16[128,2304]{1,0:T(8,128)(2,1)S(1)}, u32[]{:S(2)}, u32[]{:S(2)}) collective-permute-start(bf16[128,2304]{1,0:T(8,128)(2,1)S(1)} %add_convert_fusion.1), channel_id=1, source_target_pairs={{0,4},{1,5},{2,6},{3,7},{4,8},{5,9},{6,10},{7,11},{8,12},{9,13},{1... | collective-permute-start | bytes 1769480 | tf_op jit(solution)/shard_map/ppermute | solution.py:28
  147.3 13.4 %collective-permute-start.38 = (bf16[128,2304]{1,0:T(8,128)(2,1)S(1)}, bf16[128,2304]{1,0:T(8,128)(2,1)S(1)}, u32[]{:S(2)}, u32[]{:S(2)}) collective-permute-start(bf16[128,2304]{1,0:T(8,128)(2,1)S(1)} %add_convert_fusion), channel_id=1, source_target_pairs={{0,12},{1,13},{2,14},{3,15},{4,0},{5,1},{6,2},{7,3},{8,4},{9,5},{1... | collective-permute-start | bytes 1769480 | tf_op jit(solution)/shard_map/ppermute | solution.py:28
  167.6 11.2 %collective-permute-start.40 = (f32[64,2304]{1,0:T(8,128)S(1)}, f32[64,2304]{1,0:T(8,128)S(1)}, u32[]{:S(2)}, u32[]{:S(2)}) collective-permute-start(f32[64,2304]{1,0:T(8,128)S(1)} %pad_maximum_fusion), channel_id=1, source_target_pairs={{0,1},{1,2},{2,3},{3,0},{4,5},{5,6},{6,7},{7,4},{8,9},{9,10},{10,1... | collective-permute-start | bytes 1769480 | tf_op jit(solution)/shard_map/ppermute | solution.py:28
  167.8 11.0 %collective-permute-start.42 = (f32[64,2304]{1,0:T(8,128)S(1)}, f32[64,2304]{1,0:T(8,128)}, u32[]{:S(2)}, u32[]{:S(2)}) collective-permute-start(f32[64,2304]{1,0:T(8,128)S(1)} %pad_maximum_fusion.1), channel_id=1, source_target_pairs={{0,3},{1,0},{2,1},{3,2},{4,7},{5,4},{6,5},{7,6},{8,11},{9,8},{10,9... | collective-permute-start | bytes 1769480 | tf_op jit(solution)/shard_map/ppermute | solution.py:28
  (26 other events, 286.3 us)

commit v6 on v4

--- a/solution.py
+++ b/solution.py
@@ -408,15 +408,12 @@
     late_high = send_outer((three_high + far_high.astype(F32)).astype(BF16), -1)
     low = own[:128] + early_low.astype(F32) + late_low.astype(F32)
     high = own[128:] + early_high.astype(F32) + late_high.astype(F32)
-    halves = []
-    for columns in (slice(0, features // 2), slice(features // 2, features)):
-        here, one = low[:64, columns], low[64:, columns]
-        two, three = high[:64, columns], high[64:, columns]
-        far_low, far_high = send_inner(two[:32], 1), send_inner(two[32:], -1)
-        one = jnp.concatenate([one[:32] + far_low, one[32:]], 0)
-        three = jnp.concatenate([three[:32], three[32:] + far_high], 0)
-        halves.append(here + send_inner(one, 1) + send_inner(three, -1))
-    branch = jnp.concatenate(halves, 1)
+    here, one, two, three = low[:64], low[64:], high[:64], high[64:]
+    two = two.astype(BF16)
+    far_low, far_high = send_inner(two[:32], 1), send_inner(two[32:], -1)
+    one = jnp.concatenate([one[:32] + far_low.astype(F32), one[32:]], 0)
+    three = jnp.concatenate([three[:32], three[32:] + far_high.astype(F32)], 0)
+    branch = here + send_inner(one, 1) + send_inner(three, -1)
     mixed = (raw.astype(F32) + branch).astype(BF16).reshape(tokens.shape)
     return (mixed, new_keyval.reshape(seqs, 2, 2 * HEAD))
 

time: 180 us -> 179 us (level)
  starting transfers between devices: 56.1 us -> 52.4 us
  waiting for transfers between devices: 72.9 us -> 75.5 us
    ppermute x38 -> x34, starting transfers between devices: 54 us -> 50.2 us  [shift(): return lax.ppermute(value, ('gx', 'yz'), pairs)]
    ppermute x38 -> x34, waiting for transfers between devices: 71.3 us -> 73.9 us  [shift(): return lax.ppermute(value, ('gx', 'yz'), pairs)]
  transfers between devices with their start and end apart: 47 -> 43, of which waited for: 26 -> 22; matrix products, arithmetic and copies ran while one was open for 2% -> 1% of each run, Pallas kernels for 5% -> 5%
where the time goes in v6:
time: 179 us
  waiting for transfers between devices  75.5 us (42%)
  starting transfers between devices  52.4 us (29%)
  blocking collectives  25.5 us (14%)
  Pallas kernels  18.4 us (10%)
  local copies, waits for them, and re-layouts  3.59 us (2%)
  other arithmetic  2.43 us (1%)
    ppermute x34, waiting for transfers between devices, shift(): return lax.ppermute(value, ('gx', 'yz'), pairs)  73.9 us
    ppermute x34, starting transfers between devices, shift(): return lax.ppermute(value, ('gx', 'yz'), pairs)  50.2 us
    all_to_all x1, blocking collectives, body(): query = lax.all_to_all(query, 'yz', split_axis=0, concat_axis=0)  13.9 us
    all_to_all x1, blocking collectives, body(): lax.all_to_all(heads_out.reshape(16, 8, columns), 'yz', split_axis=0, con...  11.6 us
    pallas_call x2, Pallas kernels, project_query(): pl.pallas_call(functools.partial(query_kernel, pair), out_shape=[half, ha...  6.35 us
    pallas_call x2, Pallas kernels, project_output(): pl.pallas_call(functools.partial(output_kernel, groups), out_shape=shapes...  5.86 us
    pallas_call x1, Pallas kernels, attend(): pl.pallas_call(attend_kernel, out_shape=[jax.ShapeDtypeStruct((rows, colu...  4.36 us
  transfers between devices with their start and end apart: 43, of which 22 were waited for; matrix products, arithmetic and copies ran while one was open for 1% of the time, Pallas kernels for 5%

profile of v6, /device:TPU:0, one launch (start us, length us, event | category | flops | bytes accessed | tf_op | source)
XLA Modules:
  0.0 178.8 jit_solution(5378941887307564238)
XLA Ops:
  3.3 4.1 %collective-permute-start.5 = (bf16[64,2304]{1,0:T(8,128)(2,1)S(1)}, bf16[64,2304]{1,0:T(8,128)(2,1)S(1)}, u32[]{:S(2)}, u32[]{:S(2)}) collective-permute-start(bf16[64,2304]{1,0:T(8,128)(2,1)S(1)} %reshape.66.rows_ref.one_ref), channel_id=1, source_target_pairs={{0,3},{1,0},{2,1},{3,2},{4,7},{5,4},{6,5},{7,6},{8,11},{9,8},{10,9... | collective-permute-start | bytes 884744 | tf_op jit(solution)/shard_map/ppermute | solution.py:28
  11.9 3.7 %collective-permute-done.2 = f32[64,2]{1,0:T(8,128)S(1)} collective-permute-done((f32[64,2]{1,0:T(8,128)S(1)}, f32[64,2]{1,0:T(8,128)S(1)}, u32[]{:S(2)}, u32[]{:S(2)}) %collective-permute-start.2) | collective-permute-done | bytes 544 | tf_op jit(solution)/shard_map/ppermute | solution.py:28
  16.3 5.1 %collective-permute-done.6.two_sums = f32[64,2]{1,0:T(8,128)S(1)} collective-permute-done((f32[64,2]{1,0:T(8,128)S(1)}, f32[64,2]{1,0:T(8,128)S(1)}, u32[]{:S(2)}, u32[]{:S(2)}) %collective-permute-start.6) | collective-permute-done | bytes 544 | tf_op jit(solution)/shard_map/ppermute | solution.py:28
  25.9 3.7 %collective-permute-start.11 = (f32[64,2]{1,0:T(8,128)S(1)}, f32[64,2]{1,0:T(8,128)S(1)}, u32[]{:S(2)}, u32[]{:S(2)}) collective-permute-start(f32[64,2]{1,0:T(8,128)S(1)} %add_add_fusion.one_sums), channel_id=1, source_target_pairs={{0,2},{1,3},{2,0},{3,1},{4,6},{5,7},{6,4},{7,5},{8,10},{9,11},{10,... | collective-permute-start | bytes 1544 | tf_op jit(solution)/shard_map/ppermute | solution.py:28
  30.4 3.7 %collective-permute-done.11.two_sums = f32[64,2]{1,0:T(8,128)S(1)} collective-permute-done((f32[64,2]{1,0:T(8,128)S(1)}, f32[64,2]{1,0:T(8,128)S(1)}, u32[]{:S(2)}, u32[]{:S(2)}) %collective-permute-start.11) | collective-permute-done | bytes 544 | tf_op jit(solution)/shard_map/ppermute | solution.py:28
  36.2 3.2 %collective-permute-start.15 = (bf16[128,2304]{1,0:T(8,128)(2,1)S(1)}, bf16[128,2304]{1,0:T(8,128)(2,1)S(1)}, u32[]{:S(2)}, u32[]{:S(2)}) collective-permute-start(bf16[128,2304]{1,0:T(8,128)(2,1)S(1)} %normalize.3.refs_4_), channel_id=1, source_target_pairs={{0,12},{1,13},{2,14},{3,15},{4,0},{5,1},{6,2},{7,3},{8,4},{9,5},{1... | collective-permute-start | bytes 1769480 | tf_op jit(solution)/shard_map/ppermute | solution.py:28
  39.4 7.9 %collective-permute-done.13.refs_3_ = bf16[128,2304]{1,0:T(8,128)(2,1)S(1)} collective-permute-done((bf16[128,2304]{1,0:T(8,128)(2,1)S(1)}, bf16[128,2304]{1,0:T(8,128)(2,1)S(1)}, u32[]{:S(2)}, u32[]{:S(2)}) %collective-permute-start.13) | collective-permute-done | bytes 589856 | tf_op jit(solution)/shard_map/ppermute | solution.py:28
  47.3 3.2 %collective-permute-start.16 = (bf16[128,2304]{1,0:T(8,128)(2,1)S(1)}, bf16[128,2304]{1,0:T(8,128)(2,1)S(1)}, u32[]{:S(2)}, u32[]{:S(2)}) collective-permute-start(bf16[128,2304]{1,0:T(8,128)(2,1)S(1)} %collective-permute-done.15.refs_6_), channel_id=1, source_target_pairs={{0,12},{1,13},{2,14},{3,15},{4,0},{5,1},{6,2},{7,3},{8,4},{9,5},{1... | collective-permute-start | bytes 1769480 | tf_op jit(solution)/shard_map/ppermute | solution.py:28
  55.5 3.5 %collective-permute-done.18 = f32[8,512]{1,0:T(8,128)S(1)} collective-permute-done((f32[8,512]{1,0:T(8,128)S(1)}, f32[8,512]{1,0:T(8,128)S(1)}, u32[]{:S(2)}, u32[]{:S(2)}) %collective-permute-start.18) | collective-permute-done | bytes 16416 | tf_op jit(solution)/shard_map/ppermute | solution.py:28
  62.2 3.3 %query_projection.2 = (f32[256,768]{1,0:T(8,128)S(1)}, f32[256,768]{1,0:T(8,128)S(1)}) custom-call(s32[4]{0:T(128)S(1)} %pad_add_fusion.place, bf16[128,2304]{1,0:T(8,128)(2,1)S(1)} %normalize.2.rows_ref.refs_0_, bf16[128,2304]{1,0:T(8,128)(2,1)S(1)} %collective-permute-done.7.refs_1_, bf16[128,2304]{1,0:T(8,128)(2,1)S(1)} %collective-permute-done.8.refs_2_, ...), custom_call_target="tpu_custom_call" | custom-call | flops 1811939328 | bytes 8388608 | tf_op jit(solution)/shard_map/query_projection/pallas_call | solution.py:159
  67.2 4.3 %collective-permute-start.25 = (f32[128,768]{1,0:T(8,128)S(1)}, f32[128,768]{1,0:T(8,128)S(1)}, u32[]{:S(2)}, u32[]{:S(2)}) collective-permute-start(f32[128,768]{1,0:T(8,128)S(1)} %get-tuple-element.98), channel_id=1, source_target_pairs={{0,96},{1,97},{2,98},{3,99},{4,100},{5,101},{6,102},{7,103},{8,104... | collective-permute-start | bytes 1179656 | tf_op jit(solution)/shard_map/ppermute | solution.py:28
  71.6 6.1 %collective-permute-done.22 = f32[128,768]{1,0:T(8,128)S(1)} collective-permute-done((f32[128,768]{1,0:T(8,128)S(1)}, f32[128,768]{1,0:T(8,128)S(1)}, u32[]{:S(2)}, u32[]{:S(2)}) %collective-permute-start.22) | collective-permute-done | bytes 393248 | tf_op jit(solution)/shard_map/ppermute | solution.py:28
  77.8 9.0 %collective-permute-done.24 = f32[128,768]{1,0:T(8,128)S(1)} collective-permute-done((f32[128,768]{1,0:T(8,128)S(1)}, f32[128,768]{1,0:T(8,128)S(1)}, u32[]{:S(2)}, u32[]{:S(2)}) %collective-permute-start.24) | collective-permute-done | bytes 393248 | tf_op jit(solution)/shard_map/ppermute | solution.py:28
  86.9 13.9 %all_to_all.10 = bf16[16,8,768]{2,1,0:T(8,128)(2,1)S(1)} all-to-all(bf16[16,8,768]{2,1,0:T(8,128)(2,1)S(1)} %fusion.5), channel_id=1, replica_groups=mesh['gx'=8,'yz'=16] {'yz'}, dimensions={0} | all-to-all | bytes 393216 | tf_op jit(solution)/shard_map/all_to_all | solution.py:387
  100.8 4.4 %attention.1 = (bf16[128,768]{1,0:T(8,128)(2,1)S(1)}, bf16[8,512]{1,0:T(8,128)(2,1)S(1)}) custom-call(s32[4]{0:T(128)S(1)} %copy-done.5, bf16[128,768]{1,0:T(8,128)(2,1)S(1)} %bitcast.14, f32[8,128]{1,0:T(8,128)S(1)} %get-tuple-element.76.cos_ref, f32[8,128]{1,0:T(8,128)S(1)} %get-tuple-element.77.sin_ref, ...), custom_call_target="tpu_custom_call" | custom-call | flops 805306368 | bytes 8388608 | tf_op jit(solution)/shard_map/attention/pallas_call | solution.py:256
  105.2 11.6 %all_to_all.11 = bf16[16,8,768]{2,1,0:T(8,128)(2,1)S(1)} all-to-all(bf16[16,8,768]{2,1,0:T(8,128)(2,1)S(1)} %bitcast.15), channel_id=1, replica_groups=mesh['gx'=8,'yz'=16] {'yz'}, dimensions={0} | all-to-all | bytes 393216 | tf_op jit(solution)/shard_map/all_to_all | solution.py:392
  120.0 3.6 %collective-permute-done.26.refs_1_ = bf16[128,768]{1,0:T(8,128)(2,1)S(1)} collective-permute-done((bf16[128,768]{1,0:T(8,128)(2,1)S(1)}, bf16[128,768]{1,0:T(8,128)(2,1)S(1)}, u32[]{:S(2)}, u32[]{:S(2)}) %collective-permute-start.26) | collective-permute-done | bytes 196640 | tf_op jit(solution)/shard_map/ppermute | solution.py:28
  125.2 5.3 %collective-permute-done.28.refs_3_ = bf16[128,768]{1,0:T(8,128)(2,1)S(1)} collective-permute-done((bf16[128,768]{1,0:T(8,128)(2,1)S(1)}, bf16[128,768]{1,0:T(8,128)(2,1)S(1)}, u32[]{:S(2)}, u32[]{:S(2)}) %collective-permute-start.28) | collective-permute-done | bytes 196640 | tf_op jit(solution)/shard_map/ppermute | solution.py:28
  137.1 4.1 %output_projection.2 = (f32[128,2304]{1,0:T(8,128)S(1)}, bf16[128,2304]{1,0:T(8,128)(2,1)S(1)}, bf16[128,2304]{1,0:T(8,128)(2,1)S(1)}, f32[128,2304]{1,0:T(8,128)S(1)}, f32[256,2304]{1,0:T(8,128)S(1)}) custom-call(s32[4]{0:T(128)S(1)} %pad_add_fusion.place, bf16[128,768]{1,0:T(8,128)(2,1)S(1)} %bitcast.13, ...), custom_call_target="tpu_custom_call" | custom-call | flops 2717908992 | bytes 8388608 | tf_op jit(solution)/shard_map/output_projection/pallas_call | solution.py:316
  145.3 3.2 %collective-permute-start.38 = (bf16[128,2304]{1,0:T(8,128)(2,1)S(1)}, bf16[128,2304]{1,0:T(8,128)(2,1)S(1)}, u32[]{:S(2)}, u32[]{:S(2)}) collective-permute-start(bf16[128,2304]{1,0:T(8,128)(2,1)S(1)} %add_convert_fusion), channel_id=1, source_target_pairs={{0,12},{1,13},{2,14},{3,15},{4,0},{5,1},{6,2},{7,3},{8,4},{9,5},{1... | collective-permute-start | bytes 1769480 | tf_op jit(solution)/shard_map/ppermute | solution.py:28
  152.4 6.3 %collective-permute-done.36 = bf16[128,2304]{1,0:T(8,128)(2,1)S(1)} collective-permute-done((bf16[128,2304]{1,0:T(8,128)(2,1)S(1)}, bf16[128,2304]{1,0:T(8,128)(2,1)S(1)}, u32[]{:S(2)}, u32[]{:S(2)}) %collective-permute-start.36) | collective-permute-done | bytes 589856 | tf_op jit(solution)/shard_map/ppermute | solution.py:28
  162.4 3.1 %collective-permute-done.39 = bf16[32,2304]{1,0:T(8,128)(2,1)S(1)} collective-permute-done((bf16[32,2304]{1,0:T(8,128)(2,1)S(1)}, bf16[32,2304]{1,0:T(8,128)(2,1)S(1)}, u32[]{:S(2)}, u32[]{:S(2)}) %collective-permute-start.39) | collective-permute-done | bytes 147488 | tf_op jit(solution)/shard_map/ppermute | solution.py:28
  165.8 3.3 %collective-permute-start.42 = (f32[64,2304]{1,0:T(8,128)S(1)}, f32[64,2304]{1,0:T(8,128)}, u32[]{:S(2)}, u32[]{:S(2)}) collective-permute-start(f32[64,2304]{1,0:T(8,128)S(1)} %pad_maximum_fusion.1), channel_id=1, source_target_pairs={{0,3},{1,0},{2,1},{3,2},{4,7},{5,4},{6,5},{7,6},{8,11},{9,8},{10,9... | collective-permute-start | bytes 1769480 | tf_op jit(solution)/shard_map/ppermute | solution.py:28
  169.7 7.1 %collective-permute-done.40 = f32[64,2304]{1,0:T(8,128)S(1)} collective-permute-done((f32[64,2304]{1,0:T(8,128)S(1)}, f32[64,2304]{1,0:T(8,128)S(1)}, u32[]{:S(2)}, u32[]{:S(2)}) %collective-permute-start.40) | collective-permute-done | bytes 589856 | tf_op jit(solution)/shard_map/ppermute | solution.py:28
  (116 shorter events, 51.1 us)
Async XLA Ops:
  3.3 12.8 %collective-permute-start.5 = (bf16[64,2304]{1,0:T(8,128)(2,1)S(1)}, bf16[64,2304]{1,0:T(8,128)(2,1)S(1)}, u32[]{:S(2)}, u32[]{:S(2)}) collective-permute-start(bf16[64,2304]{1,0:T(8,128)(2,1)S(1)} %reshape.66.rows_ref.one_ref), channel_id=1, source_target_pairs={{0,3},{1,0},{2,1},{3,2},{4,7},{5,4},{6,5},{7,6},{8,11},{9,8},{10,9... | collective-permute-start | bytes 884744 | tf_op jit(solution)/shard_map/ppermute | solution.py:28
  7.4 8.7 %collective-permute-start.4 = (bf16[64,2304]{1,0:T(8,128)(2,1)S(1)}, bf16[64,2304]{1,0:T(8,128)(2,1)S(1)}, u32[]{:S(2)}, u32[]{:S(2)}) collective-permute-start(bf16[64,2304]{1,0:T(8,128)(2,1)S(1)} %reshape.66.rows_ref.one_ref), channel_id=1, source_target_pairs={{0,1},{1,2},{2,3},{3,0},{4,5},{5,6},{6,7},{7,4},{8,9},{9,10},{10,1... | collective-permute-start | bytes 884744 | tf_op jit(solution)/shard_map/ppermute | solution.py:28
  21.7 13.7 %collective-permute-start.8 = (bf16[128,2304]{1,0:T(8,128)(2,1)S(1)}, bf16[128,2304]{1,0:T(8,128)(2,1)S(1)}, u32[]{:S(2)}, u32[]{:S(2)}) collective-permute-start(bf16[128,2304]{1,0:T(8,128)(2,1)S(1)} %normalize.2.rows_ref.refs_0_), channel_id=1, source_target_pairs={{0,12},{1,13},{2,14},{3,15},{4,0},{5,1},{6,2},{7,3},{8,4},{9,5},{1... | collective-permute-start | bytes 1769480 | tf_op jit(solution)/shard_map/ppermute | solution.py:28
  24.7 11.4 %collective-permute-start.7 = (bf16[128,2304]{1,0:T(8,128)(2,1)S(1)}, bf16[128,2304]{1,0:T(8,128)(2,1)S(1)}, u32[]{:S(2)}, u32[]{:S(2)}) collective-permute-start(bf16[128,2304]{1,0:T(8,128)(2,1)S(1)} %normalize.2.rows_ref.refs_0_), channel_id=1, source_target_pairs={{0,4},{1,5},{2,6},{3,7},{4,8},{5,9},{6,10},{7,11},{8,12},{9,13},{1... | collective-permute-start | bytes 1769480 | tf_op jit(solution)/shard_map/ppermute | solution.py:28
  24.7 10.3 %collective-permute-start.9 = (bf16[64,2304]{1,0:T(8,128)(2,1)S(1)}, bf16[64,2304]{1,0:T(8,128)(2,1)S(1)}, u32[]{:S(2)}, u32[]{:S(2)}) collective-permute-start(bf16[64,2304]{1,0:T(8,128)(2,1)S(1)} %collective-permute-done.4.two_ref), channel_id=1, source_target_pairs={{0,1},{1,2},{2,3},{3,0},{4,5},{5,6},{6,7},{7,4},{8,9},{9,10},{10,1... | collective-permute-start | bytes 884744 | tf_op jit(solution)/shard_map/ppermute | solution.py:28
  25.9 8.2 %collective-permute-start.11 = (f32[64,2]{1,0:T(8,128)S(1)}, f32[64,2]{1,0:T(8,128)S(1)}, u32[]{:S(2)}, u32[]{:S(2)}) collective-permute-start(f32[64,2]{1,0:T(8,128)S(1)} %add_add_fusion.one_sums), channel_id=1, source_target_pairs={{0,2},{1,3},{2,0},{3,1},{4,6},{5,7},{6,4},{7,5},{8,10},{9,11},{10,... | collective-permute-start | bytes 1544 | tf_op jit(solution)/shard_map/ppermute | solution.py:28
  36.2 11.1 %collective-permute-start.13 = (bf16[128,2304]{1,0:T(8,128)(2,1)S(1)}, bf16[128,2304]{1,0:T(8,128)(2,1)S(1)}, u32[]{:S(2)}, u32[]{:S(2)}) collective-permute-start(bf16[128,2304]{1,0:T(8,128)(2,1)S(1)} %collective-permute-done.7.refs_1_), channel_id=1, source_target_pairs={{0,4},{1,5},{2,6},{3,7},{4,8},{5,9},{6,10},{7,11},{8,12},{9,13},{1... | collective-permute-start | bytes 1769480 | tf_op jit(solution)/shard_map/ppermute | solution.py:28
  36.2 11.1 %collective-permute-start.15 = (bf16[128,2304]{1,0:T(8,128)(2,1)S(1)}, bf16[128,2304]{1,0:T(8,128)(2,1)S(1)}, u32[]{:S(2)}, u32[]{:S(2)}) collective-permute-start(bf16[128,2304]{1,0:T(8,128)(2,1)S(1)} %normalize.3.refs_4_), channel_id=1, source_target_pairs={{0,12},{1,13},{2,14},{3,15},{4,0},{5,1},{6,2},{7,3},{8,4},{9,5},{1... | collective-permute-start | bytes 1769480 | tf_op jit(solution)/shard_map/ppermute | solution.py:28
  47.3 11.7 %collective-permute-start.14 = (bf16[128,2304]{1,0:T(8,128)(2,1)S(1)}, bf16[128,2304]{1,0:T(8,128)(2,1)S(1)}, u32[]{:S(2)}, u32[]{:S(2)}) collective-permute-start(bf16[128,2304]{1,0:T(8,128)(2,1)S(1)} %normalize.3.refs_4_), channel_id=1, source_target_pairs={{0,4},{1,5},{2,6},{3,7},{4,8},{5,9},{6,10},{7,11},{8,12},{9,13},{1... | collective-permute-start | bytes 1769480 | tf_op jit(solution)/shard_map/ppermute | solution.py:28
  47.3 11.7 %collective-permute-start.16 = (bf16[128,2304]{1,0:T(8,128)(2,1)S(1)}, bf16[128,2304]{1,0:T(8,128)(2,1)S(1)}, u32[]{:S(2)}, u32[]{:S(2)}) collective-permute-start(bf16[128,2304]{1,0:T(8,128)(2,1)S(1)} %collective-permute-done.15.refs_6_), channel_id=1, source_target_pairs={{0,12},{1,13},{2,14},{3,15},{4,0},{5,1},{6,2},{7,3},{8,4},{9,5},{1... | collective-permute-start | bytes 1769480 | tf_op jit(solution)/shard_map/ppermute | solution.py:28
  66.2 11.4 %collective-permute-start.22 = (f32[128,768]{1,0:T(8,128)S(1)}, f32[128,768]{1,0:T(8,128)S(1)}, u32[]{:S(2)}, u32[]{:S(2)}) collective-permute-start(f32[128,768]{1,0:T(8,128)S(1)} %get-tuple-element.97), channel_id=1, source_target_pairs={{0,32},{1,33},{2,34},{3,35},{4,36},{5,37},{6,38},{7,39},{8,40},{9,... | collective-permute-start | bytes 1179656 | tf_op jit(solution)/shard_map/ppermute | solution.py:28
  67.2 10.6 %collective-permute-start.25 = (f32[128,768]{1,0:T(8,128)S(1)}, f32[128,768]{1,0:T(8,128)S(1)}, u32[]{:S(2)}, u32[]{:S(2)}) collective-permute-start(f32[128,768]{1,0:T(8,128)S(1)} %get-tuple-element.98), channel_id=1, source_target_pairs={{0,96},{1,97},{2,98},{3,99},{4,100},{5,101},{6,102},{7,103},{8,104... | collective-permute-start | bytes 1179656 | tf_op jit(solution)/shard_map/ppermute | solution.py:28
  77.8 9.1 %collective-permute-start.24 = (f32[128,768]{1,0:T(8,128)S(1)}, f32[128,768]{1,0:T(8,128)S(1)}, u32[]{:S(2)}, u32[]{:S(2)}) collective-permute-start(f32[128,768]{1,0:T(8,128)S(1)} %slice_add_fusion.1), channel_id=1, source_target_pairs={{0,32},{1,33},{2,34},{3,35},{4,36},{5,37},{6,38},{7,39},{8,40},{9,... | collective-permute-start | bytes 1179656 | tf_op jit(solution)/shard_map/ppermute | solution.py:28
  117.7 7.5 %collective-permute-start.27 = (bf16[128,768]{1,0:T(8,128)(2,1)S(1)}, bf16[128,768]{1,0:T(8,128)(2,1)S(1)}, u32[]{:S(2)}, u32[]{:S(2)}) collective-permute-start(bf16[128,768]{1,0:T(8,128)(2,1)S(1)} %bitcast.10), channel_id=1, source_target_pairs={{0,96},{1,97},{2,98},{3,99},{4,100},{5,101},{6,102},{7,103},{8,104... | collective-permute-start | bytes 589832 | tf_op jit(solution)/shard_map/ppermute | solution.py:28
  123.6 6.9 %collective-permute-start.29 = (bf16[128,768]{1,0:T(8,128)(2,1)S(1)}, bf16[128,768]{1,0:T(8,128)(2,1)S(1)}, u32[]{:S(2)}, u32[]{:S(2)}) collective-permute-start(bf16[128,768]{1,0:T(8,128)(2,1)S(1)} %bitcast.11), channel_id=1, source_target_pairs={{0,16},{16,0},{32,48},{48,32},{64,80},{80,64},{96,112},{112,96},{1... | collective-permute-start | bytes 589832 | tf_op jit(solution)/shard_map/ppermute | solution.py:33
  123.6 6.9 %collective-permute-start.30 = (bf16[128,768]{1,0:T(8,128)(2,1)S(1)}, bf16[128,768]{1,0:T(8,128)(2,1)S(1)}, u32[]{:S(2)}, u32[]{:S(2)}) collective-permute-start(bf16[128,768]{1,0:T(8,128)(2,1)S(1)} %collective-permute-done.26.refs_1_), channel_id=1, source_target_pairs={{0,16},{16,0},{32,48},{48,32},{64,80},{80,64},{96,112},{112,96},{1... | collective-permute-start | bytes 589832 | tf_op jit(solution)/shard_map/ppermute | solution.py:33
  133.7 11.2 %collective-permute-start.34 = (bf16[128,2304]{1,0:T(8,128)(2,1)S(1)}, bf16[128,2304]{1,0:T(8,128)(2,1)S(1)}, u32[]{:S(2)}, u32[]{:S(2)}) collective-permute-start(bf16[128,2304]{1,0:T(8,128)(2,1)S(1)} %get-tuple-element.83), channel_id=1, source_target_pairs={{0,4},{1,5},{2,6},{3,7},{4,8},{5,9},{6,10},{7,11},{8,12},{9,13},{1... | collective-permute-start | bytes 1769480 | tf_op jit(solution)/shard_map/ppermute | solution.py:28
  134.3 10.7 %collective-permute-start.35 = (bf16[128,2304]{1,0:T(8,128)(2,1)S(1)}, bf16[128,2304]{1,0:T(8,128)(2,1)S(1)}, u32[]{:S(2)}, u32[]{:S(2)}) collective-permute-start(bf16[128,2304]{1,0:T(8,128)(2,1)S(1)} %get-tuple-element.84), channel_id=1, source_target_pairs={{0,12},{1,13},{2,14},{3,15},{4,0},{5,1},{6,2},{7,3},{8,4},{9,5},{1... | collective-permute-start | bytes 1769480 | tf_op jit(solution)/shard_map/ppermute | solution.py:28
  141.1 10.0 %collective-permute-start.33 = (bf16[128,2304]{1,0:T(8,128)(2,1)S(1)}, bf16[128,2304]{1,0:T(8,128)(2,1)S(1)}, u32[]{:S(2)}, u32[]{:S(2)}) collective-permute-start(bf16[128,2304]{1,0:T(8,128)(2,1)S(1)} %get-tuple-element.81), channel_id=1, source_target_pairs={{0,12},{1,13},{2,14},{3,15},{4,0},{5,1},{6,2},{7,3},{8,4},{9,5},{1... | collective-permute-start | bytes 1769480 | tf_op jit(solution)/shard_map/ppermute | solution.py:28
  141.2 11.2 %collective-permute-start.37 = (bf16[128,2304]{1,0:T(8,128)(2,1)S(1)}, bf16[128,2304]{1,0:T(8,128)(2,1)S(1)}, u32[]{:S(2)}, u32[]{:S(2)}) collective-permute-start(bf16[128,2304]{1,0:T(8,128)(2,1)S(1)} %get-tuple-element.86), channel_id=1, source_target_pairs={{0,4},{1,5},{2,6},{3,7},{4,8},{5,9},{6,10},{7,11},{8,12},{9,13},{1... | collective-permute-start | bytes 1769480 | tf_op jit(solution)/shard_map/ppermute | solution.py:28
  145.0 13.7 %collective-permute-start.36 = (bf16[128,2304]{1,0:T(8,128)(2,1)S(1)}, bf16[128,2304]{1,0:T(8,128)(2,1)S(1)}, u32[]{:S(2)}, u32[]{:S(2)}) collective-permute-start(bf16[128,2304]{1,0:T(8,128)(2,1)S(1)} %add_convert_fusion.1), channel_id=1, source_target_pairs={{0,4},{1,5},{2,6},{3,7},{4,8},{5,9},{6,10},{7,11},{8,12},{9,13},{1... | collective-permute-start | bytes 1769480 | tf_op jit(solution)/shard_map/ppermute | solution.py:28
  145.3 13.4 %collective-permute-start.38 = (bf16[128,2304]{1,0:T(8,128)(2,1)S(1)}, bf16[128,2304]{1,0:T(8,128)(2,1)S(1)}, u32[]{:S(2)}, u32[]{:S(2)}) collective-permute-start(bf16[128,2304]{1,0:T(8,128)(2,1)S(1)} %add_convert_fusion), channel_id=1, source_target_pairs={{0,12},{1,13},{2,14},{3,15},{4,0},{5,1},{6,2},{7,3},{8,4},{9,5},{1... | collective-permute-start | bytes 1769480 | tf_op jit(solution)/shard_map/ppermute | solution.py:28
  165.6 11.2 %collective-permute-start.40 = (f32[64,2304]{1,0:T(8,128)S(1)}, f32[64,2304]{1,0:T(8,128)S(1)}, u32[]{:S(2)}, u32[]{:S(2)}) collective-permute-start(f32[64,2304]{1,0:T(8,128)S(1)} %pad_maximum_fusion), channel_id=1, source_target_pairs={{0,1},{1,2},{2,3},{3,0},{4,5},{5,6},{6,7},{7,4},{8,9},{9,10},{10,1... | collective-permute-start | bytes 1769480 | tf_op jit(solution)/shard_map/ppermute | solution.py:28
  165.8 11.0 %collective-permute-start.42 = (f32[64,2304]{1,0:T(8,128)S(1)}, f32[64,2304]{1,0:T(8,128)}, u32[]{:S(2)}, u32[]{:S(2)}) collective-permute-start(f32[64,2304]{1,0:T(8,128)S(1)} %pad_maximum_fusion.1), channel_id=1, source_target_pairs={{0,3},{1,0},{2,1},{3,2},{4,7},{5,4},{6,5},{7,6},{8,11},{9,8},{10,9... | collective-permute-start | bytes 1769480 | tf_op jit(solution)/shard_map/ppermute | solution.py:28
  (26 other events, 284.4 us)

commit v7 on v6

--- a/solution.py
+++ b/solution.py
@@ -342,9 +342,10 @@
     sums = row_sums(raw)
     sums = sums + send_core(sums)
     sums, cosine, sine, place, raw = lax.optimization_barrier((sums, cosine, sine, place, raw))
-    before, after = send_inner(raw, 1), send_inner(raw, -1)
+    before = send_inner(raw, 1)
     sums = sums + send_x(sums, 1) + send_x(sums, 2) + send_x(sums, 3)
-    sums, before, after = lax.optimization_barrier((sums, before, after))
+    sums, before, raw = lax.optimization_barrier((sums, before, raw))
+    after = send_inner(raw, -1)
     before_sums, after_sums = send_inner(sums, 1), send_inner(sums, -1)
     before, before_sums = lax.optimization_barrier((before, before_sums))
     far, far_sums = send_inner(before, 1), send_inner(sums, 2)

time: 179 us -> 180 us (level)
  transfers between devices with their start and end apart: 43 -> 43, of which waited for: 22 -> 23; matrix products, arithmetic and copies ran while one was open for 1% -> 1% of each run, Pallas kernels for 5% -> 5%
where the time goes in v7:
time: 180 us
  waiting for transfers between devices  77 us (43%)
  starting transfers between devices  52.7 us (29%)
  blocking collectives  25.1 us (14%)
  Pallas kernels  18.4 us (10%)
  local copies, waits for them, and re-layouts  3.59 us (2%)
  other arithmetic  2.43 us (1%)
    ppermute x34, waiting for transfers between devices, shift(): return lax.ppermute(value, ('gx', 'yz'), pairs)  74.2 us
    ppermute x34, starting transfers between devices, shift(): return lax.ppermute(value, ('gx', 'yz'), pairs)  50.6 us
    all_to_all x1, blocking collectives, body(): query = lax.all_to_all(query, 'yz', split_axis=0, concat_axis=0)  13.5 us
    all_to_all x1, blocking collectives, body(): lax.all_to_all(heads_out.reshape(16, 8, columns), 'yz', split_axis=0, con...  11.6 us
    pallas_call x2, Pallas kernels, project_query(): pl.pallas_call(functools.partial(query_kernel, pair), out_shape=[half, ha...  6.35 us
    pallas_call x2, Pallas kernels, project_output(): pl.pallas_call(functools.partial(output_kernel, groups), out_shape=shapes...  5.86 us
    pallas_call x1, Pallas kernels, attend(): pl.pallas_call(attend_kernel, out_shape=[jax.ShapeDtypeStruct((rows, colu...  4.36 us
  transfers between devices with their start and end apart: 43, of which 23 were waited for; matrix products, arithmetic and copies ran while one was open for 1% of the time, Pallas kernels for 5%

profile of v7, /device:TPU:0, one launch (start us, length us, event | category | flops | bytes accessed | tf_op | source)
XLA Modules:
  0.0 180.1 jit_solution(2427865318896048067)
XLA Ops:
  9.8 3.7 %collective-permute-done.2 = f32[64,2]{1,0:T(8,128)S(1)} collective-permute-done((f32[64,2]{1,0:T(8,128)S(1)}, f32[64,2]{1,0:T(8,128)S(1)}, u32[]{:S(2)}, u32[]{:S(2)}) %collective-permute-start.2) | collective-permute-done | bytes 544 | tf_op jit(solution)/shard_map/ppermute | solution.py:28
  16.0 3.2 %collective-permute-done.5.two_sums = f32[64,2]{1,0:T(8,128)S(1)} collective-permute-done((f32[64,2]{1,0:T(8,128)S(1)}, f32[64,2]{1,0:T(8,128)S(1)}, u32[]{:S(2)}, u32[]{:S(2)}) %collective-permute-start.5) | collective-permute-done | bytes 544 | tf_op jit(solution)/shard_map/ppermute | solution.py:28
  19.5 3.1 %collective-permute-start.7 = (bf16[128,2304]{1,0:T(8,128)(2,1)S(1)}, bf16[128,2304]{1,0:T(8,128)(2,1)S(1)}, u32[]{:S(2)}, u32[]{:S(2)}) collective-permute-start(bf16[128,2304]{1,0:T(8,128)(2,1)S(1)} %normalize.2.rows_ref.refs_0_), channel_id=1, source_target_pairs={{0,12},{1,13},{2,14},{3,15},{4,0},{5,1},{6,2},{7,3},{8,4},{9,5},{1... | collective-permute-start | bytes 1769480 | tf_op jit(solution)/shard_map/ppermute | solution.py:28
  28.4 4.1 %collective-permute-done.11.two_sums = f32[64,2]{1,0:T(8,128)S(1)} collective-permute-done((f32[64,2]{1,0:T(8,128)S(1)}, f32[64,2]{1,0:T(8,128)S(1)}, u32[]{:S(2)}, u32[]{:S(2)}) %collective-permute-start.11) | collective-permute-done | bytes 544 | tf_op jit(solution)/shard_map/ppermute | solution.py:28
  34.5 3.2 %collective-permute-done.10.one_sums = f32[64,2]{1,0:T(8,128)S(1)} collective-permute-done((f32[64,2]{1,0:T(8,128)S(1)}, f32[64,2]{1,0:T(8,128)S(1)}, u32[]{:S(2)}, u32[]{:S(2)}) %collective-permute-start.10) | collective-permute-done | bytes 544 | tf_op jit(solution)/shard_map/ppermute | solution.py:28
  41.3 7.9 %collective-permute-done.13.refs_3_ = bf16[128,2304]{1,0:T(8,128)(2,1)S(1)} collective-permute-done((bf16[128,2304]{1,0:T(8,128)(2,1)S(1)}, bf16[128,2304]{1,0:T(8,128)(2,1)S(1)}, u32[]{:S(2)}, u32[]{:S(2)}) %collective-permute-start.13) | collective-permute-done | bytes 589856 | tf_op jit(solution)/shard_map/ppermute | solution.py:28
  49.1 3.2 %collective-permute-start.16 = (bf16[128,2304]{1,0:T(8,128)(2,1)S(1)}, bf16[128,2304]{1,0:T(8,128)(2,1)S(1)}, u32[]{:S(2)}, u32[]{:S(2)}) collective-permute-start(bf16[128,2304]{1,0:T(8,128)(2,1)S(1)} %collective-permute-done.15.refs_6_), channel_id=1, source_target_pairs={{0,12},{1,13},{2,14},{3,15},{4,0},{5,1},{6,2},{7,3},{8,4},{9,5},{1... | collective-permute-start | bytes 1769480 | tf_op jit(solution)/shard_map/ppermute | solution.py:28
  57.3 3.5 %collective-permute-done.18 = f32[8,512]{1,0:T(8,128)S(1)} collective-permute-done((f32[8,512]{1,0:T(8,128)S(1)}, f32[8,512]{1,0:T(8,128)S(1)}, u32[]{:S(2)}, u32[]{:S(2)}) %collective-permute-start.18) | collective-permute-done | bytes 16416 | tf_op jit(solution)/shard_map/ppermute | solution.py:28
  60.9 3.1 %query_projection.3 = (f32[256,768]{1,0:T(8,128)S(1)}, f32[256,768]{1,0:T(8,128)S(1)}) custom-call(s32[4]{0:T(128)S(1)} %pad_add_fusion.place, bf16[128,2304]{1,0:T(8,128)(2,1)S(1)} %normalize.2.rows_ref.refs_0_, bf16[128,2304]{1,0:T(8,128)(2,1)S(1)} %collective-permute-done.6.refs_1_, bf16[128,2304]{1,0:T(8,128)(2,1)S(1)} %collective-permute-done.7.refs_2_, ...), custom_call_target="tpu_custom_call" | custom-call | flops 1811939328 | bytes 8388608 | tf_op jit(solution)/shard_map/query_projection/pallas_call | solution.py:159
  64.1 3.3 %query_projection.2 = (f32[256,768]{1,0:T(8,128)S(1)}, f32[256,768]{1,0:T(8,128)S(1)}) custom-call(s32[4]{0:T(128)S(1)} %pad_add_fusion.place, bf16[128,2304]{1,0:T(8,128)(2,1)S(1)} %normalize.2.rows_ref.refs_0_, bf16[128,2304]{1,0:T(8,128)(2,1)S(1)} %collective-permute-done.6.refs_1_, bf16[128,2304]{1,0:T(8,128)(2,1)S(1)} %collective-permute-done.7.refs_2_, ...), custom_call_target="tpu_custom_call" | custom-call | flops 1811939328 | bytes 8388608 | tf_op jit(solution)/shard_map/query_projection/pallas_call | solution.py:159
  69.0 4.4 %collective-permute-start.25 = (f32[128,768]{1,0:T(8,128)S(1)}, f32[128,768]{1,0:T(8,128)S(1)}, u32[]{:S(2)}, u32[]{:S(2)}) collective-permute-start(f32[128,768]{1,0:T(8,128)S(1)} %get-tuple-element.98), channel_id=1, source_target_pairs={{0,96},{1,97},{2,98},{3,99},{4,100},{5,101},{6,102},{7,103},{8,104... | collective-permute-start | bytes 1179656 | tf_op jit(solution)/shard_map/ppermute | solution.py:28
  73.5 5.7 %collective-permute-done.22 = f32[128,768]{1,0:T(8,128)S(1)} collective-permute-done((f32[128,768]{1,0:T(8,128)S(1)}, f32[128,768]{1,0:T(8,128)S(1)}, u32[]{:S(2)}, u32[]{:S(2)}) %collective-permute-start.22) | collective-permute-done | bytes 393248 | tf_op jit(solution)/shard_map/ppermute | solution.py:28
  79.5 8.8 %collective-permute-done.24 = f32[128,768]{1,0:T(8,128)S(1)} collective-permute-done((f32[128,768]{1,0:T(8,128)S(1)}, f32[128,768]{1,0:T(8,128)S(1)}, u32[]{:S(2)}, u32[]{:S(2)}) %collective-permute-start.24) | collective-permute-done | bytes 393248 | tf_op jit(solution)/shard_map/ppermute | solution.py:28
  88.4 13.5 %all_to_all.10 = bf16[16,8,768]{2,1,0:T(8,128)(2,1)S(1)} all-to-all(bf16[16,8,768]{2,1,0:T(8,128)(2,1)S(1)} %fusion.5), channel_id=1, replica_groups=mesh['gx'=8,'yz'=16] {'yz'}, dimensions={0} | all-to-all | bytes 393216 | tf_op jit(solution)/shard_map/all_to_all | solution.py:388
  101.9 4.4 %attention.1 = (bf16[128,768]{1,0:T(8,128)(2,1)S(1)}, bf16[8,512]{1,0:T(8,128)(2,1)S(1)}) custom-call(s32[4]{0:T(128)S(1)} %copy-done.5, bf16[128,768]{1,0:T(8,128)(2,1)S(1)} %bitcast.14, f32[8,128]{1,0:T(8,128)S(1)} %get-tuple-element.76.cos_ref, f32[8,128]{1,0:T(8,128)S(1)} %get-tuple-element.77.sin_ref, ...), custom_call_target="tpu_custom_call" | custom-call | flops 805306368 | bytes 8388608 | tf_op jit(solution)/shard_map/attention/pallas_call | solution.py:256
  106.3 11.6 %all_to_all.11 = bf16[16,8,768]{2,1,0:T(8,128)(2,1)S(1)} all-to-all(bf16[16,8,768]{2,1,0:T(8,128)(2,1)S(1)} %bitcast.15), channel_id=1, replica_groups=mesh['gx'=8,'yz'=16] {'yz'}, dimensions={0} | all-to-all | bytes 393216 | tf_op jit(solution)/shard_map/all_to_all | solution.py:393
  121.1 3.9 %collective-permute-done.26.refs_1_ = bf16[128,768]{1,0:T(8,128)(2,1)S(1)} collective-permute-done((bf16[128,768]{1,0:T(8,128)(2,1)S(1)}, bf16[128,768]{1,0:T(8,128)(2,1)S(1)}, u32[]{:S(2)}, u32[]{:S(2)}) %collective-permute-start.26) | collective-permute-done | bytes 196640 | tf_op jit(solution)/shard_map/ppermute | solution.py:28
  125.9 5.9 %collective-permute-done.28.refs_3_ = bf16[128,768]{1,0:T(8,128)(2,1)S(1)} collective-permute-done((bf16[128,768]{1,0:T(8,128)(2,1)S(1)}, bf16[128,768]{1,0:T(8,128)(2,1)S(1)}, u32[]{:S(2)}, u32[]{:S(2)}) %collective-permute-start.28) | collective-permute-done | bytes 196640 | tf_op jit(solution)/shard_map/ppermute | solution.py:28
  138.4 4.1 %output_projection.2 = (f32[128,2304]{1,0:T(8,128)S(1)}, bf16[128,2304]{1,0:T(8,128)(2,1)S(1)}, bf16[128,2304]{1,0:T(8,128)(2,1)S(1)}, f32[128,2304]{1,0:T(8,128)S(1)}, f32[256,2304]{1,0:T(8,128)S(1)}) custom-call(s32[4]{0:T(128)S(1)} %pad_add_fusion.place, bf16[128,768]{1,0:T(8,128)(2,1)S(1)} %bitcast.13, ...), custom_call_target="tpu_custom_call" | custom-call | flops 2717908992 | bytes 8388608 | tf_op jit(solution)/shard_map/output_projection/pallas_call | solution.py:316
  146.6 3.3 %collective-permute-start.38 = (bf16[128,2304]{1,0:T(8,128)(2,1)S(1)}, bf16[128,2304]{1,0:T(8,128)(2,1)S(1)}, u32[]{:S(2)}, u32[]{:S(2)}) collective-permute-start(bf16[128,2304]{1,0:T(8,128)(2,1)S(1)} %add_convert_fusion), channel_id=1, source_target_pairs={{0,12},{1,13},{2,14},{3,15},{4,0},{5,1},{6,2},{7,3},{8,4},{9,5},{1... | collective-permute-start | bytes 1769480 | tf_op jit(solution)/shard_map/ppermute | solution.py:28
  153.7 6.3 %collective-permute-done.36 = bf16[128,2304]{1,0:T(8,128)(2,1)S(1)} collective-permute-done((bf16[128,2304]{1,0:T(8,128)(2,1)S(1)}, bf16[128,2304]{1,0:T(8,128)(2,1)S(1)}, u32[]{:S(2)}, u32[]{:S(2)}) %collective-permute-start.36) | collective-permute-done | bytes 589856 | tf_op jit(solution)/shard_map/ppermute | solution.py:28
  163.7 3.1 %collective-permute-done.39 = bf16[32,2304]{1,0:T(8,128)(2,1)S(1)} collective-permute-done((bf16[32,2304]{1,0:T(8,128)(2,1)S(1)}, bf16[32,2304]{1,0:T(8,128)(2,1)S(1)}, u32[]{:S(2)}, u32[]{:S(2)}) %collective-permute-start.39) | collective-permute-done | bytes 147488 | tf_op jit(solution)/shard_map/ppermute | solution.py:28
  167.1 3.3 %collective-permute-start.42 = (f32[64,2304]{1,0:T(8,128)S(1)}, f32[64,2304]{1,0:T(8,128)}, u32[]{:S(2)}, u32[]{:S(2)}) collective-permute-start(f32[64,2304]{1,0:T(8,128)S(1)} %pad_maximum_fusion.1), channel_id=1, source_target_pairs={{0,3},{1,0},{2,1},{3,2},{4,7},{5,4},{6,5},{7,6},{8,11},{9,8},{10,9... | collective-permute-start | bytes 1769480 | tf_op jit(solution)/shard_map/ppermute | solution.py:28
  171.0 7.1 %collective-permute-done.40 = f32[64,2304]{1,0:T(8,128)S(1)} collective-permute-done((f32[64,2304]{1,0:T(8,128)S(1)}, f32[64,2304]{1,0:T(8,128)S(1)}, u32[]{:S(2)}, u32[]{:S(2)}) %collective-permute-start.40) | collective-permute-done | bytes 589856 | tf_op jit(solution)/shard_map/ppermute | solution.py:28
  (116 shorter events, 55.5 us)
Async XLA Ops:
  3.3 10.7 %collective-permute-start.4 = (bf16[64,2304]{1,0:T(8,128)(2,1)S(1)}, bf16[64,2304]{1,0:T(8,128)(2,1)S(1)}, u32[]{:S(2)}, u32[]{:S(2)}) collective-permute-start(bf16[64,2304]{1,0:T(8,128)(2,1)S(1)} %reshape.66.rows_ref.one_ref), channel_id=1, source_target_pairs={{0,1},{1,2},{2,3},{3,0},{4,5},{5,6},{6,7},{7,4},{8,9},{9,10},{10,1... | collective-permute-start | bytes 884744 | tf_op jit(solution)/shard_map/ppermute | solution.py:28
  19.5 18.4 %collective-permute-start.7 = (bf16[128,2304]{1,0:T(8,128)(2,1)S(1)}, bf16[128,2304]{1,0:T(8,128)(2,1)S(1)}, u32[]{:S(2)}, u32[]{:S(2)}) collective-permute-start(bf16[128,2304]{1,0:T(8,128)(2,1)S(1)} %normalize.2.rows_ref.refs_0_), channel_id=1, source_target_pairs={{0,12},{1,13},{2,14},{3,15},{4,0},{5,1},{6,2},{7,3},{8,4},{9,5},{1... | collective-permute-start | bytes 1769480 | tf_op jit(solution)/shard_map/ppermute | solution.py:28
  22.6 15.3 %collective-permute-start.6 = (bf16[128,2304]{1,0:T(8,128)(2,1)S(1)}, bf16[128,2304]{1,0:T(8,128)(2,1)S(1)}, u32[]{:S(2)}, u32[]{:S(2)}) collective-permute-start(bf16[128,2304]{1,0:T(8,128)(2,1)S(1)} %normalize.2.rows_ref.refs_0_), channel_id=1, source_target_pairs={{0,4},{1,5},{2,6},{3,7},{4,8},{5,9},{6,10},{7,11},{8,12},{9,13},{1... | collective-permute-start | bytes 1769480 | tf_op jit(solution)/shard_map/ppermute | solution.py:28
  22.6 15.0 %collective-permute-start.8 = (bf16[64,2304]{1,0:T(8,128)(2,1)S(1)}, bf16[64,2304]{1,0:T(8,128)(2,1)S(1)}, u32[]{:S(2)}, u32[]{:S(2)}) collective-permute-start(bf16[64,2304]{1,0:T(8,128)(2,1)S(1)} %reshape.66.rows_ref.one_ref), channel_id=1, source_target_pairs={{0,3},{1,0},{2,1},{3,2},{4,7},{5,4},{6,5},{7,6},{8,11},{9,8},{10,9... | collective-permute-start | bytes 884744 | tf_op jit(solution)/shard_map/ppermute | solution.py:28
  23.6 14.0 %collective-permute-start.9 = (bf16[64,2304]{1,0:T(8,128)(2,1)S(1)}, bf16[64,2304]{1,0:T(8,128)(2,1)S(1)}, u32[]{:S(2)}, u32[]{:S(2)}) collective-permute-start(bf16[64,2304]{1,0:T(8,128)(2,1)S(1)} %collective-permute-done.4.two_ref), channel_id=1, source_target_pairs={{0,1},{1,2},{2,3},{3,0},{4,5},{5,6},{6,7},{7,4},{8,9},{9,10},{10,1... | collective-permute-start | bytes 884744 | tf_op jit(solution)/shard_map/ppermute | solution.py:28
  24.6 7.8 %collective-permute-start.11 = (f32[64,2]{1,0:T(8,128)S(1)}, f32[64,2]{1,0:T(8,128)S(1)}, u32[]{:S(2)}, u32[]{:S(2)}) collective-permute-start(f32[64,2]{1,0:T(8,128)S(1)} %add_add_fusion.one_sums), channel_id=1, source_target_pairs={{0,2},{1,3},{2,0},{3,1},{4,6},{5,7},{6,4},{7,5},{8,10},{9,11},{10,... | collective-permute-start | bytes 1544 | tf_op jit(solution)/shard_map/ppermute | solution.py:28
  38.0 11.2 %collective-permute-start.13 = (bf16[128,2304]{1,0:T(8,128)(2,1)S(1)}, bf16[128,2304]{1,0:T(8,128)(2,1)S(1)}, u32[]{:S(2)}, u32[]{:S(2)}) collective-permute-start(bf16[128,2304]{1,0:T(8,128)(2,1)S(1)} %collective-permute-done.6.refs_1_), channel_id=1, source_target_pairs={{0,4},{1,5},{2,6},{3,7},{4,8},{5,9},{6,10},{7,11},{8,12},{9,13},{1... | collective-permute-start | bytes 1769480 | tf_op jit(solution)/shard_map/ppermute | solution.py:28
  38.6 10.6 %collective-permute-start.15 = (bf16[128,2304]{1,0:T(8,128)(2,1)S(1)}, bf16[128,2304]{1,0:T(8,128)(2,1)S(1)}, u32[]{:S(2)}, u32[]{:S(2)}) collective-permute-start(bf16[128,2304]{1,0:T(8,128)(2,1)S(1)} %normalize.3.refs_4_), channel_id=1, source_target_pairs={{0,12},{1,13},{2,14},{3,15},{4,0},{5,1},{6,2},{7,3},{8,4},{9,5},{1... | collective-permute-start | bytes 1769480 | tf_op jit(solution)/shard_map/ppermute | solution.py:28
  49.1 11.7 %collective-permute-start.14 = (bf16[128,2304]{1,0:T(8,128)(2,1)S(1)}, bf16[128,2304]{1,0:T(8,128)(2,1)S(1)}, u32[]{:S(2)}, u32[]{:S(2)}) collective-permute-start(bf16[128,2304]{1,0:T(8,128)(2,1)S(1)} %normalize.3.refs_4_), channel_id=1, source_target_pairs={{0,4},{1,5},{2,6},{3,7},{4,8},{5,9},{6,10},{7,11},{8,12},{9,13},{1... | collective-permute-start | bytes 1769480 | tf_op jit(solution)/shard_map/ppermute | solution.py:28
  49.1 11.7 %collective-permute-start.16 = (bf16[128,2304]{1,0:T(8,128)(2,1)S(1)}, bf16[128,2304]{1,0:T(8,128)(2,1)S(1)}, u32[]{:S(2)}, u32[]{:S(2)}) collective-permute-start(bf16[128,2304]{1,0:T(8,128)(2,1)S(1)} %collective-permute-done.15.refs_6_), channel_id=1, source_target_pairs={{0,12},{1,13},{2,14},{3,15},{4,0},{5,1},{6,2},{7,3},{8,4},{9,5},{1... | collective-permute-start | bytes 1769480 | tf_op jit(solution)/shard_map/ppermute | solution.py:28
  68.1 11.1 %collective-permute-start.22 = (f32[128,768]{1,0:T(8,128)S(1)}, f32[128,768]{1,0:T(8,128)S(1)}, u32[]{:S(2)}, u32[]{:S(2)}) collective-permute-start(f32[128,768]{1,0:T(8,128)S(1)} %get-tuple-element.97), channel_id=1, source_target_pairs={{0,32},{1,33},{2,34},{3,35},{4,36},{5,37},{6,38},{7,39},{8,40},{9,... | collective-permute-start | bytes 1179656 | tf_op jit(solution)/shard_map/ppermute | solution.py:28
  69.0 10.5 %collective-permute-start.25 = (f32[128,768]{1,0:T(8,128)S(1)}, f32[128,768]{1,0:T(8,128)S(1)}, u32[]{:S(2)}, u32[]{:S(2)}) collective-permute-start(f32[128,768]{1,0:T(8,128)S(1)} %get-tuple-element.98), channel_id=1, source_target_pairs={{0,96},{1,97},{2,98},{3,99},{4,100},{5,101},{6,102},{7,103},{8,104... | collective-permute-start | bytes 1179656 | tf_op jit(solution)/shard_map/ppermute | solution.py:28
  79.3 9.1 %collective-permute-start.24 = (f32[128,768]{1,0:T(8,128)S(1)}, f32[128,768]{1,0:T(8,128)S(1)}, u32[]{:S(2)}, u32[]{:S(2)}) collective-permute-start(f32[128,768]{1,0:T(8,128)S(1)} %slice_add_fusion.1), channel_id=1, source_target_pairs={{0,32},{1,33},{2,34},{3,35},{4,36},{5,37},{6,38},{7,39},{8,40},{9,... | collective-permute-start | bytes 1179656 | tf_op jit(solution)/shard_map/ppermute | solution.py:28
  117.9 7.1 %collective-permute-start.26 = (bf16[128,768]{1,0:T(8,128)(2,1)S(1)}, bf16[128,768]{1,0:T(8,128)(2,1)S(1)}, u32[]{:S(2)}, u32[]{:S(2)}) collective-permute-start(bf16[128,768]{1,0:T(8,128)(2,1)S(1)} %bitcast.9), channel_id=1, source_target_pairs={{0,32},{1,33},{2,34},{3,35},{4,36},{5,37},{6,38},{7,39},{8,40},{9,... | collective-permute-start | bytes 589832 | tf_op jit(solution)/shard_map/ppermute | solution.py:28
  118.4 7.5 %collective-permute-start.27 = (bf16[128,768]{1,0:T(8,128)(2,1)S(1)}, bf16[128,768]{1,0:T(8,128)(2,1)S(1)}, u32[]{:S(2)}, u32[]{:S(2)}) collective-permute-start(bf16[128,768]{1,0:T(8,128)(2,1)S(1)} %bitcast.10), channel_id=1, source_target_pairs={{0,96},{1,97},{2,98},{3,99},{4,100},{5,101},{6,102},{7,103},{8,104... | collective-permute-start | bytes 589832 | tf_op jit(solution)/shard_map/ppermute | solution.py:28
  125.0 6.9 %collective-permute-start.30 = (bf16[128,768]{1,0:T(8,128)(2,1)S(1)}, bf16[128,768]{1,0:T(8,128)(2,1)S(1)}, u32[]{:S(2)}, u32[]{:S(2)}) collective-permute-start(bf16[128,768]{1,0:T(8,128)(2,1)S(1)} %collective-permute-done.26.refs_1_), channel_id=1, source_target_pairs={{0,16},{16,0},{32,48},{48,32},{64,80},{80,64},{96,112},{112,96},{1... | collective-permute-start | bytes 589832 | tf_op jit(solution)/shard_map/ppermute | solution.py:33
  135.1 11.2 %collective-permute-start.34 = (bf16[128,2304]{1,0:T(8,128)(2,1)S(1)}, bf16[128,2304]{1,0:T(8,128)(2,1)S(1)}, u32[]{:S(2)}, u32[]{:S(2)}) collective-permute-start(bf16[128,2304]{1,0:T(8,128)(2,1)S(1)} %get-tuple-element.83), channel_id=1, source_target_pairs={{0,4},{1,5},{2,6},{3,7},{4,8},{5,9},{6,10},{7,11},{8,12},{9,13},{1... | collective-permute-start | bytes 1769480 | tf_op jit(solution)/shard_map/ppermute | solution.py:28
  135.5 10.8 %collective-permute-start.35 = (bf16[128,2304]{1,0:T(8,128)(2,1)S(1)}, bf16[128,2304]{1,0:T(8,128)(2,1)S(1)}, u32[]{:S(2)}, u32[]{:S(2)}) collective-permute-start(bf16[128,2304]{1,0:T(8,128)(2,1)S(1)} %get-tuple-element.84), channel_id=1, source_target_pairs={{0,12},{1,13},{2,14},{3,15},{4,0},{5,1},{6,2},{7,3},{8,4},{9,5},{1... | collective-permute-start | bytes 1769480 | tf_op jit(solution)/shard_map/ppermute | solution.py:28
  142.5 10.0 %collective-permute-start.33 = (bf16[128,2304]{1,0:T(8,128)(2,1)S(1)}, bf16[128,2304]{1,0:T(8,128)(2,1)S(1)}, u32[]{:S(2)}, u32[]{:S(2)}) collective-permute-start(bf16[128,2304]{1,0:T(8,128)(2,1)S(1)} %get-tuple-element.81), channel_id=1, source_target_pairs={{0,12},{1,13},{2,14},{3,15},{4,0},{5,1},{6,2},{7,3},{8,4},{9,5},{1... | collective-permute-start | bytes 1769480 | tf_op jit(solution)/shard_map/ppermute | solution.py:28
  142.6 11.2 %collective-permute-start.37 = (bf16[128,2304]{1,0:T(8,128)(2,1)S(1)}, bf16[128,2304]{1,0:T(8,128)(2,1)S(1)}, u32[]{:S(2)}, u32[]{:S(2)}) collective-permute-start(bf16[128,2304]{1,0:T(8,128)(2,1)S(1)} %get-tuple-element.86), channel_id=1, source_target_pairs={{0,4},{1,5},{2,6},{3,7},{4,8},{5,9},{6,10},{7,11},{8,12},{9,13},{1... | collective-permute-start | bytes 1769480 | tf_op jit(solution)/shard_map/ppermute | solution.py:28
  146.4 13.7 %collective-permute-start.36 = (bf16[128,2304]{1,0:T(8,128)(2,1)S(1)}, bf16[128,2304]{1,0:T(8,128)(2,1)S(1)}, u32[]{:S(2)}, u32[]{:S(2)}) collective-permute-start(bf16[128,2304]{1,0:T(8,128)(2,1)S(1)} %add_convert_fusion.1), channel_id=1, source_target_pairs={{0,4},{1,5},{2,6},{3,7},{4,8},{5,9},{6,10},{7,11},{8,12},{9,13},{1... | collective-permute-start | bytes 1769480 | tf_op jit(solution)/shard_map/ppermute | solution.py:28
  146.6 13.5 %collective-permute-start.38 = (bf16[128,2304]{1,0:T(8,128)(2,1)S(1)}, bf16[128,2304]{1,0:T(8,128)(2,1)S(1)}, u32[]{:S(2)}, u32[]{:S(2)}) collective-permute-start(bf16[128,2304]{1,0:T(8,128)(2,1)S(1)} %add_convert_fusion), channel_id=1, source_target_pairs={{0,12},{1,13},{2,14},{3,15},{4,0},{5,1},{6,2},{7,3},{8,4},{9,5},{1... | collective-permute-start | bytes 1769480 | tf_op jit(solution)/shard_map/ppermute | solution.py:28
  166.9 11.2 %collective-permute-start.40 = (f32[64,2304]{1,0:T(8,128)S(1)}, f32[64,2304]{1,0:T(8,128)S(1)}, u32[]{:S(2)}, u32[]{:S(2)}) collective-permute-start(f32[64,2304]{1,0:T(8,128)S(1)} %pad_maximum_fusion), channel_id=1, source_target_pairs={{0,1},{1,2},{2,3},{3,0},{4,5},{5,6},{6,7},{7,4},{8,9},{9,10},{10,1... | collective-permute-start | bytes 1769480 | tf_op jit(solution)/shard_map/ppermute | solution.py:28
  167.1 11.0 %collective-permute-start.42 = (f32[64,2304]{1,0:T(8,128)S(1)}, f32[64,2304]{1,0:T(8,128)}, u32[]{:S(2)}, u32[]{:S(2)}) collective-permute-start(f32[64,2304]{1,0:T(8,128)S(1)} %pad_maximum_fusion.1), channel_id=1, source_target_pairs={{0,3},{1,0},{2,1},{3,2},{4,7},{5,4},{6,5},{7,6},{8,11},{9,8},{10,9... | collective-permute-start | bytes 1769480 | tf_op jit(solution)/shard_map/ppermute | solution.py:28
  (26 other events, 282.3 us)

commit v8 on v6

--- a/solution.py
+++ b/solution.py
@@ -346,22 +346,20 @@
     sums = sums + send_x(sums, 1) + send_x(sums, 2) + send_x(sums, 3)
     sums, before, after = lax.optimization_barrier((sums, before, after))
     before_sums, after_sums = send_inner(sums, 1), send_inner(sums, -1)
-    before, before_sums = lax.optimization_barrier((before, before_sums))
-    far, far_sums = send_inner(before, 1), send_inner(sums, 2)
+    far, far_sums = send_inner(after, -1), send_inner(sums, 2)
     scale = gain.reshape(1, features)
     near = normalize(raw, before, sums, before_sums, scale)
+    near, far = lax.optimization_barrier((near, far))
     wide = normalize(after, far, after_sums, far_sums, scale)
 
     keyval_away, keyval_keep = project_keyval(place, near, w_keyval)
     kept = keyval_keep + send_core(keyval_away)
 
     near_before, near_after = send_outer(near, 1), send_outer(near, -1)
-    near_before, near_after, wide, kept = lax.optimization_barrier(
-        (near_before, near_after, wide, kept)
-    )
+    near_before, near_after, wide = lax.optimization_barrier((near_before, near_after, wide))
     wide_after = send_outer(wide, -1)
     near_far = send_outer(near_before, 1)
-    near_far, wide_again = lax.optimization_barrier((near_far, wide))
+    near_far, wide_again, kept = lax.optimization_barrier((near_far, wide, kept))
     wide_before = send_outer(wide_again, 1)
     wide_far = send_outer(wide_after, -1)
 

time: 179 us -> 182 us (1.017)
  waiting for transfers between devices: 75.5 us -> 77.9 us
  transfers between devices with their start and end apart: 43 -> 43, of which waited for: 22 -> 23; matrix products, arithmetic and copies ran while one was open for 1% -> 1% of each run, Pallas kernels for 5% -> 5%
where the time goes in v8:
time: 182 us
  waiting for transfers between devices  77.9 us (43%)
  starting transfers between devices  53 us (29%)
  blocking collectives  25.4 us (14%)
  Pallas kernels  18.4 us (10%)
  local copies, waits for them, and re-layouts  3.44 us (2%)
  other arithmetic  2.43 us (1%)
    ppermute x34, waiting for transfers between devices, shift(): return lax.ppermute(value, ('gx', 'yz'), pairs)  75.1 us
    ppermute x34, starting transfers between devices, shift(): return lax.ppermute(value, ('gx', 'yz'), pairs)  50.9 us
    all_to_all x1, blocking collectives, body(): query = lax.all_to_all(query, 'yz', split_axis=0, concat_axis=0)  13.8 us
    all_to_all x1, blocking collectives, body(): lax.all_to_all(heads_out.reshape(16, 8, columns), 'yz', split_axis=0, con...  11.6 us
    pallas_call x2, Pallas kernels, project_query(): pl.pallas_call(functools.partial(query_kernel, pair), out_shape=[half, ha...  6.35 us
    pallas_call x2, Pallas kernels, project_output(): pl.pallas_call(functools.partial(output_kernel, groups), out_shape=shapes...  5.86 us
    pallas_call x1, Pallas kernels, attend(): pl.pallas_call(attend_kernel, out_shape=[jax.ShapeDtypeStruct((rows, colu...  4.36 us
  transfers between devices with their start and end apart: 43, of which 23 were waited for; matrix products, arithmetic and copies ran while one was open for 1% of the time, Pallas kernels for 5%

profile of v8, /device:TPU:0, one launch (start us, length us, event | category | flops | bytes accessed | tf_op | source)
XLA Modules:
  0.0 181.6 jit_solution(14083829477600462698)
XLA Ops:
  3.2 4.1 %collective-permute-start.5 = (bf16[64,2304]{1,0:T(8,128)(2,1)S(1)}, bf16[64,2304]{1,0:T(8,128)(2,1)S(1)}, u32[]{:S(2)}, u32[]{:S(2)}) collective-permute-start(bf16[64,2304]{1,0:T(8,128)(2,1)S(1)} %reshape.66.rows_ref.one_ref), channel_id=1, source_target_pairs={{0,3},{1,0},{2,1},{3,2},{4,7},{5,4},{6,5},{7,6},{8,11},{9,8},{10,9... | collective-permute-start | bytes 884744 | tf_op jit(solution)/shard_map/ppermute | solution.py:28
  11.7 3.7 %collective-permute-done.2 = f32[64,2]{1,0:T(8,128)S(1)} collective-permute-done((f32[64,2]{1,0:T(8,128)S(1)}, f32[64,2]{1,0:T(8,128)S(1)}, u32[]{:S(2)}, u32[]{:S(2)}) %collective-permute-start.2) | collective-permute-done | bytes 544 | tf_op jit(solution)/shard_map/ppermute | solution.py:28
  16.0 3.3 %collective-permute-start.7 = (bf16[64,2304]{1,0:T(8,128)(2,1)S(1)}, bf16[64,2304]{1,0:T(8,128)(2,1)S(1)}, u32[]{:S(2)}, u32[]{:S(2)}) collective-permute-start(bf16[64,2304]{1,0:T(8,128)(2,1)S(1)} %collective-permute-done.5.one_ref), channel_id=1, source_target_pairs={{0,3},{1,0},{2,1},{3,2},{4,7},{5,4},{6,5},{7,6},{8,11},{9,8},{10,9... | collective-permute-start | bytes 884744 | tf_op jit(solution)/shard_map/ppermute | solution.py:28
  19.3 5.1 %collective-permute-done.6.two_sums = f32[64,2]{1,0:T(8,128)S(1)} collective-permute-done((f32[64,2]{1,0:T(8,128)S(1)}, f32[64,2]{1,0:T(8,128)S(1)}, u32[]{:S(2)}, u32[]{:S(2)}) %collective-permute-start.6) | collective-permute-done | bytes 544 | tf_op jit(solution)/shard_map/ppermute | solution.py:28
  35.4 3.5 %collective-permute-done.8.refs_1_ = bf16[128,2304]{1,0:T(8,128)(2,1)S(1)} collective-permute-done((bf16[128,2304]{1,0:T(8,128)(2,1)S(1)}, bf16[128,2304]{1,0:T(8,128)(2,1)S(1)}, u32[]{:S(2)}, u32[]{:S(2)}) %collective-permute-start.8) | collective-permute-done | bytes 589856 | tf_op jit(solution)/shard_map/ppermute | solution.py:28
  38.9 3.2 %collective-permute-start.15 = (bf16[128,2304]{1,0:T(8,128)(2,1)S(1)}, bf16[128,2304]{1,0:T(8,128)(2,1)S(1)}, u32[]{:S(2)}, u32[]{:S(2)}) collective-permute-start(bf16[128,2304]{1,0:T(8,128)(2,1)S(1)} %normalize.3.refs_4_), channel_id=1, source_target_pairs={{0,12},{1,13},{2,14},{3,15},{4,0},{5,1},{6,2},{7,3},{8,4},{9,5},{1... | collective-permute-start | bytes 1769480 | tf_op jit(solution)/shard_map/ppermute | solution.py:28
  44.6 5.4 %collective-permute-done.12.refs_3_ = bf16[128,2304]{1,0:T(8,128)(2,1)S(1)} collective-permute-done((bf16[128,2304]{1,0:T(8,128)(2,1)S(1)}, bf16[128,2304]{1,0:T(8,128)(2,1)S(1)}, u32[]{:S(2)}, u32[]{:S(2)}) %collective-permute-start.12) | collective-permute-done | bytes 589856 | tf_op jit(solution)/shard_map/ppermute | solution.py:28
  50.0 3.2 %collective-permute-start.16 = (bf16[128,2304]{1,0:T(8,128)(2,1)S(1)}, bf16[128,2304]{1,0:T(8,128)(2,1)S(1)}, u32[]{:S(2)}, u32[]{:S(2)}) collective-permute-start(bf16[128,2304]{1,0:T(8,128)(2,1)S(1)} %collective-permute-done.15.refs_6_), channel_id=1, source_target_pairs={{0,12},{1,13},{2,14},{3,15},{4,0},{5,1},{6,2},{7,3},{8,4},{9,5},{1... | collective-permute-start | bytes 1769480 | tf_op jit(solution)/shard_map/ppermute | solution.py:28
  53.3 3.2 %collective-permute-start.19 = (f32[8,512]{1,0:T(8,128)S(1)}, f32[8,512]{1,0:T(8,128)S(1)}, u32[]{:S(2)}, u32[]{:S(2)}) collective-permute-start(f32[8,512]{1,0:T(8,128)S(1)} %get-tuple-element.102), channel_id=1, source_target_pairs={{0,96},{1,97},{2,98},{3,99},{4,100},{5,101},{6,102},{7,103},{8,104... | collective-permute-start | bytes 49160 | tf_op jit(solution)/shard_map/ppermute | solution.py:28
  58.2 3.5 %collective-permute-done.18 = f32[8,512]{1,0:T(8,128)S(1)} collective-permute-done((f32[8,512]{1,0:T(8,128)S(1)}, f32[8,512]{1,0:T(8,128)S(1)}, u32[]{:S(2)}, u32[]{:S(2)}) %collective-permute-start.18) | collective-permute-done | bytes 16416 | tf_op jit(solution)/shard_map/ppermute | solution.py:28
  65.0 3.3 %query_projection.2 = (f32[256,768]{1,0:T(8,128)S(1)}, f32[256,768]{1,0:T(8,128)S(1)}) custom-call(s32[4]{0:T(128)S(1)} %pad_add_fusion.place, bf16[128,2304]{1,0:T(8,128)(2,1)S(1)} %normalize.2.rows_ref.refs_0_, bf16[128,2304]{1,0:T(8,128)(2,1)S(1)} %collective-permute-done.8.refs_1_, bf16[128,2304]{1,0:T(8,128)(2,1)S(1)} %collective-permute-done.9.refs_2_, ...), custom_call_target="tpu_custom_call" | custom-call | flops 1811939328 | bytes 8388608 | tf_op jit(solution)/shard_map/query_projection/pallas_call | solution.py:159
  69.9 4.4 %collective-permute-start.25 = (f32[128,768]{1,0:T(8,128)S(1)}, f32[128,768]{1,0:T(8,128)S(1)}, u32[]{:S(2)}, u32[]{:S(2)}) collective-permute-start(f32[128,768]{1,0:T(8,128)S(1)} %get-tuple-element.98), channel_id=1, source_target_pairs={{0,96},{1,97},{2,98},{3,99},{4,100},{5,101},{6,102},{7,103},{8,104... | collective-permute-start | bytes 1179656 | tf_op jit(solution)/shard_map/ppermute | solution.py:28
  74.4 6.2 %collective-permute-done.22 = f32[128,768]{1,0:T(8,128)S(1)} collective-permute-done((f32[128,768]{1,0:T(8,128)S(1)}, f32[128,768]{1,0:T(8,128)S(1)}, u32[]{:S(2)}, u32[]{:S(2)}) %collective-permute-start.22) | collective-permute-done | bytes 393248 | tf_op jit(solution)/shard_map/ppermute | solution.py:28
  80.7 9.0 %collective-permute-done.24 = f32[128,768]{1,0:T(8,128)S(1)} collective-permute-done((f32[128,768]{1,0:T(8,128)S(1)}, f32[128,768]{1,0:T(8,128)S(1)}, u32[]{:S(2)}, u32[]{:S(2)}) %collective-permute-start.24) | collective-permute-done | bytes 393248 | tf_op jit(solution)/shard_map/ppermute | solution.py:28
  89.8 13.8 %all_to_all.10 = bf16[16,8,768]{2,1,0:T(8,128)(2,1)S(1)} all-to-all(bf16[16,8,768]{2,1,0:T(8,128)(2,1)S(1)} %fusion.5), channel_id=1, replica_groups=mesh['gx'=8,'yz'=16] {'yz'}, dimensions={0} | all-to-all | bytes 393216 | tf_op jit(solution)/shard_map/all_to_all | solution.py:385
  103.6 4.4 %attention.1 = (bf16[128,768]{1,0:T(8,128)(2,1)S(1)}, bf16[8,512]{1,0:T(8,128)(2,1)S(1)}) custom-call(s32[4]{0:T(128)S(1)} %copy-done.5, bf16[128,768]{1,0:T(8,128)(2,1)S(1)} %bitcast.14, f32[8,128]{1,0:T(8,128)S(1)} %get-tuple-element.76.cos_ref, f32[8,128]{1,0:T(8,128)S(1)} %get-tuple-element.77.sin_ref, ...), custom_call_target="tpu_custom_call" | custom-call | flops 805306368 | bytes 8388608 | tf_op jit(solution)/shard_map/attention/pallas_call | solution.py:256
  108.0 11.6 %all_to_all.11 = bf16[16,8,768]{2,1,0:T(8,128)(2,1)S(1)} all-to-all(bf16[16,8,768]{2,1,0:T(8,128)(2,1)S(1)} %bitcast.15), channel_id=1, replica_groups=mesh['gx'=8,'yz'=16] {'yz'}, dimensions={0} | all-to-all | bytes 393216 | tf_op jit(solution)/shard_map/all_to_all | solution.py:390
  119.6 3.2 %collective-permute-start.27 = (bf16[128,768]{1,0:T(8,128)(2,1)S(1)}, bf16[128,768]{1,0:T(8,128)(2,1)S(1)}, u32[]{:S(2)}, u32[]{:S(2)}) collective-permute-start(bf16[128,768]{1,0:T(8,128)(2,1)S(1)} %bitcast.10), channel_id=1, source_target_pairs={{0,96},{1,97},{2,98},{3,99},{4,100},{5,101},{6,102},{7,103},{8,104... | collective-permute-start | bytes 589832 | tf_op jit(solution)/shard_map/ppermute | solution.py:28
  122.8 3.6 %collective-permute-done.26.refs_1_ = bf16[128,768]{1,0:T(8,128)(2,1)S(1)} collective-permute-done((bf16[128,768]{1,0:T(8,128)(2,1)S(1)}, bf16[128,768]{1,0:T(8,128)(2,1)S(1)}, u32[]{:S(2)}, u32[]{:S(2)}) %collective-permute-start.26) | collective-permute-done | bytes 196640 | tf_op jit(solution)/shard_map/ppermute | solution.py:28
  127.0 6.4 %collective-permute-done.28.refs_3_ = bf16[128,768]{1,0:T(8,128)(2,1)S(1)} collective-permute-done((bf16[128,768]{1,0:T(8,128)(2,1)S(1)}, bf16[128,768]{1,0:T(8,128)(2,1)S(1)}, u32[]{:S(2)}, u32[]{:S(2)}) %collective-permute-start.28) | collective-permute-done | bytes 196640 | tf_op jit(solution)/shard_map/ppermute | solution.py:28
  139.9 4.1 %output_projection.2 = (f32[128,2304]{1,0:T(8,128)S(1)}, bf16[128,2304]{1,0:T(8,128)(2,1)S(1)}, bf16[128,2304]{1,0:T(8,128)(2,1)S(1)}, f32[128,2304]{1,0:T(8,128)S(1)}, f32[256,2304]{1,0:T(8,128)S(1)}) custom-call(s32[4]{0:T(128)S(1)} %pad_add_fusion.place, bf16[128,768]{1,0:T(8,128)(2,1)S(1)} %bitcast.13, ...), custom_call_target="tpu_custom_call" | custom-call | flops 2717908992 | bytes 8388608 | tf_op jit(solution)/shard_map/output_projection/pallas_call | solution.py:316
  155.2 6.3 %collective-permute-done.36 = bf16[128,2304]{1,0:T(8,128)(2,1)S(1)} collective-permute-done((bf16[128,2304]{1,0:T(8,128)(2,1)S(1)}, bf16[128,2304]{1,0:T(8,128)(2,1)S(1)}, u32[]{:S(2)}, u32[]{:S(2)}) %collective-permute-start.36) | collective-permute-done | bytes 589856 | tf_op jit(solution)/shard_map/ppermute | solution.py:28
  168.6 3.3 %collective-permute-start.42 = (f32[64,2304]{1,0:T(8,128)S(1)}, f32[64,2304]{1,0:T(8,128)}, u32[]{:S(2)}, u32[]{:S(2)}) collective-permute-start(f32[64,2304]{1,0:T(8,128)S(1)} %pad_maximum_fusion.1), channel_id=1, source_target_pairs={{0,3},{1,0},{2,1},{3,2},{4,7},{5,4},{6,5},{7,6},{8,11},{9,8},{10,9... | collective-permute-start | bytes 1769480 | tf_op jit(solution)/shard_map/ppermute | solution.py:28
  172.5 7.1 %collective-permute-done.40 = f32[64,2304]{1,0:T(8,128)S(1)} collective-permute-done((f32[64,2304]{1,0:T(8,128)S(1)}, f32[64,2304]{1,0:T(8,128)S(1)}, u32[]{:S(2)}, u32[]{:S(2)}) %collective-permute-start.40) | collective-permute-done | bytes 589856 | tf_op jit(solution)/shard_map/ppermute | solution.py:28
  (116 shorter events, 55.5 us)
Async XLA Ops:
  3.2 12.8 %collective-permute-start.5 = (bf16[64,2304]{1,0:T(8,128)(2,1)S(1)}, bf16[64,2304]{1,0:T(8,128)(2,1)S(1)}, u32[]{:S(2)}, u32[]{:S(2)}) collective-permute-start(bf16[64,2304]{1,0:T(8,128)(2,1)S(1)} %reshape.66.rows_ref.one_ref), channel_id=1, source_target_pairs={{0,3},{1,0},{2,1},{3,2},{4,7},{5,4},{6,5},{7,6},{8,11},{9,8},{10,9... | collective-permute-start | bytes 884744 | tf_op jit(solution)/shard_map/ppermute | solution.py:28
  7.3 8.7 %collective-permute-start.4 = (bf16[64,2304]{1,0:T(8,128)(2,1)S(1)}, bf16[64,2304]{1,0:T(8,128)(2,1)S(1)}, u32[]{:S(2)}, u32[]{:S(2)}) collective-permute-start(bf16[64,2304]{1,0:T(8,128)(2,1)S(1)} %reshape.66.rows_ref.one_ref), channel_id=1, source_target_pairs={{0,1},{1,2},{2,3},{3,0},{4,5},{5,6},{6,7},{7,4},{8,9},{9,10},{10,1... | collective-permute-start | bytes 884744 | tf_op jit(solution)/shard_map/ppermute | solution.py:28
  16.0 8.7 %collective-permute-start.7 = (bf16[64,2304]{1,0:T(8,128)(2,1)S(1)}, bf16[64,2304]{1,0:T(8,128)(2,1)S(1)}, u32[]{:S(2)}, u32[]{:S(2)}) collective-permute-start(bf16[64,2304]{1,0:T(8,128)(2,1)S(1)} %collective-permute-done.5.one_ref), channel_id=1, source_target_pairs={{0,3},{1,0},{2,1},{3,2},{4,7},{5,4},{6,5},{7,6},{8,11},{9,8},{10,9... | collective-permute-start | bytes 884744 | tf_op jit(solution)/shard_map/ppermute | solution.py:28
  24.7 10.6 %collective-permute-start.9 = (bf16[128,2304]{1,0:T(8,128)(2,1)S(1)}, bf16[128,2304]{1,0:T(8,128)(2,1)S(1)}, u32[]{:S(2)}, u32[]{:S(2)}) collective-permute-start(bf16[128,2304]{1,0:T(8,128)(2,1)S(1)} %normalize.2.rows_ref.refs_0_), channel_id=1, source_target_pairs={{0,12},{1,13},{2,14},{3,15},{4,0},{5,1},{6,2},{7,3},{8,4},{9,5},{1... | collective-permute-start | bytes 1769480 | tf_op jit(solution)/shard_map/ppermute | solution.py:28
  27.8 11.1 %collective-permute-start.8 = (bf16[128,2304]{1,0:T(8,128)(2,1)S(1)}, bf16[128,2304]{1,0:T(8,128)(2,1)S(1)}, u32[]{:S(2)}, u32[]{:S(2)}) collective-permute-start(bf16[128,2304]{1,0:T(8,128)(2,1)S(1)} %normalize.2.rows_ref.refs_0_), channel_id=1, source_target_pairs={{0,4},{1,5},{2,6},{3,7},{4,8},{5,9},{6,10},{7,11},{8,12},{9,13},{1... | collective-permute-start | bytes 1769480 | tf_op jit(solution)/shard_map/ppermute | solution.py:28
  38.9 11.1 %collective-permute-start.12 = (bf16[128,2304]{1,0:T(8,128)(2,1)S(1)}, bf16[128,2304]{1,0:T(8,128)(2,1)S(1)}, u32[]{:S(2)}, u32[]{:S(2)}) collective-permute-start(bf16[128,2304]{1,0:T(8,128)(2,1)S(1)} %collective-permute-done.8.refs_1_), channel_id=1, source_target_pairs={{0,4},{1,5},{2,6},{3,7},{4,8},{5,9},{6,10},{7,11},{8,12},{9,13},{1... | collective-permute-start | bytes 1769480 | tf_op jit(solution)/shard_map/ppermute | solution.py:28
  38.9 11.1 %collective-permute-start.15 = (bf16[128,2304]{1,0:T(8,128)(2,1)S(1)}, bf16[128,2304]{1,0:T(8,128)(2,1)S(1)}, u32[]{:S(2)}, u32[]{:S(2)}) collective-permute-start(bf16[128,2304]{1,0:T(8,128)(2,1)S(1)} %normalize.3.refs_4_), channel_id=1, source_target_pairs={{0,12},{1,13},{2,14},{3,15},{4,0},{5,1},{6,2},{7,3},{8,4},{9,5},{1... | collective-permute-start | bytes 1769480 | tf_op jit(solution)/shard_map/ppermute | solution.py:28
  50.0 11.7 %collective-permute-start.14 = (bf16[128,2304]{1,0:T(8,128)(2,1)S(1)}, bf16[128,2304]{1,0:T(8,128)(2,1)S(1)}, u32[]{:S(2)}, u32[]{:S(2)}) collective-permute-start(bf16[128,2304]{1,0:T(8,128)(2,1)S(1)} %normalize.3.refs_4_), channel_id=1, source_target_pairs={{0,4},{1,5},{2,6},{3,7},{4,8},{5,9},{6,10},{7,11},{8,12},{9,13},{1... | collective-permute-start | bytes 1769480 | tf_op jit(solution)/shard_map/ppermute | solution.py:28
  50.0 11.7 %collective-permute-start.16 = (bf16[128,2304]{1,0:T(8,128)(2,1)S(1)}, bf16[128,2304]{1,0:T(8,128)(2,1)S(1)}, u32[]{:S(2)}, u32[]{:S(2)}) collective-permute-start(bf16[128,2304]{1,0:T(8,128)(2,1)S(1)} %collective-permute-done.15.refs_6_), channel_id=1, source_target_pairs={{0,12},{1,13},{2,14},{3,15},{4,0},{5,1},{6,2},{7,3},{8,4},{9,5},{1... | collective-permute-start | bytes 1769480 | tf_op jit(solution)/shard_map/ppermute | solution.py:28
  69.0 11.6 %collective-permute-start.22 = (f32[128,768]{1,0:T(8,128)S(1)}, f32[128,768]{1,0:T(8,128)S(1)}, u32[]{:S(2)}, u32[]{:S(2)}) collective-permute-start(f32[128,768]{1,0:T(8,128)S(1)} %get-tuple-element.97), channel_id=1, source_target_pairs={{0,32},{1,33},{2,34},{3,35},{4,36},{5,37},{6,38},{7,39},{8,40},{9,... | collective-permute-start | bytes 1179656 | tf_op jit(solution)/shard_map/ppermute | solution.py:28
  69.9 10.9 %collective-permute-start.25 = (f32[128,768]{1,0:T(8,128)S(1)}, f32[128,768]{1,0:T(8,128)S(1)}, u32[]{:S(2)}, u32[]{:S(2)}) collective-permute-start(f32[128,768]{1,0:T(8,128)S(1)} %get-tuple-element.98), channel_id=1, source_target_pairs={{0,96},{1,97},{2,98},{3,99},{4,100},{5,101},{6,102},{7,103},{8,104... | collective-permute-start | bytes 1179656 | tf_op jit(solution)/shard_map/ppermute | solution.py:28
  80.6 9.1 %collective-permute-start.24 = (f32[128,768]{1,0:T(8,128)S(1)}, f32[128,768]{1,0:T(8,128)S(1)}, u32[]{:S(2)}, u32[]{:S(2)}) collective-permute-start(f32[128,768]{1,0:T(8,128)S(1)} %slice_add_fusion.1), channel_id=1, source_target_pairs={{0,32},{1,33},{2,34},{3,35},{4,36},{5,37},{6,38},{7,39},{8,40},{9,... | collective-permute-start | bytes 1179656 | tf_op jit(solution)/shard_map/ppermute | solution.py:28
  119.6 6.9 %collective-permute-start.26 = (bf16[128,768]{1,0:T(8,128)(2,1)S(1)}, bf16[128,768]{1,0:T(8,128)(2,1)S(1)}, u32[]{:S(2)}, u32[]{:S(2)}) collective-permute-start(bf16[128,768]{1,0:T(8,128)(2,1)S(1)} %bitcast.9), channel_id=1, source_target_pairs={{0,32},{1,33},{2,34},{3,35},{4,36},{5,37},{6,38},{7,39},{8,40},{9,... | collective-permute-start | bytes 589832 | tf_op jit(solution)/shard_map/ppermute | solution.py:28
  119.6 7.4 %collective-permute-start.27 = (bf16[128,768]{1,0:T(8,128)(2,1)S(1)}, bf16[128,768]{1,0:T(8,128)(2,1)S(1)}, u32[]{:S(2)}, u32[]{:S(2)}) collective-permute-start(bf16[128,768]{1,0:T(8,128)(2,1)S(1)} %bitcast.10), channel_id=1, source_target_pairs={{0,96},{1,97},{2,98},{3,99},{4,100},{5,101},{6,102},{7,103},{8,104... | collective-permute-start | bytes 589832 | tf_op jit(solution)/shard_map/ppermute | solution.py:28
  126.5 6.9 %collective-permute-start.29 = (bf16[128,768]{1,0:T(8,128)(2,1)S(1)}, bf16[128,768]{1,0:T(8,128)(2,1)S(1)}, u32[]{:S(2)}, u32[]{:S(2)}) collective-permute-start(bf16[128,768]{1,0:T(8,128)(2,1)S(1)} %bitcast.11), channel_id=1, source_target_pairs={{0,16},{16,0},{32,48},{48,32},{64,80},{80,64},{96,112},{112,96},{1... | collective-permute-start | bytes 589832 | tf_op jit(solution)/shard_map/ppermute | solution.py:33
  126.5 6.9 %collective-permute-start.30 = (bf16[128,768]{1,0:T(8,128)(2,1)S(1)}, bf16[128,768]{1,0:T(8,128)(2,1)S(1)}, u32[]{:S(2)}, u32[]{:S(2)}) collective-permute-start(bf16[128,768]{1,0:T(8,128)(2,1)S(1)} %collective-permute-done.26.refs_1_), channel_id=1, source_target_pairs={{0,16},{16,0},{32,48},{48,32},{64,80},{80,64},{96,112},{112,96},{1... | collective-permute-start | bytes 589832 | tf_op jit(solution)/shard_map/ppermute | solution.py:33
  136.6 11.2 %collective-permute-start.34 = (bf16[128,2304]{1,0:T(8,128)(2,1)S(1)}, bf16[128,2304]{1,0:T(8,128)(2,1)S(1)}, u32[]{:S(2)}, u32[]{:S(2)}) collective-permute-start(bf16[128,2304]{1,0:T(8,128)(2,1)S(1)} %get-tuple-element.83), channel_id=1, source_target_pairs={{0,4},{1,5},{2,6},{3,7},{4,8},{5,9},{6,10},{7,11},{8,12},{9,13},{1... | collective-permute-start | bytes 1769480 | tf_op jit(solution)/shard_map/ppermute | solution.py:28
  137.1 10.7 %collective-permute-start.35 = (bf16[128,2304]{1,0:T(8,128)(2,1)S(1)}, bf16[128,2304]{1,0:T(8,128)(2,1)S(1)}, u32[]{:S(2)}, u32[]{:S(2)}) collective-permute-start(bf16[128,2304]{1,0:T(8,128)(2,1)S(1)} %get-tuple-element.84), channel_id=1, source_target_pairs={{0,12},{1,13},{2,14},{3,15},{4,0},{5,1},{6,2},{7,3},{8,4},{9,5},{1... | collective-permute-start | bytes 1769480 | tf_op jit(solution)/shard_map/ppermute | solution.py:28
  144.0 10.0 %collective-permute-start.33 = (bf16[128,2304]{1,0:T(8,128)(2,1)S(1)}, bf16[128,2304]{1,0:T(8,128)(2,1)S(1)}, u32[]{:S(2)}, u32[]{:S(2)}) collective-permute-start(bf16[128,2304]{1,0:T(8,128)(2,1)S(1)} %get-tuple-element.81), channel_id=1, source_target_pairs={{0,12},{1,13},{2,14},{3,15},{4,0},{5,1},{6,2},{7,3},{8,4},{9,5},{1... | collective-permute-start | bytes 1769480 | tf_op jit(solution)/shard_map/ppermute | solution.py:28
  144.1 11.2 %collective-permute-start.37 = (bf16[128,2304]{1,0:T(8,128)(2,1)S(1)}, bf16[128,2304]{1,0:T(8,128)(2,1)S(1)}, u32[]{:S(2)}, u32[]{:S(2)}) collective-permute-start(bf16[128,2304]{1,0:T(8,128)(2,1)S(1)} %get-tuple-element.86), channel_id=1, source_target_pairs={{0,4},{1,5},{2,6},{3,7},{4,8},{5,9},{6,10},{7,11},{8,12},{9,13},{1... | collective-permute-start | bytes 1769480 | tf_op jit(solution)/shard_map/ppermute | solution.py:28
  147.9 13.7 %collective-permute-start.36 = (bf16[128,2304]{1,0:T(8,128)(2,1)S(1)}, bf16[128,2304]{1,0:T(8,128)(2,1)S(1)}, u32[]{:S(2)}, u32[]{:S(2)}) collective-permute-start(bf16[128,2304]{1,0:T(8,128)(2,1)S(1)} %add_convert_fusion.1), channel_id=1, source_target_pairs={{0,4},{1,5},{2,6},{3,7},{4,8},{5,9},{6,10},{7,11},{8,12},{9,13},{1... | collective-permute-start | bytes 1769480 | tf_op jit(solution)/shard_map/ppermute | solution.py:28
  148.2 13.4 %collective-permute-start.38 = (bf16[128,2304]{1,0:T(8,128)(2,1)S(1)}, bf16[128,2304]{1,0:T(8,128)(2,1)S(1)}, u32[]{:S(2)}, u32[]{:S(2)}) collective-permute-start(bf16[128,2304]{1,0:T(8,128)(2,1)S(1)} %add_convert_fusion), channel_id=1, source_target_pairs={{0,12},{1,13},{2,14},{3,15},{4,0},{5,1},{6,2},{7,3},{8,4},{9,5},{1... | collective-permute-start | bytes 1769480 | tf_op jit(solution)/shard_map/ppermute | solution.py:28
  168.4 11.2 %collective-permute-start.40 = (f32[64,2304]{1,0:T(8,128)S(1)}, f32[64,2304]{1,0:T(8,128)S(1)}, u32[]{:S(2)}, u32[]{:S(2)}) collective-permute-start(f32[64,2304]{1,0:T(8,128)S(1)} %pad_maximum_fusion), channel_id=1, source_target_pairs={{0,1},{1,2},{2,3},{3,0},{4,5},{5,6},{6,7},{7,4},{8,9},{9,10},{10,1... | collective-permute-start | bytes 1769480 | tf_op jit(solution)/shard_map/ppermute | solution.py:28
  168.6 11.0 %collective-permute-start.42 = (f32[64,2304]{1,0:T(8,128)S(1)}, f32[64,2304]{1,0:T(8,128)}, u32[]{:S(2)}, u32[]{:S(2)}) collective-permute-start(f32[64,2304]{1,0:T(8,128)S(1)} %pad_maximum_fusion.1), channel_id=1, source_target_pairs={{0,3},{1,0},{2,1},{3,2},{4,7},{5,4},{6,5},{7,6},{8,11},{9,8},{10,9... | collective-permute-start | bytes 1769480 | tf_op jit(solution)/shard_map/ppermute | solution.py:28
  (26 other events, 282.3 us)

commit v9 on v6

--- a/solution.py
+++ b/solution.py
@@ -293,8 +293,9 @@
     for position, group in enumerate(groups):
         rows = rows_ref[RING * position : RING * position + RING].reshape(256, w_ref.shape[0])
         targets = [outs.pop(0)] if group == 0 else [outs.pop(0), outs.pop(0)]
-        for start in range(0, w_ref.shape[1], 768):
-            columns = slice(start, start + 768)
+        width = w_ref.shape[1] if len(groups) == 1 else 768
+        for start in range(0, w_ref.shape[1], width):
+            columns = slice(start, start + width)
             result = jnp.dot(rows, w_ref[:, columns], preferred_element_type=F32)
             if group == 0:
                 targets[0][:, columns] = result
@@ -329,6 +330,23 @@
     )(place, *pieces, w_out)
 
 
+def finish_kernel(rows_ref, here_ref, one_ref, two_ref, out_ref):
+    total = here_ref[...] + one_ref[...] + two_ref[...]
+    out_ref[...] = (rows_ref[...].astype(F32) + total).astype(BF16)
+
+
+def finish(rows, here, one, two):
+    vmem_spec = pl.BlockSpec(memory_space=pltpu.VMEM)
+    return pl.pallas_call(
+        finish_kernel,
+        out_shape=jax.ShapeDtypeStruct(rows.shape, BF16),
+        in_specs=[vmem_spec] * 4,
+        out_specs=vmem_spec,
+        compiler_params=pltpu.CompilerParams(vmem_limit_bytes=12 * 2**20),
+        name="finish",
+    )(rows, here, one, two)
+
+
 def body(tokens, gain, w_query, w_keyval, w_out, key_cache, value_cache, lengths):
     seqs = lengths.shape[0]
     gx, yz = lax.axis_index("gx"), lax.axis_index("yz")
@@ -342,7 +360,7 @@
     sums = row_sums(raw)
     sums = sums + send_core(sums)
     sums, cosine, sine, place, raw = lax.optimization_barrier((sums, cosine, sine, place, raw))
-    before, after = send_inner(raw, 1), send_inner(raw, -1)
+    after, before = send_inner(raw, -1), send_inner(raw, 1)
     sums = sums + send_x(sums, 1) + send_x(sums, 2) + send_x(sums, 3)
     sums, before, after = lax.optimization_barrier((sums, before, after))
     before_sums, after_sums = send_inner(sums, 1), send_inner(sums, -1)
@@ -413,8 +431,7 @@
     far_low, far_high = send_inner(two[:32], 1), send_inner(two[32:], -1)
     one = jnp.concatenate([one[:32] + far_low.astype(F32), one[32:]], 0)
     three = jnp.concatenate([three[:32], three[32:] + far_high.astype(F32)], 0)
-    branch = here + send_inner(one, 1) + send_inner(three, -1)
-    mixed = (raw.astype(F32) + branch).astype(BF16).reshape(tokens.shape)
+    mixed = finish(raw, here, send_inner(one, 1), send_inner(three, -1)).reshape(tokens.shape)
     return (mixed, new_keyval.reshape(seqs, 2, 2 * HEAD))
 
 

time: 179 us -> 179 us (level)
  transfers between devices with their start and end apart: 43 -> 43, of which waited for: 22 -> 23; matrix products, arithmetic and copies ran while one was open for 1% -> 2% of each run, Pallas kernels for 5% -> 5%
where the time goes in v9:
time: 179 us
  waiting for transfers between devices  75.5 us (42%)
  starting transfers between devices  52.3 us (29%)
  blocking collectives  25.5 us (14%)
  Pallas kernels  18.5 us (10%)
  local copies, waits for them, and re-layouts  3.63 us (2%)
  other arithmetic  2.1 us (1%)
    ppermute x34, waiting for transfers between devices, shift(): return lax.ppermute(value, ('gx', 'yz'), pairs)  73.9 us
    ppermute x34, starting transfers between devices, shift(): return lax.ppermute(value, ('gx', 'yz'), pairs)  50.2 us
    all_to_all x1, blocking collectives, body(): query = lax.all_to_all(query, 'yz', split_axis=0, concat_axis=0)  13.9 us
    all_to_all x1, blocking collectives, body(): lax.all_to_all(heads_out.reshape(16, 8, columns), 'yz', split_axis=0, con...  11.6 us
    pallas_call x2, Pallas kernels, project_query(): pl.pallas_call(functools.partial(query_kernel, pair), out_shape=[half, ha...  6.35 us
    pallas_call x2, Pallas kernels, project_output(): pl.pallas_call(functools.partial(output_kernel, groups), out_shape=shapes...  5.86 us
    pallas_call x1, Pallas kernels, attend(): pl.pallas_call(attend_kernel, out_shape=[jax.ShapeDtypeStruct((rows, colu...  4.36 us
  transfers between devices with their start and end apart: 43, of which 23 were waited for; matrix products, arithmetic and copies ran while one was open for 2% of the time, Pallas kernels for 5%

profile of v9, /device:TPU:0, one launch (start us, length us, event | category | flops | bytes accessed | tf_op | source)
XLA Modules:
  0.0 178.5 jit_solution(1220694702505790288)
XLA Ops:
  3.3 4.1 %collective-permute-start.5 = (bf16[64,2304]{1,0:T(8,128)(2,1)S(1)}, bf16[64,2304]{1,0:T(8,128)(2,1)S(1)}, u32[]{:S(2)}, u32[]{:S(2)}) collective-permute-start(bf16[64,2304]{1,0:T(8,128)(2,1)S(1)} %reshape.66.rows_ref.one_ref), channel_id=1, source_target_pairs={{0,3},{1,0},{2,1},{3,2},{4,7},{5,4},{6,5},{7,6},{8,11},{9,8},{10,9... | collective-permute-start | bytes 884744 | tf_op jit(solution)/shard_map/ppermute | solution.py:28
  11.9 3.7 %collective-permute-done.2 = f32[64,2]{1,0:T(8,128)S(1)} collective-permute-done((f32[64,2]{1,0:T(8,128)S(1)}, f32[64,2]{1,0:T(8,128)S(1)}, u32[]{:S(2)}, u32[]{:S(2)}) %collective-permute-start.2) | collective-permute-done | bytes 544 | tf_op jit(solution)/shard_map/ppermute | solution.py:28
  16.3 5.1 %collective-permute-done.6.two_sums = f32[64,2]{1,0:T(8,128)S(1)} collective-permute-done((f32[64,2]{1,0:T(8,128)S(1)}, f32[64,2]{1,0:T(8,128)S(1)}, u32[]{:S(2)}, u32[]{:S(2)}) %collective-permute-start.6) | collective-permute-done | bytes 544 | tf_op jit(solution)/shard_map/ppermute | solution.py:28
  25.9 3.7 %collective-permute-start.11 = (f32[64,2]{1,0:T(8,128)S(1)}, f32[64,2]{1,0:T(8,128)S(1)}, u32[]{:S(2)}, u32[]{:S(2)}) collective-permute-start(f32[64,2]{1,0:T(8,128)S(1)} %add_add_fusion.one_sums), channel_id=1, source_target_pairs={{0,2},{1,3},{2,0},{3,1},{4,6},{5,7},{6,4},{7,5},{8,10},{9,11},{10,... | collective-permute-start | bytes 1544 | tf_op jit(solution)/shard_map/ppermute | solution.py:28
  30.4 3.7 %collective-permute-done.11.two_sums = f32[64,2]{1,0:T(8,128)S(1)} collective-permute-done((f32[64,2]{1,0:T(8,128)S(1)}, f32[64,2]{1,0:T(8,128)S(1)}, u32[]{:S(2)}, u32[]{:S(2)}) %collective-permute-start.11) | collective-permute-done | bytes 544 | tf_op jit(solution)/shard_map/ppermute | solution.py:28
  36.2 3.2 %collective-permute-start.15 = (bf16[128,2304]{1,0:T(8,128)(2,1)S(1)}, bf16[128,2304]{1,0:T(8,128)(2,1)S(1)}, u32[]{:S(2)}, u32[]{:S(2)}) collective-permute-start(bf16[128,2304]{1,0:T(8,128)(2,1)S(1)} %normalize.3.refs_4_), channel_id=1, source_target_pairs={{0,12},{1,13},{2,14},{3,15},{4,0},{5,1},{6,2},{7,3},{8,4},{9,5},{1... | collective-permute-start | bytes 1769480 | tf_op jit(solution)/shard_map/ppermute | solution.py:28
  39.4 7.9 %collective-permute-done.13.refs_3_ = bf16[128,2304]{1,0:T(8,128)(2,1)S(1)} collective-permute-done((bf16[128,2304]{1,0:T(8,128)(2,1)S(1)}, bf16[128,2304]{1,0:T(8,128)(2,1)S(1)}, u32[]{:S(2)}, u32[]{:S(2)}) %collective-permute-start.13) | collective-permute-done | bytes 589856 | tf_op jit(solution)/shard_map/ppermute | solution.py:28
  47.3 3.2 %collective-permute-start.16 = (bf16[128,2304]{1,0:T(8,128)(2,1)S(1)}, bf16[128,2304]{1,0:T(8,128)(2,1)S(1)}, u32[]{:S(2)}, u32[]{:S(2)}) collective-permute-start(bf16[128,2304]{1,0:T(8,128)(2,1)S(1)} %collective-permute-done.15.refs_6_), channel_id=1, source_target_pairs={{0,12},{1,13},{2,14},{3,15},{4,0},{5,1},{6,2},{7,3},{8,4},{9,5},{1... | collective-permute-start | bytes 1769480 | tf_op jit(solution)/shard_map/ppermute | solution.py:28
  55.5 3.5 %collective-permute-done.18 = f32[8,512]{1,0:T(8,128)S(1)} collective-permute-done((f32[8,512]{1,0:T(8,128)S(1)}, f32[8,512]{1,0:T(8,128)S(1)}, u32[]{:S(2)}, u32[]{:S(2)}) %collective-permute-start.18) | collective-permute-done | bytes 16416 | tf_op jit(solution)/shard_map/ppermute | solution.py:28
  62.2 3.3 %query_projection.2 = (f32[256,768]{1,0:T(8,128)S(1)}, f32[256,768]{1,0:T(8,128)S(1)}) custom-call(s32[4]{0:T(128)S(1)} %pad_add_fusion.place, bf16[128,2304]{1,0:T(8,128)(2,1)S(1)} %normalize.2.rows_ref.refs_0_, bf16[128,2304]{1,0:T(8,128)(2,1)S(1)} %collective-permute-done.7.refs_1_, bf16[128,2304]{1,0:T(8,128)(2,1)S(1)} %collective-permute-done.8.refs_2_, ...), custom_call_target="tpu_custom_call" | custom-call | flops 1811939328 | bytes 8388608 | tf_op jit(solution)/shard_map/query_projection/pallas_call | solution.py:159
  67.2 4.3 %collective-permute-start.25 = (f32[128,768]{1,0:T(8,128)S(1)}, f32[128,768]{1,0:T(8,128)S(1)}, u32[]{:S(2)}, u32[]{:S(2)}) collective-permute-start(f32[128,768]{1,0:T(8,128)S(1)} %get-tuple-element.98), channel_id=1, source_target_pairs={{0,96},{1,97},{2,98},{3,99},{4,100},{5,101},{6,102},{7,103},{8,104... | collective-permute-start | bytes 1179656 | tf_op jit(solution)/shard_map/ppermute | solution.py:28
  71.6 6.1 %collective-permute-done.22 = f32[128,768]{1,0:T(8,128)S(1)} collective-permute-done((f32[128,768]{1,0:T(8,128)S(1)}, f32[128,768]{1,0:T(8,128)S(1)}, u32[]{:S(2)}, u32[]{:S(2)}) %collective-permute-start.22) | collective-permute-done | bytes 393248 | tf_op jit(solution)/shard_map/ppermute | solution.py:28
  77.8 9.0 %collective-permute-done.24 = f32[128,768]{1,0:T(8,128)S(1)} collective-permute-done((f32[128,768]{1,0:T(8,128)S(1)}, f32[128,768]{1,0:T(8,128)S(1)}, u32[]{:S(2)}, u32[]{:S(2)}) %collective-permute-start.24) | collective-permute-done | bytes 393248 | tf_op jit(solution)/shard_map/ppermute | solution.py:28
  86.9 13.9 %all_to_all.10 = bf16[16,8,768]{2,1,0:T(8,128)(2,1)S(1)} all-to-all(bf16[16,8,768]{2,1,0:T(8,128)(2,1)S(1)} %fusion.2), channel_id=1, replica_groups=mesh['gx'=8,'yz'=16] {'yz'}, dimensions={0} | all-to-all | bytes 393216 | tf_op jit(solution)/shard_map/all_to_all | solution.py:405
  100.8 4.4 %attention.1 = (bf16[128,768]{1,0:T(8,128)(2,1)S(1)}, bf16[8,512]{1,0:T(8,128)(2,1)S(1)}) custom-call(s32[4]{0:T(128)S(1)} %copy-done.5, bf16[128,768]{1,0:T(8,128)(2,1)S(1)} %bitcast.14, f32[8,128]{1,0:T(8,128)S(1)} %get-tuple-element.76.cos_ref, f32[8,128]{1,0:T(8,128)S(1)} %get-tuple-element.77.sin_ref, ...), custom_call_target="tpu_custom_call" | custom-call | flops 805306368 | bytes 8388608 | tf_op jit(solution)/shard_map/attention/pallas_call | solution.py:256
  105.2 11.6 %all_to_all.11 = bf16[16,8,768]{2,1,0:T(8,128)(2,1)S(1)} all-to-all(bf16[16,8,768]{2,1,0:T(8,128)(2,1)S(1)} %bitcast.15), channel_id=1, replica_groups=mesh['gx'=8,'yz'=16] {'yz'}, dimensions={0} | all-to-all | bytes 393216 | tf_op jit(solution)/shard_map/all_to_all | solution.py:410
  120.0 3.6 %collective-permute-done.26.refs_1_ = bf16[128,768]{1,0:T(8,128)(2,1)S(1)} collective-permute-done((bf16[128,768]{1,0:T(8,128)(2,1)S(1)}, bf16[128,768]{1,0:T(8,128)(2,1)S(1)}, u32[]{:S(2)}, u32[]{:S(2)}) %collective-permute-start.26) | collective-permute-done | bytes 196640 | tf_op jit(solution)/shard_map/ppermute | solution.py:28
  125.2 5.3 %collective-permute-done.28.refs_3_ = bf16[128,768]{1,0:T(8,128)(2,1)S(1)} collective-permute-done((bf16[128,768]{1,0:T(8,128)(2,1)S(1)}, bf16[128,768]{1,0:T(8,128)(2,1)S(1)}, u32[]{:S(2)}, u32[]{:S(2)}) %collective-permute-start.28) | collective-permute-done | bytes 196640 | tf_op jit(solution)/shard_map/ppermute | solution.py:28
  137.1 4.1 %output_projection.2 = (f32[128,2304]{1,0:T(8,128)S(1)}, bf16[128,2304]{1,0:T(8,128)(2,1)S(1)}, bf16[128,2304]{1,0:T(8,128)(2,1)S(1)}, f32[128,2304]{1,0:T(8,128)S(1)}, f32[256,2304]{1,0:T(8,128)S(1)}) custom-call(s32[4]{0:T(128)S(1)} %pad_add_fusion.place, bf16[128,768]{1,0:T(8,128)(2,1)S(1)} %bitcast.13, ...), custom_call_target="tpu_custom_call" | custom-call | flops 2717908992 | bytes 8388608 | tf_op jit(solution)/shard_map/output_projection/pallas_call | solution.py:317
  145.3 3.2 %collective-permute-start.38 = (bf16[128,2304]{1,0:T(8,128)(2,1)S(1)}, bf16[128,2304]{1,0:T(8,128)(2,1)S(1)}, u32[]{:S(2)}, u32[]{:S(2)}) collective-permute-start(bf16[128,2304]{1,0:T(8,128)(2,1)S(1)} %add_convert_fusion), channel_id=1, source_target_pairs={{0,12},{1,13},{2,14},{3,15},{4,0},{5,1},{6,2},{7,3},{8,4},{9,5},{1... | collective-permute-start | bytes 1769480 | tf_op jit(solution)/shard_map/ppermute | solution.py:28
  152.4 6.3 %collective-permute-done.36 = bf16[128,2304]{1,0:T(8,128)(2,1)S(1)} collective-permute-done((bf16[128,2304]{1,0:T(8,128)(2,1)S(1)}, bf16[128,2304]{1,0:T(8,128)(2,1)S(1)}, u32[]{:S(2)}, u32[]{:S(2)}) %collective-permute-start.36) | collective-permute-done | bytes 589856 | tf_op jit(solution)/shard_map/ppermute | solution.py:28
  162.4 3.1 %collective-permute-done.39 = bf16[32,2304]{1,0:T(8,128)(2,1)S(1)} collective-permute-done((bf16[32,2304]{1,0:T(8,128)(2,1)S(1)}, bf16[32,2304]{1,0:T(8,128)(2,1)S(1)}, u32[]{:S(2)}, u32[]{:S(2)}) %collective-permute-start.39) | collective-permute-done | bytes 147488 | tf_op jit(solution)/shard_map/ppermute | solution.py:28
  166.6 3.2 %collective-permute-start.42 = (f32[64,2304]{1,0:T(8,128)}, f32[64,2304]{1,0:T(8,128)S(1)}, u32[]{:S(2)}, u32[]{:S(2)}) collective-permute-start(f32[64,2304]{1,0:T(8,128)} %pad_maximum_fusion.1), channel_id=1, source_target_pairs={{0,3},{1,0},{2,1},{3,2},{4,7},{5,4},{6,5},{7,6},{8,11},{9,8},{10,9... | collective-permute-start | bytes 1769480 | tf_op jit(solution)/shard_map/ppermute | solution.py:28
  170.5 6.3 %collective-permute-done.40.one_ref = f32[64,2304]{1,0:T(8,128)S(1)} collective-permute-done((f32[64,2304]{1,0:T(8,128)S(1)}, f32[64,2304]{1,0:T(8,128)S(1)}, u32[]{:S(2)}, u32[]{:S(2)}) %collective-permute-start.40) | collective-permute-done | bytes 589856 | tf_op jit(solution)/shard_map/ppermute | solution.py:28
  (117 shorter events, 51.7 us)
Async XLA Ops:
  3.3 12.8 %collective-permute-start.5 = (bf16[64,2304]{1,0:T(8,128)(2,1)S(1)}, bf16[64,2304]{1,0:T(8,128)(2,1)S(1)}, u32[]{:S(2)}, u32[]{:S(2)}) collective-permute-start(bf16[64,2304]{1,0:T(8,128)(2,1)S(1)} %reshape.66.rows_ref.one_ref), channel_id=1, source_target_pairs={{0,3},{1,0},{2,1},{3,2},{4,7},{5,4},{6,5},{7,6},{8,11},{9,8},{10,9... | collective-permute-start | bytes 884744 | tf_op jit(solution)/shard_map/ppermute | solution.py:28
  7.4 8.7 %collective-permute-start.4 = (bf16[64,2304]{1,0:T(8,128)(2,1)S(1)}, bf16[64,2304]{1,0:T(8,128)(2,1)S(1)}, u32[]{:S(2)}, u32[]{:S(2)}) collective-permute-start(bf16[64,2304]{1,0:T(8,128)(2,1)S(1)} %reshape.66.rows_ref.one_ref), channel_id=1, source_target_pairs={{0,1},{1,2},{2,3},{3,0},{4,5},{5,6},{6,7},{7,4},{8,9},{9,10},{10,1... | collective-permute-start | bytes 884744 | tf_op jit(solution)/shard_map/ppermute | solution.py:28
  21.7 13.7 %collective-permute-start.8 = (bf16[128,2304]{1,0:T(8,128)(2,1)S(1)}, bf16[128,2304]{1,0:T(8,128)(2,1)S(1)}, u32[]{:S(2)}, u32[]{:S(2)}) collective-permute-start(bf16[128,2304]{1,0:T(8,128)(2,1)S(1)} %normalize.2.rows_ref.refs_0_), channel_id=1, source_target_pairs={{0,12},{1,13},{2,14},{3,15},{4,0},{5,1},{6,2},{7,3},{8,4},{9,5},{1... | collective-permute-start | bytes 1769480 | tf_op jit(solution)/shard_map/ppermute | solution.py:28
  24.7 11.4 %collective-permute-start.7 = (bf16[128,2304]{1,0:T(8,128)(2,1)S(1)}, bf16[128,2304]{1,0:T(8,128)(2,1)S(1)}, u32[]{:S(2)}, u32[]{:S(2)}) collective-permute-start(bf16[128,2304]{1,0:T(8,128)(2,1)S(1)} %normalize.2.rows_ref.refs_0_), channel_id=1, source_target_pairs={{0,4},{1,5},{2,6},{3,7},{4,8},{5,9},{6,10},{7,11},{8,12},{9,13},{1... | collective-permute-start | bytes 1769480 | tf_op jit(solution)/shard_map/ppermute | solution.py:28
  24.7 10.3 %collective-permute-start.9 = (bf16[64,2304]{1,0:T(8,128)(2,1)S(1)}, bf16[64,2304]{1,0:T(8,128)(2,1)S(1)}, u32[]{:S(2)}, u32[]{:S(2)}) collective-permute-start(bf16[64,2304]{1,0:T(8,128)(2,1)S(1)} %collective-permute-done.4.two_ref), channel_id=1, source_target_pairs={{0,1},{1,2},{2,3},{3,0},{4,5},{5,6},{6,7},{7,4},{8,9},{9,10},{10,1... | collective-permute-start | bytes 884744 | tf_op jit(solution)/shard_map/ppermute | solution.py:28
  25.9 8.2 %collective-permute-start.11 = (f32[64,2]{1,0:T(8,128)S(1)}, f32[64,2]{1,0:T(8,128)S(1)}, u32[]{:S(2)}, u32[]{:S(2)}) collective-permute-start(f32[64,2]{1,0:T(8,128)S(1)} %add_add_fusion.one_sums), channel_id=1, source_target_pairs={{0,2},{1,3},{2,0},{3,1},{4,6},{5,7},{6,4},{7,5},{8,10},{9,11},{10,... | collective-permute-start | bytes 1544 | tf_op jit(solution)/shard_map/ppermute | solution.py:28
  36.2 11.1 %collective-permute-start.13 = (bf16[128,2304]{1,0:T(8,128)(2,1)S(1)}, bf16[128,2304]{1,0:T(8,128)(2,1)S(1)}, u32[]{:S(2)}, u32[]{:S(2)}) collective-permute-start(bf16[128,2304]{1,0:T(8,128)(2,1)S(1)} %collective-permute-done.7.refs_1_), channel_id=1, source_target_pairs={{0,4},{1,5},{2,6},{3,7},{4,8},{5,9},{6,10},{7,11},{8,12},{9,13},{1... | collective-permute-start | bytes 1769480 | tf_op jit(solution)/shard_map/ppermute | solution.py:28
  36.2 11.1 %collective-permute-start.15 = (bf16[128,2304]{1,0:T(8,128)(2,1)S(1)}, bf16[128,2304]{1,0:T(8,128)(2,1)S(1)}, u32[]{:S(2)}, u32[]{:S(2)}) collective-permute-start(bf16[128,2304]{1,0:T(8,128)(2,1)S(1)} %normalize.3.refs_4_), channel_id=1, source_target_pairs={{0,12},{1,13},{2,14},{3,15},{4,0},{5,1},{6,2},{7,3},{8,4},{9,5},{1... | collective-permute-start | bytes 1769480 | tf_op jit(solution)/shard_map/ppermute | solution.py:28
  47.3 11.7 %collective-permute-start.14 = (bf16[128,2304]{1,0:T(8,128)(2,1)S(1)}, bf16[128,2304]{1,0:T(8,128)(2,1)S(1)}, u32[]{:S(2)}, u32[]{:S(2)}) collective-permute-start(bf16[128,2304]{1,0:T(8,128)(2,1)S(1)} %normalize.3.refs_4_), channel_id=1, source_target_pairs={{0,4},{1,5},{2,6},{3,7},{4,8},{5,9},{6,10},{7,11},{8,12},{9,13},{1... | collective-permute-start | bytes 1769480 | tf_op jit(solution)/shard_map/ppermute | solution.py:28
  47.3 11.7 %collective-permute-start.16 = (bf16[128,2304]{1,0:T(8,128)(2,1)S(1)}, bf16[128,2304]{1,0:T(8,128)(2,1)S(1)}, u32[]{:S(2)}, u32[]{:S(2)}) collective-permute-start(bf16[128,2304]{1,0:T(8,128)(2,1)S(1)} %collective-permute-done.15.refs_6_), channel_id=1, source_target_pairs={{0,12},{1,13},{2,14},{3,15},{4,0},{5,1},{6,2},{7,3},{8,4},{9,5},{1... | collective-permute-start | bytes 1769480 | tf_op jit(solution)/shard_map/ppermute | solution.py:28
  66.2 11.4 %collective-permute-start.22 = (f32[128,768]{1,0:T(8,128)S(1)}, f32[128,768]{1,0:T(8,128)S(1)}, u32[]{:S(2)}, u32[]{:S(2)}) collective-permute-start(f32[128,768]{1,0:T(8,128)S(1)} %get-tuple-element.97), channel_id=1, source_target_pairs={{0,32},{1,33},{2,34},{3,35},{4,36},{5,37},{6,38},{7,39},{8,40},{9,... | collective-permute-start | bytes 1179656 | tf_op jit(solution)/shard_map/ppermute | solution.py:28
  67.2 10.6 %collective-permute-start.25 = (f32[128,768]{1,0:T(8,128)S(1)}, f32[128,768]{1,0:T(8,128)S(1)}, u32[]{:S(2)}, u32[]{:S(2)}) collective-permute-start(f32[128,768]{1,0:T(8,128)S(1)} %get-tuple-element.98), channel_id=1, source_target_pairs={{0,96},{1,97},{2,98},{3,99},{4,100},{5,101},{6,102},{7,103},{8,104... | collective-permute-start | bytes 1179656 | tf_op jit(solution)/shard_map/ppermute | solution.py:28
  77.8 9.1 %collective-permute-start.24 = (f32[128,768]{1,0:T(8,128)S(1)}, f32[128,768]{1,0:T(8,128)S(1)}, u32[]{:S(2)}, u32[]{:S(2)}) collective-permute-start(f32[128,768]{1,0:T(8,128)S(1)} %slice_add_fusion), channel_id=1, source_target_pairs={{0,32},{1,33},{2,34},{3,35},{4,36},{5,37},{6,38},{7,39},{8,40},{9,... | collective-permute-start | bytes 1179656 | tf_op jit(solution)/shard_map/ppermute | solution.py:28
  117.7 7.5 %collective-permute-start.27 = (bf16[128,768]{1,0:T(8,128)(2,1)S(1)}, bf16[128,768]{1,0:T(8,128)(2,1)S(1)}, u32[]{:S(2)}, u32[]{:S(2)}) collective-permute-start(bf16[128,768]{1,0:T(8,128)(2,1)S(1)} %bitcast.10), channel_id=1, source_target_pairs={{0,96},{1,97},{2,98},{3,99},{4,100},{5,101},{6,102},{7,103},{8,104... | collective-permute-start | bytes 589832 | tf_op jit(solution)/shard_map/ppermute | solution.py:28
  123.6 6.9 %collective-permute-start.29 = (bf16[128,768]{1,0:T(8,128)(2,1)S(1)}, bf16[128,768]{1,0:T(8,128)(2,1)S(1)}, u32[]{:S(2)}, u32[]{:S(2)}) collective-permute-start(bf16[128,768]{1,0:T(8,128)(2,1)S(1)} %bitcast.11), channel_id=1, source_target_pairs={{0,16},{16,0},{32,48},{48,32},{64,80},{80,64},{96,112},{112,96},{1... | collective-permute-start | bytes 589832 | tf_op jit(solution)/shard_map/ppermute | solution.py:33
  123.6 6.9 %collective-permute-start.30 = (bf16[128,768]{1,0:T(8,128)(2,1)S(1)}, bf16[128,768]{1,0:T(8,128)(2,1)S(1)}, u32[]{:S(2)}, u32[]{:S(2)}) collective-permute-start(bf16[128,768]{1,0:T(8,128)(2,1)S(1)} %collective-permute-done.26.refs_1_), channel_id=1, source_target_pairs={{0,16},{16,0},{32,48},{48,32},{64,80},{80,64},{96,112},{112,96},{1... | collective-permute-start | bytes 589832 | tf_op jit(solution)/shard_map/ppermute | solution.py:33
  133.7 11.2 %collective-permute-start.34 = (bf16[128,2304]{1,0:T(8,128)(2,1)S(1)}, bf16[128,2304]{1,0:T(8,128)(2,1)S(1)}, u32[]{:S(2)}, u32[]{:S(2)}) collective-permute-start(bf16[128,2304]{1,0:T(8,128)(2,1)S(1)} %get-tuple-element.83), channel_id=1, source_target_pairs={{0,4},{1,5},{2,6},{3,7},{4,8},{5,9},{6,10},{7,11},{8,12},{9,13},{1... | collective-permute-start | bytes 1769480 | tf_op jit(solution)/shard_map/ppermute | solution.py:28
  134.3 10.7 %collective-permute-start.35 = (bf16[128,2304]{1,0:T(8,128)(2,1)S(1)}, bf16[128,2304]{1,0:T(8,128)(2,1)S(1)}, u32[]{:S(2)}, u32[]{:S(2)}) collective-permute-start(bf16[128,2304]{1,0:T(8,128)(2,1)S(1)} %get-tuple-element.84), channel_id=1, source_target_pairs={{0,12},{1,13},{2,14},{3,15},{4,0},{5,1},{6,2},{7,3},{8,4},{9,5},{1... | collective-permute-start | bytes 1769480 | tf_op jit(solution)/shard_map/ppermute | solution.py:28
  141.1 10.0 %collective-permute-start.33 = (bf16[128,2304]{1,0:T(8,128)(2,1)S(1)}, bf16[128,2304]{1,0:T(8,128)(2,1)S(1)}, u32[]{:S(2)}, u32[]{:S(2)}) collective-permute-start(bf16[128,2304]{1,0:T(8,128)(2,1)S(1)} %get-tuple-element.81), channel_id=1, source_target_pairs={{0,12},{1,13},{2,14},{3,15},{4,0},{5,1},{6,2},{7,3},{8,4},{9,5},{1... | collective-permute-start | bytes 1769480 | tf_op jit(solution)/shard_map/ppermute | solution.py:28
  141.2 11.2 %collective-permute-start.37 = (bf16[128,2304]{1,0:T(8,128)(2,1)S(1)}, bf16[128,2304]{1,0:T(8,128)(2,1)S(1)}, u32[]{:S(2)}, u32[]{:S(2)}) collective-permute-start(bf16[128,2304]{1,0:T(8,128)(2,1)S(1)} %get-tuple-element.86), channel_id=1, source_target_pairs={{0,4},{1,5},{2,6},{3,7},{4,8},{5,9},{6,10},{7,11},{8,12},{9,13},{1... | collective-permute-start | bytes 1769480 | tf_op jit(solution)/shard_map/ppermute | solution.py:28
  145.0 13.7 %collective-permute-start.36 = (bf16[128,2304]{1,0:T(8,128)(2,1)S(1)}, bf16[128,2304]{1,0:T(8,128)(2,1)S(1)}, u32[]{:S(2)}, u32[]{:S(2)}) collective-permute-start(bf16[128,2304]{1,0:T(8,128)(2,1)S(1)} %add_convert_fusion.1), channel_id=1, source_target_pairs={{0,4},{1,5},{2,6},{3,7},{4,8},{5,9},{6,10},{7,11},{8,12},{9,13},{1... | collective-permute-start | bytes 1769480 | tf_op jit(solution)/shard_map/ppermute | solution.py:28
  145.3 13.4 %collective-permute-start.38 = (bf16[128,2304]{1,0:T(8,128)(2,1)S(1)}, bf16[128,2304]{1,0:T(8,128)(2,1)S(1)}, u32[]{:S(2)}, u32[]{:S(2)}) collective-permute-start(bf16[128,2304]{1,0:T(8,128)(2,1)S(1)} %add_convert_fusion), channel_id=1, source_target_pairs={{0,12},{1,13},{2,14},{3,15},{4,0},{5,1},{6,2},{7,3},{8,4},{9,5},{1... | collective-permute-start | bytes 1769480 | tf_op jit(solution)/shard_map/ppermute | solution.py:28
  165.6 11.2 %collective-permute-start.40 = (f32[64,2304]{1,0:T(8,128)S(1)}, f32[64,2304]{1,0:T(8,128)S(1)}, u32[]{:S(2)}, u32[]{:S(2)}) collective-permute-start(f32[64,2304]{1,0:T(8,128)S(1)} %pad_maximum_fusion), channel_id=1, source_target_pairs={{0,1},{1,2},{2,3},{3,0},{4,5},{5,6},{6,7},{7,4},{8,9},{9,10},{10,1... | collective-permute-start | bytes 1769480 | tf_op jit(solution)/shard_map/ppermute | solution.py:28
  166.6 10.9 %collective-permute-start.42 = (f32[64,2304]{1,0:T(8,128)}, f32[64,2304]{1,0:T(8,128)S(1)}, u32[]{:S(2)}, u32[]{:S(2)}) collective-permute-start(f32[64,2304]{1,0:T(8,128)} %pad_maximum_fusion.1), channel_id=1, source_target_pairs={{0,3},{1,0},{2,1},{3,2},{4,7},{5,4},{6,5},{7,6},{8,11},{9,8},{10,9... | collective-permute-start | bytes 1769480 | tf_op jit(solution)/shard_map/ppermute | solution.py:28
  (26 other events, 284.4 us)

commit v10 on v9

--- a/solution.py
+++ b/solution.py
@@ -360,12 +360,13 @@
     sums = row_sums(raw)
     sums = sums + send_core(sums)
     sums, cosine, sine, place, raw = lax.optimization_barrier((sums, cosine, sine, place, raw))
-    after, before = send_inner(raw, -1), send_inner(raw, 1)
+    before = send_inner(raw, 1)
     sums = sums + send_x(sums, 1) + send_x(sums, 2) + send_x(sums, 3)
-    sums, before, after = lax.optimization_barrier((sums, before, after))
-    before_sums, after_sums = send_inner(sums, 1), send_inner(sums, -1)
-    before, before_sums = lax.optimization_barrier((before, before_sums))
-    far, far_sums = send_inner(before, 1), send_inner(sums, 2)
+    before_sums, after_sums, far_sums = (send_inner(sums, step) for step in (1, -1, 2))
+    before_sums, after_sums, far_sums, before, raw = lax.optimization_barrier(
+        (before_sums, after_sums, far_sums, before, raw)
+    )
+    after, far = send_inner(raw, -1), send_inner(before, 1)
     scale = gain.reshape(1, features)
     near = normalize(raw, before, sums, before_sums, scale)
     wide = normalize(after, far, after_sums, far_sums, scale)

time: 179 us -> 181 us (1.011)
  no operation moved by 1% of the time
where the time goes in v10:
time: 181 us
  waiting for transfers between devices  76.8 us (42%)
  starting transfers between devices  53.8 us (30%)
  blocking collectives  24.9 us (14%)
  Pallas kernels  18.5 us (10%)
  local copies, waits for them, and re-layouts  3.63 us (2%)
  other arithmetic  2.1 us (1%)
    ppermute x34, waiting for transfers between devices, shift(): return lax.ppermute(value, ('gx', 'yz'), pairs)  74 us
    ppermute x34, starting transfers between devices, shift(): return lax.ppermute(value, ('gx', 'yz'), pairs)  51.6 us
    all_to_all x1, blocking collectives, body(): query = lax.all_to_all(query, 'yz', split_axis=0, concat_axis=0)  13.3 us
    all_to_all x1, blocking collectives, body(): lax.all_to_all(heads_out.reshape(16, 8, columns), 'yz', split_axis=0, con...  11.6 us
    pallas_call x2, Pallas kernels, project_query(): pl.pallas_call(functools.partial(query_kernel, pair), out_shape=[half, ha...  6.35 us
    pallas_call x2, Pallas kernels, project_output(): pl.pallas_call(functools.partial(output_kernel, groups), out_shape=shapes...  5.86 us
    pallas_call x1, Pallas kernels, attend(): pl.pallas_call(attend_kernel, out_shape=[jax.ShapeDtypeStruct((rows, colu...  4.36 us
  transfers between devices with their start and end apart: 43, of which 23 were waited for; matrix products, arithmetic and copies ran while one was open for 2% of the time, Pallas kernels for 5%

profile of v10, /device:TPU:0, one launch (start us, length us, event | category | flops | bytes accessed | tf_op | source)
XLA Modules:
  0.0 180.7 jit_solution(1240250025209052860)
XLA Ops:
  9.8 3.7 %collective-permute-done.2 = f32[64,2]{1,0:T(8,128)S(1)} collective-permute-done((f32[64,2]{1,0:T(8,128)S(1)}, f32[64,2]{1,0:T(8,128)S(1)}, u32[]{:S(2)}, u32[]{:S(2)}) %collective-permute-start.2) | collective-permute-done | bytes 544 | tf_op jit(solution)/shard_map/ppermute | solution.py:28
  14.0 3.7 %collective-permute-start.6 = (f32[64,2]{1,0:T(8,128)S(1)}, f32[64,2]{1,0:T(8,128)S(1)}, u32[]{:S(2)}, u32[]{:S(2)}) collective-permute-start(f32[64,2]{1,0:T(8,128)S(1)} %add_add_fusion.one_sums), channel_id=1, source_target_pairs={{0,2},{1,3},{2,0},{3,1},{4,6},{5,7},{6,4},{7,5},{8,10},{9,11},{10,... | collective-permute-start | bytes 1544 | tf_op jit(solution)/shard_map/ppermute | solution.py:28
  27.2 3.2 %collective-permute-start.10 = (bf16[64,2304]{1,0:T(8,128)(2,1)S(1)}, bf16[64,2304]{1,0:T(8,128)(2,1)S(1)}, u32[]{:S(2)}, u32[]{:S(2)}) collective-permute-start(bf16[64,2304]{1,0:T(8,128)(2,1)S(1)} %reshape.66.rows_ref.one_ref), channel_id=1, source_target_pairs={{0,3},{1,0},{2,1},{3,2},{4,7},{5,4},{6,5},{7,6},{8,11},{9,8},{10,9... | collective-permute-start | bytes 884744 | tf_op jit(solution)/shard_map/ppermute | solution.py:28
  32.9 4.4 %collective-permute-done.11.two_ref = bf16[64,2304]{1,0:T(8,128)(2,1)S(1)} collective-permute-done((bf16[64,2304]{1,0:T(8,128)(2,1)S(1)}, bf16[64,2304]{1,0:T(8,128)(2,1)S(1)}, u32[]{:S(2)}, u32[]{:S(2)}) %collective-permute-start.11) | collective-permute-done | bytes 294944 | tf_op jit(solution)/shard_map/ppermute | solution.py:28
  38.3 3.2 %collective-permute-start.15 = (bf16[128,2304]{1,0:T(8,128)(2,1)S(1)}, bf16[128,2304]{1,0:T(8,128)(2,1)S(1)}, u32[]{:S(2)}, u32[]{:S(2)}) collective-permute-start(bf16[128,2304]{1,0:T(8,128)(2,1)S(1)} %normalize.3.refs_4_), channel_id=1, source_target_pairs={{0,12},{1,13},{2,14},{3,15},{4,0},{5,1},{6,2},{7,3},{8,4},{9,5},{1... | collective-permute-start | bytes 1769480 | tf_op jit(solution)/shard_map/ppermute | solution.py:28
  41.5 7.9 %collective-permute-done.13.refs_3_ = bf16[128,2304]{1,0:T(8,128)(2,1)S(1)} collective-permute-done((bf16[128,2304]{1,0:T(8,128)(2,1)S(1)}, bf16[128,2304]{1,0:T(8,128)(2,1)S(1)}, u32[]{:S(2)}, u32[]{:S(2)}) %collective-permute-start.13) | collective-permute-done | bytes 589856 | tf_op jit(solution)/shard_map/ppermute | solution.py:28
  49.4 3.2 %collective-permute-start.16 = (bf16[128,2304]{1,0:T(8,128)(2,1)S(1)}, bf16[128,2304]{1,0:T(8,128)(2,1)S(1)}, u32[]{:S(2)}, u32[]{:S(2)}) collective-permute-start(bf16[128,2304]{1,0:T(8,128)(2,1)S(1)} %collective-permute-done.15.refs_6_), channel_id=1, source_target_pairs={{0,12},{1,13},{2,14},{3,15},{4,0},{5,1},{6,2},{7,3},{8,4},{9,5},{1... | collective-permute-start | bytes 1769480 | tf_op jit(solution)/shard_map/ppermute | solution.py:28
  52.6 3.2 %collective-permute-start.19 = (f32[8,512]{1,0:T(8,128)S(1)}, f32[8,512]{1,0:T(8,128)S(1)}, u32[]{:S(2)}, u32[]{:S(2)}) collective-permute-start(f32[8,512]{1,0:T(8,128)S(1)} %get-tuple-element.102), channel_id=1, source_target_pairs={{0,96},{1,97},{2,98},{3,99},{4,100},{5,101},{6,102},{7,103},{8,104... | collective-permute-start | bytes 49160 | tf_op jit(solution)/shard_map/ppermute | solution.py:28
  57.6 3.5 %collective-permute-done.18 = f32[8,512]{1,0:T(8,128)S(1)} collective-permute-done((f32[8,512]{1,0:T(8,128)S(1)}, f32[8,512]{1,0:T(8,128)S(1)}, u32[]{:S(2)}, u32[]{:S(2)}) %collective-permute-start.18) | collective-permute-done | bytes 16416 | tf_op jit(solution)/shard_map/ppermute | solution.py:28
  64.3 3.3 %query_projection.2 = (f32[256,768]{1,0:T(8,128)S(1)}, f32[256,768]{1,0:T(8,128)S(1)}) custom-call(s32[4]{0:T(128)S(1)} %pad_add_fusion.place, bf16[128,2304]{1,0:T(8,128)(2,1)S(1)} %normalize.2.rows_ref.refs_0_, bf16[128,2304]{1,0:T(8,128)(2,1)S(1)} %collective-permute-done.8.refs_1_, bf16[128,2304]{1,0:T(8,128)(2,1)S(1)} %collective-permute-done.9.refs_2_, ...), custom_call_target="tpu_custom_call" | custom-call | flops 1811939328 | bytes 8388608 | tf_op jit(solution)/shard_map/query_projection/pallas_call | solution.py:159
  69.2 4.4 %collective-permute-start.25 = (f32[128,768]{1,0:T(8,128)S(1)}, f32[128,768]{1,0:T(8,128)S(1)}, u32[]{:S(2)}, u32[]{:S(2)}) collective-permute-start(f32[128,768]{1,0:T(8,128)S(1)} %get-tuple-element.98), channel_id=1, source_target_pairs={{0,96},{1,97},{2,98},{3,99},{4,100},{5,101},{6,102},{7,103},{8,104... | collective-permute-start | bytes 1179656 | tf_op jit(solution)/shard_map/ppermute | solution.py:28
  73.8 6.7 %collective-permute-done.22 = f32[128,768]{1,0:T(8,128)S(1)} collective-permute-done((f32[128,768]{1,0:T(8,128)S(1)}, f32[128,768]{1,0:T(8,128)S(1)}, u32[]{:S(2)}, u32[]{:S(2)}) %collective-permute-start.22) | collective-permute-done | bytes 393248 | tf_op jit(solution)/shard_map/ppermute | solution.py:28
  80.6 9.0 %collective-permute-done.24 = f32[128,768]{1,0:T(8,128)S(1)} collective-permute-done((f32[128,768]{1,0:T(8,128)S(1)}, f32[128,768]{1,0:T(8,128)S(1)}, u32[]{:S(2)}, u32[]{:S(2)}) %collective-permute-start.24) | collective-permute-done | bytes 393248 | tf_op jit(solution)/shard_map/ppermute | solution.py:28
  89.6 13.3 %all_to_all.10 = bf16[16,8,768]{2,1,0:T(8,128)(2,1)S(1)} all-to-all(bf16[16,8,768]{2,1,0:T(8,128)(2,1)S(1)} %fusion.2), channel_id=1, replica_groups=mesh['gx'=8,'yz'=16] {'yz'}, dimensions={0} | all-to-all | bytes 393216 | tf_op jit(solution)/shard_map/all_to_all | solution.py:406
  103.0 4.4 %attention.1 = (bf16[128,768]{1,0:T(8,128)(2,1)S(1)}, bf16[8,512]{1,0:T(8,128)(2,1)S(1)}) custom-call(s32[4]{0:T(128)S(1)} %copy-done.5, bf16[128,768]{1,0:T(8,128)(2,1)S(1)} %bitcast.14, f32[8,128]{1,0:T(8,128)S(1)} %get-tuple-element.76.cos_ref, f32[8,128]{1,0:T(8,128)S(1)} %get-tuple-element.77.sin_ref, ...), custom_call_target="tpu_custom_call" | custom-call | flops 805306368 | bytes 8388608 | tf_op jit(solution)/shard_map/attention/pallas_call | solution.py:256
  107.3 11.6 %all_to_all.11 = bf16[16,8,768]{2,1,0:T(8,128)(2,1)S(1)} all-to-all(bf16[16,8,768]{2,1,0:T(8,128)(2,1)S(1)} %bitcast.15), channel_id=1, replica_groups=mesh['gx'=8,'yz'=16] {'yz'}, dimensions={0} | all-to-all | bytes 393216 | tf_op jit(solution)/shard_map/all_to_all | solution.py:411
  118.9 3.2 %collective-permute-start.27 = (bf16[128,768]{1,0:T(8,128)(2,1)S(1)}, bf16[128,768]{1,0:T(8,128)(2,1)S(1)}, u32[]{:S(2)}, u32[]{:S(2)}) collective-permute-start(bf16[128,768]{1,0:T(8,128)(2,1)S(1)} %bitcast.10), channel_id=1, source_target_pairs={{0,96},{1,97},{2,98},{3,99},{4,100},{5,101},{6,102},{7,103},{8,104... | collective-permute-start | bytes 589832 | tf_op jit(solution)/shard_map/ppermute | solution.py:28
  122.2 3.6 %collective-permute-done.26.refs_1_ = bf16[128,768]{1,0:T(8,128)(2,1)S(1)} collective-permute-done((bf16[128,768]{1,0:T(8,128)(2,1)S(1)}, bf16[128,768]{1,0:T(8,128)(2,1)S(1)}, u32[]{:S(2)}, u32[]{:S(2)}) %collective-permute-start.26) | collective-permute-done | bytes 196640 | tf_op jit(solution)/shard_map/ppermute | solution.py:28
  126.3 6.4 %collective-permute-done.28.refs_3_ = bf16[128,768]{1,0:T(8,128)(2,1)S(1)} collective-permute-done((bf16[128,768]{1,0:T(8,128)(2,1)S(1)}, bf16[128,768]{1,0:T(8,128)(2,1)S(1)}, u32[]{:S(2)}, u32[]{:S(2)}) %collective-permute-start.28) | collective-permute-done | bytes 196640 | tf_op jit(solution)/shard_map/ppermute | solution.py:28
  139.2 4.1 %output_projection.2 = (f32[128,2304]{1,0:T(8,128)S(1)}, bf16[128,2304]{1,0:T(8,128)(2,1)S(1)}, bf16[128,2304]{1,0:T(8,128)(2,1)S(1)}, f32[128,2304]{1,0:T(8,128)S(1)}, f32[256,2304]{1,0:T(8,128)S(1)}) custom-call(s32[4]{0:T(128)S(1)} %pad_add_fusion.place, bf16[128,768]{1,0:T(8,128)(2,1)S(1)} %bitcast.13, ...), custom_call_target="tpu_custom_call" | custom-call | flops 2717908992 | bytes 8388608 | tf_op jit(solution)/shard_map/output_projection/pallas_call | solution.py:317
  147.5 3.2 %collective-permute-start.38 = (bf16[128,2304]{1,0:T(8,128)(2,1)S(1)}, bf16[128,2304]{1,0:T(8,128)(2,1)S(1)}, u32[]{:S(2)}, u32[]{:S(2)}) collective-permute-start(bf16[128,2304]{1,0:T(8,128)(2,1)S(1)} %add_convert_fusion), channel_id=1, source_target_pairs={{0,12},{1,13},{2,14},{3,15},{4,0},{5,1},{6,2},{7,3},{8,4},{9,5},{1... | collective-permute-start | bytes 1769480 | tf_op jit(solution)/shard_map/ppermute | solution.py:28
  154.6 6.3 %collective-permute-done.36 = bf16[128,2304]{1,0:T(8,128)(2,1)S(1)} collective-permute-done((bf16[128,2304]{1,0:T(8,128)(2,1)S(1)}, bf16[128,2304]{1,0:T(8,128)(2,1)S(1)}, u32[]{:S(2)}, u32[]{:S(2)}) %collective-permute-start.36) | collective-permute-done | bytes 589856 | tf_op jit(solution)/shard_map/ppermute | solution.py:28
  168.8 3.2 %collective-permute-start.42 = (f32[64,2304]{1,0:T(8,128)}, f32[64,2304]{1,0:T(8,128)S(1)}, u32[]{:S(2)}, u32[]{:S(2)}) collective-permute-start(f32[64,2304]{1,0:T(8,128)} %pad_maximum_fusion.1), channel_id=1, source_target_pairs={{0,3},{1,0},{2,1},{3,2},{4,7},{5,4},{6,5},{7,6},{8,11},{9,8},{10,9... | collective-permute-start | bytes 1769480 | tf_op jit(solution)/shard_map/ppermute | solution.py:28
  172.7 6.3 %collective-permute-done.40.one_ref = f32[64,2304]{1,0:T(8,128)S(1)} collective-permute-done((f32[64,2304]{1,0:T(8,128)S(1)}, f32[64,2304]{1,0:T(8,128)S(1)}, u32[]{:S(2)}, u32[]{:S(2)}) %collective-permute-start.40) | collective-permute-done | bytes 589856 | tf_op jit(solution)/shard_map/ppermute | solution.py:28
  (117 shorter events, 54.6 us)
Async XLA Ops:
  3.3 20.5 %collective-permute-start.7 = (bf16[64,2304]{1,0:T(8,128)(2,1)S(1)}, bf16[64,2304]{1,0:T(8,128)(2,1)S(1)}, u32[]{:S(2)}, u32[]{:S(2)}) collective-permute-start(bf16[64,2304]{1,0:T(8,128)(2,1)S(1)} %reshape.66.rows_ref.one_ref), channel_id=1, source_target_pairs={{0,1},{1,2},{2,3},{3,0},{4,5},{5,6},{6,7},{7,4},{8,9},{9,10},{10,1... | collective-permute-start | bytes 884744 | tf_op jit(solution)/shard_map/ppermute | solution.py:28
  24.1 13.5 %collective-permute-start.9 = (bf16[128,2304]{1,0:T(8,128)(2,1)S(1)}, bf16[128,2304]{1,0:T(8,128)(2,1)S(1)}, u32[]{:S(2)}, u32[]{:S(2)}) collective-permute-start(bf16[128,2304]{1,0:T(8,128)(2,1)S(1)} %normalize.2.rows_ref.refs_0_), channel_id=1, source_target_pairs={{0,12},{1,13},{2,14},{3,15},{4,0},{5,1},{6,2},{7,3},{8,4},{9,5},{1... | collective-permute-start | bytes 1769480 | tf_op jit(solution)/shard_map/ppermute | solution.py:28
  27.2 11.1 %collective-permute-start.8 = (bf16[128,2304]{1,0:T(8,128)(2,1)S(1)}, bf16[128,2304]{1,0:T(8,128)(2,1)S(1)}, u32[]{:S(2)}, u32[]{:S(2)}) collective-permute-start(bf16[128,2304]{1,0:T(8,128)(2,1)S(1)} %normalize.2.rows_ref.refs_0_), channel_id=1, source_target_pairs={{0,4},{1,5},{2,6},{3,7},{4,8},{5,9},{6,10},{7,11},{8,12},{9,13},{1... | collective-permute-start | bytes 1769480 | tf_op jit(solution)/shard_map/ppermute | solution.py:28
  27.2 10.1 %collective-permute-start.11 = (bf16[64,2304]{1,0:T(8,128)(2,1)S(1)}, bf16[64,2304]{1,0:T(8,128)(2,1)S(1)}, u32[]{:S(2)}, u32[]{:S(2)}) collective-permute-start(bf16[64,2304]{1,0:T(8,128)(2,1)S(1)} %collective-permute-done.7.two_ref), channel_id=1, source_target_pairs={{0,1},{1,2},{2,3},{3,0},{4,5},{5,6},{6,7},{7,4},{8,9},{9,10},{10,1... | collective-permute-start | bytes 884744 | tf_op jit(solution)/shard_map/ppermute | solution.py:28
  27.2 10.1 %collective-permute-start.10 = (bf16[64,2304]{1,0:T(8,128)(2,1)S(1)}, bf16[64,2304]{1,0:T(8,128)(2,1)S(1)}, u32[]{:S(2)}, u32[]{:S(2)}) collective-permute-start(bf16[64,2304]{1,0:T(8,128)(2,1)S(1)} %reshape.66.rows_ref.one_ref), channel_id=1, source_target_pairs={{0,3},{1,0},{2,1},{3,2},{4,7},{5,4},{6,5},{7,6},{8,11},{9,8},{10,9... | collective-permute-start | bytes 884744 | tf_op jit(solution)/shard_map/ppermute | solution.py:28
  38.3 11.1 %collective-permute-start.13 = (bf16[128,2304]{1,0:T(8,128)(2,1)S(1)}, bf16[128,2304]{1,0:T(8,128)(2,1)S(1)}, u32[]{:S(2)}, u32[]{:S(2)}) collective-permute-start(bf16[128,2304]{1,0:T(8,128)(2,1)S(1)} %collective-permute-done.8.refs_1_), channel_id=1, source_target_pairs={{0,4},{1,5},{2,6},{3,7},{4,8},{5,9},{6,10},{7,11},{8,12},{9,13},{1... | collective-permute-start | bytes 1769480 | tf_op jit(solution)/shard_map/ppermute | solution.py:28
  38.3 11.1 %collective-permute-start.15 = (bf16[128,2304]{1,0:T(8,128)(2,1)S(1)}, bf16[128,2304]{1,0:T(8,128)(2,1)S(1)}, u32[]{:S(2)}, u32[]{:S(2)}) collective-permute-start(bf16[128,2304]{1,0:T(8,128)(2,1)S(1)} %normalize.3.refs_4_), channel_id=1, source_target_pairs={{0,12},{1,13},{2,14},{3,15},{4,0},{5,1},{6,2},{7,3},{8,4},{9,5},{1... | collective-permute-start | bytes 1769480 | tf_op jit(solution)/shard_map/ppermute | solution.py:28
  49.4 11.7 %collective-permute-start.14 = (bf16[128,2304]{1,0:T(8,128)(2,1)S(1)}, bf16[128,2304]{1,0:T(8,128)(2,1)S(1)}, u32[]{:S(2)}, u32[]{:S(2)}) collective-permute-start(bf16[128,2304]{1,0:T(8,128)(2,1)S(1)} %normalize.3.refs_4_), channel_id=1, source_target_pairs={{0,4},{1,5},{2,6},{3,7},{4,8},{5,9},{6,10},{7,11},{8,12},{9,13},{1... | collective-permute-start | bytes 1769480 | tf_op jit(solution)/shard_map/ppermute | solution.py:28
  49.4 11.7 %collective-permute-start.16 = (bf16[128,2304]{1,0:T(8,128)(2,1)S(1)}, bf16[128,2304]{1,0:T(8,128)(2,1)S(1)}, u32[]{:S(2)}, u32[]{:S(2)}) collective-permute-start(bf16[128,2304]{1,0:T(8,128)(2,1)S(1)} %collective-permute-done.15.refs_6_), channel_id=1, source_target_pairs={{0,12},{1,13},{2,14},{3,15},{4,0},{5,1},{6,2},{7,3},{8,4},{9,5},{1... | collective-permute-start | bytes 1769480 | tf_op jit(solution)/shard_map/ppermute | solution.py:28
  68.4 12.1 %collective-permute-start.22 = (f32[128,768]{1,0:T(8,128)S(1)}, f32[128,768]{1,0:T(8,128)S(1)}, u32[]{:S(2)}, u32[]{:S(2)}) collective-permute-start(f32[128,768]{1,0:T(8,128)S(1)} %get-tuple-element.97), channel_id=1, source_target_pairs={{0,32},{1,33},{2,34},{3,35},{4,36},{5,37},{6,38},{7,39},{8,40},{9,... | collective-permute-start | bytes 1179656 | tf_op jit(solution)/shard_map/ppermute | solution.py:28
  69.2 11.4 %collective-permute-start.25 = (f32[128,768]{1,0:T(8,128)S(1)}, f32[128,768]{1,0:T(8,128)S(1)}, u32[]{:S(2)}, u32[]{:S(2)}) collective-permute-start(f32[128,768]{1,0:T(8,128)S(1)} %get-tuple-element.98), channel_id=1, source_target_pairs={{0,96},{1,97},{2,98},{3,99},{4,100},{5,101},{6,102},{7,103},{8,104... | collective-permute-start | bytes 1179656 | tf_op jit(solution)/shard_map/ppermute | solution.py:28
  80.5 9.1 %collective-permute-start.24 = (f32[128,768]{1,0:T(8,128)S(1)}, f32[128,768]{1,0:T(8,128)S(1)}, u32[]{:S(2)}, u32[]{:S(2)}) collective-permute-start(f32[128,768]{1,0:T(8,128)S(1)} %slice_add_fusion), channel_id=1, source_target_pairs={{0,32},{1,33},{2,34},{3,35},{4,36},{5,37},{6,38},{7,39},{8,40},{9,... | collective-permute-start | bytes 1179656 | tf_op jit(solution)/shard_map/ppermute | solution.py:28
  118.9 7.4 %collective-permute-start.27 = (bf16[128,768]{1,0:T(8,128)(2,1)S(1)}, bf16[128,768]{1,0:T(8,128)(2,1)S(1)}, u32[]{:S(2)}, u32[]{:S(2)}) collective-permute-start(bf16[128,768]{1,0:T(8,128)(2,1)S(1)} %bitcast.10), channel_id=1, source_target_pairs={{0,96},{1,97},{2,98},{3,99},{4,100},{5,101},{6,102},{7,103},{8,104... | collective-permute-start | bytes 589832 | tf_op jit(solution)/shard_map/ppermute | solution.py:28
  125.8 6.9 %collective-permute-start.28 = (bf16[128,768]{1,0:T(8,128)(2,1)S(1)}, bf16[128,768]{1,0:T(8,128)(2,1)S(1)}, u32[]{:S(2)}, u32[]{:S(2)}) collective-permute-start(bf16[128,768]{1,0:T(8,128)(2,1)S(1)} %collective-permute-done.26.refs_1_), channel_id=1, source_target_pairs={{0,32},{1,33},{2,34},{3,35},{4,36},{5,37},{6,38},{7,39},{8,40},{9,... | collective-permute-start | bytes 589832 | tf_op jit(solution)/shard_map/ppermute | solution.py:28
  125.8 6.9 %collective-permute-start.29 = (bf16[128,768]{1,0:T(8,128)(2,1)S(1)}, bf16[128,768]{1,0:T(8,128)(2,1)S(1)}, u32[]{:S(2)}, u32[]{:S(2)}) collective-permute-start(bf16[128,768]{1,0:T(8,128)(2,1)S(1)} %bitcast.11), channel_id=1, source_target_pairs={{0,16},{16,0},{32,48},{48,32},{64,80},{80,64},{96,112},{112,96},{1... | collective-permute-start | bytes 589832 | tf_op jit(solution)/shard_map/ppermute | solution.py:33
  125.8 6.9 %collective-permute-start.30 = (bf16[128,768]{1,0:T(8,128)(2,1)S(1)}, bf16[128,768]{1,0:T(8,128)(2,1)S(1)}, u32[]{:S(2)}, u32[]{:S(2)}) collective-permute-start(bf16[128,768]{1,0:T(8,128)(2,1)S(1)} %collective-permute-done.26.refs_1_), channel_id=1, source_target_pairs={{0,16},{16,0},{32,48},{48,32},{64,80},{80,64},{96,112},{112,96},{1... | collective-permute-start | bytes 589832 | tf_op jit(solution)/shard_map/ppermute | solution.py:33
  135.9 11.2 %collective-permute-start.34 = (bf16[128,2304]{1,0:T(8,128)(2,1)S(1)}, bf16[128,2304]{1,0:T(8,128)(2,1)S(1)}, u32[]{:S(2)}, u32[]{:S(2)}) collective-permute-start(bf16[128,2304]{1,0:T(8,128)(2,1)S(1)} %get-tuple-element.83), channel_id=1, source_target_pairs={{0,4},{1,5},{2,6},{3,7},{4,8},{5,9},{6,10},{7,11},{8,12},{9,13},{1... | collective-permute-start | bytes 1769480 | tf_op jit(solution)/shard_map/ppermute | solution.py:28
  136.4 10.7 %collective-permute-start.35 = (bf16[128,2304]{1,0:T(8,128)(2,1)S(1)}, bf16[128,2304]{1,0:T(8,128)(2,1)S(1)}, u32[]{:S(2)}, u32[]{:S(2)}) collective-permute-start(bf16[128,2304]{1,0:T(8,128)(2,1)S(1)} %get-tuple-element.84), channel_id=1, source_target_pairs={{0,12},{1,13},{2,14},{3,15},{4,0},{5,1},{6,2},{7,3},{8,4},{9,5},{1... | collective-permute-start | bytes 1769480 | tf_op jit(solution)/shard_map/ppermute | solution.py:28
  143.3 10.0 %collective-permute-start.33 = (bf16[128,2304]{1,0:T(8,128)(2,1)S(1)}, bf16[128,2304]{1,0:T(8,128)(2,1)S(1)}, u32[]{:S(2)}, u32[]{:S(2)}) collective-permute-start(bf16[128,2304]{1,0:T(8,128)(2,1)S(1)} %get-tuple-element.81), channel_id=1, source_target_pairs={{0,12},{1,13},{2,14},{3,15},{4,0},{5,1},{6,2},{7,3},{8,4},{9,5},{1... | collective-permute-start | bytes 1769480 | tf_op jit(solution)/shard_map/ppermute | solution.py:28
  143.4 11.2 %collective-permute-start.37 = (bf16[128,2304]{1,0:T(8,128)(2,1)S(1)}, bf16[128,2304]{1,0:T(8,128)(2,1)S(1)}, u32[]{:S(2)}, u32[]{:S(2)}) collective-permute-start(bf16[128,2304]{1,0:T(8,128)(2,1)S(1)} %get-tuple-element.86), channel_id=1, source_target_pairs={{0,4},{1,5},{2,6},{3,7},{4,8},{5,9},{6,10},{7,11},{8,12},{9,13},{1... | collective-permute-start | bytes 1769480 | tf_op jit(solution)/shard_map/ppermute | solution.py:28
  147.2 13.7 %collective-permute-start.36 = (bf16[128,2304]{1,0:T(8,128)(2,1)S(1)}, bf16[128,2304]{1,0:T(8,128)(2,1)S(1)}, u32[]{:S(2)}, u32[]{:S(2)}) collective-permute-start(bf16[128,2304]{1,0:T(8,128)(2,1)S(1)} %add_convert_fusion.1), channel_id=1, source_target_pairs={{0,4},{1,5},{2,6},{3,7},{4,8},{5,9},{6,10},{7,11},{8,12},{9,13},{1... | collective-permute-start | bytes 1769480 | tf_op jit(solution)/shard_map/ppermute | solution.py:28
  147.5 13.4 %collective-permute-start.38 = (bf16[128,2304]{1,0:T(8,128)(2,1)S(1)}, bf16[128,2304]{1,0:T(8,128)(2,1)S(1)}, u32[]{:S(2)}, u32[]{:S(2)}) collective-permute-start(bf16[128,2304]{1,0:T(8,128)(2,1)S(1)} %add_convert_fusion), channel_id=1, source_target_pairs={{0,12},{1,13},{2,14},{3,15},{4,0},{5,1},{6,2},{7,3},{8,4},{9,5},{1... | collective-permute-start | bytes 1769480 | tf_op jit(solution)/shard_map/ppermute | solution.py:28
  167.8 11.2 %collective-permute-start.40 = (f32[64,2304]{1,0:T(8,128)S(1)}, f32[64,2304]{1,0:T(8,128)S(1)}, u32[]{:S(2)}, u32[]{:S(2)}) collective-permute-start(f32[64,2304]{1,0:T(8,128)S(1)} %pad_maximum_fusion), channel_id=1, source_target_pairs={{0,1},{1,2},{2,3},{3,0},{4,5},{5,6},{6,7},{7,4},{8,9},{9,10},{10,1... | collective-permute-start | bytes 1769480 | tf_op jit(solution)/shard_map/ppermute | solution.py:28
  168.8 10.9 %collective-permute-start.42 = (f32[64,2304]{1,0:T(8,128)}, f32[64,2304]{1,0:T(8,128)S(1)}, u32[]{:S(2)}, u32[]{:S(2)}) collective-permute-start(f32[64,2304]{1,0:T(8,128)} %pad_maximum_fusion.1), channel_id=1, source_target_pairs={{0,3},{1,0},{2,1},{3,2},{4,7},{5,4},{6,5},{7,6},{8,11},{9,8},{10,9... | collective-permute-start | bytes 1769480 | tf_op jit(solution)/shard_map/ppermute | solution.py:28
  (26 other events, 287.2 us)
